TPU v7x, 32 devices: a whole 2x2x4 slice. The times are simulated.
32 devices in a mesh: seq: 16 (over z, y, core), tensor: 2 (over x).
Axes of the slice: x: 2, y: 2, z: 4, core: 2. Of those that a mesh axis runs over, the one named last changes fastest.
Arguments:
- latents: bfloat16 [2, 4096, 1536], P(None, 'seq'), may hold values from -6 to 6
- context: bfloat16 [2, 512, 768], replicated, may hold values from -6 to 6
- lengths: int32 [2, 4], replicated, may hold values from 512 to 1536, as said below
- text_len: int32 [2, 4], replicated, may hold values from 1 to 128, as said below
- timesteps: int32 [2, 4], replicated, may hold values from 0 to 999
- self_qkv: bfloat16 [3, 1536, 1536], P(None, 'seq', 'tensor'), may hold values from -0.15625 to 0.15625
- self_out: bfloat16 [1536, 1536], P('tensor', 'seq'), may hold values from -0.625 to 0.625
- cross_query: bfloat16 [1536, 1536], P('seq', 'tensor'), may hold values from -0.15625 to 0.15625
- cross_kv: bfloat16 [2, 768, 1536], P(None, 'seq', 'tensor'), may hold values from -0.21875 to 0.21875
- cross_out: bfloat16 [1536, 1536], P('tensor', 'seq'), may hold values from -0.4375 to 0.4375
- ffn_in: bfloat16 [2, 1536, 6144], P(None, 'seq', 'tensor'), may hold values from -0.15625 to 0.15625
- ffn_out: bfloat16 [6144, 1536], P('tensor', 'seq'), may hold values from -0.15625 to 0.15625
- mod_weight: bfloat16 [256, 6, 1536], P('seq'), may hold values from -0.1875 to 0.1875
- mod_bias: bfloat16 [6, 1536], P(None, 'seq'), may hold values from -1.5 to 1.5
- out_grad: bfloat16 [2, 4096, 1536], P(None, 'seq'), may hold values from -6 to 6
Outputs:
- block_out: bfloat16 [2, 4096, 1536], P(None, 'seq')
- latent_grad: float32 [2, 4096, 1536], P(None, 'seq')
- grad_self_qkv: float32 [3, 1536, 1536], P(None, 'seq', 'tensor')
- grad_self_out: float32 [1536, 1536], P('tensor', 'seq')
- grad_cross_query: float32 [1536, 1536], P('seq', 'tensor')
- grad_cross_kv: float32 [2, 768, 1536], P(None, 'seq', 'tensor')
- grad_cross_out: float32 [1536, 1536], P('tensor', 'seq')
- grad_ffn_in: float32 [2, 1536, 6144], P(None, 'seq', 'tensor')
- grad_ffn_out: float32 [6144, 1536], P('tensor', 'seq')
- grad_mod_weight: float32 [256, 6, 1536], P('seq')
- grad_mod_bias: float32 [6, 1536], P(None, 'seq')
Inputs may be any that keep to these rules, and one draw needn't show every extreme that they name: Within each micro-batch the lengths sum to 4096; in every micro-batch some item has exactly 1536 frames and some exactly 512. `text_len`: in every micro-batch some item uses all 128 slots and some item one slot.
All inputs are finite; a program needn't handle non-finite values.
Results may differ from a plain program's by a relative error of at most 0.023.
Values may be sent and summed in bfloat16 or wider, within the bound.
A program may use at most 384 MiB of HBM per device.

v0:
```python
import math

import jax
import jax.numpy as jnp
from jax import lax
from jax.sharding import PartitionSpec as P

HD = 64
TXT = 128
TEMB = 256
HALF = 128


norm_eps = 1e-05
highest = lax.Precision.HIGHEST


def padded(block, sides, width):
    for axis, dim in sides:
        count = lax.axis_size(axis)
        forward = [(i, i + 1) for i in range(count - 1)]
        backward = [(target, source) for source, target in forward]
        low = lax.ppermute(
            lax.slice_in_dim(block, block.shape[dim] - width, None, axis=dim), axis, forward
        )
        high = lax.ppermute(lax.slice_in_dim(block, 0, width, axis=dim), axis, backward)
        block = jnp.concatenate([low, block, high], axis=dim)
    return block


def modulated_norm(hidden, offset, factor):
    center = hidden - jnp.mean(hidden, axis=-1, keepdims=True)
    spread = jnp.mean(center * center, axis=-1, keepdims=True)
    return center * lax.rsqrt(spread + norm_eps) * (1.0 + factor) + offset


def rotary(values, places):
    quarter = HD // 4
    ladder = jnp.exp(-math.log(10000.0) * jnp.arange(quarter, dtype=jnp.float32) / quarter)
    angles = places.astype(jnp.float32)[:, None] * ladder[None, :]
    cosine = jnp.cos(angles)[:, None, :]
    sine_part = jnp.sin(angles)[:, None, :]
    first_half = values[..., :quarter]
    second_half = values[..., quarter : 2 * quarter]
    return jnp.concatenate(
        [
            first_half * cosine - second_half * sine_part,
            second_half * cosine + first_half * sine_part,
            values[..., 2 * quarter :],
        ],
        axis=-1,
    )


def time_features(steps_row):
    half_width = TEMB // 2
    ladder = jnp.exp(-math.log(10000.0) * jnp.arange(half_width, dtype=jnp.float32) / half_width)
    angles = steps_row.astype(jnp.float32)[:, None] * ladder[None, :]
    return jnp.concatenate([jnp.cos(angles), jnp.sin(angles)], axis=-1)


def gated(gate_part, up_part):
    return jax.nn.silu(gate_part) * up_part


def masked_scores(query_rows, key_rows, allowed, factor):
    scores = (
        jnp.einsum("qhd,khd->hqk", query_rows, key_rows, preferred_element_type=jnp.float32)
        * factor
    )
    return jnp.where(allowed[None], scores, -1e30)


def attend(query_rows, key_rows, value_rows, allowed, factor):
    scores = masked_scores(query_rows, key_rows, allowed, factor)
    row_peak = jnp.max(scores, axis=-1, keepdims=True)
    log_total = row_peak + jnp.log(jnp.sum(jnp.exp(scores - row_peak), axis=-1, keepdims=True))
    weights = jnp.exp(scores - log_total).astype(jnp.bfloat16)
    mixed = jnp.einsum("hqk,khd->qhd", weights, value_rows, preferred_element_type=jnp.float32)
    return (mixed, log_total)


def attend_back(query_rows, key_rows, value_rows, allowed, factor, log_total, mixed_grad):
    scores = masked_scores(query_rows, key_rows, allowed, factor)
    chances = jnp.exp(scores - log_total)
    weights = chances.astype(jnp.bfloat16)
    chance_grad = jnp.einsum(
        "qhd,khd->hqk", mixed_grad, value_rows, preferred_element_type=jnp.float32
    )
    value_grad = jnp.einsum("hqk,qhd->khd", weights, mixed_grad, preferred_element_type=jnp.float32)
    score_grad = (
        chances * (chance_grad - jnp.sum(chances * chance_grad, axis=-1, keepdims=True))
    ).astype(jnp.bfloat16)
    query_grad = (
        jnp.einsum("hqk,khd->qhd", score_grad, key_rows, preferred_element_type=jnp.float32)
        * factor
    )
    key_grad = (
        jnp.einsum("hqk,qhd->khd", score_grad, query_rows, preferred_element_type=jnp.float32)
        * factor
    )
    return (query_grad, key_grad, value_grad)


def fetch(
    self_qkv, self_out, cross_query, cross_kv, cross_out, ffn_in, ffn_out, mod_weight, mod_bias
):
    return (
        lax.all_gather(self_qkv, "seq", axis=1, tiled=True),
        lax.all_gather(self_out, "seq", axis=1, tiled=True),
        lax.all_gather(cross_query, "seq", axis=0, tiled=True),
        lax.all_gather(cross_kv, "seq", axis=1, tiled=True),
        lax.all_gather(cross_out, "seq", axis=1, tiled=True),
        lax.all_gather(ffn_in, "seq", axis=1, tiled=True),
        lax.all_gather(ffn_out, "seq", axis=1, tiled=True),
        lax.all_gather(mod_weight, "seq", axis=0, tiled=True),
        lax.all_gather(mod_bias, "seq", axis=1, tiled=True),
    )


def spread_grads(grads):
    return (
        lax.psum_scatter(grads[0], "seq", scatter_dimension=1, tiled=True),
        lax.psum_scatter(grads[1], "seq", scatter_dimension=1, tiled=True),
        lax.psum_scatter(grads[2], "seq", scatter_dimension=0, tiled=True),
        lax.psum_scatter(grads[3], "seq", scatter_dimension=1, tiled=True),
        lax.psum_scatter(grads[4], "seq", scatter_dimension=1, tiled=True),
        lax.psum_scatter(grads[5], "seq", scatter_dimension=1, tiled=True),
        lax.psum_scatter(grads[6], "seq", scatter_dimension=1, tiled=True),
        lax.psum_scatter(grads[7], "seq", scatter_dimension=0, tiled=True),
        lax.psum_scatter(grads[8], "seq", scatter_dimension=1, tiled=True),
    )


def on_device(
    latents,
    context,
    lengths,
    text_len,
    timesteps,
    self_qkv,
    self_out,
    cross_query,
    cross_kv,
    cross_out,
    ffn_in,
    ffn_out,
    mod_weight,
    mod_bias,
    out_grad,
):
    block_rows = latents.shape[1]
    model_width = latents.shape[2]
    frame_count = block_rows * lax.axis_size("seq")
    item_count = lengths.shape[1]
    factor = HD ** (-0.5)
    first_frame = lax.axis_index("seq") * block_rows
    own_places = first_frame + jnp.arange(block_rows, dtype=jnp.int32)
    near_places = first_frame - HALF + jnp.arange(block_rows + 2 * HALF, dtype=jnp.int32)
    near_inside = (near_places >= 0) & (near_places < frame_count)
    catalog = jnp.arange(item_count, dtype=jnp.int32)

    def micro_batch(latent, context_rows, lengths_row, text_row, steps_row, cotangent, gathered):
        (
            qkv_weight,
            self_weight,
            query_weight,
            pair_weight,
            cross_weight,
            inner_weight,
            outer_weight,
            mod_full,
            bias_full,
        ) = gathered
        local_width = qkv_weight.shape[2]
        head_count = local_width // HD
        item_ends = jnp.cumsum(lengths_row)
        item_starts = item_ends - lengths_row
        own_ids = jnp.sum((item_ends[None, :] <= own_places[:, None]).astype(jnp.int32), axis=1)
        near_ids = jnp.sum((item_ends[None, :] <= near_places[:, None]).astype(jnp.int32), axis=1)
        choose = own_ids[:, None] == catalog[None, :]
        offsets_in = own_places - jnp.sum(choose.astype(jnp.int32) * item_starts[None, :], axis=1)
        features = time_features(steps_row)
        modulation = jnp.dot(
            features, mod_full.astype(jnp.float32).reshape(mod_full.shape[0], -1), precision=highest
        ) + bias_full.astype(jnp.float32).reshape(1, -1)
        pick = choose.astype(jnp.float32)
        framewise = jnp.dot(pick, modulation, precision=highest).reshape(block_rows, 6, model_width)
        latent_full = latent.astype(jnp.float32)

        def rotate(flat):
            return rotary(flat.reshape(block_rows, head_count, HD), offsets_in).reshape(
                block_rows, local_width
            )

        normed_one = modulated_norm(latent_full, framewise[:, 0], framewise[:, 1]).astype(
            jnp.bfloat16
        )
        projected = jnp.einsum(
            "nd,tde->tne", normed_one, qkv_weight, preferred_element_type=jnp.float32
        )
        query_one = rotate(projected[0]).astype(jnp.bfloat16).reshape(block_rows, head_count, HD)
        key_value = jnp.stack([rotate(projected[1]), projected[2]]).astype(jnp.bfloat16)
        near_pairs = padded(key_value, (("seq", 1),), HALF)
        near_heads = near_pairs.reshape(2, block_rows + 2 * HALF, head_count, HD)
        self_allowed = (
            (own_ids[:, None] == near_ids[None, :])
            & near_inside[None, :]
            & (jnp.abs(own_places[:, None] - near_places[None, :]) <= HALF)
        )
        mixed_one, total_one = attend(query_one, near_heads[0], near_heads[1], self_allowed, factor)
        mixed_one = mixed_one.reshape(block_rows, local_width).astype(jnp.bfloat16)
        hidden_one = latent_full + lax.psum(
            jnp.dot(mixed_one, self_weight, preferred_element_type=jnp.float32), "tensor"
        )
        normed_two = modulated_norm(hidden_one, framewise[:, 2], framewise[:, 3]).astype(
            jnp.bfloat16
        )
        query_two = (
            jnp.dot(normed_two, query_weight, preferred_element_type=jnp.float32)
            .astype(jnp.bfloat16)
            .reshape(block_rows, head_count, HD)
        )
        base_item = jnp.minimum(own_ids[0], item_count - 2)
        near_context = lax.dynamic_slice_in_dim(context_rows, base_item * TXT, 2 * TXT, 0)
        near_text = (
            jnp.einsum("rc,tce->tre", near_context, pair_weight, preferred_element_type=jnp.float32)
            .astype(jnp.bfloat16)
            .reshape(2, 2 * TXT, head_count, HD)
        )
        text_slots = jnp.arange(2 * TXT, dtype=jnp.int32)
        key_items = base_item + text_slots // TXT
        key_lengths = jnp.sum(
            (key_items[:, None] == catalog[None, :]).astype(jnp.int32) * text_row[None, :], axis=1
        )
        cross_allowed = (own_ids[:, None] == key_items[None, :]) & (text_slots % TXT < key_lengths)[
            None, :
        ]
        mixed_two, total_two = attend(query_two, near_text[0], near_text[1], cross_allowed, factor)
        mixed_two = mixed_two.reshape(block_rows, local_width).astype(jnp.bfloat16)
        hidden_two = hidden_one + lax.psum(
            jnp.dot(mixed_two, cross_weight, preferred_element_type=jnp.float32).astype(
                jnp.bfloat16
            ),
            "tensor",
        ).astype(jnp.float32)
        normed_three = modulated_norm(hidden_two, framewise[:, 4], framewise[:, 5]).astype(
            jnp.bfloat16
        )
        gate_up = jnp.einsum(
            "nd,tdf->tnf", normed_three, inner_weight, preferred_element_type=jnp.float32
        )
        activated = gated(gate_up[0], gate_up[1]).astype(jnp.bfloat16)
        block_out = hidden_two + lax.psum(
            jnp.dot(activated, outer_weight, preferred_element_type=jnp.float32).astype(
                jnp.bfloat16
            ),
            "tensor",
        ).astype(jnp.float32)
        outer_grad = jnp.einsum(
            "nf,nd->fd", activated, cotangent, preferred_element_type=jnp.float32
        )
        activated_grad = jnp.einsum(
            "nd,fd->nf", cotangent, outer_weight, preferred_element_type=jnp.float32
        )
        gate_grad, up_grad = jax.vjp(gated, gate_up[0], gate_up[1])[1](activated_grad)
        gate_up_grad = jnp.stack([gate_grad, up_grad]).astype(jnp.bfloat16)
        inner_grad = jnp.einsum(
            "nd,tnf->tdf", normed_three, gate_up_grad, preferred_element_type=jnp.float32
        )
        normed_three_grad = lax.psum(
            jnp.einsum(
                "tnf,tdf->nd", gate_up_grad, inner_weight, preferred_element_type=jnp.float32
            ).astype(jnp.bfloat16),
            "tensor",
        ).astype(jnp.float32)
        hidden_three_part, offset_three, factor_three = jax.vjp(
            modulated_norm, hidden_two, framewise[:, 4], framewise[:, 5]
        )[1](normed_three_grad)
        hidden_two_grad = cotangent.astype(jnp.float32) + hidden_three_part
        two_low = hidden_two_grad.astype(jnp.bfloat16)
        cross_grad = jnp.einsum("nh,nd->hd", mixed_two, two_low, preferred_element_type=jnp.float32)
        mixed_two_grad = (
            jnp.einsum("nd,hd->nh", two_low, cross_weight, preferred_element_type=jnp.float32)
            .astype(jnp.bfloat16)
            .reshape(block_rows, head_count, HD)
        )
        query_two_grad, text_key_grad, text_value_grad = attend_back(
            query_two, near_text[0], near_text[1], cross_allowed, factor, total_two, mixed_two_grad
        )
        query_two_low = query_two_grad.reshape(block_rows, local_width).astype(jnp.bfloat16)
        query_grad = jnp.einsum(
            "nd,ne->de", normed_two, query_two_low, preferred_element_type=jnp.float32
        )
        normed_two_part = jnp.einsum(
            "ne,de->nd", query_two_low, query_weight, preferred_element_type=jnp.float32
        )
        text_grads = (
            jnp.stack([text_key_grad, text_value_grad])
            .reshape(2, 2 * TXT, local_width)
            .astype(jnp.bfloat16)
        )
        pair_grad = jnp.einsum(
            "rc,tre->tce", near_context, text_grads, preferred_element_type=jnp.float32
        )
        normed_two_grad = lax.psum(normed_two_part.astype(jnp.bfloat16), "tensor").astype(
            jnp.float32
        )
        hidden_two_part, offset_two, factor_two = jax.vjp(
            modulated_norm, hidden_one, framewise[:, 2], framewise[:, 3]
        )[1](normed_two_grad)
        hidden_one_grad = hidden_two_grad + hidden_two_part
        one_low = hidden_one_grad.astype(jnp.bfloat16)
        self_grad = jnp.einsum("nh,nd->hd", mixed_one, one_low, preferred_element_type=jnp.float32)
        mixed_one_grad = (
            jnp.einsum("nd,hd->nh", one_low, self_weight, preferred_element_type=jnp.float32)
            .astype(jnp.bfloat16)
            .reshape(block_rows, head_count, HD)
        )
        query_one_grad, near_key_grad, near_value_grad = attend_back(
            query_one, near_heads[0], near_heads[1], self_allowed, factor, total_one, mixed_one_grad
        )
        near_grads = jnp.stack([near_key_grad, near_value_grad]).reshape(
            2, block_rows + 2 * HALF, local_width
        )
        rim_grads = jnp.concatenate(
            [near_grads[:, :HALF], near_grads[:, block_rows + HALF :]], axis=1
        )
        returned = padded(rim_grads.astype(jnp.bfloat16), (("seq", 1),), HALF).astype(
            rim_grads.dtype
        )
        pair_grads = near_grads[:, HALF : HALF + block_rows]
        pair_grads = pair_grads + jnp.pad(
            returned[:, :HALF], ((0, 0), (0, block_rows - HALF), (0, 0))
        )
        pair_grads = pair_grads + jnp.pad(
            returned[:, 3 * HALF :], ((0, 0), (block_rows - HALF, 0), (0, 0))
        )
        rotate_back = jax.vjp(rotate, projected[0])[1]
        projected_grad = jnp.stack(
            [
                rotate_back(query_one_grad.reshape(block_rows, local_width))[0],
                rotate_back(pair_grads[0])[0],
                pair_grads[1],
            ]
        ).astype(jnp.bfloat16)
        qkv_grad = jnp.einsum(
            "nd,tne->tde", normed_one, projected_grad, preferred_element_type=jnp.float32
        )
        normed_one_grad = lax.psum(
            jnp.einsum(
                "tne,tde->nd", projected_grad, qkv_weight, preferred_element_type=jnp.float32
            ).astype(jnp.bfloat16),
            "tensor",
        ).astype(jnp.float32)
        latent_part, offset_one, factor_one = jax.vjp(
            modulated_norm, latent_full, framewise[:, 0], framewise[:, 1]
        )[1](normed_one_grad)
        latent_grad = hidden_one_grad + latent_part
        framewise_grad = jnp.stack(
            [offset_one, factor_one, offset_two, factor_two, offset_three, factor_three], axis=1
        ).reshape(block_rows, -1)
        item_grad = jnp.dot(pick.T, framewise_grad, precision=highest)
        mod_grad = jnp.dot(features.T, item_grad, precision=highest).reshape(mod_full.shape)
        bias_grad = jnp.sum(item_grad, axis=0).reshape(bias_full.shape)
        grads = (
            qkv_grad,
            self_grad,
            query_grad,
            pair_grad,
            cross_grad,
            inner_grad,
            outer_grad,
            mod_grad,
            bias_grad,
        )
        return (block_out.astype(jnp.bfloat16), latent_grad, grads)

    results = []
    input_grads = []
    summed = None
    for micro_index in range(latents.shape[0]):
        gathered = fetch(
            self_qkv,
            self_out,
            cross_query,
            cross_kv,
            cross_out,
            ffn_in,
            ffn_out,
            mod_weight,
            mod_bias,
        )
        block_out, latent_grad, grads = micro_batch(
            latents[micro_index],
            context[micro_index],
            lengths[micro_index],
            text_len[micro_index],
            timesteps[micro_index],
            out_grad[micro_index],
            gathered,
        )
        results.append(block_out)
        input_grads.append(latent_grad)
        shares = spread_grads(grads)
        summed = shares if summed is None else jax.tree.map(jnp.add, summed, shares)
    return (jnp.stack(results), jnp.stack(input_grads)) + tuple(summed)


def solution(mesh):
    return jax.shard_map(
        on_device,
        mesh=mesh,
        in_specs=(
            P(None, "seq", None),
            P(),
            P(),
            P(),
            P(),
            P(None, "seq", "tensor"),
            P("tensor", "seq"),
            P("seq", "tensor"),
            P(None, "seq", "tensor"),
            P("tensor", "seq"),
            P(None, "seq", "tensor"),
            P("tensor", "seq"),
            P("seq", None, None),
            P(None, "seq"),
            P(None, "seq", None),
        ),
        out_specs=(
            P(None, "seq", None),
            P(None, "seq", None),
            P(None, "seq", "tensor"),
            P("tensor", "seq"),
            P("seq", "tensor"),
            P(None, "seq", "tensor"),
            P("tensor", "seq"),
            P(None, "seq", "tensor"),
            P("tensor", "seq"),
            P("seq", None, None),
            P(None, "seq"),
        ),
        check_vma=False,
    )
```

profile of v0, /device:TPU:0, one launch (start us, length us, event | category | flops | bytes accessed | tf_op | source)
XLA Modules:
  0.0 2583.2 jit_solution(16061919408594287471)
XLA Ops:
  10.1 23.5 all-gather
  40.9 25.6 all-gather.10.cloned.1.call-done
  115.5 18.5 all-gather.12.cloned.1.call-done
  204.1 25.0 all-gather.16.cloned.1.call-done
  244.5 71.6 %all-reduce.33.cloned.1.call-done = (f32[256,1536]{1,0:T(8,128)}, f32[256,1536]{1,0:T(8,128)}) async-done(((f32[256,1536]{1,0:T(8,128)}, f32[256,1536]{1,0:T(8,128)}), (f32[256,1536]{1,0:T(8,128)}, f32[256,1536]{1,0:T(8,128)})) %all-reduce.33.cloned.1.call-update) | async-done | bytes 3145744 | tf_op jit(solution)/shard_map/psum | solution.py:213
  322.9 37.9 %all-gather.18.cloned.1.call-done = bf16[1536,768]{1,0:T(8,128)(2,1)} async-done(((bf16[96,768]{1,0:T(8,128)(2,1)}), bf16[1536,768]{1,0:T(8,128)(2,1)}) %all-gather.18.cloned.1.call-update) | async-done | bytes 2359312 | tf_op jit(solution)/shard_map/all_gather | solution.py:111
  377.3 27.1 %all-gather.20.cloned.1.call-done = bf16[768,1536]{0,1:T(8,128)(2,1)} async-done(((bf16[768,96]{0,1:T(8,128)(2,1)}), bf16[768,1536]{0,1:T(8,128)(2,1)}) %all-gather.20.cloned.1.call-update) | async-done | bytes 2359312 | tf_op jit(solution)/shard_map/all_gather | solution.py:113
  421.2 39.6 %all-reduce.41.cloned.1.call-done = (bf16[256,1536]{1,0:T(8,128)(2,1)}, bf16[256,1536]{1,0:T(8,128)(2,1)}) async-done(((bf16[256,1536]{1,0:T(8,128)(2,1)}, bf16[256,1536]{1,0:T(8,128)(2,1)}), (bf16[256,1536]{1,0:T(8,128)(2,1)}, bf16[256,1536]{1,0:T(8,128)(2,1)})) %all-reduce.41.cloned.1.call-update) | async-done | bytes 1572880 | tf_op jit(solution)/shard_map/psum | solution.py:241
  470.1 91.2 %all-gather.22.cloned.1.call-done = bf16[2,1536,3072]{2,1,0:T(8,128)(2,1)} async-done(((bf16[2,96,3072]{2,1,0:T(8,128)(2,1)}), bf16[2,1536,3072]{2,1,0:T(8,128)(2,1)}) %all-gather.22.cloned.1.call-update) | async-done | bytes 18874384 | tf_op jit(solution)/shard_map/all_gather | solution.py:114
  561.3 11.1 convolution_bitcast_fusion
  582.9 62.0 %all-gather.24.cloned.1.call-done = bf16[3072,1536]{0,1:T(8,128)(2,1)} async-done(((bf16[3072,96]{0,1:T(8,128)(2,1)}), bf16[3072,1536]{0,1:T(8,128)(2,1)}) %all-gather.24.cloned.1.call-update) | async-done | bytes 9437200 | tf_op jit(solution)/shard_map/all_gather | solution.py:115
  659.5 11.1 fusion.22
  670.6 10.2 fusion.20
  680.9 49.9 %all-reduce.39.cloned.1.call-done = (bf16[256,1536]{1,0:T(8,128)(2,1)}, bf16[256,1536]{1,0:T(8,128)(2,1)}) async-done(((bf16[256,1536]{1,0:T(8,128)(2,1)}, bf16[256,1536]{1,0:T(8,128)(2,1)}), (bf16[256,1536]{1,0:T(8,128)(2,1)}, bf16[256,1536]{1,0:T(8,128)(2,1)})) %all-reduce.39.cloned.1.call-update) | async-done | bytes 1572880 | tf_op jit(solution)/shard_map/psum | solution.py:271
  780.7 33.1 %all-reduce.37.cloned.1.call-done = (bf16[256,1536]{1,0:T(8,128)(2,1)}, bf16[256,1536]{1,0:T(8,128)(2,1)}) async-done(((bf16[256,1536]{1,0:T(8,128)(2,1)}, bf16[256,1536]{1,0:T(8,128)(2,1)}), (bf16[256,1536]{1,0:T(8,128)(2,1)}, bf16[256,1536]{1,0:T(8,128)(2,1)})) %all-reduce.37.cloned.1.call-update) | async-done | bytes 1572880 | tf_op jit(solution)/shard_map/psum | solution.py:306
  944.3 17.4 fusion.26
  978.9 57.8 %all-reduce.35.cloned.1.call-done = (bf16[256,1536]{1,0:T(8,128)(2,1)}, bf16[256,1536]{1,0:T(8,128)(2,1)}, bf16[256,1536]{1,0:T(8,128)(2,1)}, bf16[256,1536]{1,0:T(8,128)(2,1)}) async-done(((bf16[256,1536]{1,0:T(8,128)(2,1)}, bf16[256,1536]{1,0:T(8,128)(2,1)}, bf16[256,1536]{1,0:T(8,128)(2,1)}, bf16[256,1536]{1,0:T(8,128)(2,1)}), (bf16[256,1536]{1,0:T(8,128)(2,1)}, bf16[256,1536]{1,0:T(8,128)(2,1)}, ...) | async-done | bytes 3145744 | tf_op jit(solution)/shard_map/psum | solution.py:254
  1090.2 28.9 %add_bitcast_fusion = f32[2,1536,3072]{1,2,0:T(8,128)} fusion(f32[2,3072,1536]{2,1,0:T(8,128)} %fusion.26, bf16[256,1536,1]{1,0,2:T(8,128)(2,1)S(1)} %copy-done.75, bf16[1,256,3072]{2,1,0:T(8,128)(2,1)} %copy-done.151, bf16[1,256,3072]{2,1,0:T(8,128)(2,1)S(1)} %copy-done.150), kind=kOutput, calls=%fused_computation | convolution fusion | flops 4842848256 | bytes 79429632 | tf_op jit(solution)/shard_map/nd,tnf->tdf/dot_general | solution.py:268
  1119.1 55.6 %copy.356 = f32[2,1536,3072]{2,0,1:T(2,128)} copy(f32[2,1536,3072]{1,2,0:T(8,128)} %add_bitcast_fusion) | data formatting | bytes 75497472 | tf_op jit(solution)/shard_map/add | solution.py:406
  1183.0 10.7 convolution_add_fusion.1
  1203.3 11.9 copy.360
  1225.9 20.4 copy.379
  1246.3 14.8 copy.396
  1278.2 13.2 fusion.80
  1291.4 18.0 convolution_add_fusion
  1326.4 524.3 %all-reduce.31.cloned.1.call-done = f32[2,1536,3072]{2,0,1:T(2,128)} async-done(((f32[2,1536,3072]{2,0,1:T(2,128)}), f32[2,1536,3072]{2,0,1:T(2,128)}) %all-reduce.31.cloned.1.call-update) | async-done | bytes 37748752
  1854.7 135.4 %reduce-scatter.20.cloned.1.call-done = f32[16,6,1536]{2,1,0:T(8,128)} async-done(((f32[256,6,1536]{2,1,0:T(8,128)}), f32[16,6,1536]{2,1,0:T(8,128)}) %reduce-scatter.20.cloned.1.call-update) | async-done | bytes 589840 | tf_op jit(solution)/shard_map/reduce_scatter | solution.py:130
  1992.3 147.1 %reduce-scatter.22.cloned.1.call-done = f32[96,2304]{1,0:T(8,128)} async-done(((f32[1536,2304]{1,0:T(8,128)}), f32[96,2304]{1,0:T(8,128)}) %reduce-scatter.22.cloned.1.call-update) | async-done | bytes 884752
  2142.1 76.9 %reduce-scatter.14.cloned.1.call-done = f32[96,768]{1,0:T(8,128)} async-done(((f32[1536,768]{1,0:T(8,128)}), f32[96,768]{1,0:T(8,128)}) %reduce-scatter.14.cloned.1.call-update) | async-done | bytes 294928 | tf_op jit(solution)/shard_map/reduce_scatter | solution.py:125
  2219.0 78.9 %reduce-scatter.16.cloned.1.call-done = f32[768,96]{0,1:T(8,128)} async-done(((f32[768,1536]{0,1:T(8,128)}), f32[768,96]{0,1:T(8,128)}) %reduce-scatter.16.cloned.1.call-update) | async-done | bytes 294928 | tf_op jit(solution)/shard_map/reduce_scatter | solution.py:127
  2297.9 79.6 %reduce-scatter.12.cloned.1.call-done = f32[768,96]{0,1:T(8,128)} async-done(((f32[768,1536]{0,1:T(8,128)}), f32[768,96]{0,1:T(8,128)}) %reduce-scatter.12.cloned.1.call-update) | async-done | bytes 294928 | tf_op jit(solution)/shard_map/reduce_scatter | solution.py:124
  2377.4 198.7 %reduce-scatter.18.cloned.1.call-done = f32[3072,96]{0,1:T(8,128)} async-done(((f32[3072,1536]{0,1:T(8,128)}), f32[3072,96]{0,1:T(8,128)}) %reduce-scatter.18.cloned.1.call-update) | async-done | bytes 1179664 | tf_op jit(solution)/shard_map/reduce_scatter | solution.py:129
  (892 shorter events, 536.4 us)
Async XLA Ops:
  7.2 59.3 %all-gather.10.cloned.1.call-start = ((), (), s32[]{:S(2)}) async-start(), calls=%async_computation.7 | async-start | bytes 5013504 | tf_op jit(solution)/shard_map/all_gather | solution.py:116
  7.9 126.1 %all-gather.12.cloned.1.call-start = ((), (), s32[]{:S(2)}) async-start(), calls=%async_computation.8 | async-start | bytes 7520256 | tf_op jit(solution)/shard_map/all_gather | solution.py:109
  8.7 177.7 %all-gather.14.cloned.1.call-start = ((), (), s32[]{:S(2)}) async-start(), calls=%async_computation.9 | async-start | bytes 2506752 | tf_op jit(solution)/shard_map/all_gather | solution.py:110
  9.4 219.7 %all-gather.16.cloned.1.call-start = ((), (), s32[]{:S(2)}) async-start(), calls=%async_computation.10 | async-start | bytes 2506752 | tf_op jit(solution)/shard_map/all_gather | solution.py:112
  10.0 306.1 %all-reduce.33.cloned.1.call-start = ((), (), s32[]{:S(2)}) async-start(), calls=%async_computation.24 | async-start | bytes 6291456 | tf_op jit(solution)/shard_map/psum | solution.py:213
  152.3 15.0 collective-permute-start.3
  153.6 13.7 collective-permute-start.2
  162.0 7.3 collective-permute-start.1
  163.3 6.0 collective-permute-start
  197.5 163.3 %all-gather.18.cloned.1.call-start = ((), (), s32[]{:S(2)}) async-start(), calls=%async_computation.11 | async-start | bytes 2506752 | tf_op jit(solution)/shard_map/all_gather | solution.py:111
  198.1 206.4 %all-gather.20.cloned.1.call-start = ((), (), s32[]{:S(2)}) async-start(), calls=%async_computation.12 | async-start | bytes 2506752 | tf_op jit(solution)/shard_map/all_gather | solution.py:113
  198.8 262.0 %all-reduce.41.cloned.1.call-start = ((), (), s32[]{:S(2)}) async-start(), calls=%async_computation.28 | async-start | bytes 3145728 | tf_op jit(solution)/shard_map/psum | solution.py:241
  410.2 151.2 %all-gather.22.cloned.1.call-start = ((), (), s32[]{:S(2)}) async-start(), calls=%async_computation.13 | async-start | bytes 20054016 | tf_op jit(solution)/shard_map/all_gather | solution.py:114
  410.9 234.0 %all-gather.24.cloned.1.call-start = ((), (), s32[]{:S(2)}) async-start(), calls=%async_computation.14 | async-start | bytes 10027008 | tf_op jit(solution)/shard_map/all_gather | solution.py:115
  411.5 319.3 %all-reduce.39.cloned.1.call-start = ((), (), s32[]{:S(2)}) async-start(), calls=%async_computation.27 | async-start | bytes 3145728 | tf_op jit(solution)/shard_map/psum | solution.py:271
  462.2 602.9 %copy-start.1 = (f32[256,1536]{1,0:T(8,128)}, f32[256,1536]{1,0:T(8,128)S(1)}, u32[]{:S(2)}) copy-start(f32[256,1536]{1,0:T(8,128)S(1)} %get-tuple-element.103) | copy-start | bytes 4718596
  464.4 584.3 %copy-start.3 = (f32[256,1536]{1,0:T(8,128)}, f32[256,1536]{1,0:T(8,128)S(1)}, u32[]{:S(2)}) copy-start(f32[256,1536]{1,0:T(8,128)S(1)} %get-tuple-element.101) | copy-start | bytes 4718596
  680.8 133.0 %all-reduce.37.cloned.1.call-start = ((), (), s32[]{:S(2)}) async-start(), calls=%async_computation.26 | async-start | bytes 3145728 | tf_op jit(solution)/shard_map/psum | solution.py:306
  762.0 274.7 %all-reduce.35.cloned.1.call-start = ((), (), s32[]{:S(2)}) async-start(), calls=%async_computation.25 | async-start | bytes 6291456 | tf_op jit(solution)/shard_map/psum | solution.py:254
  876.2 19.3 collective-permute-start.5
  877.5 18.0 collective-permute-start.4
  889.7 8.6 collective-permute-start.7
  891.1 7.2 collective-permute-start.6
  944.0 367.9 %all-reduce.29.cloned.1.call-start = ((), (), s32[]{:S(2)}) async-start(), calls=%async_computation.22 | async-start | bytes 9437184
  978.9 346.1 %reduce-scatter.24.cloned.1.call-start = ((), (), s32[]{:S(2)}) async-start(), calls=%async_computation.21 | async-start | bytes 835584
  1090.2 760.6 %all-reduce.31.cloned.1.call-start = ((), (), s32[]{:S(2)}) async-start(), calls=%async_computation.23 | async-start | bytes 75497472
  1174.7 815.3 %reduce-scatter.20.cloned.1.call-start = ((), (), s32[]{:S(2)}) async-start(), calls=%async_computation.19 | async-start | bytes 13369344 | tf_op jit(solution)/shard_map/reduce_scatter | solution.py:130
  1215.3 924.1 %reduce-scatter.22.cloned.1.call-start = ((), (), s32[]{:S(2)}) async-start(), calls=%async_computation.20 | async-start | bytes 15040512
  1261.1 957.9 %reduce-scatter.14.cloned.1.call-start = ((), (), s32[]{:S(2)}) async-start(), calls=%async_computation.16 | async-start | bytes 5013504 | tf_op jit(solution)/shard_map/reduce_scatter | solution.py:125
  1266.1 1031.7 %reduce-scatter.16.cloned.1.call-start = ((), (), s32[]{:S(2)}) async-start(), calls=%async_computation.17 | async-start | bytes 5013504 | tf_op jit(solution)/shard_map/reduce_scatter | solution.py:127
  1271.2 1106.2 %reduce-scatter.12.cloned.1.call-start = ((), (), s32[]{:S(2)}) async-start(), calls=%async_computation.15 | async-start | bytes 5013504 | tf_op jit(solution)/shard_map/reduce_scatter | solution.py:124
  1276.8 1299.3 %reduce-scatter.18.cloned.1.call-start = ((), (), s32[]{:S(2)}) async-start(), calls=%async_computation.18 | async-start | bytes 20054016 | tf_op jit(solution)/shard_map/reduce_scatter | solution.py:129
  (272 other events, 1892.1 us)
Sparse Core Ops, SparseCore 0:
  10.3 56.1 all-gather.9
  68.8 65.1 all-gather.11
  136.3 50.0 all-gather.13
  188.5 40.5 all-gather.15
  231.3 84.7 all-reduce.32
  318.5 42.2 all-gather.17
  363.3 41.1 all-gather.19
  410.3 50.4 all-reduce.40
  462.3 98.9 all-gather.21
  563.4 81.4 all-gather.23
  680.9 49.7 all-reduce.38
  762.1 51.6 all-reduce.36
  944.1 92.5 all-reduce.34
  1040.6 117.0 all-reduce.28
  1161.5 56.2 reduce-scatter.23
  1221.8 628.8 all-reduce.30
  1855.2 134.8 reduce-scatter.19
  1994.6 144.7 reduce-scatter.21
  2144.3 74.6 reduce-scatter.13
  2223.2 74.5 reduce-scatter.15
  2302.8 74.5 reduce-scatter.11
  2382.1 193.9 reduce-scatter.17
where the time goes:
time: 2590 us; the launch traced here: 2580 us
  waiting for transfers between devices  1790 us (69%)
  matrix products  331 us (13%)
  local copies, waits for them, and re-layouts  300 us (12%)
  other arithmetic  97.1 us (4%)
    unnamed x26, waiting for transfers between devices  677 us
    reduce_scatter x1, waiting for transfers between devices, spread_grads(): lax.psum_scatter(grads[6], 'seq', scatter_dimension=1, tiled=True)  199 us
    reduce_scatter x1, waiting for transfers between devices, spread_grads(): lax.psum_scatter(grads[7], 'seq', scatter_dimension=0, tiled=True)  135 us
    unnamed x568, local copies, waits for them, and re-layouts  124 us
    all_gather x1, waiting for transfers between devices, fetch(): lax.all_gather(ffn_in, 'seq', axis=1, tiled=True)  91.2 us
    add x5, local copies, waits for them, and re-layouts, on_device(): summed = shares if summed is None else jax.tree.map(jnp.add, summed, shares)  85.3 us
    reduce_scatter x1, waiting for transfers between devices, spread_grads(): lax.psum_scatter(grads[1], 'seq', scatter_dimension=1, tiled=True)  79.6 us
    reduce_scatter x1, waiting for transfers between devices, spread_grads(): lax.psum_scatter(grads[4], 'seq', scatter_dimension=1, tiled=True)  78.9 us
  transfers between devices with their start and end apart: 30, of which 20 were waited for; matrix products, arithmetic and copies ran while one was open for 20% of the time, Pallas kernels for 0%

commit v1 on v0

v1 whole, which is shorter than its diff:
```python
import math

import jax
import jax.numpy as jnp
from jax import lax
from jax.sharding import PartitionSpec as P

HD = 64
TXT = 128
TEMB = 256
HALF = 128


norm_eps = 1e-05
highest = lax.Precision.HIGHEST
f32 = jnp.float32
bf16 = jnp.bfloat16


def dot(a, b, dims):
    return lax.dot_general(a, b, ((dims[0], dims[1]), ((), ())), preferred_element_type=f32)


def nn(a, b):
    return dot(a, b, ((1,), (0,)))


def nt(a, b):
    return dot(a, b, ((1,), (1,)))


def tn(a, b):
    return dot(a, b, ((0,), (0,)))


def halves(count):
    stride = 1
    strides = []
    while stride < count:
        strides.append(stride)
        stride *= 2
    return strides


def flip(block, stride):
    count = lax.axis_size("seq")
    return lax.ppermute(block, "seq", [(i, i ^ stride) for i in range(count)])


def pair_sum(part):
    count = lax.axis_size("tensor")
    other = lax.ppermute(part, "tensor", [(i, (i + 1) % count) for i in range(count)])
    return part.astype(f32) + other.astype(f32)


def seq_sum(part):
    for stride in halves(lax.axis_size("seq")):
        part = part + flip(part, stride)
    return part


def scatter_sum(grad):
    count = lax.axis_size("seq")
    me = lax.axis_index("seq")
    width = grad.shape[1]
    rows = grad.shape[0] // count
    cur = grad.reshape(count, rows, width)
    for stride in halves(count):
        digit = (me // stride) % 2
        pairs = cur.reshape(cur.shape[0] // 2, 2, rows, width)
        kept = lax.dynamic_index_in_dim(pairs, digit, 1, keepdims=False)
        sent = lax.dynamic_index_in_dim(pairs, 1 - digit, 1, keepdims=False)
        got = flip(sent, stride)
        cur = kept.astype(f32) + got.astype(f32)
        if cur.shape[0] > 1:
            cur = cur.astype(bf16)
    return cur[0]


def rotary_tables(places):
    quarter = HD // 4
    ladder = jnp.exp(-math.log(10000.0) * jnp.arange(quarter, dtype=f32) / quarter)
    angles = places.astype(f32)[:, None] * ladder[None, :]
    return jnp.cos(angles), jnp.sin(angles)


def rotate(values, cosine, sine, sign):
    rows, width = values.shape
    quarter = HD // 4
    heads = values.reshape(rows, width // HD, HD)
    cosine = cosine[:, None, :]
    sine = sign * sine[:, None, :]
    first = heads[..., :quarter]
    second = heads[..., quarter : 2 * quarter]
    return jnp.concatenate(
        [
            first * cosine - second * sine,
            second * cosine + first * sine,
            heads[..., 2 * quarter :],
        ],
        axis=-1,
    ).reshape(rows, width)


def time_features(steps_row):
    half_width = TEMB // 2
    ladder = jnp.exp(-math.log(10000.0) * jnp.arange(half_width, dtype=f32) / half_width)
    angles = steps_row.astype(f32)[:, None] * ladder[None, :]
    return jnp.concatenate([jnp.cos(angles), jnp.sin(angles)], axis=-1)


def normalize(hidden):
    center = hidden - jnp.mean(hidden, axis=-1, keepdims=True)
    spread = jnp.mean(center * center, axis=-1, keepdims=True)
    scale = lax.rsqrt(spread + norm_eps)
    return center * scale, scale


def masked_scores(query_rows, key_rows, allowed, factor):
    scores = (
        jnp.einsum("mqhd,mkhd->mhqk", query_rows, key_rows, preferred_element_type=f32) * factor
    )
    return jnp.where(allowed[:, None], scores, -1e30)


def attend(query_rows, key_rows, value_rows, allowed, factor):
    scores = masked_scores(query_rows, key_rows, allowed, factor)
    row_peak = jnp.max(scores, axis=-1, keepdims=True)
    log_total = row_peak + jnp.log(jnp.sum(jnp.exp(scores - row_peak), axis=-1, keepdims=True))
    weights = jnp.exp(scores - log_total).astype(bf16)
    mixed = jnp.einsum("mhqk,mkhd->mqhd", weights, value_rows, preferred_element_type=f32)
    return (mixed, log_total)


def attend_back(query_rows, key_rows, value_rows, allowed, factor, log_total, mixed_grad):
    scores = masked_scores(query_rows, key_rows, allowed, factor)
    chances = jnp.exp(scores - log_total)
    weights = chances.astype(bf16)
    chance_grad = jnp.einsum("mqhd,mkhd->mhqk", mixed_grad, value_rows, preferred_element_type=f32)
    value_grad = jnp.einsum("mhqk,mqhd->mkhd", weights, mixed_grad, preferred_element_type=f32)
    score_grad = (
        chances * (chance_grad - jnp.sum(chances * chance_grad, axis=-1, keepdims=True))
    ).astype(bf16)
    query_grad = (
        jnp.einsum("mhqk,mkhd->mqhd", score_grad, key_rows, preferred_element_type=f32) * factor
    )
    key_grad = (
        jnp.einsum("mhqk,mqhd->mkhd", score_grad, query_rows, preferred_element_type=f32) * factor
    )
    return (query_grad, key_grad, value_grad)


def on_device(
    latents,
    context,
    lengths,
    text_len,
    timesteps,
    self_qkv,
    self_out,
    cross_query,
    cross_kv,
    cross_out,
    ffn_in,
    ffn_out,
    mod_weight,
    mod_bias,
    out_grad,
):
    micro, block_rows, model_width = latents.shape
    seq_count = lax.axis_size("seq")
    me = lax.axis_index("seq")
    frame_count = block_rows * seq_count
    item_count = lengths.shape[1]
    local = self_qkv.shape[2]
    hidden = ffn_in.shape[2]
    heads = local // HD
    rows = micro * block_rows
    text_width = context.shape[2]
    factor = HD ** (-0.5)

    attn_share = jnp.concatenate(
        [
            self_qkv[0],
            self_qkv[1],
            self_qkv[2],
            self_out.T,
            cross_query,
            cross_out.T,
            jnp.concatenate([cross_kv[0], cross_kv[1]], axis=0),
        ],
        axis=1,
    )
    ffn_share = jnp.concatenate([ffn_out.T, ffn_in[0], ffn_in[1]], axis=1)
    attn_all = lax.all_gather(attn_share, "seq", axis=0, tiled=True)
    ffn_all = lax.all_gather(ffn_share, "seq", axis=0, tiled=True)
    qkv_w = attn_all[:, : 3 * local]
    self_wt = attn_all[:, 3 * local : 4 * local]
    query_w = attn_all[:, 4 * local : 5 * local]
    cross_wt = attn_all[:, 5 * local : 6 * local]
    pair_w = attn_all[:, 6 * local :].reshape(seq_count, 2, text_width // seq_count, local)
    key_w = pair_w[:, 0].reshape(text_width, local)
    value_w = pair_w[:, 1].reshape(text_width, local)
    outer_wt = ffn_all[:, :hidden]
    inner_w = ffn_all[:, hidden:]
    gate_w = inner_w[:, :hidden]
    up_w = inner_w[:, hidden:]

    features = time_features(timesteps.reshape(-1))
    own_features = lax.dynamic_slice_in_dim(
        features, me * mod_weight.shape[0], mod_weight.shape[0], 1
    )
    bias_share = mod_bias.shape[1]
    bias_wide = lax.dynamic_update_slice_in_dim(
        jnp.zeros((6, model_width), f32), mod_bias.astype(f32), me * bias_share, 1
    )
    mod_part = jnp.dot(
        own_features, mod_weight.astype(f32).reshape(mod_weight.shape[0], -1), precision=highest
    ) + bias_wide.reshape(1, -1)
    modulation = seq_sum(mod_part).reshape(micro, item_count, 6, model_width)

    first_frame = me * block_rows
    own_places = first_frame + jnp.arange(block_rows, dtype=jnp.int32)
    near_places = first_frame - HALF + jnp.arange(block_rows + 2 * HALF, dtype=jnp.int32)
    near_inside = (near_places >= 0) & (near_places < frame_count)
    item_ends = jnp.cumsum(lengths, axis=1)
    item_starts = item_ends - lengths
    own_ids = jnp.sum(
        (item_ends[:, None, :] <= own_places[None, :, None]).astype(jnp.int32), axis=2
    )
    near_ids = jnp.sum(
        (item_ends[:, None, :] <= near_places[None, :, None]).astype(jnp.int32), axis=2
    )
    base_item = jnp.minimum(own_ids[:, 0], item_count - 2)
    catalog = jnp.arange(item_count, dtype=jnp.int32)
    choose = own_ids[:, :, None] == catalog[None, None, :]
    offsets_in = own_places[None, :] - jnp.sum(
        choose.astype(jnp.int32) * item_starts[:, None, :], axis=2
    )
    later = (own_ids != base_item[:, None])[:, :, None]
    two = jax.vmap(lambda table, start: lax.dynamic_slice_in_dim(table, start, 2, 0))(
        modulation, base_item
    )

    def framewise(index):
        chosen = jnp.where(later, two[:, 1, index][:, None, :], two[:, 0, index][:, None, :])
        return chosen.reshape(rows, model_width)

    cosine, sine = rotary_tables(offsets_in.reshape(-1))
    self_allowed = (
        (own_ids[:, :, None] == near_ids[:, None, :])
        & near_inside[None, None, :]
        & (jnp.abs(own_places[:, None] - near_places[None, :]) <= HALF)[None]
    )
    text_slots = jnp.arange(2 * TXT, dtype=jnp.int32)
    key_items = base_item[:, None] + (text_slots // TXT)[None, :]
    key_lengths = jnp.sum(
        (key_items[:, :, None] == catalog[None, None, :]).astype(jnp.int32) * text_len[:, None, :],
        axis=2,
    )
    cross_allowed = (own_ids[:, :, None] == key_items[:, None, :]) & (
        (text_slots % TXT)[None, :] < key_lengths
    )[:, None, :]

    def by_heads(flat, count):
        return flat.reshape(micro, count, heads, HD)

    latent = latents.astype(f32).reshape(rows, model_width)
    cotangent = out_grad.reshape(rows, model_width)
    xhat_one, inv_one = normalize(latent)
    normed_one = (xhat_one * (1.0 + framewise(1)) + framewise(0)).astype(bf16)
    projected = nn(normed_one, qkv_w)
    query_one = rotate(projected[:, :local], cosine, sine, 1.0).astype(bf16)
    key_one = rotate(projected[:, local : 2 * local], cosine, sine, 1.0).astype(bf16)
    value_one = projected[:, 2 * local :].astype(bf16)
    key_value = jnp.stack([key_one, value_one]).reshape(2, micro, block_rows, local)
    ahead = [(i, i + 1) for i in range(seq_count - 1)]
    behind = [(i + 1, i) for i in range(seq_count - 1)]
    low_rows = lax.ppermute(key_value[:, :, block_rows - HALF :], "seq", ahead)
    high_rows = lax.ppermute(key_value[:, :, :HALF], "seq", behind)
    near_pairs = jnp.concatenate([low_rows, key_value, high_rows], axis=2)
    near_keys = by_heads(near_pairs[0], block_rows + 2 * HALF)
    near_values = by_heads(near_pairs[1], block_rows + 2 * HALF)
    query_heads = by_heads(query_one, block_rows)
    mixed_one, total_one = attend(query_heads, near_keys, near_values, self_allowed, factor)
    mixed_one = mixed_one.reshape(rows, local).astype(bf16)
    hidden_one = latent + pair_sum(nt(mixed_one, self_wt).astype(bf16))

    xhat_two, inv_two = normalize(hidden_one)
    normed_two = (xhat_two * (1.0 + framewise(3)) + framewise(2)).astype(bf16)
    query_two = nn(normed_two, query_w).astype(bf16)
    near_context = jax.vmap(
        lambda table, start: lax.dynamic_slice_in_dim(table, start * TXT, 2 * TXT, 0)
    )(context, base_item).reshape(micro * 2 * TXT, text_width)
    text_keys = by_heads(nn(near_context, key_w).astype(bf16), 2 * TXT)
    text_values = by_heads(nn(near_context, value_w).astype(bf16), 2 * TXT)
    query_two_heads = by_heads(query_two, block_rows)
    mixed_two, total_two = attend(query_two_heads, text_keys, text_values, cross_allowed, factor)
    mixed_two = mixed_two.reshape(rows, local).astype(bf16)
    hidden_two = hidden_one + pair_sum(nt(mixed_two, cross_wt).astype(bf16))

    xhat_three, inv_three = normalize(hidden_two)
    normed_three = (xhat_three * (1.0 + framewise(5)) + framewise(4)).astype(bf16)
    gate = nn(normed_three, gate_w)
    up = nn(normed_three, up_w)
    chance = jax.nn.sigmoid(gate)
    swish = gate * chance
    activated = (swish * up).astype(bf16)
    block_out = (hidden_two + pair_sum(nt(activated, outer_wt).astype(bf16))).astype(bf16)

    activated_grad = nn(cotangent, outer_wt)
    gate_grad = (activated_grad * up * (chance * (1.0 + gate * (1.0 - chance)))).astype(bf16)
    up_grad = (activated_grad * swish).astype(bf16)
    outer_total = scatter_sum(tn(cotangent, activated).astype(bf16))
    gate_total = scatter_sum(tn(normed_three, gate_grad).astype(bf16))
    up_total = scatter_sum(tn(normed_three, up_grad).astype(bf16))
    normed_three_grad = pair_sum((nt(gate_grad, gate_w) + nt(up_grad, up_w)).astype(bf16))

    def norm_back(normed_grad, xhat, inv, scale_row):
        inner = normed_grad * (1.0 + scale_row)
        mean_inner = jnp.mean(inner, axis=-1, keepdims=True)
        mean_cross = jnp.mean(inner * xhat, axis=-1, keepdims=True)
        back = inv * (inner - mean_inner - xhat * mean_cross)
        cube = normed_grad.reshape(micro, block_rows, model_width)
        scaled = (normed_grad * xhat).reshape(micro, block_rows, model_width)

        def by_item(values):
            high_part = jnp.sum(jnp.where(later, values, 0.0), axis=1)
            low_part = jnp.sum(jnp.where(later, 0.0, values), axis=1)
            return jnp.stack([low_part, high_part], axis=1)

        return back, by_item(cube), by_item(scaled)

    back_three, shift_three, scale_three = norm_back(
        normed_three_grad, xhat_three, inv_three, framewise(5)
    )
    hidden_two_grad = cotangent.astype(f32) + back_three
    two_low = hidden_two_grad.astype(bf16)
    mixed_two_grad = by_heads(nn(two_low, cross_wt).astype(bf16), block_rows)
    query_two_grad, text_key_grad, text_value_grad = attend_back(
        query_two_heads, text_keys, text_values, cross_allowed, factor, total_two, mixed_two_grad
    )
    query_two_low = query_two_grad.reshape(rows, local).astype(bf16)
    text_key_low = text_key_grad.reshape(micro * 2 * TXT, local).astype(bf16)
    text_value_low = text_value_grad.reshape(micro * 2 * TXT, local).astype(bf16)
    normed_two_grad = pair_sum(nt(query_two_low, query_w).astype(bf16))
    share = text_width // seq_count
    pair_grad = jnp.concatenate(
        [
            tn(near_context, text_key_low).reshape(seq_count, share, local),
            tn(near_context, text_value_low).reshape(seq_count, share, local),
        ],
        axis=1,
    ).reshape(2 * text_width, local)
    cross_total = scatter_sum(
        jnp.concatenate(
            [tn(two_low, mixed_two), tn(normed_two, query_two_low), pair_grad], axis=1
        ).astype(bf16)
    )
    back_two, shift_two, scale_two = norm_back(normed_two_grad, xhat_two, inv_two, framewise(3))
    hidden_one_grad = hidden_two_grad + back_two
    one_low = hidden_one_grad.astype(bf16)
    mixed_one_grad = by_heads(nn(one_low, self_wt).astype(bf16), block_rows)
    query_one_grad, near_key_grad, near_value_grad = attend_back(
        query_heads, near_keys, near_values, self_allowed, factor, total_one, mixed_one_grad
    )
    near_grads = jnp.stack([near_key_grad, near_value_grad]).reshape(
        2, micro, block_rows + 2 * HALF, local
    )
    to_behind = lax.ppermute(near_grads[:, :, :HALF].astype(bf16), "seq", behind)
    to_ahead = lax.ppermute(near_grads[:, :, block_rows + HALF :].astype(bf16), "seq", ahead)
    pair_grads = near_grads[:, :, HALF : HALF + block_rows]
    pair_grads = pair_grads + jnp.pad(
        to_ahead.astype(f32), ((0, 0), (0, 0), (0, block_rows - HALF), (0, 0))
    )
    pair_grads = pair_grads + jnp.pad(
        to_behind.astype(f32), ((0, 0), (0, 0), (block_rows - HALF, 0), (0, 0))
    )
    projected_grad = jnp.concatenate(
        [
            rotate(query_one_grad.reshape(rows, local), cosine, sine, -1.0),
            rotate(pair_grads[0].reshape(rows, local), cosine, sine, -1.0),
            pair_grads[1].reshape(rows, local),
        ],
        axis=1,
    ).astype(bf16)
    normed_one_grad = pair_sum(nt(projected_grad, qkv_w).astype(bf16))
    self_total = scatter_sum(
        jnp.concatenate(
            [tn(normed_one, projected_grad).astype(bf16), tn(one_low, mixed_one).astype(bf16)],
            axis=1,
        )
    )
    back_one, shift_one, scale_one = norm_back(normed_one_grad, xhat_one, inv_one, framewise(1))
    latent_grad = hidden_one_grad + back_one

    pieces = jnp.stack(
        [shift_one, scale_one, shift_two, scale_two, shift_three, scale_three], axis=2
    )
    spots = (base_item[:, None] + jnp.arange(2)[None, :])[:, :, None] == catalog[None, None, :]
    item_grad = jnp.sum(
        jnp.where(spots[:, :, :, None, None], pieces[:, :, None], 0.0), axis=1
    ).reshape(micro * item_count, 6 * model_width)
    item_total = seq_sum(item_grad)
    mod_grad = jnp.dot(own_features.T, item_total, precision=highest).reshape(mod_weight.shape)
    bias_grad = lax.dynamic_slice_in_dim(
        jnp.sum(item_total, axis=0).reshape(6, model_width), me * bias_share, bias_share, 1
    )

    grad_qkv = jnp.stack([self_total[:, i * local : (i + 1) * local] for i in range(3)])
    grad_self_out = self_total[:, 3 * local :].T
    grad_cross_out = cross_total[:, :local].T
    grad_cross_query = cross_total[:, local : 2 * local]
    grad_cross_kv = cross_total[:, 2 * local :].reshape(2, share, local)
    return (
        block_out.reshape(latents.shape),
        latent_grad.reshape(latents.shape),
        grad_qkv,
        grad_self_out,
        grad_cross_query,
        grad_cross_kv,
        grad_cross_out,
        jnp.stack([gate_total, up_total]),
        outer_total.T,
        mod_grad,
        bias_grad,
    )


def solution(mesh):
    return jax.shard_map(
        on_device,
        mesh=mesh,
        in_specs=(
            P(None, "seq", None),
            P(),
            P(),
            P(),
            P(),
            P(None, "seq", "tensor"),
            P("tensor", "seq"),
            P("seq", "tensor"),
            P(None, "seq", "tensor"),
            P("tensor", "seq"),
            P(None, "seq", "tensor"),
            P("tensor", "seq"),
            P("seq", None, None),
            P(None, "seq"),
            P(None, "seq", None),
        ),
        out_specs=(
            P(None, "seq", None),
            P(None, "seq", None),
            P(None, "seq", "tensor"),
            P("tensor", "seq"),
            P("seq", "tensor"),
            P(None, "seq", "tensor"),
            P("tensor", "seq"),
            P(None, "seq", "tensor"),
            P("tensor", "seq"),
            P("seq", None, None),
            P(None, "seq"),
        ),
        check_vma=False,
    )
```

time: 2590 us -> 1070 us (0.41)
  waiting for transfers between devices: 1790 us -> 500 us
  local copies, waits for them, and re-layouts: 300 us -> 143 us
  matrix products: 331 us -> 193 us
  starting transfers between devices: 21.8 us -> 70.7 us
  other arithmetic: 97.1 us -> 140 us
    unnamed x26 -> x2, waiting for transfers between devices: 677 us -> 0.03 us
    reduce_scatter x5 -> x0, waiting for transfers between devices: 569 us -> none  [the longest x1 199 us: spread_grads(): lax.psum_scatter(grads[6], 'seq', scatter_dimension=1, tiled=True)]
    ppermute x8 -> x38, waiting for transfers between devices: 0.02 us -> 412 us  [the longest x28 341 us: flip(): return lax.ppermute(block, 'seq', [(i, i ^ stride) for i in range(count)])]
    psum x5 -> x0, waiting for transfers between devices: 252 us -> none  [the longest x1 71.6 us: micro_batch(): lax.psum(jnp.dot(mixed_one, self_weight, preferred_element_type=jnp.float...]
    all_gather x8 -> x2, waiting for transfers between devices: 291 us -> 88.3 us  [the longest x1 68.5 us: on_device(): attn_all = lax.all_gather(attn_share, 'seq', axis=0, tiled=True)]
    dot_general x72 -> x39, matrix products: 331 us -> 193 us  [the longest x25 144 us: dot(): lax.dot_general(a, b, ((dims[0], dims[1]), ((), ())), preferred_element_t...]
    unnamed x568 -> x274, local copies, waits for them, and re-layouts: 124 us -> 30.6 us
    add x7 -> x1, local copies, waits for them, and re-layouts: 85.4 us -> 0.01 us  [on_device(): jnp.dot(own_features, mod_weight.astype(f32).reshape(mod_weight.shape[0],...]
  transfers between devices with their start and end apart: 30 -> 40, of which waited for: 20 -> 22; matrix products, arithmetic and copies ran while one was open for 20% -> 35% of each run, Pallas kernels for 0% -> 0%
where the time goes in v1:
time: 1070 us; the launch traced here: 1060 us
  waiting for transfers between devices  500 us (47%)
  matrix products  193 us (18%)
  local copies, waits for them, and re-layouts  143 us (13%)
  other arithmetic  140 us (13%)
  starting transfers between devices  70.7 us (7%)
  between operations  16.7 us (2%)
    ppermute x28, waiting for transfers between devices, flip(): return lax.ppermute(block, 'seq', [(i, i ^ stride) for i in range(count)])  341 us
    dot_general x25, matrix products, dot(): lax.dot_general(a, b, ((dims[0], dims[1]), ((), ())), preferred_element_t...  144 us
    ppermute x6, waiting for transfers between devices, pair_sum(): lax.ppermute(part, 'tensor', [(i, (i + 1) % count) for i in range(count)])  70.4 us
    all_gather x1, waiting for transfers between devices, on_device(): attn_all = lax.all_gather(attn_share, 'seq', axis=0, tiled=True)  68.5 us
    ppermute x28, starting transfers between devices, flip(): return lax.ppermute(block, 'seq', [(i, i ^ stride) for i in range(count)])  55.3 us
    convert_element_type x15, other arithmetic, scatter_sum(): cur = cur.astype(bf16)  44.2 us
    unnamed x274, local copies, waits for them, and re-layouts  30.6 us
    squeeze x20, local copies, waits for them, and re-layouts, scatter_sum(): sent = lax.dynamic_index_in_dim(pairs, 1 - digit, 1, keepdims=False)  28.1 us
  transfers between devices with their start and end apart: 40, of which 22 were waited for; matrix products, arithmetic and copies ran while one was open for 35% of the time, Pallas kernels for 0%

profile of v1, /device:TPU:0, one launch (start us, length us, event | category | flops | bytes accessed | tf_op | source)
XLA Modules:
  0.0 1063.7 jit_solution(1408036146475742517)
XLA Ops:
  24.2 11.0 %collective-permute-done.1 = f32[8,9216]{1,0:T(8,128)S(1)} collective-permute-done((f32[8,9216]{1,0:T(8,128)S(1)}, f32[8,9216]{1,0:T(8,128)S(1)}, u32[]{:S(2)}, u32[]{:S(2)}) %collective-permute-start.1) | collective-permute-done | bytes 294944 | tf_op jit(solution)/shard_map/ppermute | solution.py:47
  37.6 25.5 %collective-permute-done.2 = f32[8,9216]{1,0:T(8,128)S(1)} collective-permute-done((f32[8,9216]{1,0:T(8,128)S(1)}, f32[8,9216]{1,0:T(8,128)S(1)}, u32[]{:S(2)}, u32[]{:S(2)}) %collective-permute-start.2) | collective-permute-done | bytes 294944 | tf_op jit(solution)/shard_map/ppermute | solution.py:47
  64.2 15.6 %collective-permute-done.3 = f32[8,9216]{1,0:T(8,128)S(1)} collective-permute-done((f32[8,9216]{1,0:T(8,128)S(1)}, f32[8,9216]{1,0:T(8,128)S(1)}, u32[]{:S(2)}, u32[]{:S(2)}) %collective-permute-start.3) | collective-permute-done | bytes 294944 | tf_op jit(solution)/shard_map/ppermute | solution.py:47
  84.4 68.5 %all-gather.3.cloned.1.call-done = bf16[1536,5376]{1,0:T(8,128)(2,1)} async-done(((bf16[96,5376]{1,0:T(8,128)(2,1)}), bf16[1536,5376]{1,0:T(8,128)(2,1)}) %all-gather.3.cloned.1.call-update) | async-done | bytes 16515088 | tf_op jit(solution)/shard_map/all_gather | solution.py:195
  224.7 9.6 collective-permute-done.6
  268.9 13.6 %collective-permute-done.7 = bf16[512,1536]{1,0:T(8,128)(2,1)} collective-permute-done((bf16[512,1536]{1,0:T(8,128)(2,1)}, bf16[512,1536]{1,0:T(8,128)(2,1)}, u32[]{:S(2)}, u32[]{:S(2)}) %collective-permute-start.7) | collective-permute-done | bytes 1572896 | tf_op jit(solution)/shard_map/ppermute | solution.py:52
  289.6 19.8 %all-gather.5.cloned.1.call-done = bf16[1536,9216]{1,0:T(8,128)(2,1)} async-done(((bf16[96,9216]{1,0:T(8,128)(2,1)}), bf16[1536,9216]{1,0:T(8,128)(2,1)}) %all-gather.5.cloned.1.call-update) | async-done | bytes 28311568 | tf_op jit(solution)/shard_map/all_gather | solution.py:196
  309.4 8.2 fusion.15
  317.6 11.3 %fusion.5 = f32[3072,512]{0,1:T(8,128)} fusion(bf16[512,1536]{1,0:T(8,128)(2,1)S(1)} %bitcast.565, bf16[1536,9216]{1,0:T(8,128)(2,1)} %all-gather.5.cloned.1.call-done), kind=kOutput, calls=%fused_computation.23 | convolution fusion | flops 4831838208 | bytes 17301504 | tf_op jit(solution)/shard_map/dot_general | solution.py:21
  328.9 12.8 %fusion.21 = (bf16[512,3072]{1,0:T(8,128)(2,1)}, bf16[512,3072]{1,0:T(8,128)(2,1)}, bf16[512,3072]{1,0:T(8,128)(2,1)}) fusion(f32[3072,512]{0,1:T(8,128)} %fusion.5, f32[512,3072]{1,0:T(8,128)S(1)} %fusion.15, bf16[512,1536]{1,0:T(8,128)(2,1)S(1)} %copy-done.50, bf16[1536,9216]{1,0:T(8,128)(2,1)} %all-gather.5.cloned.1.call-done), kind=kOutput, calls=%fused_computation.46 | convolution fusion | flops 4855431168 | bytes 33030144 | tf_op jit(solution)/shard_map/dot_general | solution.py:21
  341.7 9.6 convolution_convert_fusion.2
  356.7 12.7 %fusion.9 = f32[512,1536]{1,0:T(8,128)} fusion(bf16[512,3072]{1,0:T(8,128)(2,1)S(1)} %copy-done.108, bf16[1536,9216]{1,0:T(8,128)(2,1)} %all-gather.5.cloned.1.call-done), kind=kOutput, calls=%fused_computation.27 | convolution fusion | flops 4831838208 | bytes 15728640 | tf_op jit(solution)/shard_map/dot_general | solution.py:21
  369.3 10.1 fusion.69
  381.2 9.5 fusion.72
  390.7 9.5 convolution_convert_fusion
  417.6 31.9 %collective-permute-done.8 = bf16[512,1536]{1,0:T(8,128)(2,1)S(1)} collective-permute-done((bf16[512,1536]{1,0:T(8,128)(2,1)S(1)}, bf16[512,1536]{1,0:T(8,128)(2,1)S(1)}, u32[]{:S(2)}, u32[]{:S(2)}) %collective-permute-start.8) | collective-permute-done | bytes 1572896 | tf_op jit(solution)/shard_map/ppermute | solution.py:52
  509.6 14.4 %collective-permute-done.10 = bf16[512,1536]{1,0:T(8,128)(2,1)} collective-permute-done((bf16[512,1536]{1,0:T(8,128)(2,1)}, bf16[512,1536]{1,0:T(8,128)(2,1)}, u32[]{:S(2)}, u32[]{:S(2)}) %collective-permute-start.10) | collective-permute-done | bytes 1572896 | tf_op jit(solution)/shard_map/ppermute | solution.py:52
  539.5 10.7 %multiply_reduce_fusion = (f32[2,12,256]{2,1,0:T(8,128)S(1)}, f32[2,12,256,512]{3,2,1,0:T(8,128)}) fusion(f32[2,12,256,512]{3,2,1,0:T(8,128)} %copy-done, f32[2,12,256]{2,1,0:T(8,128)S(1)} %copy-done.66, pred[2,256,512]{2,1,0:T(8,128)(4,1)S(1)} %copy-done.33, bf16[2,512,12,64]{1,3,2,0:T(8,128)(2,1)} %bitcast.548, bf16[2,256,12,64]{1,0,3,2:T(2,128)(2,1)} %reshape.716), kind=kOutput, calls=%fused_computation.4 | convolution fusion | flops 418375680 | bytes 27836416 | tf_op jit(solution)/shard_map/mqhd,mkhd->mhqk/dot_general | solution.py:139
  561.1 9.9 multiply_convert_fusion
  592.7 15.6 %collective-permute-start.18 = (bf16[8,96,2304]{2,1,0:T(8,128)(2,1)}, bf16[8,96,2304]{2,1,0:T(8,128)(2,1)}, u32[]{:S(2)}, u32[]{:S(2)}) collective-permute-start(bf16[8,96,2304]{2,1,0:T(8,128)(2,1)} %dynamic-slice_bitcast_fusion.4), channel_id=1, source_target_pairs={{0,2},{2,0},{4,6},{6,4},{8,10},{10,8},{12,14},{14,12},{16,18},{18,... | collective-permute-start | bytes 10616840 | tf_op jit(solution)/shard_map/ppermute | solution.py:47
  624.4 8.1 fusion.66
  671.3 10.9 %select_reduce_fusion.1 = (f32[2,1536]{1,0:T(2,128)S(1)}, f32[2,1536]{1,0:T(2,128)S(1)}, f32[2,1536]{1,0:T(2,128)S(1)}, f32[2,1536]{1,0:T(2,128)S(1)}, f32[2,153...) fusion(pred[2,256]{1,0:T(4,128)(4,1)S(1)} %copy-done.101, ...), kind=kLoop, calls=%fused_computation.119 | loop fusion | flops 33779712 | bytes 17461760 | tf_op jit(solution)/shard_map/reduce_sum | solution.py:329
  694.5 108.9 %collective-permute-done.35 = f32[8,9216]{1,0:T(8,128)S(1)} collective-permute-done((f32[8,9216]{1,0:T(8,128)S(1)}, f32[8,9216]{1,0:T(8,128)S(1)}, u32[]{:S(2)}, u32[]{:S(2)}) %collective-permute-start.35) | collective-permute-done | bytes 294944 | tf_op jit(solution)/shard_map/ppermute | solution.py:47
  851.5 12.2 %collective-permute-done.20 = bf16[2,96,2304]{2,1,0:T(8,128)(2,1)S(1)} collective-permute-done((bf16[2,96,2304]{2,1,0:T(8,128)(2,1)S(1)}, bf16[2,96,2304]{2,1,0:T(8,128)(2,1)S(1)}, u32[]{:S(2)}, u32[]{:S(2)}) %collective-permute-start.20) | collective-permute-done | bytes 884768 | tf_op jit(solution)/shard_map/ppermute | solution.py:47
  866.0 17.7 %collective-permute-done.27 = bf16[4,96,3072]{2,1,0:T(8,128)(2,1)} collective-permute-done((bf16[4,96,3072]{2,1,0:T(8,128)(2,1)}, bf16[4,96,3072]{2,1,0:T(8,128)(2,1)}, u32[]{:S(2)}, u32[]{:S(2)}) %collective-permute-start.27) | collective-permute-done | bytes 2359328 | tf_op jit(solution)/shard_map/ppermute | solution.py:47
  889.1 32.8 %collective-permute-done.21 = bf16[1,96,2304]{2,1,0:T(8,128)(2,1)S(1)} collective-permute-done((bf16[1,96,2304]{2,1,0:T(8,128)(2,1)S(1)}, bf16[1,96,2304]{2,1,0:T(8,128)(2,1)S(1)}, u32[]{:S(2)}, u32[]{:S(2)}) %collective-permute-start.21) | collective-permute-done | bytes 442400 | tf_op jit(solution)/shard_map/ppermute | solution.py:47
  935.3 29.2 %collective-permute-done.28 = bf16[2,96,3072]{2,1,0:T(8,128)(2,1)} collective-permute-done((bf16[2,96,3072]{2,1,0:T(8,128)(2,1)}, bf16[2,96,3072]{2,1,0:T(8,128)(2,1)}, u32[]{:S(2)}, u32[]{:S(2)}) %collective-permute-start.28) | collective-permute-done | bytes 1179680 | tf_op jit(solution)/shard_map/ppermute | solution.py:47
  966.4 13.3 %collective-permute-done.15 = bf16[4,96,3072]{2,1,0:T(8,128)(2,1)S(1)} collective-permute-done((bf16[4,96,3072]{2,1,0:T(8,128)(2,1)S(1)}, bf16[4,96,3072]{2,1,0:T(8,128)(2,1)S(1)}, u32[]{:S(2)}, u32[]{:S(2)}) %collective-permute-start.15) | collective-permute-done | bytes 2359328 | tf_op jit(solution)/shard_map/ppermute | solution.py:47
  985.1 13.3 %collective-permute-done.25 = bf16[1,96,3072]{2,1,0:T(8,128)(2,1)S(1)} collective-permute-done((bf16[1,96,3072]{2,1,0:T(8,128)(2,1)S(1)}, bf16[1,96,3072]{2,1,0:T(8,128)(2,1)S(1)}, u32[]{:S(2)}, u32[]{:S(2)}) %collective-permute-start.25) | collective-permute-done | bytes 589856 | tf_op jit(solution)/shard_map/ppermute | solution.py:47
  998.5 9.3 collective-permute-done.29
  1009.5 19.2 %collective-permute-done.16 = bf16[2,96,3072]{2,1,0:T(8,128)(2,1)S(1)} collective-permute-done((bf16[2,96,3072]{2,1,0:T(8,128)(2,1)S(1)}, bf16[2,96,3072]{2,1,0:T(8,128)(2,1)S(1)}, u32[]{:S(2)}, u32[]{:S(2)}) %collective-permute-start.16) | collective-permute-done | bytes 1179680 | tf_op jit(solution)/shard_map/ppermute | solution.py:47
  1032.0 22.7 %collective-permute-done.17 = bf16[1,96,3072]{2,1,0:T(8,128)(2,1)S(1)} collective-permute-done((bf16[1,96,3072]{2,1,0:T(8,128)(2,1)S(1)}, bf16[1,96,3072]{2,1,0:T(8,128)(2,1)S(1)}, u32[]{:S(2)}, u32[]{:S(2)}) %collective-permute-start.17) | collective-permute-done | bytes 589856 | tf_op jit(solution)/shard_map/ppermute | solution.py:47
  (590 shorter events, 427.2 us)
Async XLA Ops:
  7.2 145.7 %all-gather.3.cloned.1.call-start = ((), (), s32[]{:S(2)}) async-start(), calls=%async_computation | async-start | bytes 17547264 | tf_op jit(solution)/shard_map/all_gather | solution.py:195
  14.9 294.5 %all-gather.5.cloned.1.call-start = ((), (), s32[]{:S(2)}) async-start(), calls=%async_computation.1 | async-start | bytes 30081024 | tf_op jit(solution)/shard_map/all_gather | solution.py:196
  35.2 27.8 %collective-permute-start.2 = (f32[8,9216]{1,0:T(8,128)S(1)}, f32[8,9216]{1,0:T(8,128)S(1)}, u32[]{:S(2)}, u32[]{:S(2)}) collective-permute-start(f32[8,9216]{1,0:T(8,128)S(1)} %add.440), channel_id=1, source_target_pairs={{0,8},{2,10},{4,12},{6,14},{8,0},{10,2},{12,4},{14,6},{16,24},{18,... | collective-permute-start | bytes 884744 | tf_op jit(solution)/shard_map/ppermute | solution.py:47
  213.5 20.7 %collective-permute-start.6 = (bf16[512,1536]{1,0:T(8,128)(2,1)}, bf16[512,1536]{1,0:T(8,128)(2,1)}, u32[]{:S(2)}, u32[]{:S(2)}) collective-permute-start(bf16[512,1536]{1,0:T(8,128)(2,1)} %convolution_convert_fusion.7), channel_id=1, source_target_pairs={{0,1},{1,0},{2,3},{3,2},{4,5},{5,4},{6,7},{7,6},{8,9},{9,8},{10,11... | collective-permute-start | bytes 4718600 | tf_op jit(solution)/shard_map/ppermute | solution.py:52
  261.8 20.7 %collective-permute-start.7 = (bf16[512,1536]{1,0:T(8,128)(2,1)}, bf16[512,1536]{1,0:T(8,128)(2,1)}, u32[]{:S(2)}, u32[]{:S(2)}) collective-permute-start(bf16[512,1536]{1,0:T(8,128)(2,1)} %convolution_convert_fusion.6), channel_id=1, source_target_pairs={{0,1},{1,0},{2,3},{3,2},{4,5},{5,4},{6,7},{7,6},{8,9},{9,8},{10,11... | collective-permute-start | bytes 4718600 | tf_op jit(solution)/shard_map/ppermute | solution.py:52
  379.5 36.4 %collective-permute-start.9 = (bf16[512,1536]{1,0:T(8,128)(2,1)S(1)}, bf16[512,1536]{1,0:T(8,128)(2,1)S(1)}, u32[]{:S(2)}, u32[]{:S(2)}) collective-permute-start(bf16[512,1536]{1,0:T(8,128)(2,1)S(1)} %fusion.69), channel_id=1, source_target_pairs={{0,1},{1,0},{2,3},{3,2},{4,5},{5,4},{6,7},{7,6},{8,9},{9,8},{10,11... | collective-permute-start | bytes 4718600 | tf_op jit(solution)/shard_map/ppermute | solution.py:52
  400.2 49.3 %collective-permute-start.8 = (bf16[512,1536]{1,0:T(8,128)(2,1)S(1)}, bf16[512,1536]{1,0:T(8,128)(2,1)S(1)}, u32[]{:S(2)}, u32[]{:S(2)}) collective-permute-start(bf16[512,1536]{1,0:T(8,128)(2,1)S(1)} %fusion.72), channel_id=1, source_target_pairs={{0,1},{1,0},{2,3},{3,2},{4,5},{5,4},{6,7},{7,6},{8,9},{9,8},{10,11... | collective-permute-start | bytes 4718600 | tf_op jit(solution)/shard_map/ppermute | solution.py:52
  405.5 239.0 %collective-permute-start.30 = (bf16[8,96,3072]{2,1,0:T(8,128)(2,1)}, bf16[8,96,3072]{2,1,0:T(8,128)(2,1)}, u32[]{:S(2)}, u32[]{:S(2)}) collective-permute-start(bf16[8,96,3072]{2,1,0:T(8,128)(2,1)} %dynamic-slice_bitcast_fusion), channel_id=1, source_target_pairs={{0,2},{2,0},{4,6},{6,4},{8,10},{10,8},{12,14},{14,12},{16,18},{18,... | collective-permute-start | bytes 14155784 | tf_op jit(solution)/shard_map/ppermute | solution.py:47
  411.8 243.4 %collective-permute-start.22 = (bf16[8,96,3072]{2,1,0:T(8,128)(2,1)}, bf16[8,96,3072]{2,1,0:T(8,128)(2,1)}, u32[]{:S(2)}, u32[]{:S(2)}) collective-permute-start(bf16[8,96,3072]{2,1,0:T(8,128)(2,1)} %dynamic-slice_bitcast_fusion.2), channel_id=1, source_target_pairs={{0,2},{2,0},{4,6},{6,4},{8,10},{10,8},{12,14},{14,12},{16,18},{18,... | collective-permute-start | bytes 14155784 | tf_op jit(solution)/shard_map/ppermute | solution.py:47
  414.4 273.0 %collective-permute-start.26 = (bf16[8,96,3072]{2,1,0:T(8,128)(2,1)}, bf16[8,96,3072]{2,1,0:T(8,128)(2,1)}, u32[]{:S(2)}, u32[]{:S(2)}) collective-permute-start(bf16[8,96,3072]{2,1,0:T(8,128)(2,1)} %dynamic-slice_bitcast_fusion.1), channel_id=1, source_target_pairs={{0,2},{2,0},{4,6},{6,4},{8,10},{10,8},{12,14},{14,12},{16,18},{18,... | collective-permute-start | bytes 14155784 | tf_op jit(solution)/shard_map/ppermute | solution.py:47
  486.5 37.4 %collective-permute-start.10 = (bf16[512,1536]{1,0:T(8,128)(2,1)}, bf16[512,1536]{1,0:T(8,128)(2,1)}, u32[]{:S(2)}, u32[]{:S(2)}) collective-permute-start(bf16[512,1536]{1,0:T(8,128)(2,1)} %convolution_convert_fusion.5), channel_id=1, source_target_pairs={{0,1},{1,0},{2,3},{3,2},{4,5},{5,4},{6,7},{7,6},{8,9},{9,8},{10,11... | collective-permute-start | bytes 4718600 | tf_op jit(solution)/shard_map/ppermute | solution.py:52
  583.8 24.5 %collective-permute-start.12 = (bf16[2,2,128,768]{3,2,1,0:T(8,128)(2,1)S(1)}, bf16[2,2,128,768]{3,2,1,0:T(8,128)(2,1)S(1)}, u32[]{:S(2)}, u32[]{:S(2)}) collective-permute-start(bf16[2,2,128,768]{3,2,1,0:T(8,128)(2,1)S(1)} %get-tuple-element.113), channel_id=1, source_target_pairs={{2,0},{4,2},{6,4},{8,6},{10,8},{12,10},{14,12},{16,14},{18,16},{20... | collective-permute-start | bytes 2359304 | tf_op jit(solution)/shard_map/ppermute | solution.py:370
  592.7 71.7 %collective-permute-start.18 = (bf16[8,96,2304]{2,1,0:T(8,128)(2,1)}, bf16[8,96,2304]{2,1,0:T(8,128)(2,1)}, u32[]{:S(2)}, u32[]{:S(2)}) collective-permute-start(bf16[8,96,2304]{2,1,0:T(8,128)(2,1)} %dynamic-slice_bitcast_fusion.4), channel_id=1, source_target_pairs={{0,2},{2,0},{4,6},{6,4},{8,10},{10,8},{12,14},{14,12},{16,18},{18,... | collective-permute-start | bytes 10616840 | tf_op jit(solution)/shard_map/ppermute | solution.py:47
  632.6 38.6 %collective-permute-start.13 = (bf16[512,1536]{1,0:T(8,128)(2,1)}, bf16[512,1536]{1,0:T(8,128)(2,1)}, u32[]{:S(2)}, u32[]{:S(2)}) collective-permute-start(bf16[512,1536]{1,0:T(8,128)(2,1)} %fusion.66), channel_id=1, source_target_pairs={{0,1},{1,0},{2,3},{3,2},{4,5},{5,4},{6,7},{7,6},{8,9},{9,8},{10,11... | collective-permute-start | bytes 4718600 | tf_op jit(solution)/shard_map/ppermute | solution.py:52
  644.5 279.8 %collective-permute-start.14 = (bf16[8,96,3072]{2,1,0:T(8,128)(2,1)}, bf16[8,96,3072]{2,1,0:T(8,128)(2,1)}, u32[]{:S(2)}, u32[]{:S(2)}) collective-permute-start(bf16[8,96,3072]{2,1,0:T(8,128)(2,1)} %dynamic-slice_bitcast_fusion.3), channel_id=1, source_target_pairs={{0,2},{2,0},{4,6},{6,4},{8,10},{10,8},{12,14},{14,12},{16,18},{18,... | collective-permute-start | bytes 14155784 | tf_op jit(solution)/shard_map/ppermute | solution.py:47
  655.2 186.6 %collective-permute-start.31 = (bf16[4,96,3072]{2,1,0:T(8,128)(2,1)}, bf16[4,96,3072]{2,1,0:T(8,128)(2,1)}, u32[]{:S(2)}, u32[]{:S(2)}) collective-permute-start(bf16[4,96,3072]{2,1,0:T(8,128)(2,1)} %dynamic-slice_bitcast_fusion.5), channel_id=1, source_target_pairs={{0,4},{2,6},{4,0},{6,2},{8,12},{10,14},{12,8},{14,10},{16,20},{18,... | collective-permute-start | bytes 7077896 | tf_op jit(solution)/shard_map/ppermute | solution.py:47
  664.3 182.3 %collective-permute-start.23 = (bf16[4,96,3072]{2,1,0:T(8,128)(2,1)}, bf16[4,96,3072]{2,1,0:T(8,128)(2,1)}, u32[]{:S(2)}, u32[]{:S(2)}) collective-permute-start(bf16[4,96,3072]{2,1,0:T(8,128)(2,1)} %dynamic-slice_bitcast_fusion.7), channel_id=1, source_target_pairs={{0,4},{2,6},{4,0},{6,2},{8,12},{10,14},{12,8},{14,10},{16,20},{18,... | collective-permute-start | bytes 7077896 | tf_op jit(solution)/shard_map/ppermute | solution.py:47
  686.5 152.5 %collective-permute-start.19 = (bf16[4,96,2304]{2,1,0:T(8,128)(2,1)}, bf16[4,96,2304]{2,1,0:T(8,128)(2,1)}, u32[]{:S(2)}, u32[]{:S(2)}) collective-permute-start(bf16[4,96,2304]{2,1,0:T(8,128)(2,1)} %dynamic-slice_bitcast_fusion.9), channel_id=1, source_target_pairs={{0,4},{2,6},{4,0},{6,2},{8,12},{10,14},{12,8},{14,10},{16,20},{18,... | collective-permute-start | bytes 5308424 | tf_op jit(solution)/shard_map/ppermute | solution.py:47
  687.4 115.9 %collective-permute-start.35 = (f32[8,9216]{1,0:T(8,128)S(1)}, f32[8,9216]{1,0:T(8,128)S(1)}, u32[]{:S(2)}, u32[]{:S(2)}) collective-permute-start(f32[8,9216]{1,0:T(8,128)S(1)} %add.516), channel_id=1, source_target_pairs={{0,4},{2,6},{4,0},{6,2},{8,12},{10,14},{12,8},{14,10},{16,20},{18,... | collective-permute-start | bytes 884744 | tf_op jit(solution)/shard_map/ppermute | solution.py:47
  811.6 19.6 %collective-permute-start.37 = (f32[8,9216]{1,0:T(8,128)S(1)}, f32[8,9216]{1,0:T(8,128)S(1)}, u32[]{:S(2)}, u32[]{:S(2)}) collective-permute-start(f32[8,9216]{1,0:T(8,128)S(1)} %add.518), channel_id=1, source_target_pairs={{0,16},{2,18},{4,20},{6,22},{8,24},{10,26},{12,28},{14,30},{16,0},... | collective-permute-start | bytes 884744 | tf_op jit(solution)/shard_map/ppermute | solution.py:47
  831.2 52.5 %collective-permute-start.27 = (bf16[4,96,3072]{2,1,0:T(8,128)(2,1)}, bf16[4,96,3072]{2,1,0:T(8,128)(2,1)}, u32[]{:S(2)}, u32[]{:S(2)}) collective-permute-start(bf16[4,96,3072]{2,1,0:T(8,128)(2,1)} %dynamic-slice_bitcast_fusion.6), channel_id=1, source_target_pairs={{0,4},{2,6},{4,0},{6,2},{8,12},{10,14},{12,8},{14,10},{16,20},{18,... | collective-permute-start | bytes 7077896 | tf_op jit(solution)/shard_map/ppermute | solution.py:47
  841.0 22.6 %collective-permute-start.20 = (bf16[2,96,2304]{2,1,0:T(8,128)(2,1)S(1)}, bf16[2,96,2304]{2,1,0:T(8,128)(2,1)S(1)}, u32[]{:S(2)}, u32[]{:S(2)}) collective-permute-start(bf16[2,96,2304]{2,1,0:T(8,128)(2,1)S(1)} %dynamic-slice_bitcast_fusion.14), channel_id=1, source_target_pairs={{0,8},{2,10},{4,12},{6,14},{8,0},{10,2},{12,4},{14,6},{16,24},{18,... | collective-permute-start | bytes 2654216 | tf_op jit(solution)/shard_map/ppermute | solution.py:47
  845.6 77.3 %collective-permute-start.32 = (bf16[2,96,3072]{2,1,0:T(8,128)(2,1)S(1)}, bf16[2,96,3072]{2,1,0:T(8,128)(2,1)S(1)}, u32[]{:S(2)}, u32[]{:S(2)}) collective-permute-start(bf16[2,96,3072]{2,1,0:T(8,128)(2,1)S(1)} %dynamic-slice_bitcast_fusion.10), channel_id=1, source_target_pairs={{0,8},{2,10},{4,12},{6,14},{8,0},{10,2},{12,4},{14,6},{16,24},{18,... | collective-permute-start | bytes 3538952 | tf_op jit(solution)/shard_map/ppermute | solution.py:47
  850.6 82.9 %collective-permute-start.24 = (bf16[2,96,3072]{2,1,0:T(8,128)(2,1)}, bf16[2,96,3072]{2,1,0:T(8,128)(2,1)}, u32[]{:S(2)}, u32[]{:S(2)}) collective-permute-start(bf16[2,96,3072]{2,1,0:T(8,128)(2,1)} %dynamic-slice_bitcast_fusion.12), channel_id=1, source_target_pairs={{0,8},{2,10},{4,12},{6,14},{8,0},{10,2},{12,4},{14,6},{16,24},{18,... | collective-permute-start | bytes 3538952 | tf_op jit(solution)/shard_map/ppermute | solution.py:47
  864.0 57.9 %collective-permute-start.21 = (bf16[1,96,2304]{2,1,0:T(8,128)(2,1)S(1)}, bf16[1,96,2304]{2,1,0:T(8,128)(2,1)S(1)}, u32[]{:S(2)}, u32[]{:S(2)}) collective-permute-start(bf16[1,96,2304]{2,1,0:T(8,128)(2,1)S(1)} %constant_dynamic-slice_fusion.5), channel_id=1, source_target_pairs={{0,16},{2,18},{4,20},{6,22},{8,24},{10,26},{12,28},{14,30},{16,0},... | collective-permute-start | bytes 1327112 | tf_op jit(solution)/shard_map/ppermute | solution.py:47
  887.4 77.1 %collective-permute-start.28 = (bf16[2,96,3072]{2,1,0:T(8,128)(2,1)}, bf16[2,96,3072]{2,1,0:T(8,128)(2,1)}, u32[]{:S(2)}, u32[]{:S(2)}) collective-permute-start(bf16[2,96,3072]{2,1,0:T(8,128)(2,1)} %dynamic-slice_bitcast_fusion.11), channel_id=1, source_target_pairs={{0,8},{2,10},{4,12},{6,14},{8,0},{10,2},{12,4},{14,6},{16,24},{18,... | collective-permute-start | bytes 3538952 | tf_op jit(solution)/shard_map/ppermute | solution.py:47
  928.9 50.7 %collective-permute-start.15 = (bf16[4,96,3072]{2,1,0:T(8,128)(2,1)S(1)}, bf16[4,96,3072]{2,1,0:T(8,128)(2,1)S(1)}, u32[]{:S(2)}, u32[]{:S(2)}) collective-permute-start(bf16[4,96,3072]{2,1,0:T(8,128)(2,1)S(1)} %dynamic-slice_bitcast_fusion.8), channel_id=1, source_target_pairs={{0,4},{2,6},{4,0},{6,2},{8,12},{10,14},{12,8},{14,10},{16,20},{18,... | collective-permute-start | bytes 7077896 | tf_op jit(solution)/shard_map/ppermute | solution.py:47
  930.1 100.7 %collective-permute-start.33 = (bf16[1,96,3072]{2,1,0:T(8,128)(2,1)S(1)}, bf16[1,96,3072]{2,1,0:T(8,128)(2,1)S(1)}, u32[]{:S(2)}, u32[]{:S(2)}) collective-permute-start(bf16[1,96,3072]{2,1,0:T(8,128)(2,1)S(1)} %constant_dynamic-slice_fusion.2), channel_id=1, source_target_pairs={{0,16},{2,18},{4,20},{6,22},{8,24},{10,26},{12,28},{14,30},{16,0},... | collective-permute-start | bytes 1769480 | tf_op jit(solution)/shard_map/ppermute | solution.py:47
  935.2 63.2 %collective-permute-start.25 = (bf16[1,96,3072]{2,1,0:T(8,128)(2,1)S(1)}, bf16[1,96,3072]{2,1,0:T(8,128)(2,1)S(1)}, u32[]{:S(2)}, u32[]{:S(2)}) collective-permute-start(bf16[1,96,3072]{2,1,0:T(8,128)(2,1)S(1)} %constant_dynamic-slice_fusion.4), channel_id=1, source_target_pairs={{0,16},{2,18},{4,20},{6,22},{8,24},{10,26},{12,28},{14,30},{16,0},... | collective-permute-start | bytes 1769480 | tf_op jit(solution)/shard_map/ppermute | solution.py:47
  966.3 41.6 %collective-permute-start.29 = (bf16[1,96,3072]{2,1,0:T(8,128)(2,1)S(1)}, bf16[1,96,3072]{2,1,0:T(8,128)(2,1)S(1)}, u32[]{:S(2)}, u32[]{:S(2)}) collective-permute-start(bf16[1,96,3072]{2,1,0:T(8,128)(2,1)S(1)} %constant_dynamic-slice_fusion.3), channel_id=1, source_target_pairs={{0,16},{2,18},{4,20},{6,22},{8,24},{10,26},{12,28},{14,30},{16,0},... | collective-permute-start | bytes 1769480 | tf_op jit(solution)/shard_map/ppermute | solution.py:47
  980.6 48.1 %collective-permute-start.16 = (bf16[2,96,3072]{2,1,0:T(8,128)(2,1)S(1)}, bf16[2,96,3072]{2,1,0:T(8,128)(2,1)S(1)}, u32[]{:S(2)}, u32[]{:S(2)}) collective-permute-start(bf16[2,96,3072]{2,1,0:T(8,128)(2,1)S(1)} %dynamic-slice_bitcast_fusion.13), channel_id=1, source_target_pairs={{0,8},{2,10},{4,12},{6,14},{8,0},{10,2},{12,4},{14,6},{16,24},{18,... | collective-permute-start | bytes 3538952 | tf_op jit(solution)/shard_map/ppermute | solution.py:47
  1029.2 25.5 %collective-permute-start.17 = (bf16[1,96,3072]{2,1,0:T(8,128)(2,1)S(1)}, bf16[1,96,3072]{2,1,0:T(8,128)(2,1)S(1)}, u32[]{:S(2)}, u32[]{:S(2)}) collective-permute-start(bf16[1,96,3072]{2,1,0:T(8,128)(2,1)S(1)} %constant_dynamic-slice_fusion.6), channel_id=1, source_target_pairs={{0,16},{2,18},{4,20},{6,22},{8,24},{10,26},{12,28},{14,30},{16,0},... | collective-permute-start | bytes 1769480 | tf_op jit(solution)/shard_map/ppermute | solution.py:47
  (135 other events, 2647.2 us)
Sparse Core Ops, SparseCore 0:
  15.0 137.8 all-gather.2
  155.1 154.2 all-gather.4

commit v2 on v1

v2 whole, which is shorter than its diff:
```python
import functools
import math

import jax
import jax.numpy as jnp
from jax import lax
from jax.experimental import pallas as pl
from jax.experimental.pallas import tpu as pltpu
from jax.sharding import PartitionSpec as P

HD = 64
TXT = 128
TEMB = 256
HALF = 128


norm_eps = 1e-05
highest = lax.Precision.HIGHEST
f32 = jnp.float32
bf16 = jnp.bfloat16


def dot(a, b, dims):
    return lax.dot_general(a, b, ((dims[0], dims[1]), ((), ())), preferred_element_type=f32)


def nn(a, b):
    return dot(a, b, ((1,), (0,)))


def nt(a, b):
    return dot(a, b, ((1,), (1,)))


def tn(a, b):
    return dot(a, b, ((0,), (0,)))


def halves(count):
    stride = 1
    strides = []
    while stride < count:
        strides.append(stride)
        stride *= 2
    return strides


def flip(block, stride):
    count = lax.axis_size("seq")
    return lax.ppermute(block, "seq", [(i, i ^ stride) for i in range(count)])


def pair_sum(part):
    count = lax.axis_size("tensor")
    other = lax.ppermute(part, "tensor", [(i, (i + 1) % count) for i in range(count)])
    return part.astype(f32) + other.astype(f32)


def seq_sum(part):
    for stride in halves(lax.axis_size("seq")):
        part = part + flip(part, stride)
    return part


def kernel_params(grid_rank, mib):
    return pltpu.CompilerParams(
        dimension_semantics=("arbitrary",) * grid_rank, vmem_limit_bytes=mib * 1024 * 1024
    )


SLOTS = 5


def scatter_kernel(*refs, widths, step):
    sources = refs[: len(widths)]
    out_ref = refs[len(widths)]
    (own, got0, got1, got2, got3, staged, own_sem, out_sem, send_sem, recv_sem) = refs[
        len(widths) + 1 :
    ]
    me = lax.axis_index("seq")
    core, y, z_lo, z_hi = [(me // stride) % 2 for stride in (1, 2, 4, 8)]
    partners = [
        me + stride * (1 - 2 * digit)
        for stride, digit in zip((1, 2, 4, 8), (core, y, z_lo, z_hi))
    ]
    barrier = pltpu.get_barrier_semaphore()
    for partner in partners:
        pl.semaphore_signal(
            barrier, inc=1, device_id={"seq": partner}, device_id_type=pl.DeviceIdType.MESH
        )
    pl.semaphore_wait(barrier, len(partners))
    count = sum(widths) // step

    def exchange(stage, source, target, slot):
        return pltpu.make_async_remote_copy(
            src_ref=source,
            dst_ref=target,
            send_sem=send_sem.at[stage, slot],
            recv_sem=recv_sem.at[stage, slot],
            device_id={"seq": partners[stage]},
            device_id_type=pl.DeviceIdType.MESH,
        )

    def over_core(source, column, slot):
        return exchange(
            0, source.at[:, :, :, 1 - core, :, pl.ds(column, step)], got0.at[slot], slot
        )

    def load(source, column, slot):
        return pltpu.make_async_copy(
            source.at[:, :, :, core, :, pl.ds(column, step)], own.at[slot], own_sem.at[slot]
        )

    def over_y(slot):
        return exchange(1, own.at[slot, :, :, 1 - y], got1.at[slot], slot)

    def over_z_lo(slot):
        return exchange(2, own.at[slot, :, 1 - z_lo, y], got2.at[slot], slot)

    def over_z_hi(slot):
        return exchange(3, own.at[slot, 1 - z_hi, z_lo, y], got3.at[slot], slot)

    def store(item, slot):
        return pltpu.make_async_copy(
            staged.at[slot],
            out_ref.at[:, pl.ds(pl.multiple_of(item * step, step), step)],
            out_sem.at[slot],
        )

    def added(left, right):
        return left.astype(f32) + right.astype(f32)

    def tick(t, carry):
        @pl.when(t < count)
        def _():
            slot = t % SLOTS

            @pl.when(t >= SLOTS)
            def _():
                over_y(slot).wait_send()
                over_z_lo(slot).wait_send()
                over_z_hi(slot).wait_send()

            first = 0
            for source, width in zip(sources, widths):
                pieces = width // step

                @pl.when((t >= first) & (t < first + pieces))
                def _(source=source, first=first):
                    column = pl.multiple_of((t - first) * step, step)
                    over_core(source, column, slot).start()
                    load(source, column, slot).start()

                first += pieces

        @pl.when((t >= 1) & (t - 1 < count))
        def _():
            slot = (t - 1) % SLOTS
            load(sources[0], 0, slot).wait()
            over_core(sources[0], 0, slot).wait()
            for i in range(2):
                for j in range(2):
                    for k in range(2):
                        own[slot, i, j, k] = added(own[slot, i, j, k], got0[slot, i, j, k]).astype(
                            bf16
                        )
            over_y(slot).start()

        @pl.when((t >= 2) & (t - 2 < count))
        def _():
            slot = (t - 2) % SLOTS
            over_y(slot).wait_recv()
            for i in range(2):
                for j in range(2):
                    own[slot, i, j, y] = added(own[slot, i, j, y], got1[slot, i, j]).astype(bf16)
            over_z_lo(slot).start()

        @pl.when((t >= 3) & (t - 3 < count))
        def _():
            slot = (t - 3) % SLOTS
            over_z_lo(slot).wait_recv()
            for i in range(2):
                own[slot, i, z_lo, y] = added(own[slot, i, z_lo, y], got2[slot, i]).astype(bf16)
            over_z_hi(slot).start()

        @pl.when((t >= 4) & (t - 4 < count))
        def _():
            slot = (t - 4) % SLOTS
            over_z_hi(slot).wait_recv()

            @pl.when(t - 4 >= SLOTS)
            def _():
                store(0, slot).wait()

            staged[slot] = added(own[slot, z_hi, z_lo, y], got3[slot])
            store(t - 4, slot).start()

        return carry

    lax.fori_loop(0, count + 4, tick, 0)
    for back in range(min(SLOTS, count)):
        slot = (count - 1 - back) % SLOTS
        store(0, slot).wait()
        over_y(slot).wait_send()
        over_z_lo(slot).wait_send()
        over_z_hi(slot).wait_send()


def scatter_sums(grads, step=256):
    count = lax.axis_size("seq")
    rows = grads[0].shape[0] // count
    widths = tuple(grad.shape[1] for grad in grads)
    if count != 16 or rows % 16 or any(width % step for width in widths):
        return [
            lax.psum_scatter(grad.astype(f32), "seq", scatter_dimension=0, tiled=True)
            for grad in grads
        ]
    any_space = pl.BlockSpec(memory_space=pl.ANY)
    total = pl.pallas_call(
        functools.partial(scatter_kernel, widths=widths, step=step),
        out_shape=jax.ShapeDtypeStruct((rows, sum(widths)), f32),
        in_specs=[any_space] * len(grads),
        out_specs=any_space,
        scratch_shapes=[
            pltpu.VMEM((SLOTS, 2, 2, 2, rows, step), bf16),
            pltpu.VMEM((SLOTS, 2, 2, 2, rows, step), bf16),
            pltpu.VMEM((SLOTS, 2, 2, rows, step), bf16),
            pltpu.VMEM((SLOTS, 2, rows, step), bf16),
            pltpu.VMEM((SLOTS, rows, step), bf16),
            pltpu.VMEM((SLOTS, rows, step), f32),
            pltpu.SemaphoreType.DMA((SLOTS,)),
            pltpu.SemaphoreType.DMA((SLOTS,)),
            pltpu.SemaphoreType.DMA((4, SLOTS)),
            pltpu.SemaphoreType.DMA((4, SLOTS)),
        ],
        compiler_params=pltpu.CompilerParams(
            collective_id=0, has_side_effects=True, vmem_limit_bytes=40 * 1024 * 1024
        ),
        cost_estimate=pl.CostEstimate(
            flops=0, bytes_accessed=8 * count * rows * sum(widths), transcendentals=0
        ),
        name="scatter_sums",
    )(*[grad.reshape(2, 2, 2, 2, rows, grad.shape[1]) for grad in grads])
    firsts = [sum(widths[:i]) for i in range(len(widths))]
    return [total[:, first : first + width] for first, width in zip(firsts, widths)]


def early_sum(grad):
    return lax.psum_scatter(grad, "seq", scatter_dimension=0, tiled=True).astype(f32)


def rotary_tables(places):
    quarter = HD // 4
    ladder = jnp.exp(-math.log(10000.0) * jnp.arange(quarter, dtype=f32) / quarter)
    angles = places.astype(f32)[:, None] * ladder[None, :]
    cosine = jnp.cos(angles)
    sine = jnp.sin(angles)
    one = jnp.ones_like(cosine)
    zero = jnp.zeros_like(cosine)
    own = jnp.concatenate([cosine, cosine, one, one] * 2, axis=1)
    below = jnp.concatenate([zero, sine, zero, zero] * 2, axis=1)
    above = jnp.concatenate([-sine, zero, zero, zero] * 2, axis=1)
    return jnp.stack([own, below, above])


def turn(values, own, below, above):
    quarter = HD // 4
    return (
        values * own
        + pltpu.roll(values, quarter, 1) * below
        + pltpu.roll(values, 2 * HD - quarter, 1) * above
    )


def project_kernel(normed_ref, weight_ref, table_ref, out_ref, *, turned):
    j = pl.program_id(0)
    product = nn(normed_ref[...], weight_ref[...])

    @pl.when(j < turned)
    def _():
        for part in range(product.shape[1] // 128):
            lanes = slice(part * 128, (part + 1) * 128)
            out_ref[:, lanes] = turn(
                product[:, lanes], table_ref[0], table_ref[1], table_ref[2]
            ).astype(bf16)

    @pl.when(j >= turned)
    def _():
        out_ref[...] = product.astype(bf16)


def project(normed, weights, table, local, step=256):
    rows, width = normed.shape
    return pl.pallas_call(
        functools.partial(project_kernel, turned=2 * local // step),
        grid=(3 * local // step,),
        in_specs=[
            pl.BlockSpec((rows, width), lambda j: (0, 0)),
            pl.BlockSpec((width, step), lambda j: (0, j)),
            pl.BlockSpec((3, rows, 128), lambda j: (0, 0, 0)),
        ],
        out_specs=pl.BlockSpec((rows, step), lambda j: (0, j)),
        out_shape=jax.ShapeDtypeStruct((rows, 3 * local), bf16),
        compiler_params=kernel_params(1, 32),
        cost_estimate=pl.CostEstimate(
            flops=2 * rows * width * 3 * local,
            bytes_accessed=2 * (rows * width + 3 * local * (width + rows)),
            transcendentals=0,
        ),
        name="qkv_projection",
    )(normed, weights, table)


def head_lanes(shape):
    return lax.broadcasted_iota(jnp.int32, shape, 1) < HD


def one_head(values, first, which):
    return jnp.where(first if which == 0 else ~first, values, jnp.zeros_like(values))


def soft_rows(scores):
    peak = jnp.max(scores, axis=-1, keepdims=True)
    raised = jnp.exp(scores - peak)
    total = jnp.sum(raised, axis=-1, keepdims=True)
    return raised * (1.0 / total), peak + jnp.log(total)


def attend_rows(query, keys, values, bias):
    first = head_lanes(query.shape)
    out = None
    logs = []
    for which in range(2):
        scores = nt(one_head(query, first, which), keys) * (HD**-0.5) + bias
        weights, log_total = soft_rows(scores)
        mixed = nn(weights.astype(bf16), values)
        out = mixed if which == 0 else jnp.where(first, out, mixed)
        logs.append(log_total)
    return out, logs


def attend_rows_back(query, keys, values, bias, logs, grad):
    first = head_lanes(query.shape)
    query_grad = key_grad = value_grad = None
    for which in range(2):
        own_query = one_head(query, first, which)
        own_grad = one_head(grad, first, which)
        scores = nt(own_query, keys) * (HD**-0.5) + bias
        chances = jnp.exp(scores - logs[which])
        chance_grad = nt(own_grad, values)
        score_grad = (
            chances * (chance_grad - jnp.sum(chances * chance_grad, axis=-1, keepdims=True))
        ).astype(bf16)
        to_query = nn(score_grad, keys) * (HD**-0.5)
        to_key = tn(score_grad, own_query) * (HD**-0.5)
        to_value = tn(chances.astype(bf16), own_grad)
        if which == 0:
            query_grad, key_grad, value_grad = to_query, to_key, to_value
        else:
            query_grad = jnp.where(first, query_grad, to_query)
            key_grad = key_grad + to_key
            value_grad = value_grad + to_value
    return query_grad, key_grad, value_grad


def put_logs(log_ref, rows, logs, pair):
    lane = lax.broadcasted_iota(jnp.int32, (logs[0].shape[0], 128), 1)
    kept = log_ref[rows, :]
    kept = jnp.where(lane == 2 * pair, logs[0], kept)
    log_ref[rows, :] = jnp.where(lane == 2 * pair + 1, logs[1], kept)


def get_logs(log_ref, rows, pair):
    kept = log_ref[rows, :]
    lane = lax.broadcasted_iota(jnp.int32, kept.shape, 1)
    return [
        jnp.sum(jnp.where(lane == 2 * pair + which, kept, 0.0), axis=1, keepdims=True)
        for which in range(2)
    ]


def near(low_ref, own_ref, high_ref):
    return jnp.concatenate([low_ref[...], own_ref[...], high_ref[...]], axis=0)


def self_kernel(q_ref, k_ref, v_ref, kl_ref, vl_ref, kh_ref, vh_ref, bias_ref, out_ref, log_ref):
    pair = pl.program_id(1)
    keys = near(kl_ref, k_ref, kh_ref)
    values = near(vl_ref, v_ref, vh_ref)
    for part in range(q_ref.shape[0] // HALF):
        rows = slice(part * HALF, (part + 1) * HALF)
        span = slice(part * HALF, (part + 3) * HALF)
        out, logs = attend_rows(q_ref[rows, :], keys[span], values[span], bias_ref[rows, :])
        out_ref[rows, :] = out.astype(bf16)
        put_logs(log_ref, rows, logs, pair)


def self_specs(block_rows, pairs):
    own = lambda first: pl.BlockSpec((block_rows, 128), lambda m, h: (m, first + h))
    edge = lambda first: pl.BlockSpec((None, HALF, 128), lambda m, h: (m, 0, first + h))
    return [
        own(0),
        own(pairs),
        own(2 * pairs),
        edge(0),
        edge(pairs),
        edge(0),
        edge(pairs),
        pl.BlockSpec((block_rows, 3 * HALF), lambda m, h: (m, 0)),
    ]


def self_attention(qkv, low_rows, high_rows, bias, micro, block_rows):
    rows, width = qkv.shape
    pairs = width // 3 // 128
    return pl.pallas_call(
        self_kernel,
        grid=(micro, pairs),
        in_specs=self_specs(block_rows, pairs),
        out_specs=[
            pl.BlockSpec((block_rows, 128), lambda m, h: (m, h)),
            pl.BlockSpec((block_rows, 128), lambda m, h: (m, 0)),
        ],
        out_shape=[
            jax.ShapeDtypeStruct((rows, width // 3), bf16),
            jax.ShapeDtypeStruct((rows, 128), f32),
        ],
        compiler_params=kernel_params(2, 32),
        cost_estimate=pl.CostEstimate(
            flops=4 * rows * 3 * HALF * 128 * 2 * pairs,
            bytes_accessed=10 * rows * width,
            transcendentals=rows * 3 * HALF * 2 * pairs,
        ),
        name="self_attention",
    )(qkv, qkv, qkv, low_rows, low_rows, high_rows, high_rows, bias)


def self_back_kernel(
    q_ref, k_ref, v_ref, kl_ref, vl_ref, kh_ref, vh_ref, bias_ref, grad_ref, log_ref,
    own_ref, to_low_ref, to_high_ref,
):
    pair = pl.program_id(1)
    keys = near(kl_ref, k_ref, kh_ref)
    values = near(vl_ref, v_ref, vh_ref)
    parts = q_ref.shape[0] // HALF
    pieces = [[None] * (parts + 2), [None] * (parts + 2)]
    for part in range(parts):
        rows = slice(part * HALF, (part + 1) * HALF)
        span = slice(part * HALF, (part + 3) * HALF)
        query_grad, key_grad, value_grad = attend_rows_back(
            q_ref[rows, :],
            keys[span],
            values[span],
            bias_ref[rows, :],
            get_logs(log_ref, rows, pair),
            grad_ref[rows, :],
        )
        own_ref[0, rows, :] = query_grad
        for kind, near_grad in enumerate((key_grad, value_grad)):
            for third in range(3):
                piece = near_grad[third * HALF : (third + 1) * HALF]
                held = pieces[kind][part + third]
                pieces[kind][part + third] = piece if held is None else held + piece
    for kind in range(2):
        to_low_ref[kind] = pieces[kind][0].astype(bf16)
        for part in range(parts):
            own_ref[1 + kind, part * HALF : (part + 1) * HALF, :] = pieces[kind][part + 1]
        to_high_ref[kind] = pieces[kind][parts + 1].astype(bf16)


def self_attention_back(qkv, low_rows, high_rows, bias, grad, logs, micro, block_rows):
    rows, width = qkv.shape
    local = width // 3
    pairs = local // 128
    edge = pl.BlockSpec((2, None, HALF, 128), lambda m, h: (0, m, 0, h))
    return pl.pallas_call(
        self_back_kernel,
        grid=(micro, pairs),
        in_specs=self_specs(block_rows, pairs)
        + [
            pl.BlockSpec((block_rows, 128), lambda m, h: (m, h)),
            pl.BlockSpec((block_rows, 128), lambda m, h: (m, 0)),
        ],
        out_specs=[
            pl.BlockSpec((3, block_rows, 128), lambda m, h: (0, m, h)),
            edge,
            edge,
        ],
        out_shape=[
            jax.ShapeDtypeStruct((3, rows, local), f32),
            jax.ShapeDtypeStruct((2, micro, HALF, local), bf16),
            jax.ShapeDtypeStruct((2, micro, HALF, local), bf16),
        ],
        compiler_params=kernel_params(2, 32),
        cost_estimate=pl.CostEstimate(
            flops=10 * rows * 3 * HALF * 128 * 2 * pairs,
            bytes_accessed=20 * rows * width,
            transcendentals=rows * 3 * HALF * 2 * pairs,
        ),
        name="self_attention_back",
    )(qkv, qkv, qkv, low_rows, low_rows, high_rows, high_rows, bias, grad, logs)


def cross_kernel(q_ref, k_ref, v_ref, bias_ref, out_ref, log_ref):
    pair = pl.program_id(1)
    for part in range(q_ref.shape[0] // HALF):
        rows = slice(part * HALF, (part + 1) * HALF)
        out, logs = attend_rows(q_ref[rows, :], k_ref[...], v_ref[...], bias_ref[rows, :])
        out_ref[rows, :] = out.astype(bf16)
        put_logs(log_ref, rows, logs, pair)


def cross_specs(block_rows, pairs):
    return [
        pl.BlockSpec((block_rows, 128), lambda m, h: (m, h)),
        pl.BlockSpec((2 * TXT, 128), lambda m, h: (m, h)),
        pl.BlockSpec((2 * TXT, 128), lambda m, h: (m, h)),
        pl.BlockSpec((block_rows, 2 * TXT), lambda m, h: (m, 0)),
    ]


def cross_attention(query, keys, values, bias, micro, block_rows):
    rows, local = query.shape
    pairs = local // 128
    return pl.pallas_call(
        cross_kernel,
        grid=(micro, pairs),
        in_specs=cross_specs(block_rows, pairs),
        out_specs=[
            pl.BlockSpec((block_rows, 128), lambda m, h: (m, h)),
            pl.BlockSpec((block_rows, 128), lambda m, h: (m, 0)),
        ],
        out_shape=[
            jax.ShapeDtypeStruct((rows, local), bf16),
            jax.ShapeDtypeStruct((rows, 128), f32),
        ],
        compiler_params=kernel_params(2, 32),
        cost_estimate=pl.CostEstimate(
            flops=4 * rows * 2 * TXT * 128 * 2 * pairs,
            bytes_accessed=8 * rows * local,
            transcendentals=rows * 2 * TXT * 2 * pairs,
        ),
        name="cross_attention",
    )(query, keys, values, bias)


def cross_back_kernel(q_ref, k_ref, v_ref, bias_ref, grad_ref, log_ref, dq_ref, dk_ref, dv_ref):
    pair = pl.program_id(1)
    key_total = value_total = None
    for part in range(q_ref.shape[0] // HALF):
        rows = slice(part * HALF, (part + 1) * HALF)
        query_grad, key_grad, value_grad = attend_rows_back(
            q_ref[rows, :],
            k_ref[...],
            v_ref[...],
            bias_ref[rows, :],
            get_logs(log_ref, rows, pair),
            grad_ref[rows, :],
        )
        dq_ref[rows, :] = query_grad.astype(bf16)
        key_total = key_grad if part == 0 else key_total + key_grad
        value_total = value_grad if part == 0 else value_total + value_grad
    dk_ref[...] = key_total.astype(bf16)
    dv_ref[...] = value_total.astype(bf16)


def cross_attention_back(query, keys, values, bias, grad, logs, micro, block_rows):
    rows, local = query.shape
    pairs = local // 128
    text = pl.BlockSpec((2 * TXT, 128), lambda m, h: (m, h))
    return pl.pallas_call(
        cross_back_kernel,
        grid=(micro, pairs),
        in_specs=cross_specs(block_rows, pairs)
        + [
            pl.BlockSpec((block_rows, 128), lambda m, h: (m, h)),
            pl.BlockSpec((block_rows, 128), lambda m, h: (m, 0)),
        ],
        out_specs=[pl.BlockSpec((block_rows, 128), lambda m, h: (m, h)), text, text],
        out_shape=[
            jax.ShapeDtypeStruct((rows, local), bf16),
            jax.ShapeDtypeStruct(keys.shape, bf16),
            jax.ShapeDtypeStruct(keys.shape, bf16),
        ],
        compiler_params=kernel_params(2, 32),
        cost_estimate=pl.CostEstimate(
            flops=10 * rows * 2 * TXT * 128 * 2 * pairs,
            bytes_accessed=16 * rows * local,
            transcendentals=rows * 2 * TXT * 2 * pairs,
        ),
        name="cross_attention_back",
    )(query, keys, values, bias, grad, logs)


def ffn_kernel(
    normed_ref, normed_t_ref, cot_ref, cot_t_ref, outer_ref, gate_ref, up_ref,
    g_early_ref, g_up_ref, out_ref, back_ref, out_acc, back_acc,
):
    j = pl.program_id(0)
    gate = nn(normed_ref[...], gate_ref[...])
    up = nn(normed_ref[...], up_ref[...])
    grad = nn(cot_ref[...], outer_ref[...])
    chance = 1.0 / (1.0 + jnp.exp(-gate))
    swish = gate * chance
    active = (swish * up).astype(bf16)
    gate_grad = (grad * up * (chance * (1.0 + gate * (1.0 - chance)))).astype(bf16)
    up_grad = (grad * swish).astype(bf16)
    step = active.shape[1]
    g_early_ref[:, :step] = nn(cot_t_ref[...], active).astype(bf16)
    g_early_ref[:, step:] = nn(normed_t_ref[...], gate_grad).astype(bf16)
    g_up_ref[...] = nn(normed_t_ref[...], up_grad).astype(bf16)
    out_part = nt(active, outer_ref[...])
    back_part = nt(gate_grad, gate_ref[...]) + nt(up_grad, up_ref[...])

    @pl.when(j == 0)
    def _():
        out_acc[...] = out_part
        back_acc[...] = back_part

    @pl.when(j > 0)
    def _():
        out_acc[...] += out_part
        back_acc[...] += back_part

    @pl.when(j == pl.num_programs(0) - 1)
    def _():
        out_ref[...] = out_acc[...].astype(bf16)
        back_ref[...] = back_acc[...].astype(bf16)


FFN_STEP = 256


def feed_forward(normed, cotangent, weights, hidden, step=FFN_STEP):
    rows, width = normed.shape
    steps = hidden // step
    whole = lambda shape: pl.BlockSpec(shape, lambda j: (0, 0))
    column = lambda first: pl.BlockSpec((width, step), lambda j: (0, first + j))
    return pl.pallas_call(
        ffn_kernel,
        grid=(steps,),
        in_specs=[
            whole((rows, width)),
            whole((width, rows)),
            whole((rows, width)),
            whole((width, rows)),
            column(0),
            column(steps),
            column(2 * steps),
        ],
        out_specs=[
            pl.BlockSpec((width, 2 * step), lambda j: (0, j)),
            column(0),
            whole((rows, width)),
            whole((rows, width)),
        ],
        out_shape=[
            jax.ShapeDtypeStruct((width, 2 * hidden), bf16),
            jax.ShapeDtypeStruct((width, hidden), bf16),
            jax.ShapeDtypeStruct((rows, width), bf16),
            jax.ShapeDtypeStruct((rows, width), bf16),
        ],
        scratch_shapes=[pltpu.VMEM((rows, width), f32)] * 2,
        compiler_params=kernel_params(1, 56),
        cost_estimate=pl.CostEstimate(
            flops=18 * rows * width * hidden,
            bytes_accessed=12 * width * hidden,
            transcendentals=rows * hidden,
        ),
        name="feed_forward",
    )(normed, normed.T, cotangent, cotangent.T, weights, weights, weights)


def qkv_back_kernel(
    own_ref, after_ref, before_ref, normed_t_ref, weight_ref, table_ref,
    grad_ref, back_ref, acc, *, kind_steps, micro, block_rows,
):
    j = pl.program_id(0)
    kind = j // kind_steps
    edges = (kind > 0).astype(f32)
    turned = kind < 2
    own_factor = jnp.where(turned, table_ref[0], 1.0)
    below_factor = jnp.where(turned, -table_ref[1], 0.0)
    above_factor = jnp.where(turned, -table_ref[2], 0.0)
    total = []
    for m in range(micro):
        first = m * block_rows
        total.append(own_ref[first : first + HALF] + edges * after_ref[m].astype(f32))
        if block_rows > 2 * HALF:
            total.append(own_ref[first + HALF : first + block_rows - HALF])
        total.append(
            own_ref[first + block_rows - HALF : first + block_rows]
            + edges * before_ref[m].astype(f32)
        )
    total = jnp.concatenate(total, axis=0)
    grad = jnp.concatenate(
        [
            turn(total[:, i : i + 128], own_factor, below_factor, above_factor)
            for i in range(0, total.shape[1], 128)
        ],
        axis=1,
    ).astype(bf16)
    grad_ref[...] = nn(normed_t_ref[...], grad).astype(bf16)
    part = nt(grad, weight_ref[...])

    @pl.when(j == 0)
    def _():
        acc[...] = part

    @pl.when(j > 0)
    def _():
        acc[...] += part

    @pl.when(j == pl.num_programs(0) - 1)
    def _():
        back_ref[...] = acc[...].astype(bf16)


def qkv_back(own, after, before, normed, weights, table, micro, block_rows, step=256):
    _, rows, local = own.shape
    width = normed.shape[1]
    kind_steps = local // step
    edge = pl.BlockSpec(
        (None, micro, HALF, step),
        lambda j: (jnp.maximum(j // kind_steps - 1, 0), 0, 0, j % kind_steps),
    )
    return pl.pallas_call(
        functools.partial(
            qkv_back_kernel, kind_steps=kind_steps, micro=micro, block_rows=block_rows
        ),
        grid=(3 * kind_steps,),
        in_specs=[
            pl.BlockSpec((None, rows, step), lambda j: (j // kind_steps, 0, j % kind_steps)),
            edge,
            edge,
            pl.BlockSpec((width, rows), lambda j: (0, 0)),
            pl.BlockSpec((width, step), lambda j: (0, j)),
            pl.BlockSpec((3, rows, 128), lambda j: (0, 0, 0)),
        ],
        out_specs=[
            pl.BlockSpec((width, step), lambda j: (0, j)),
            pl.BlockSpec((rows, width), lambda j: (0, 0)),
        ],
        out_shape=[
            jax.ShapeDtypeStruct((width, 3 * local), bf16),
            jax.ShapeDtypeStruct((rows, width), bf16),
        ],
        scratch_shapes=[pltpu.VMEM((rows, width), f32)],
        compiler_params=kernel_params(1, 40),
        cost_estimate=pl.CostEstimate(
            flops=12 * rows * width * local,
            bytes_accessed=12 * width * local + 12 * rows * local,
            transcendentals=0,
        ),
        name="qkv_back",
    )(own, after, before, normed.T, weights, table)


def time_features(steps_row):
    half_width = TEMB // 2
    ladder = jnp.exp(-math.log(10000.0) * jnp.arange(half_width, dtype=f32) / half_width)
    angles = steps_row.astype(f32)[:, None] * ladder[None, :]
    return jnp.concatenate([jnp.cos(angles), jnp.sin(angles)], axis=-1)


def normalize(hidden):
    center = hidden - jnp.mean(hidden, axis=-1, keepdims=True)
    spread = jnp.mean(center * center, axis=-1, keepdims=True)
    scale = lax.rsqrt(spread + norm_eps)
    return center * scale, scale


def on_device(
    latents,
    context,
    lengths,
    text_len,
    timesteps,
    self_qkv,
    self_out,
    cross_query,
    cross_kv,
    cross_out,
    ffn_in,
    ffn_out,
    mod_weight,
    mod_bias,
    out_grad,
):
    micro, block_rows, model_width = latents.shape
    seq_count = lax.axis_size("seq")
    me = lax.axis_index("seq")
    frame_count = block_rows * seq_count
    item_count = lengths.shape[1]
    local = self_qkv.shape[2]
    hidden = ffn_in.shape[2]
    rows = micro * block_rows
    text_width = context.shape[2]

    attn_share = jnp.concatenate(
        [
            self_qkv[0],
            self_qkv[1],
            self_qkv[2],
            self_out.T,
            cross_query,
            cross_out.T,
            jnp.concatenate([cross_kv[0], cross_kv[1]], axis=0),
        ],
        axis=1,
    )
    ffn_share = jnp.concatenate([ffn_out.T, ffn_in[0], ffn_in[1]], axis=1)
    attn_all = lax.all_gather(attn_share, "seq", axis=0, tiled=True)
    ffn_all = lax.all_gather(ffn_share, "seq", axis=0, tiled=True)
    self_wt = attn_all[:, 3 * local : 4 * local]
    query_w = attn_all[:, 4 * local : 5 * local]
    cross_wt = attn_all[:, 5 * local : 6 * local]
    pair_w = attn_all[:, 6 * local :].reshape(seq_count, 2, text_width // seq_count, local)
    key_w = pair_w[:, 0].reshape(text_width, local)
    value_w = pair_w[:, 1].reshape(text_width, local)

    features = time_features(timesteps.reshape(-1))
    own_features = lax.dynamic_slice_in_dim(
        features, me * mod_weight.shape[0], mod_weight.shape[0], 1
    )
    bias_share = mod_bias.shape[1]
    bias_wide = lax.dynamic_update_slice_in_dim(
        jnp.zeros((6, model_width), f32), mod_bias.astype(f32), me * bias_share, 1
    )
    mod_part = jnp.dot(
        own_features, mod_weight.astype(f32).reshape(mod_weight.shape[0], -1), precision=highest
    ) + bias_wide.reshape(1, -1)
    modulation = seq_sum(mod_part).reshape(micro, item_count, 6, model_width)

    first_frame = me * block_rows
    own_places = first_frame + jnp.arange(block_rows, dtype=jnp.int32)
    near_places = first_frame - HALF + jnp.arange(block_rows + 2 * HALF, dtype=jnp.int32)
    near_inside = (near_places >= 0) & (near_places < frame_count)
    item_ends = jnp.cumsum(lengths, axis=1)
    item_starts = item_ends - lengths
    own_ids = jnp.sum(
        (item_ends[:, None, :] <= own_places[None, :, None]).astype(jnp.int32), axis=2
    )
    near_ids = jnp.sum(
        (item_ends[:, None, :] <= near_places[None, :, None]).astype(jnp.int32), axis=2
    )
    base_item = jnp.minimum(own_ids[:, 0], item_count - 2)
    catalog = jnp.arange(item_count, dtype=jnp.int32)
    choose = own_ids[:, :, None] == catalog[None, None, :]
    offsets_in = own_places[None, :] - jnp.sum(
        choose.astype(jnp.int32) * item_starts[:, None, :], axis=2
    )
    later = (own_ids != base_item[:, None])[:, :, None]
    two = jax.vmap(lambda table, start: lax.dynamic_slice_in_dim(table, start, 2, 0))(
        modulation, base_item
    )

    def framewise(index):
        chosen = jnp.where(later, two[:, 1, index][:, None, :], two[:, 0, index][:, None, :])
        return chosen.reshape(rows, model_width)

    table = rotary_tables(offsets_in.reshape(-1))
    windows = jnp.stack(
        [
            near_ids[:, part * HALF : (part + 3) * HALF]
            for part in range(block_rows // HALF)
        ],
        axis=1,
    )
    inside = jnp.stack(
        [near_inside[part * HALF : (part + 3) * HALF] for part in range(block_rows // HALF)]
    )
    row_in = jnp.arange(HALF, dtype=jnp.int32)
    key_in = jnp.arange(3 * HALF, dtype=jnp.int32) - HALF
    self_allowed = (
        (own_ids.reshape(micro, -1, HALF, 1) == windows[:, :, None, :])
        & inside[None, :, None, :]
        & (jnp.abs(row_in[:, None] - key_in[None, :]) <= HALF)[None, None]
    )
    self_bias = jnp.where(self_allowed, 0.0, -1e30).astype(f32).reshape(rows, 3 * HALF)
    text_slots = jnp.arange(2 * TXT, dtype=jnp.int32)
    key_items = base_item[:, None] + (text_slots // TXT)[None, :]
    key_lengths = jnp.sum(
        (key_items[:, :, None] == catalog[None, None, :]).astype(jnp.int32) * text_len[:, None, :],
        axis=2,
    )
    cross_allowed = (own_ids[:, :, None] == key_items[:, None, :]) & (
        (text_slots % TXT)[None, :] < key_lengths
    )[:, None, :]
    cross_bias = jnp.where(cross_allowed, 0.0, -1e30).astype(f32).reshape(rows, 2 * TXT)

    latent = latents.astype(f32).reshape(rows, model_width)
    cotangent = out_grad.reshape(rows, model_width)
    xhat_one, inv_one = normalize(latent)
    normed_one = (xhat_one * (1.0 + framewise(1)) + framewise(0)).astype(bf16)
    qkv = project(normed_one, attn_all, table, local)
    edges = qkv[:, local:].reshape(micro, block_rows, 2 * local)
    ahead = [(i, i + 1) for i in range(seq_count - 1)]
    behind = [(i + 1, i) for i in range(seq_count - 1)]
    low_rows = lax.ppermute(edges[:, block_rows - HALF :], "seq", ahead)
    high_rows = lax.ppermute(edges[:, :HALF], "seq", behind)
    mixed_one, logs_one = self_attention(qkv, low_rows, high_rows, self_bias, micro, block_rows)
    hidden_one = latent + pair_sum(nt(mixed_one, self_wt).astype(bf16))

    xhat_two, inv_two = normalize(hidden_one)
    normed_two = (xhat_two * (1.0 + framewise(3)) + framewise(2)).astype(bf16)
    query_two = nn(normed_two, query_w).astype(bf16)
    near_context = jax.vmap(
        lambda table, start: lax.dynamic_slice_in_dim(table, start * TXT, 2 * TXT, 0)
    )(context, base_item).reshape(micro * 2 * TXT, text_width)
    text_keys = nn(near_context, key_w).astype(bf16)
    text_values = nn(near_context, value_w).astype(bf16)
    mixed_two, logs_two = cross_attention(
        query_two, text_keys, text_values, cross_bias, micro, block_rows
    )
    hidden_two = hidden_one + pair_sum(nt(mixed_two, cross_wt).astype(bf16))

    xhat_three, inv_three = normalize(hidden_two)
    normed_three = (xhat_three * (1.0 + framewise(5)) + framewise(4)).astype(bf16)
    g_early, g_up, out_part, back_part = feed_forward(normed_three, cotangent, ffn_all, hidden)

    normed_three_grad = pair_sum(back_part)
    early = early_sum(g_early).reshape(-1, hidden // FFN_STEP, 2, FFN_STEP)
    outer_total = early[:, :, 0].reshape(-1, hidden)
    gate_total = early[:, :, 1].reshape(-1, hidden)
    block_out = (hidden_two + pair_sum(out_part)).astype(bf16)

    def norm_back(normed_grad, xhat, inv, scale_row):
        inner = normed_grad * (1.0 + scale_row)
        mean_inner = jnp.mean(inner, axis=-1, keepdims=True)
        mean_cross = jnp.mean(inner * xhat, axis=-1, keepdims=True)
        back = inv * (inner - mean_inner - xhat * mean_cross)
        cube = normed_grad.reshape(micro, block_rows, model_width)
        scaled = (normed_grad * xhat).reshape(micro, block_rows, model_width)

        def by_item(values):
            high_part = jnp.sum(jnp.where(later, values, 0.0), axis=1)
            low_part = jnp.sum(jnp.where(later, 0.0, values), axis=1)
            return jnp.stack([low_part, high_part], axis=1)

        return back, by_item(cube), by_item(scaled)

    back_three, shift_three, scale_three = norm_back(
        normed_three_grad, xhat_three, inv_three, framewise(5)
    )
    hidden_two_grad = cotangent.astype(f32) + back_three
    two_low = hidden_two_grad.astype(bf16)
    mixed_two_grad = nn(two_low, cross_wt).astype(bf16)
    query_two_low, text_key_low, text_value_low = cross_attention_back(
        query_two, text_keys, text_values, cross_bias, mixed_two_grad, logs_two, micro, block_rows
    )
    normed_two_grad = pair_sum(nt(query_two_low, query_w).astype(bf16))
    share = text_width // seq_count
    pair_grad = jnp.concatenate(
        [
            tn(near_context, text_key_low).reshape(seq_count, share, local),
            tn(near_context, text_value_low).reshape(seq_count, share, local),
        ],
        axis=1,
    ).reshape(2 * text_width, local)
    g_cross_out = tn(two_low, mixed_two).astype(bf16)
    g_cross_query = tn(normed_two, query_two_low).astype(bf16)
    back_two, shift_two, scale_two = norm_back(normed_two_grad, xhat_two, inv_two, framewise(3))
    hidden_one_grad = hidden_two_grad + back_two
    one_low = hidden_one_grad.astype(bf16)
    mixed_one_grad = nn(one_low, self_wt).astype(bf16)
    own_grads, to_low, to_high = self_attention_back(
        qkv, low_rows, high_rows, self_bias, mixed_one_grad, logs_one, micro, block_rows
    )
    from_high = lax.ppermute(to_low, "seq", behind)
    from_low = lax.ppermute(to_high, "seq", ahead)
    g_qkv, normed_one_part = qkv_back(
        own_grads, from_low, from_high, normed_one, attn_all, table, micro, block_rows
    )
    normed_one_grad = pair_sum(normed_one_part)
    g_self_out = tn(one_low, mixed_one).astype(bf16)
    (
        up_total,
        grad_cross_out,
        grad_cross_query,
        grad_cross_kv,
        grad_self_out,
        qkv_total,
    ) = scatter_sums([g_up, g_cross_out, g_cross_query, pair_grad.astype(bf16), g_self_out, g_qkv])
    back_one, shift_one, scale_one = norm_back(normed_one_grad, xhat_one, inv_one, framewise(1))
    latent_grad = hidden_one_grad + back_one

    pieces = jnp.stack(
        [shift_one, scale_one, shift_two, scale_two, shift_three, scale_three], axis=2
    )
    spots = (base_item[:, None] + jnp.arange(2)[None, :])[:, :, None] == catalog[None, None, :]
    item_grad = jnp.sum(
        jnp.where(spots[:, :, :, None, None], pieces[:, :, None], 0.0), axis=1
    ).reshape(micro * item_count, 6 * model_width)
    item_total = seq_sum(item_grad)
    mod_grad = jnp.dot(own_features.T, item_total, precision=highest).reshape(mod_weight.shape)
    bias_grad = lax.dynamic_slice_in_dim(
        jnp.sum(item_total, axis=0).reshape(6, model_width), me * bias_share, bias_share, 1
    )

    grad_qkv = jnp.stack([qkv_total[:, i * local : (i + 1) * local] for i in range(3)])
    return (
        block_out.reshape(latents.shape),
        latent_grad.reshape(latents.shape),
        grad_qkv,
        grad_self_out.T,
        grad_cross_query,
        grad_cross_kv.reshape(2, share, local),
        grad_cross_out.T,
        jnp.stack([gate_total, up_total]),
        outer_total.T,
        mod_grad,
        bias_grad,
    )


def solution(mesh):
    return jax.shard_map(
        on_device,
        mesh=mesh,
        in_specs=(
            P(None, "seq", None),
            P(),
            P(),
            P(),
            P(),
            P(None, "seq", "tensor"),
            P("tensor", "seq"),
            P("seq", "tensor"),
            P(None, "seq", "tensor"),
            P("tensor", "seq"),
            P(None, "seq", "tensor"),
            P("tensor", "seq"),
            P("seq", None, None),
            P(None, "seq"),
            P(None, "seq", None),
        ),
        out_specs=(
            P(None, "seq", None),
            P(None, "seq", None),
            P(None, "seq", "tensor"),
            P("tensor", "seq"),
            P("seq", "tensor"),
            P(None, "seq", "tensor"),
            P("tensor", "seq"),
            P(None, "seq", "tensor"),
            P("tensor", "seq"),
            P("seq", None, None),
            P(None, "seq"),
        ),
        check_vma=False,
    )
```

time: 1070 us -> 946 us (0.88)
  Pallas kernels: 0 us -> 350 us
  waiting for transfers between devices: 500 us -> 198 us
  matrix products: 193 us -> 40.1 us
  local copies, waits for them, and re-layouts: 143 us -> 183 us
  other arithmetic: 140 us -> 102 us
  starting transfers between devices: 70.7 us -> 46.2 us
    pallas_call x0 -> x8, Pallas kernels: none -> 350 us  [the longest x1 190 us: scatter_sums(): pl.pallas_call(functools.partial(scatter_kernel, widths=widths, step=step...]
    ppermute x28 -> x8, waiting for transfers between devices: 341 us -> 71.3 us  [flip(): return lax.ppermute(block, 'seq', [(i, i ^ stride) for i in range(count)])]
    dot_general x25 -> x13, matrix products: 144 us -> 38 us  [dot(): lax.dot_general(a, b, ((dims[0], dims[1]), ((), ())), preferred_element_t...]
    convert_element_type x17 -> x0, other arithmetic: 58.9 us -> none  [the longest x15 44.2 us: scatter_sum(): cur = cur.astype(bf16)]
    dot_general x12 -> x0, matrix products: 47.3 us -> none  [the longest x2 16.2 us: attend_back(): jnp.einsum('mqhd,mkhd->mhqk', mixed_grad, value_rows, preferred_element_t...]
    ppermute x28 -> x8, starting transfers between devices: 55.3 us -> 11.6 us  [flip(): return lax.ppermute(block, 'seq', [(i, i ^ stride) for i in range(count)])]
    broadcast_in_dim x0 -> x25, local copies, waits for them, and re-layouts: none -> 38.2 us  [the longest x24 38.1 us: framewise(): jnp.where(later, two[:, 1, index][:, None, :], two[:, 0, index][:, None, :])]
    squeeze x20 -> x0, local copies, waits for them, and re-layouts: 28.1 us -> none  [scatter_sum(): sent = lax.dynamic_index_in_dim(pairs, 1 - digit, 1, keepdims=False)]
  transfers between devices with their start and end apart: 40 -> 21, of which waited for: 22 -> 13; matrix products, arithmetic and copies ran while one was open for 35% -> 29% of each run, Pallas kernels for 0% -> 31%
where the time goes in v2:
time: 946 us; the launch traced here: 934 us
  Pallas kernels  350 us (37%)
  waiting for transfers between devices  198 us (21%)
  local copies, waits for them, and re-layouts  183 us (19%)
  other arithmetic  102 us (11%)
  starting transfers between devices  46.2 us (5%)
  matrix products  40.1 us (4%)
  between operations  15.7 us (2%)
    pallas_call x1, Pallas kernels, scatter_sums(): pl.pallas_call(functools.partial(scatter_kernel, widths=widths, step=step...  190 us
    ppermute x8, waiting for transfers between devices, flip(): return lax.ppermute(block, 'seq', [(i, i ^ stride) for i in range(count)])  71.3 us
    pallas_call x1, Pallas kernels, feed_forward(): pl.pallas_call(ffn_kernel, grid=(steps,), in_specs=[whole((rows, width)),...  61.9 us
    ppermute x6, waiting for transfers between devices, pair_sum(): lax.ppermute(part, 'tensor', [(i, (i + 1) % count) for i in range(count)])  55.5 us
    unnamed x224, local copies, waits for them, and re-layouts  51.1 us
    all_gather x1, waiting for transfers between devices, on_device(): attn_all = lax.all_gather(attn_share, 'seq', axis=0, tiled=True)  50.8 us
    broadcast_in_dim x24, local copies, waits for them, and re-layouts, framewise(): jnp.where(later, two[:, 1, index][:, None, :], two[:, 0, index][:, None, :])  38.1 us
    dot_general x13, matrix products, dot(): lax.dot_general(a, b, ((dims[0], dims[1]), ((), ())), preferred_element_t...  38 us
  transfers between devices with their start and end apart: 21, of which 13 were waited for; matrix products, arithmetic and copies ran while one was open for 29% of the time, Pallas kernels for 31%

profile of v2, /device:TPU:0, one launch (start us, length us, event | category | flops | bytes accessed | tf_op | source)
XLA Modules:
  0.0 934.3 jit_solution(6044583336925472189)
XLA Ops:
  27.2 7.6 collective-permute-done.1
  37.3 25.9 %collective-permute-done.2 = f32[8,9216]{1,0:T(8,128)S(1)} collective-permute-done((f32[8,9216]{1,0:T(8,128)S(1)}, f32[8,9216]{1,0:T(8,128)S(1)}, u32[]{:S(2)}, u32[]{:S(2)}) %collective-permute-start.2) | collective-permute-done | bytes 294944 | tf_op jit(solution)/shard_map/ppermute | solution.py:50
  64.5 15.7 %collective-permute-done.3 = f32[8,9216]{1,0:T(8,128)S(1)} collective-permute-done((f32[8,9216]{1,0:T(8,128)S(1)}, f32[8,9216]{1,0:T(8,128)S(1)}, u32[]{:S(2)}, u32[]{:S(2)}) %collective-permute-start.3) | collective-permute-done | bytes 294944 | tf_op jit(solution)/shard_map/ppermute | solution.py:50
  101.6 50.8 %all-gather.3.cloned.1.call-done.weight_ref = bf16[1536,5376]{1,0:T(8,128)(2,1)} async-done(((bf16[96,5376]{1,0:T(8,128)(2,1)}), bf16[1536,5376]{1,0:T(8,128)(2,1)}) %all-gather.3.cloned.1.call-update) | async-done | bytes 16515088 | tf_op jit(solution)/shard_map/all_gather | solution.py:813
  152.4 5.7 copy-done
  159.7 8.2 qkv_projection.1.q_ref.k_ref.v_ref
  176.0 20.2 %self_attention.1 = (bf16[512,768]{1,0:T(8,128)(2,1)S(1)}, f32[512,128]{1,0:T(8,128)S(1)}) custom-call(bf16[512,2304]{1,0:T(8,128)(2,1)S(1)} %qkv_projection.1.q_ref.k_ref.v_ref, bf16[512,2304]{1,0:T(8,128)(2,1)S(1)} %qkv_projection.1.q_ref.k_ref.v_ref, bf16[512,2304]{1,0:T(8,128)(2,1)S(1)} %qkv_projection.1.q_ref.k_ref.v_ref, ...), custom_call_target="tpu_custom_call" | custom-call | flops 1207959552 | bytes 11796480 | tf_op jit(solution)/shard_map/self_attention/pallas_call | solution.py:416
  202.0 7.5 while.1
  246.9 11.5 %cross_attention.1 = (bf16[512,768]{1,0:T(8,128)(2,1)S(1)}, f32[512,128]{1,0:T(8,128)S(1)}) custom-call(bf16[512,768]{1,0:T(8,128)(2,1)S(1)} %fusion.15.q_ref, bf16[512,768]{1,0:T(8,128)(2,1)S(1)} %convolution_convert_fusion.9.k_ref, bf16[512,768]{1,0:T(8,128)(2,1)S(1)} %convolution_convert_fusion.8.v_ref, f32[512,256]{1,0:T(8,128)S(1)} %copy-done.11), custom_call_target="tpu_custom_call" | custom-call | flops 805306368 | bytes 3145728 | tf_op jit(solution)/shard_map/cross_attention/pallas_call | solution.py:525
  297.0 11.9 %all-gather.5.cloned.1.call-done.outer_ref.gate_ref.up_ref = bf16[1536,9216]{1,0:T(8,128)(2,1)} async-done(((bf16[96,9216]{1,0:T(8,128)(2,1)}), bf16[1536,9216]{1,0:T(8,128)(2,1)}) %all-gather.5.cloned.1.call-update) | async-done | bytes 28311568 | tf_op jit(solution)/shard_map/all_gather | solution.py:814
  308.9 61.9 %feed_forward.1 = (bf16[1536,6144]{1,0:T(8,128)(2,1)}, bf16[1536,3072]{1,0:T(8,128)(2,1)}, bf16[512,1536]{1,0:T(8,128)(2,1)}, bf16[512,1536]{1,0:T(8,128)(2,1)}) custom-call(bf16[512,1536]{1,0:T(8,128)(2,1)} %copy.250.normed_ref, bf16[1536,512]{1,0:T(8,128)(2,1)} %bitcast.286, bf16[512,1536]{1,0:T(8,128)(2,1)} %bitcast.316, bf16[1536,512]{1,0:T(8,128)(2,1)} %bitcast.285, ...), custom_call_target="tpu_custom_call" | custom-call | flops 43486543872 | bytes 56623104 | tf_op jit(solution)/shard_map/feed_forward/pallas_call | solution.py:639
  378.2 15.9 %collective-permute-done.9 = bf16[512,1536]{0,1:T(8,128)(2,1)} collective-permute-done((bf16[512,1536]{0,1:T(8,128)(2,1)}, bf16[512,1536]{0,1:T(8,128)(2,1)}, u32[]{:S(2)}, u32[]{:S(2)}) %collective-permute-start.9) | collective-permute-done | bytes 1572896 | tf_op jit(solution)/shard_map/ppermute | solution.py:55
  394.1 9.7 %fusion.53 = (f32[512]{0:T(512)S(1)}, f32[512]{0:T(512)S(1)}, f32[512,1536]{0,1:T(8,128)}, f32[512,1536]{0,1:T(8,128)}, f32[512,1536]{0,1:T(8,128)}) fusion(f32[512]{0:T(512)S(1)} %add_rsqrt_fusion, f32[512,1536]{0,1:T(8,128)} %copy-done.36, f32[512]{0:T(512)S(1)} %broadcast_multiply_fusion.6, f32[512,1536]{0,1:T(8,128)} %bitcast.261, ...), kind=kLoop, calls=%fused_computation.190 | loop fusion | flops 9436160 | bytes 22028800 | tf_op jit(solution)/shard_map/reduce_sum | solution.py:930
  403.8 21.2 %collective-permute-done.8 = bf16[512,1536]{0,1:T(8,128)(2,1)S(1)} collective-permute-done((bf16[512,1536]{0,1:T(8,128)(2,1)}, bf16[512,1536]{0,1:T(8,128)(2,1)S(1)}, u32[]{:S(2)}, u32[]{:S(2)}) %collective-permute-start.8) | collective-permute-done | bytes 1572896 | tf_op jit(solution)/shard_map/ppermute | solution.py:55
  426.2 6.4 multiply_add_fusion.2
  432.6 5.2 fusion.18.grad_ref
  437.9 18.5 %cross_attention_back.1 = (bf16[512,768]{1,0:T(8,128)(2,1)S(1)}, bf16[512,768]{1,0:T(8,128)(2,1)S(1)}, bf16[512,768]{1,0:T(8,128)(2,1)S(1)}) custom-call(bf16[512,768]{1,0:T(8,128)(2,1)S(1)} %copy-done.24, bf16[512,768]{1,0:T(8,128)(2,1)S(1)} %copy-done.22, bf16[512,768]{1,0:T(8,128)(2,1)S(1)} %copy-done.20, f32[512,256]{1,0:T(8,128)S(1)} %copy-done.12, ...), custom_call_target="tpu_custom_call" | custom-call | flops 2013265920 | bytes 6291456 | tf_op jit(solution)/shard_map/cross_attention_back/pallas_call | solution.py:571
  460.2 18.4 %collective-permute-done.10 = bf16[512,1536]{0,1:T(8,128)(2,1)S(1)} collective-permute-done((bf16[512,1536]{0,1:T(8,128)(2,1)S(1)}, bf16[512,1536]{0,1:T(8,128)(2,1)S(1)}, u32[]{:S(2)}, u32[]{:S(2)}) %collective-permute-start.10) | collective-permute-done | bytes 1572896 | tf_op jit(solution)/shard_map/ppermute | solution.py:55
  478.6 7.3 fusion.52
  494.3 23.2 %self_attention_back.1 = (f32[3,512,768]{2,1,0:T(8,128)S(1)}, bf16[2,2,128,768]{3,2,1,0:T(8,128)(2,1)}, bf16[2,2,128,768]{3,2,1,0:T(8,128)(2,1)}) custom-call(bf16[512,2304]{1,0:T(8,128)(2,1)S(1)} %qkv_projection.1.q_ref.k_ref.v_ref, bf16[512,2304]{1,0:T(8,128)(2,1)S(1)} %qkv_projection.1.q_ref.k_ref.v_ref, ...), custom_call_target="tpu_custom_call" | custom-call | flops 3019898880 | bytes 23592960 | tf_op jit(solution)/shard_map/self_attention_back/pallas_call | solution.py:476
  519.6 20.6 %collective-permute-start.11 = (bf16[2,2,128,768]{3,2,1,0:T(8,128)(2,1)}, bf16[2,2,128,768]{3,2,1,0:T(8,128)(2,1)S(1)}, u32[]{:S(2)}, u32[]{:S(2)}) collective-permute-start(bf16[2,2,128,768]{3,2,1,0:T(8,128)(2,1)} %get-tuple-element.35), channel_id=1, source_target_pairs={{0,2},{2,4},{4,6},{6,8},{8,10},{10,12},{12,14},{14,16},{16,18},{18... | collective-permute-start | bytes 2359304 | tf_op jit(solution)/shard_map/ppermute | solution.py:971
  551.1 5.5 reshape.480
  558.4 8.5 collective-permute-done.12.before_ref
  569.3 16.3 %qkv_back.1 = (bf16[1536,2304]{1,0:T(8,128)(2,1)}, bf16[512,1536]{1,0:T(8,128)(2,1)S(1)}) custom-call(f32[3,512,768]{2,1,0:T(8,128)S(1)} %copy-done.14, bf16[2,2,128,768]{3,2,1,0:T(8,128)(2,1)S(1)} %collective-permute-done.11.after_ref, bf16[2,2,128,768]{3,2,1,0:T(8,128)(2,1)S(1)} %collective-permute-done.12.before_ref, bf16[1536,512]{1,0:T(8,128)(2,1)S(1)} %bitcast.248, ...), custom_call_target="tpu_custom_call" | custom-call | flops 7247757312 | bytes 18874368 | tf_op jit(solution)/shard_map/qkv_back/pallas_call | solution.py:727
  601.4 5.3 reshape.478
  611.9 189.7 %scatter_sums.1 = f32[96,8448]{1,0:T(8,128)S(1)} custom-call(bf16[2,2,2,2,96,3072]{5,4,3,2,1,0:T(8,128)(2,1)} %bitcast.283, bf16[2,2,2,2,96,768]{5,4,3,2,1,0:T(8,128)(2,1)S(1)} %bitcast.250, bf16[2,2,2,2,96,768]{5,4,3,2,1,0:T(8,128)(2,1)S(1)} %bitcast.249, bf16[2,2,2,2,96,768]{5,4,3,2,1,0:T(8,128)(2,1)S(1)} %bitcast.247, ...), custom_call_target="tpu_custom_call" | custom-call | bytes 103809024 | tf_op jit(solution)/shard_map/scatter_sums/pallas_call | solution.py:219
  801.7 6.6 fusion.51
  818.6 35.2 %select_reduce_fusion.1 = (f32[2,1536]{0,1:T(8,128)}, f32[2,1536]{0,1:T(8,128)}, f32[2,1536]{0,1:T(8,128)}, f32[2,1536]{0,1:T(8,128)}, f32[2,1536]{0,1:T(8,128)}...) fusion(f32[2,256,1536]{1,0,2:T(2,128)} %reshape.481, ...), kind=kLoop, calls=%fused_computation.8 | loop fusion | flops 18837504 | bytes 19022336 | tf_op jit(solution)/shard_map/reduce_sum | solution.py:938
  876.2 6.0 collective-permute-done.15
  884.9 6.5 collective-permute-done.16
  897.3 9.1 collective-permute-done.17
  914.1 7.4 slice_reduce_fusion
  (437 shorter events, 256.7 us)
Async XLA Ops:
  7.2 145.2 %all-gather.3.cloned.1.call-start = ((), (), s32[]{:S(2)}) async-start(), calls=%async_computation.1 | async-start | bytes 17547264 | tf_op jit(solution)/shard_map/all_gather | solution.py:813
  14.9 294.0 %all-gather.5.cloned.1.call-start = ((), (), s32[]{:S(2)}) async-start(), calls=%async_computation.2 | async-start | bytes 30081024 | tf_op jit(solution)/shard_map/all_gather | solution.py:814
  16.4 894.3 %reduce-scatter.2.cloned.1.call-start = ((), (), s32[]{:S(2)}) async-start(), calls=%async_computation.3 | async-start | bytes 20054016 | tf_op jit(solution)/shard_map/reduce_scatter | solution.py:249
  17.4 3.6 collective-permute-start
  21.1 13.7 %collective-permute-start.1 = (f32[8,9216]{1,0:T(8,128)S(1)}, f32[8,9216]{1,0:T(8,128)}, u32[]{:S(2)}, u32[]{:S(2)}) collective-permute-start(f32[8,9216]{1,0:T(8,128)S(1)} %add.226), channel_id=1, source_target_pairs={{0,4},{2,6},{4,0},{6,2},{8,12},{10,14},{12,8},{14,10},{16,20},{18,... | collective-permute-start | bytes 884744 | tf_op jit(solution)/shard_map/ppermute | solution.py:50
  23.8 71.1 %copy-start.84 = (f32[1,2,2,128]{3,1,2,0:T(2,128)}, f32[1,2,2,128]{3,1,2,0:T(2,128)S(1)}, u32[]{:S(2)}) copy-start(f32[1,2,2,128]{3,1,2,0:T(2,128)S(1)} %copy.300) | copy-start | bytes 6148
  23.8 71.1 %copy-start.86 = (f32[1,2,2,128]{3,1,2,0:T(2,128)}, f32[1,2,2,128]{3,1,2,0:T(2,128)S(1)}, u32[]{:S(2)}) copy-start(f32[1,2,2,128]{3,1,2,0:T(2,128)S(1)} %copy.301) | copy-start | bytes 6148
  27.2 125.2 %copy-start.7 = (f32[3,512,128]{2,1,0:T(8,128)}, f32[3,512,128]{2,1,0:T(8,128)S(1)}, u32[]{:S(2)}) copy-start(f32[3,512,128]{2,1,0:T(8,128)S(1)} %pad_maximum_fusion.4.table_ref) | copy-start | bytes 2359300
  35.8 27.4 %collective-permute-start.2 = (f32[8,9216]{1,0:T(8,128)S(1)}, f32[8,9216]{1,0:T(8,128)S(1)}, u32[]{:S(2)}, u32[]{:S(2)}) collective-permute-start(f32[8,9216]{1,0:T(8,128)S(1)} %add.227), channel_id=1, source_target_pairs={{0,8},{2,10},{4,12},{6,14},{8,0},{10,2},{12,4},{14,6},{16,24},{18,... | collective-permute-start | bytes 884744 | tf_op jit(solution)/shard_map/ppermute | solution.py:50
  63.3 17.0 %collective-permute-start.3 = (f32[8,9216]{1,0:T(8,128)S(1)}, f32[8,9216]{1,0:T(8,128)S(1)}, u32[]{:S(2)}, u32[]{:S(2)}) collective-permute-start(f32[8,9216]{1,0:T(8,128)S(1)} %add.228), channel_id=1, source_target_pairs={{0,16},{2,18},{4,20},{6,22},{8,24},{10,26},{12,28},{14,30},{16,0},... | collective-permute-start | bytes 884744 | tf_op jit(solution)/shard_map/ppermute | solution.py:50
  169.3 6.7 collective-permute-start.5
  170.6 5.4 collective-permute-start.4
  200.7 32.1 %collective-permute-start.6 = (bf16[512,1536]{0,1:T(8,128)(2,1)}, bf16[512,1536]{0,1:T(8,128)(2,1)}, u32[]{:S(2)}, u32[]{:S(2)}) collective-permute-start(bf16[512,1536]{0,1:T(8,128)(2,1)} %convolution_convert_fusion.5), channel_id=1, source_target_pairs={{0,1},{1,0},{2,3},{3,2},{4,5},{5,4},{6,7},{7,6},{8,9},{9,8},{10,11... | collective-permute-start | bytes 4718600 | tf_op jit(solution)/shard_map/ppermute | solution.py:55
  263.1 21.1 %collective-permute-start.7 = (bf16[512,1536]{0,1:T(8,128)(2,1)}, bf16[512,1536]{0,1:T(8,128)(2,1)}, u32[]{:S(2)}, u32[]{:S(2)}) collective-permute-start(bf16[512,1536]{0,1:T(8,128)(2,1)} %convolution_convert_fusion.4), channel_id=1, source_target_pairs={{0,1},{1,0},{2,3},{3,2},{4,5},{5,4},{6,7},{7,6},{8,9},{9,8},{10,11... | collective-permute-start | bytes 4718600 | tf_op jit(solution)/shard_map/ppermute | solution.py:55
  373.4 20.7 %collective-permute-start.9 = (bf16[512,1536]{0,1:T(8,128)(2,1)}, bf16[512,1536]{0,1:T(8,128)(2,1)}, u32[]{:S(2)}, u32[]{:S(2)}) collective-permute-start(bf16[512,1536]{0,1:T(8,128)(2,1)} %copy.254), channel_id=1, source_target_pairs={{0,1},{1,0},{2,3},{3,2},{4,5},{5,4},{6,7},{7,6},{8,9},{9,8},{10,11... | collective-permute-start | bytes 4718600 | tf_op jit(solution)/shard_map/ppermute | solution.py:55
  377.8 48.3 %copy-start.37 = (f32[512,1536]{0,1:T(8,128)S(1)}, f32[512,1536]{0,1:T(8,128)}, u32[]{:S(2)}) copy-start(f32[512,1536]{0,1:T(8,128)} %copy-done.36) | copy-start | bytes 9437188
  377.8 47.2 %collective-permute-start.8 = (bf16[512,1536]{0,1:T(8,128)(2,1)}, bf16[512,1536]{0,1:T(8,128)(2,1)S(1)}, u32[]{:S(2)}, u32[]{:S(2)}) collective-permute-start(bf16[512,1536]{0,1:T(8,128)(2,1)} %copy.252), channel_id=1, source_target_pairs={{0,1},{1,0},{2,3},{3,2},{4,5},{5,4},{6,7},{7,6},{8,9},{9,8},{10,11... | collective-permute-start | bytes 4718600 | tf_op jit(solution)/shard_map/ppermute | solution.py:55
  458.0 20.5 %collective-permute-start.10 = (bf16[512,1536]{0,1:T(8,128)(2,1)S(1)}, bf16[512,1536]{0,1:T(8,128)(2,1)S(1)}, u32[]{:S(2)}, u32[]{:S(2)}) collective-permute-start(bf16[512,1536]{0,1:T(8,128)(2,1)S(1)} %convolution_convert_fusion.3), channel_id=1, source_target_pairs={{0,1},{1,0},{2,3},{3,2},{4,5},{5,4},{6,7},{7,6},{8,9},{9,8},{10,11... | collective-permute-start | bytes 4718600 | tf_op jit(solution)/shard_map/ppermute | solution.py:55
  494.2 47.3 %copy-start.89 = (s32[2]{0:T(128)S(1)}, s32[2]{0:T(128)}, u32[]{:S(2)}) copy-start(s32[2]{0:T(128)} %copy-done.88) | copy-start | bytes 28
  494.2 48.9 %copy-start.79 = (s32[2,256]{1,0:T(2,128)S(1)}, s32[2,256]{1,0:T(2,128)}, u32[]{:S(2)}) copy-start(s32[2,256]{1,0:T(2,128)} %copy-done.78) | copy-start | bytes 6148
  519.6 38.8 %collective-permute-start.11 = (bf16[2,2,128,768]{3,2,1,0:T(8,128)(2,1)}, bf16[2,2,128,768]{3,2,1,0:T(8,128)(2,1)S(1)}, u32[]{:S(2)}, u32[]{:S(2)}) collective-permute-start(bf16[2,2,128,768]{3,2,1,0:T(8,128)(2,1)} %get-tuple-element.35), channel_id=1, source_target_pairs={{0,2},{2,4},{4,6},{6,8},{8,10},{10,12},{12,14},{14,16},{16,18},{18... | collective-permute-start | bytes 2359304 | tf_op jit(solution)/shard_map/ppermute | solution.py:971
  540.2 26.7 %collective-permute-start.12 = (bf16[2,2,128,768]{3,2,1,0:T(8,128)(2,1)}, bf16[2,2,128,768]{3,2,1,0:T(8,128)(2,1)S(1)}, u32[]{:S(2)}, u32[]{:S(2)}) collective-permute-start(bf16[2,2,128,768]{3,2,1,0:T(8,128)(2,1)} %get-tuple-element.36), channel_id=1, source_target_pairs={{2,0},{4,2},{6,4},{8,6},{10,8},{12,10},{14,12},{16,14},{18,16},{20... | collective-permute-start | bytes 2359304 | tf_op jit(solution)/shard_map/ppermute | solution.py:970
  587.1 214.5 %collective-permute-start.13 = (bf16[512,1536]{0,1:T(8,128)(2,1)}, bf16[512,1536]{0,1:T(8,128)(2,1)}, u32[]{:S(2)}, u32[]{:S(2)}) collective-permute-start(bf16[512,1536]{0,1:T(8,128)(2,1)} %copy.257), channel_id=1, source_target_pairs={{0,1},{1,0},{2,3},{3,2},{4,5},{5,4},{6,7},{7,6},{8,9},{9,8},{10,11... | collective-permute-start | bytes 4718600 | tf_op jit(solution)/shard_map/ppermute | solution.py:55
  611.9 189.8 %copy-start.40 = (f32[512,1536]{0,1:T(8,128)S(1)}, f32[512,1536]{0,1:T(8,128)}, u32[]{:S(2)}) copy-start(f32[512,1536]{0,1:T(8,128)} %copy.281) | copy-start | bytes 9437188
  611.9 189.8 %copy-start.43 = (f32[192,8,2,256]{3,1,2,0:T(8,128)S(1)}, f32[192,8,2,256]{3,1,2,0:T(8,128)}, u32[]{:S(2)}) copy-start(f32[192,8,2,256]{3,1,2,0:T(8,128)} %copy-done.42) | copy-start | bytes 9437188
  611.9 189.8 %copy-start.45 = (f32[192,8,2,256]{3,1,2,0:T(8,128)S(1)}, f32[192,8,2,256]{3,1,2,0:T(8,128)}, u32[]{:S(2)}) copy-start(f32[192,8,2,256]{3,1,2,0:T(8,128)} %copy-done.44) | copy-start | bytes 9437188
  611.9 189.8 %copy-start.85 = (f32[1,2,2,128]{3,1,2,0:T(2,128)S(1)}, f32[1,2,2,128]{3,1,2,0:T(2,128)}, u32[]{:S(2)}) copy-start(f32[1,2,2,128]{3,1,2,0:T(2,128)} %copy-done.84) | copy-start | bytes 6148
  611.9 189.8 %copy-start.87 = (f32[1,2,2,128]{3,1,2,0:T(2,128)S(1)}, f32[1,2,2,128]{3,1,2,0:T(2,128)}, u32[]{:S(2)}) copy-start(f32[1,2,2,128]{3,1,2,0:T(2,128)} %copy-done.86) | copy-start | bytes 6148
  871.5 1.6 collective-permute-start.14
  873.2 9.1 collective-permute-start.15
  882.3 9.1 collective-permute-start.16
  891.4 15.0 %collective-permute-start.17 = (f32[8,9216]{1,0:T(8,128)S(1)}, f32[8,9216]{1,0:T(8,128)}, u32[]{:S(2)}, u32[]{:S(2)}) collective-permute-start(f32[8,9216]{1,0:T(8,128)S(1)} %add.262), channel_id=1, source_target_pairs={{0,16},{2,18},{4,20},{6,22},{8,24},{10,26},{12,28},{14,30},{16,0},... | collective-permute-start | bytes 884744 | tf_op jit(solution)/shard_map/ppermute | solution.py:50
  (88 other events, 660.7 us)
Sparse Core Ops, SparseCore 0:
  15.0 137.3 all-gather.2
  154.6 154.2 all-gather.4
  370.9 231.1 reduce-scatter.1

commit v3 on v2

v3 whole, which is shorter than its diff:
```python
import functools
import math

import jax
import jax.numpy as jnp
import numpy as np
from jax import lax
from jax.experimental import pallas as pl
from jax.experimental.pallas import tpu as pltpu
from jax.sharding import PartitionSpec as P

HD = 64
TXT = 128
TEMB = 256
HALF = 128


norm_eps = 1e-05
highest = lax.Precision.HIGHEST
f32 = jnp.float32
bf16 = jnp.bfloat16


def dot(a, b, dims):
    return lax.dot_general(a, b, ((dims[0], dims[1]), ((), ())), preferred_element_type=f32)


def nn(a, b):
    return dot(a, b, ((1,), (0,)))


def nt(a, b):
    return dot(a, b, ((1,), (1,)))


def tn(a, b):
    return dot(a, b, ((0,), (0,)))


def halves(count):
    stride = 1
    strides = []
    while stride < count:
        strides.append(stride)
        stride *= 2
    return strides


def flip(block, stride):
    count = lax.axis_size("seq")
    return lax.ppermute(block, "seq", [(i, i ^ stride) for i in range(count)])


def swap(part):
    count = lax.axis_size("tensor")
    return lax.ppermute(part, "tensor", [(i, (i + 1) % count) for i in range(count)])


def seq_sum(part):
    for stride in halves(lax.axis_size("seq")):
        part = part + flip(part, stride)
    return part


def kernel_params(grid_rank, mib):
    return pltpu.CompilerParams(
        dimension_semantics=("arbitrary",) * grid_rank, vmem_limit_bytes=mib * 1024 * 1024
    )


STRIDES = (1, 2, 4, 8)


def seq_digits(me):
    return [(me // stride) % 2 for stride in STRIDES]


def greet(me, digits, others=()):
    partners = [me + stride * (1 - 2 * digit) for stride, digit in zip(STRIDES, digits)]
    barrier = pltpu.get_barrier_semaphore()

    def tell(target):
        pl.semaphore_signal(
            barrier, inc=1, device_id={"seq": target}, device_id_type=pl.DeviceIdType.MESH
        )

    expected = len(partners)
    for partner in partners:
        tell(partner)
    for there, target in others:
        pl.when(there)(functools.partial(tell, target))
        expected = expected + there.astype(jnp.int32)
    pl.semaphore_wait(barrier, expected)
    return partners


def send_to(partner, source, target, send_sem, recv_sem):
    return pltpu.make_async_remote_copy(
        src_ref=source,
        dst_ref=target,
        send_sem=send_sem,
        recv_sem=recv_sem,
        device_id={"seq": partner},
        device_id_type=pl.DeviceIdType.MESH,
    )


def small_sum(partners, part_ref, held, got, total_ref, send_sem, recv_sem):
    def exchange(k):
        return send_to(partners[k], held.at[k], got.at[k], send_sem.at[k], recv_sem.at[k])

    def step(k):
        if k == 0:
            held[0] = part_ref[...]
        else:
            exchange(k - 1).wait()
            summed = held[k - 1] + got[k - 1]
            if k == len(STRIDES):
                total_ref[...] = summed
            else:
                held[k] = summed
        if k < len(STRIDES):
            exchange(k).start()

    return step


def small_scratch(shape):
    return [
        pltpu.VMEM((len(STRIDES),) + shape, f32),
        pltpu.VMEM((len(STRIDES),) + shape, f32),
        pltpu.SemaphoreType.DMA((len(STRIDES),)),
        pltpu.SemaphoreType.DMA((len(STRIDES),)),
    ]


def lane_ladder():
    quarter = HD // 4
    return np.exp(-math.log(10000.0) * (np.arange(128) % quarter) / quarter).astype(np.float32)


def prepare(first, frame_count, lengths, text_len, block_rows):
    items = len(lengths)
    ends = [lengths[0]]
    for length in lengths[1:]:
        ends.append(ends[-1] + length)

    def item_of(place):
        return sum((end <= place).astype(jnp.int32) for end in ends)

    def pick(ids, values):
        return sum(jnp.where(ids == k, value, 0) for k, value in enumerate(values))

    near_rows = block_rows + 2 * HALF
    place = first - HALF + lax.broadcasted_iota(jnp.int32, (near_rows, 1), 0)
    ids = item_of(place)
    offset = place - pick(ids, [end - length for end, length in zip(ends, lengths)])
    base = jnp.minimum(item_of(first), items - 2)
    own_ids = ids[HALF : HALF + block_rows]
    self_bias = []
    for part in range(block_rows // HALF):
        row = lax.broadcasted_iota(jnp.int32, (HALF, 1), 0)
        key = lax.broadcasted_iota(jnp.int32, (1, 3 * HALF), 1) - HALF
        key_place = first + part * HALF + key
        inside = (key_place >= 0) & (key_place < frame_count)
        key_ids = jnp.where(inside, item_of(key_place), -1)
        near_enough = jnp.abs(row - key) <= HALF
        same = own_ids[part * HALF : (part + 1) * HALF] == key_ids
        self_bias.append(jnp.where(near_enough & same, 0.0, -1e30))
    slot = lax.broadcasted_iota(jnp.int32, (1, 2 * TXT), 1)
    key_item = jnp.where(slot < TXT, base, base + 1)
    used = jnp.where(slot < TXT, slot, slot - TXT) < pick(key_item, text_len)
    key_item = jnp.where(used, key_item, -1)
    cross_bias = jnp.where(own_ids == key_item, 0.0, -1e30)
    later = (ids != base).astype(f32)
    return base, offset, later, self_bias, cross_bias


def lane_tables(offset, ladder):
    quarter = HD // 4
    angles = offset.astype(f32) * ladder
    lane = lax.broadcasted_iota(jnp.int32, angles.shape, 1) % HD
    cosine = jnp.cos(angles)
    sine = jnp.sin(angles)
    return (
        jnp.where(lane < 2 * quarter, cosine, 1.0),
        jnp.where((lane >= quarter) & (lane < 2 * quarter), sine, 0.0),
        jnp.where(lane < quarter, -sine, 0.0),
    )


def gather_kernel(
    share_ref, part_ref, latent_ref, lengths_ref, text_ref, ladder_ref,
    out_ref, near_normed_ref, normed_t_ref, two_ref, later_ref, table_ref, self_ref, cross_ref,
    near_ref, total_ref, held, got, small_send, small_recv, copy_sem, send_sem, recv_sem,
    near_sem, halo_send, halo_recv, *, pieces, step, y_first, seq_count,
):
    micro, block_rows, width = latent_ref.shape
    items = lengths_ref.shape[1]
    near_rows = block_rows + 2 * HALF
    me = lax.axis_index("seq")
    digits = seq_digits(me)
    core, y, z_lo, z_hi = digits
    first = me * block_rows
    has_low = me > 0
    has_high = me < seq_count - 1
    partners = greet(me, digits, ((has_low, me - 1), (has_high, me + 1)))
    small = small_sum(partners, part_ref, held, got, total_ref, small_send, small_recv)

    def to_low():
        return send_to(
            me - 1,
            latent_ref.at[:, :HALF],
            near_ref.at[:, near_rows - HALF :],
            halo_send.at[0],
            halo_recv.at[0],
        )

    def to_high():
        return send_to(
            me + 1,
            latent_ref.at[:, block_rows - HALF :],
            near_ref.at[:, :HALF],
            halo_send.at[1],
            halo_recv.at[1],
        )

    def load_own():
        return pltpu.make_async_copy(
            latent_ref, near_ref.at[:, HALF : near_rows - HALF], near_sem
        )

    def piece(p):
        return pl.ds(p * step, step)

    def exchange(p, stage):
        cols = piece(p)
        if p in y_first:
            axis = (1, 3, 2, 0)[stage]
            spots = ((z_hi, z_lo, y, core), (z_hi, z_lo, None, core), (None, z_lo, None, core), None)
        else:
            axis = (3, 2, 1, 0)[stage]
            spots = ((z_hi, z_lo, y, core), (None, z_lo, y, core), (None, None, y, core), None)
        spot = spots[stage] or (None, None, None, core)
        index = tuple(slice(None) if digit is None else digit for digit in spot)
        block = out_ref.at[index + (slice(None), cols)]
        source = share_ref.at[:, cols] if stage == 0 else block
        return send_to(partners[axis], source, block, send_sem.at[stage, p], recv_sem.at[stage, p])

    def own(p):
        return pltpu.make_async_copy(
            share_ref.at[:, piece(p)],
            out_ref.at[z_hi, z_lo, y, core, :, piece(p)],
            copy_sem.at[p],
        )

    def masks(m):
        base, offset, later, self_bias, cross_bias = prepare(
            first,
            seq_count * block_rows,
            [lengths_ref[m, k] for k in range(items)],
            [text_ref[m, k] for k in range(items)],
            block_rows,
        )
        rows = slice(m * block_rows, (m + 1) * block_rows)
        later_ref[rows, :] = later[HALF : HALF + block_rows]
        for part, bias in enumerate(self_bias):
            start = m * block_rows + part * HALF
            self_ref[start : start + HALF, :] = bias
        cross_ref[rows, :] = cross_bias
        state[m] = base, offset, later

    def tables(m, start):
        offset = state[m][1][start : start + HALF]
        target = m * near_rows + start
        for index, values in enumerate(lane_tables(offset, ladder_ref[...])):
            table_ref[index, target : target + HALF, :] = values

    def modulation(m, base):
        for which in range(2):
            two_ref[m, which : which + 1] = sum(
                jnp.where(base + which == k, total_ref[m * items + k : m * items + k + 1], 0.0)
                for k in range(items)
            )

    def norm(m, start):
        shift = [two_ref[m, which : which + 1, :width] for which in range(2)]
        factor = [two_ref[m, which : which + 1, width : 2 * width] for which in range(2)]
        tile = near_ref[m, start : start + HALF].astype(f32)
        chosen = state[m][2][start : start + HALF] > 0.5
        xhat, _ = spread_rows(tile)
        normed = (
            xhat * (1.0 + jnp.where(chosen, factor[1], factor[0]))
            + jnp.where(chosen, shift[1], shift[0])
        ).astype(bf16)
        target = m * near_rows + start
        near_normed_ref[target : target + HALF, :] = normed
        if HALF <= start < HALF + block_rows:
            target = m * block_rows + start - HALF
            normed_t_ref[:, target : target + HALF] = normed.T

    beside = {}
    state = {}
    gap = 4

    def add(t, work):
        beside.setdefault(t, []).append(work)

    def finish_near():
        load_own().wait()
        pl.when(has_low)(lambda: to_high().wait_recv())
        pl.when(has_high)(lambda: to_low().wait_recv())

    tick = 1
    for m in range(micro):
        add(tick, functools.partial(masks, m))
        for start in range(0, near_rows, HALF):
            tick += 1
            add(tick, functools.partial(tables, m, start))
        tick += 1
    for k in range(1, len(STRIDES) + 1):
        add(gap * k, functools.partial(small, k))
    tick = gap * len(STRIDES)
    add(tick, finish_near)
    for m in range(micro):
        tick += 1
        add(tick, lambda m=m: modulation(m, state[m][0]))
        for start in range(0, near_rows, HALF):
            add(tick, functools.partial(norm, m, start))
            tick += 1
    last_tick = tick

    small(0)
    load_own().start()
    pl.when(has_low)(lambda: to_low().start())
    pl.when(has_high)(lambda: to_high().start())

    @pl.when(jnp.logical_not(has_low))
    def _():
        near_ref[:, :HALF] = jnp.zeros((micro, HALF, width), near_ref.dtype)

    @pl.when(jnp.logical_not(has_high))
    def _():
        near_ref[:, near_rows - HALF :] = jnp.zeros((micro, HALF, width), near_ref.dtype)

    lags = (0, 3, 6, 10, 12)
    for t in range(max(pieces + lags[-1], last_tick + 1)):
        if t < pieces:
            exchange(t, 0).start()
            own(t).start()
        for stage in (1, 2, 3):
            p = t - lags[stage]
            if 0 <= p < pieces:
                if stage == 1:
                    own(p).wait()
                exchange(p, stage - 1).wait_recv()
                exchange(p, stage).start()
        if 0 <= t - lags[4] < pieces:
            exchange(t - lags[4], 3).wait_recv()
        for work in beside.get(t, ()):
            work()
    for p in range(pieces):
        for stage in range(4):
            exchange(p, stage).wait_send()
    pl.when(has_low)(lambda: to_low().wait_send())
    pl.when(has_high)(lambda: to_high().wait_send())


def gather_and_prepare(share, part, latents, lengths, text_len, step=256):
    count = lax.axis_size("seq")
    me = lax.axis_index("seq")
    rows, width = share.shape
    micro, block_rows, model_width = latents.shape
    items = lengths.shape[1]
    near_rows = block_rows + 2 * HALF
    own_rows = micro * block_rows
    ladder = jnp.asarray(lane_ladder()).reshape(1, 128)
    if count != 16 or rows % 16 or width % step:
        ahead = [(i, i + 1) for i in range(count - 1)]
        behind = [(i + 1, i) for i in range(count - 1)]
        low_rows = lax.ppermute(latents[:, block_rows - HALF :], "seq", ahead)
        high_rows = lax.ppermute(latents[:, :HALF], "seq", behind)
        near_latent = jnp.concatenate([low_rows, latents, high_rows], axis=1)
        total = seq_sum(part).reshape(micro, items, 6 * model_width)
        parts = []
        for m in range(micro):
            base, offset, later, self_bias, cross_bias = prepare(
                me * block_rows,
                count * block_rows,
                [lengths[m, k] for k in range(items)],
                [text_len[m, k] for k in range(items)],
                block_rows,
            )
            two = lax.dynamic_slice_in_dim(total[m], base, 2, 0)
            xhat, _ = spread_rows(near_latent[m].astype(f32))
            shift, factor = [
                jnp.where(later > 0.5, two[1], two[0])[:, i * model_width : (i + 1) * model_width]
                for i in range(2)
            ]
            normed = (xhat * (1.0 + factor) + shift).astype(bf16)
            parts.append(
                (
                    normed,
                    normed[HALF : HALF + block_rows].T,
                    two[None],
                    later[HALF : HALF + block_rows],
                    jnp.stack(lane_tables(offset, ladder)),
                    jnp.concatenate(self_bias, axis=0),
                    cross_bias,
                )
            )
        axes = (0, 1, 0, 0, 1, 0, 0)
        joined = [jnp.concatenate(group, axis=axis) for group, axis in zip(zip(*parts), axes)]
        return [lax.all_gather(share, "seq", axis=0, tiled=True)] + joined
    pieces = width // step
    any_space = pl.BlockSpec(memory_space=pl.ANY)
    vmem = pl.BlockSpec(memory_space=pltpu.VMEM)
    smem = pl.BlockSpec(memory_space=pltpu.SMEM)
    outs = pl.pallas_call(
        functools.partial(
            gather_kernel,
            pieces=pieces,
            step=step,
            y_first=tuple(range(pieces // 6, pieces, pieces // 3)),
            seq_count=count,
        ),
        out_shape=[
            jax.ShapeDtypeStruct((2, 2, 2, 2, rows, width), share.dtype),
            jax.ShapeDtypeStruct((micro * near_rows, model_width), bf16),
            jax.ShapeDtypeStruct((model_width, own_rows), bf16),
            jax.ShapeDtypeStruct((micro, 2, 6 * model_width), f32),
            jax.ShapeDtypeStruct((own_rows, 1), f32),
            jax.ShapeDtypeStruct((3, micro * near_rows, 128), f32),
            jax.ShapeDtypeStruct((own_rows, 3 * HALF), f32),
            jax.ShapeDtypeStruct((own_rows, 2 * TXT), f32),
        ],
        in_specs=[any_space, vmem, any_space, smem, smem, vmem],
        out_specs=[any_space] + [vmem] * 7,
        scratch_shapes=[
            pltpu.VMEM((micro, near_rows, model_width), bf16),
            pltpu.VMEM(part.shape, f32),
        ]
        + small_scratch(part.shape)
        + [
            pltpu.SemaphoreType.DMA((pieces,)),
            pltpu.SemaphoreType.DMA((4, pieces)),
            pltpu.SemaphoreType.DMA((4, pieces)),
            pltpu.SemaphoreType.DMA,
            pltpu.SemaphoreType.DMA((2,)),
            pltpu.SemaphoreType.DMA((2,)),
        ],
        compiler_params=pltpu.CompilerParams(
            collective_id=1, has_side_effects=True, vmem_limit_bytes=48 * 1024 * 1024
        ),
        cost_estimate=pl.CostEstimate(
            flops=0, bytes_accessed=20 * count * rows * width, transcendentals=0
        ),
        name="gather_and_prepare",
    )(share, part, latents, lengths, text_len, ladder)
    return [outs[0].reshape(count * rows, width)] + list(outs[1:])


SLOTS = 5


def when(condition):
    if isinstance(condition, bool):
        return (lambda work: work()) if condition else (lambda work: None)
    return pl.when(condition)


class Pieces:
    def __init__(self, refs, out_ref, partners, digits, step):
        (
            self.own, self.got0, self.got1, self.got2, self.got3, self.staged,
            self.out_sem, self.send_sem, self.recv_sem,
        ) = refs
        self.out_ref = out_ref
        self.partners = partners
        self.digits = digits
        self.step = step

    @staticmethod
    def scratch(rows, step):
        return [
            pltpu.VMEM((SLOTS, 2, 2, 2, rows, step), bf16),
            pltpu.VMEM((SLOTS, 2, 2, 2, rows, step), bf16),
            pltpu.VMEM((SLOTS, 2, 2, rows, step), bf16),
            pltpu.VMEM((SLOTS, 2, rows, step), bf16),
            pltpu.VMEM((SLOTS, rows, step), bf16),
            pltpu.VMEM((SLOTS, rows, step), f32),
            pltpu.SemaphoreType.DMA((SLOTS,)),
            pltpu.SemaphoreType.DMA((4, SLOTS)),
            pltpu.SemaphoreType.DMA((4, SLOTS)),
        ]

    def exchange(self, stage, source, target, slot):
        return send_to(
            self.partners[stage],
            source,
            target,
            self.send_sem.at[stage, slot],
            self.recv_sem.at[stage, slot],
        )

    def over_core(self, source, slot):
        return self.exchange(0, source, self.got0.at[slot], slot)

    def over_y(self, slot):
        y = self.digits[1]
        return self.exchange(1, self.own.at[slot, :, :, 1 - y], self.got1.at[slot], slot)

    def over_z_lo(self, slot):
        _, y, z_lo, _ = self.digits
        return self.exchange(2, self.own.at[slot, :, 1 - z_lo, y], self.got2.at[slot], slot)

    def over_z_hi(self, slot):
        _, y, z_lo, z_hi = self.digits
        return self.exchange(3, self.own.at[slot, 1 - z_hi, z_lo, y], self.got3.at[slot], slot)

    def store(self, item, slot):
        columns = pl.ds(pl.multiple_of(item * self.step, self.step), self.step)
        return pltpu.make_async_copy(
            self.staged.at[slot], self.out_ref.at[:, columns], self.out_sem.at[slot]
        )

    def wait_sent(self, slot):
        self.over_y(slot).wait_send()
        self.over_z_lo(slot).wait_send()
        self.over_z_hi(slot).wait_send()

    def add_core(self, slot, left):
        for i in range(2):
            for j in range(2):
                for k in range(2):
                    total = left(i, j, k).astype(f32) + self.got0[slot, i, j, k].astype(f32)
                    self.own[slot, i, j, k] = total.astype(bf16)
        self.over_y(slot).start()

    def later_steps(self, t, count):
        own = self.own
        _, y, z_lo, z_hi = self.digits

        @when((t >= 2) & (t - 2 < count))
        def _():
            slot = (t - 2) % SLOTS
            self.over_y(slot).wait_recv()
            for i in range(2):
                for j in range(2):
                    total = own[slot, i, j, y].astype(f32) + self.got1[slot, i, j].astype(f32)
                    own[slot, i, j, y] = total.astype(bf16)
            self.over_z_lo(slot).start()

        @when((t >= 3) & (t - 3 < count))
        def _():
            slot = (t - 3) % SLOTS
            self.over_z_lo(slot).wait_recv()
            for i in range(2):
                total = own[slot, i, z_lo, y].astype(f32) + self.got2[slot, i].astype(f32)
                own[slot, i, z_lo, y] = total.astype(bf16)
            self.over_z_hi(slot).start()

        @when((t >= 4) & (t - 4 < count))
        def _():
            slot = (t - 4) % SLOTS
            self.over_z_hi(slot).wait_recv()
            when(t - 4 >= SLOTS)(lambda: self.store(0, slot).wait())
            self.staged[slot] = own[slot, z_hi, z_lo, y].astype(f32) + self.got3[slot].astype(f32)
            self.store(t - 4, slot).start()

    def finish(self, count):
        for back in range(min(SLOTS, count)):
            slot = (count - 1 - back) % SLOTS
            self.store(0, slot).wait()
            self.wait_sent(slot)


PIECE_REFS = 9


def scatter_kernel(*refs, widths, step, with_small):
    refs = list(refs)
    sources = [refs.pop(0) for _ in widths]
    if with_small:
        part_ref = refs.pop(0)
    out_ref = refs.pop(0)
    if with_small:
        total_ref = refs.pop(0)
    own_sem = refs.pop(0)
    me = lax.axis_index("seq")
    digits = seq_digits(me)
    core = digits[0]
    partners = greet(me, digits)
    pieces = Pieces(refs[:PIECE_REFS], out_ref, partners, digits, step)
    if with_small:
        small = small_sum(partners, part_ref, refs[-4], refs[-3], total_ref, refs[-2], refs[-1])
        small(0)
    count = sum(widths) // step

    def over_core(source, column, slot):
        return pieces.over_core(source.at[:, :, :, 1 - core, :, pl.ds(column, step)], slot)

    def load(source, column, slot):
        return pltpu.make_async_copy(
            source.at[:, :, :, core, :, pl.ds(column, step)],
            pieces.own.at[slot],
            own_sem.at[slot],
        )

    def tick(t, carry):
        @pl.when(t < count)
        def _():
            slot = t % SLOTS
            pl.when(t >= SLOTS)(lambda: pieces.wait_sent(slot))
            first = 0
            for source, width in zip(sources, widths):

                @pl.when((t >= first) & (t < first + width // step))
                def _(source=source, first=first):
                    column = pl.multiple_of((t - first) * step, step)
                    over_core(source, column, slot).start()
                    load(source, column, slot).start()

                first += width // step

        @pl.when((t >= 1) & (t - 1 < count))
        def _():
            slot = (t - 1) % SLOTS
            load(sources[0], 0, slot).wait()
            over_core(sources[0], 0, slot).wait()
            pieces.add_core(slot, lambda i, j, k: pieces.own[slot, i, j, k])

        pieces.later_steps(t, count)
        if with_small:
            for k in range(1, len(STRIDES) + 1):
                pl.when(t == 3 * k)(functools.partial(small, k))
        return carry

    lax.fori_loop(0, count + 4, tick, 0)
    pieces.finish(count)


def scatter_sums(grads, which, part=None, step=256):
    count = lax.axis_size("seq")
    rows = grads[0].shape[0] // count
    widths = tuple(grad.shape[1] for grad in grads)
    if count != 16 or rows % 16 or any(width % step for width in widths):
        sums = [
            lax.psum_scatter(grad.astype(f32), "seq", scatter_dimension=0, tiled=True)
            for grad in grads
        ]
        return sums if part is None else sums + [seq_sum(part)]
    any_space = pl.BlockSpec(memory_space=pl.ANY)
    vmem = pl.BlockSpec(memory_space=pltpu.VMEM)
    scratch = [pltpu.SemaphoreType.DMA((SLOTS,))] + Pieces.scratch(rows, step)
    out_shape = [jax.ShapeDtypeStruct((rows, sum(widths)), f32)]
    extra = []
    if part is not None:
        scratch += small_scratch(part.shape)
        out_shape.append(jax.ShapeDtypeStruct(part.shape, f32))
        extra = [vmem]
    outs = pl.pallas_call(
        functools.partial(
            scatter_kernel, widths=widths, step=step, with_small=part is not None
        ),
        out_shape=out_shape,
        in_specs=[any_space] * len(grads) + extra,
        out_specs=[any_space] + extra,
        scratch_shapes=scratch,
        compiler_params=pltpu.CompilerParams(
            collective_id=which, has_side_effects=True, vmem_limit_bytes=40 * 1024 * 1024
        ),
        cost_estimate=pl.CostEstimate(
            flops=0, bytes_accessed=8 * count * rows * sum(widths), transcendentals=0
        ),
        name="scatter_sums",
    )(
        *[grad.reshape(2, 2, 2, 2, rows, grad.shape[1]) for grad in grads],
        *([] if part is None else [part]),
    )
    firsts = [sum(widths[:i]) for i in range(len(widths))]
    return [outs[0][:, first : first + width] for first, width in zip(firsts, widths)] + list(
        outs[1:]
    )


def early_sum(grad):
    return lax.psum_scatter(grad, "seq", scatter_dimension=0, tiled=True).astype(f32)


def turn(values, own, below, above):
    quarter = HD // 4
    return (
        values * own
        + pltpu.roll(values, quarter, 1) * below
        + pltpu.roll(values, 2 * HD - quarter, 1) * above
    )


def project_kernel(normed_ref, weight_ref, table_ref, out_ref, *, turned):
    j = pl.program_id(0)
    product = nn(normed_ref[...], weight_ref[...])

    @pl.when(j < turned)
    def _():
        for part in range(product.shape[1] // 128):
            lanes = slice(part * 128, (part + 1) * 128)
            out_ref[:, lanes] = turn(
                product[:, lanes], table_ref[0], table_ref[1], table_ref[2]
            ).astype(bf16)

    @pl.when(j >= turned)
    def _():
        out_ref[...] = product.astype(bf16)


def project(normed, weights, table, local, step=256):
    rows, width = normed.shape
    return pl.pallas_call(
        functools.partial(project_kernel, turned=2 * local // step),
        grid=(3 * local // step,),
        in_specs=[
            pl.BlockSpec((rows, width), lambda j: (0, 0)),
            pl.BlockSpec((width, step), lambda j: (0, j)),
            pl.BlockSpec((3, rows, 128), lambda j: (0, 0, 0)),
        ],
        out_specs=pl.BlockSpec((rows, step), lambda j: (0, j)),
        out_shape=jax.ShapeDtypeStruct((rows, 3 * local), bf16),
        compiler_params=kernel_params(1, 32),
        cost_estimate=pl.CostEstimate(
            flops=2 * rows * width * 3 * local,
            bytes_accessed=2 * (rows * width + 3 * local * (width + rows)),
            transcendentals=0,
        ),
        name="qkv_projection",
    )(normed, weights, table)


def head_lanes(shape):
    return lax.broadcasted_iota(jnp.int32, shape, 1) < HD


def one_head(values, first, which):
    return jnp.where(first if which == 0 else ~first, values, jnp.zeros_like(values))


def soft_rows(scores):
    peak = jnp.max(scores, axis=-1, keepdims=True)
    raised = jnp.exp(scores - peak)
    total = jnp.sum(raised, axis=-1, keepdims=True)
    return raised * (1.0 / total), peak + jnp.log(total)


def attend_rows(query, keys, values, bias):
    first = head_lanes(query.shape)
    out = None
    logs = []
    for which in range(2):
        scores = nt(one_head(query, first, which), keys) * (HD**-0.5) + bias
        weights, log_total = soft_rows(scores)
        mixed = nn(weights.astype(bf16), values)
        out = mixed if which == 0 else jnp.where(first, out, mixed)
        logs.append(log_total)
    return out, logs


def attend_rows_back(query, keys, values, bias, logs, grad):
    first = head_lanes(query.shape)
    query_grad = key_grad = value_grad = None
    for which in range(2):
        own_query = one_head(query, first, which)
        own_grad = one_head(grad, first, which)
        scores = nt(own_query, keys) * (HD**-0.5) + bias
        chances = jnp.exp(scores - logs[which])
        chance_grad = nt(own_grad, values)
        score_grad = (
            chances * (chance_grad - jnp.sum(chances * chance_grad, axis=-1, keepdims=True))
        ).astype(bf16)
        to_query = nn(score_grad, keys) * (HD**-0.5)
        to_key = tn(score_grad, own_query) * (HD**-0.5)
        to_value = tn(chances.astype(bf16), own_grad)
        if which == 0:
            query_grad, key_grad, value_grad = to_query, to_key, to_value
        else:
            query_grad = jnp.where(first, query_grad, to_query)
            key_grad = key_grad + to_key
            value_grad = value_grad + to_value
    return query_grad, key_grad, value_grad


def put_logs(log_ref, rows, logs, pair):
    lane = lax.broadcasted_iota(jnp.int32, (logs[0].shape[0], 128), 1)
    kept = log_ref[rows, :]
    kept = jnp.where(lane == 2 * pair, logs[0], kept)
    log_ref[rows, :] = jnp.where(lane == 2 * pair + 1, logs[1], kept)


def get_logs(log_ref, rows, pair):
    kept = log_ref[rows, :]
    lane = lax.broadcasted_iota(jnp.int32, kept.shape, 1)
    return [
        jnp.sum(jnp.where(lane == 2 * pair + which, kept, 0.0), axis=1, keepdims=True)
        for which in range(2)
    ]


def spread_rows(hidden):
    center = hidden - jnp.mean(hidden, axis=-1, keepdims=True)
    spread = jnp.mean(center * center, axis=-1, keepdims=True)
    scale = lax.rsqrt(spread + norm_eps)
    return center * scale, scale


def item_row(two_ref, later_ref, index):
    width = two_ref.shape[2] // 6
    lanes = slice(index * width, (index + 1) * width)
    return jnp.where(later_ref[...] > 0.5, two_ref[0, 1:2, lanes], two_ref[0, 0:1, lanes])


def norm_kernel(*refs, index, with_weight):
    refs = list(refs)
    base_ref, own_ref, got_ref, two_ref, later_ref = refs[:5]
    weight_ref = refs[5] if with_weight else None
    outs = refs[5 + with_weight :]
    hidden = (
        base_ref[...].astype(f32) + own_ref[...].astype(f32) + got_ref[...].astype(f32)
    )
    xhat, _ = spread_rows(hidden)
    normed = (
        xhat * (1.0 + item_row(two_ref, later_ref, index + 1)) + item_row(two_ref, later_ref, index)
    ).astype(bf16)
    outs[0][...] = hidden
    outs[1][...] = normed
    outs[2][...] = normed.T
    if with_weight:
        outs[3][...] = nn(normed, weight_ref[...]).astype(bf16)


def norm_forward(base, own, got, two, later, index, micro, weights=None, column=0, out_width=0):
    rows, width = base.shape
    tile = rows // micro
    row_tile = pl.BlockSpec((tile, width), lambda i: (i, 0))
    in_specs = [
        row_tile,
        row_tile,
        row_tile,
        pl.BlockSpec((1, 2, 6 * width), lambda i: (i, 0, 0)),
        pl.BlockSpec((tile, 1), lambda i: (i, 0)),
    ]
    out_specs = [row_tile, row_tile, pl.BlockSpec((width, tile), lambda i: (0, i))]
    out_shape = [
        jax.ShapeDtypeStruct((rows, width), f32),
        jax.ShapeDtypeStruct((rows, width), bf16),
        jax.ShapeDtypeStruct((width, rows), bf16),
    ]
    args = [base, own, got, two, later]
    if weights is not None:
        in_specs.append(pl.BlockSpec((width, out_width), lambda i: (0, column)))
        out_specs.append(pl.BlockSpec((tile, out_width), lambda i: (i, 0)))
        out_shape.append(jax.ShapeDtypeStruct((rows, out_width), bf16))
        args.append(weights)
    return pl.pallas_call(
        functools.partial(norm_kernel, index=index, with_weight=weights is not None),
        grid=(micro,),
        in_specs=in_specs,
        out_specs=out_specs,
        out_shape=out_shape,
        compiler_params=kernel_params(1, 40),
        cost_estimate=pl.CostEstimate(
            flops=2 * rows * width * out_width, bytes_accessed=16 * rows * width, transcendentals=0
        ),
        name="norm_forward",
    )(*args)


def norm_back_kernel(*refs, index, with_weight):
    refs = list(refs)
    up_ref, own_ref, got_ref, hidden_ref, two_ref, later_ref = refs[:6]
    weight_ref = refs[6] if with_weight else None
    outs = refs[6 + with_weight :]
    xhat, scale = spread_rows(hidden_ref[...].astype(f32))
    grad = own_ref[...].astype(f32) + got_ref[...].astype(f32)
    inner = grad * (1.0 + item_row(two_ref, later_ref, index + 1))
    mean_inner = jnp.mean(inner, axis=-1, keepdims=True)
    mean_cross = jnp.mean(inner * xhat, axis=-1, keepdims=True)
    total = up_ref[...].astype(f32) + scale * (inner - mean_inner - xhat * mean_cross)
    outs[0][...] = total
    later = later_ref[...] > 0.5
    scaled = grad * xhat
    for item in range(2):
        chosen = later if item else ~later
        outs[1][0, item, 0:1] = jnp.sum(jnp.where(chosen, grad, 0.0), axis=0, keepdims=True)
        outs[1][0, item, 1:2] = jnp.sum(jnp.where(chosen, scaled, 0.0), axis=0, keepdims=True)
    if with_weight:
        rounded = total.astype(bf16)
        outs[2][...] = rounded.T
        outs[3][...] = nn(rounded, weight_ref[...]).astype(bf16)


def norm_back(up, own, got, hidden, two, later, index, micro, weights=None, column=0, out_width=0):
    rows, width = hidden.shape
    tile = rows // micro
    row_tile = pl.BlockSpec((tile, width), lambda i: (i, 0))
    in_specs = [
        row_tile,
        row_tile,
        row_tile,
        row_tile,
        pl.BlockSpec((1, 2, 6 * width), lambda i: (i, 0, 0)),
        pl.BlockSpec((tile, 1), lambda i: (i, 0)),
    ]
    out_specs = [row_tile, pl.BlockSpec((1, 2, 2, width), lambda i: (i, 0, 0, 0))]
    out_shape = [
        jax.ShapeDtypeStruct((rows, width), f32),
        jax.ShapeDtypeStruct((micro, 2, 2, width), f32),
    ]
    args = [up, own, got, hidden, two, later]
    if weights is not None:
        in_specs.append(pl.BlockSpec((width, out_width), lambda i: (0, column)))
        out_specs += [
            pl.BlockSpec((width, tile), lambda i: (0, i)),
            pl.BlockSpec((tile, out_width), lambda i: (i, 0)),
        ]
        out_shape += [
            jax.ShapeDtypeStruct((width, rows), bf16),
            jax.ShapeDtypeStruct((rows, out_width), bf16),
        ]
        args.append(weights)
    return pl.pallas_call(
        functools.partial(norm_back_kernel, index=index, with_weight=weights is not None),
        grid=(micro,),
        in_specs=in_specs,
        out_specs=out_specs,
        out_shape=out_shape,
        compiler_params=kernel_params(1, 48),
        cost_estimate=pl.CostEstimate(
            flops=2 * rows * width * out_width, bytes_accessed=20 * rows * width, transcendentals=0
        ),
        name="norm_back",
    )(*args)


def add_product(acc_ref, out_ref, product):
    pair = pl.program_id(1)

    @pl.when(pair == 0)
    def _():
        acc_ref[...] = product

    @pl.when(pair > 0)
    def _():
        acc_ref[...] += product

    @pl.when(pair == pl.num_programs(1) - 1)
    def _():
        out_ref[...] = acc_ref[...].astype(bf16)


def self_kernel(q_ref, k_ref, v_ref, bias_ref, weight_ref, out_ref, log_ref, sum_ref, acc_ref):
    pair = pl.program_id(1)
    block_rows = out_ref.shape[0]
    for part in range(block_rows // HALF):
        rows = slice(part * HALF, (part + 1) * HALF)
        span = slice(part * HALF, (part + 3) * HALF)
        out, logs = attend_rows(
            q_ref[(part + 1) * HALF : (part + 2) * HALF, :],
            k_ref[span, :],
            v_ref[span, :],
            bias_ref[rows, :],
        )
        out_ref[rows, :] = out.astype(bf16)
        put_logs(log_ref, rows, logs, pair)
    add_product(acc_ref, sum_ref, nt(out_ref[...], weight_ref[...]))


def self_specs(block_rows, pairs):
    near = lambda first: pl.BlockSpec((block_rows + 2 * HALF, 128), lambda m, h: (m, first + h))
    return [
        near(0),
        near(pairs),
        near(2 * pairs),
        pl.BlockSpec((block_rows, 3 * HALF), lambda m, h: (m, 0)),
    ]


def self_attention(qkv, bias, weights, column, micro, block_rows):
    rows = micro * block_rows
    local = qkv.shape[1] // 3
    width = weights.shape[0]
    pairs = local // 128
    return pl.pallas_call(
        self_kernel,
        grid=(micro, pairs),
        in_specs=self_specs(block_rows, pairs)
        + [pl.BlockSpec((width, 128), lambda m, h: (0, column + h))],
        out_specs=[
            pl.BlockSpec((block_rows, 128), lambda m, h: (m, h)),
            pl.BlockSpec((block_rows, 128), lambda m, h: (m, 0)),
            pl.BlockSpec((block_rows, width), lambda m, h: (m, 0)),
        ],
        out_shape=[
            jax.ShapeDtypeStruct((rows, local), bf16),
            jax.ShapeDtypeStruct((rows, 128), f32),
            jax.ShapeDtypeStruct((rows, width), bf16),
        ],
        scratch_shapes=[pltpu.VMEM((block_rows, width), f32)],
        compiler_params=kernel_params(2, 32),
        cost_estimate=pl.CostEstimate(
            flops=rows * 2 * local * (width + 12 * HALF),
            bytes_accessed=20 * rows * local,
            transcendentals=rows * 3 * HALF * 2 * pairs,
        ),
        name="self_attention",
    )(qkv, qkv, qkv, bias, weights)


def self_back_kernel(
    q_ref, k_ref, v_ref, bias_ref, grad_ref, log_ref, own_ref, to_low_ref, to_high_ref
):
    pair = pl.program_id(1)
    parts = grad_ref.shape[0] // HALF
    pieces = [[None] * (parts + 2), [None] * (parts + 2)]
    for part in range(parts):
        rows = slice(part * HALF, (part + 1) * HALF)
        span = slice(part * HALF, (part + 3) * HALF)
        query_grad, key_grad, value_grad = attend_rows_back(
            q_ref[(part + 1) * HALF : (part + 2) * HALF, :],
            k_ref[span, :],
            v_ref[span, :],
            bias_ref[rows, :],
            get_logs(log_ref, rows, pair),
            grad_ref[rows, :],
        )
        own_ref[0, rows, :] = query_grad
        for kind, near_grad in enumerate((key_grad, value_grad)):
            for third in range(3):
                piece = near_grad[third * HALF : (third + 1) * HALF]
                held = pieces[kind][part + third]
                pieces[kind][part + third] = piece if held is None else held + piece
    for kind in range(2):
        to_low_ref[kind] = pieces[kind][0].astype(bf16)
        for part in range(parts):
            own_ref[1 + kind, part * HALF : (part + 1) * HALF, :] = pieces[kind][part + 1]
        to_high_ref[kind] = pieces[kind][parts + 1].astype(bf16)


def self_attention_back(qkv, bias, grad, logs, micro, block_rows):
    rows, local = grad.shape
    pairs = local // 128
    edge = pl.BlockSpec((2, None, HALF, 128), lambda m, h: (0, m, 0, h))
    return pl.pallas_call(
        self_back_kernel,
        grid=(micro, pairs),
        in_specs=self_specs(block_rows, pairs)
        + [
            pl.BlockSpec((block_rows, 128), lambda m, h: (m, h)),
            pl.BlockSpec((block_rows, 128), lambda m, h: (m, 0)),
        ],
        out_specs=[
            pl.BlockSpec((3, block_rows, 128), lambda m, h: (0, m, h)),
            edge,
            edge,
        ],
        out_shape=[
            jax.ShapeDtypeStruct((3, rows, local), f32),
            jax.ShapeDtypeStruct((2, micro, HALF, local), bf16),
            jax.ShapeDtypeStruct((2, micro, HALF, local), bf16),
        ],
        compiler_params=kernel_params(2, 32),
        cost_estimate=pl.CostEstimate(
            flops=20 * rows * 3 * HALF * local,
            bytes_accessed=40 * rows * local,
            transcendentals=rows * 3 * HALF * 2 * pairs,
        ),
        name="self_attention_back",
    )(qkv, qkv, qkv, bias, grad, logs)


def cross_kernel(q_ref, k_ref, v_ref, bias_ref, weight_ref, out_ref, log_ref, sum_ref, acc_ref):
    pair = pl.program_id(1)
    for part in range(q_ref.shape[0] // HALF):
        rows = slice(part * HALF, (part + 1) * HALF)
        out, logs = attend_rows(q_ref[rows, :], k_ref[...], v_ref[...], bias_ref[rows, :])
        out_ref[rows, :] = out.astype(bf16)
        put_logs(log_ref, rows, logs, pair)
    add_product(acc_ref, sum_ref, nt(out_ref[...], weight_ref[...]))


def cross_specs(block_rows, pairs):
    return [
        pl.BlockSpec((block_rows, 128), lambda m, h: (m, h)),
        pl.BlockSpec((2 * TXT, 128), lambda m, h: (m, h)),
        pl.BlockSpec((2 * TXT, 128), lambda m, h: (m, h)),
        pl.BlockSpec((block_rows, 2 * TXT), lambda m, h: (m, 0)),
    ]


def cross_attention(query, keys, values, bias, weights, column, micro, block_rows):
    rows, local = query.shape
    width = weights.shape[0]
    pairs = local // 128
    return pl.pallas_call(
        cross_kernel,
        grid=(micro, pairs),
        in_specs=cross_specs(block_rows, pairs)
        + [pl.BlockSpec((width, 128), lambda m, h: (0, column + h))],
        out_specs=[
            pl.BlockSpec((block_rows, 128), lambda m, h: (m, h)),
            pl.BlockSpec((block_rows, 128), lambda m, h: (m, 0)),
            pl.BlockSpec((block_rows, width), lambda m, h: (m, 0)),
        ],
        out_shape=[
            jax.ShapeDtypeStruct((rows, local), bf16),
            jax.ShapeDtypeStruct((rows, 128), f32),
            jax.ShapeDtypeStruct((rows, width), bf16),
        ],
        scratch_shapes=[pltpu.VMEM((block_rows, width), f32)],
        compiler_params=kernel_params(2, 32),
        cost_estimate=pl.CostEstimate(
            flops=rows * 2 * local * (width + 8 * TXT),
            bytes_accessed=16 * rows * local,
            transcendentals=rows * 2 * TXT * 2 * pairs,
        ),
        name="cross_attention",
    )(query, keys, values, bias, weights)


def cross_back_kernel(
    q_ref, k_ref, v_ref, bias_ref, grad_ref, log_ref, weight_ref,
    dq_ref, dk_ref, dv_ref, sum_ref, acc_ref,
):
    pair = pl.program_id(1)
    key_total = value_total = None
    for part in range(q_ref.shape[0] // HALF):
        rows = slice(part * HALF, (part + 1) * HALF)
        query_grad, key_grad, value_grad = attend_rows_back(
            q_ref[rows, :],
            k_ref[...],
            v_ref[...],
            bias_ref[rows, :],
            get_logs(log_ref, rows, pair),
            grad_ref[rows, :],
        )
        dq_ref[rows, :] = query_grad.astype(bf16)
        key_total = key_grad if part == 0 else key_total + key_grad
        value_total = value_grad if part == 0 else value_total + value_grad
    dk_ref[...] = key_total.astype(bf16)
    dv_ref[...] = value_total.astype(bf16)
    add_product(acc_ref, sum_ref, nt(dq_ref[...], weight_ref[...]))


def cross_attention_back(
    query, keys, values, bias, grad, logs, weights, column, micro, block_rows
):
    rows, local = query.shape
    width = weights.shape[0]
    pairs = local // 128
    text = pl.BlockSpec((2 * TXT, 128), lambda m, h: (m, h))
    return pl.pallas_call(
        cross_back_kernel,
        grid=(micro, pairs),
        in_specs=cross_specs(block_rows, pairs)
        + [
            pl.BlockSpec((block_rows, 128), lambda m, h: (m, h)),
            pl.BlockSpec((block_rows, 128), lambda m, h: (m, 0)),
            pl.BlockSpec((width, 128), lambda m, h: (0, column + h)),
        ],
        out_specs=[
            pl.BlockSpec((block_rows, 128), lambda m, h: (m, h)),
            text,
            text,
            pl.BlockSpec((block_rows, width), lambda m, h: (m, 0)),
        ],
        out_shape=[
            jax.ShapeDtypeStruct((rows, local), bf16),
            jax.ShapeDtypeStruct(keys.shape, bf16),
            jax.ShapeDtypeStruct(keys.shape, bf16),
            jax.ShapeDtypeStruct((rows, width), bf16),
        ],
        scratch_shapes=[pltpu.VMEM((block_rows, width), f32)],
        compiler_params=kernel_params(2, 32),
        cost_estimate=pl.CostEstimate(
            flops=rows * 2 * local * (width + 20 * TXT),
            bytes_accessed=30 * rows * local,
            transcendentals=rows * 2 * TXT * 2 * pairs,
        ),
        name="cross_attention_back",
    )(query, keys, values, bias, grad, logs, weights)


def ffn_kernel(*refs, summed):
    (
        normed_ref, normed_t_ref, cot_ref, cot_t_ref, outer_ref, gate_ref, up_ref,
        g_early_ref, g_up_ref, out_ref, back_ref, out_acc, back_acc,
    ) = refs[:13]
    j = pl.program_id(0)
    step = gate_ref.shape[1]
    if summed:
        full = refs[13]
        me = lax.axis_index("seq")
        digits = seq_digits(me)
        core = digits[0]
        partners = [me + stride * (1 - 2 * digit) for stride, digit in zip(STRIDES, digits)]
        pl.when(j == 0)(lambda: [greet(me, digits), None][1])
        pieces = Pieces(refs[14:], g_up_ref, partners, digits, step)
        count = summed

        def over_core(slot):
            return pieces.over_core(full.at[slot, :, :, :, 1 - core], slot)

        def tick(t):
            @when((t >= 1) & (t - 1 < count))
            def _():
                slot = (t - 1) % SLOTS
                when(t - 1 >= SLOTS)(lambda: pieces.wait_sent(slot))
                over_core(slot).wait()
                pieces.add_core(slot, lambda a, b, c: full[slot, a, b, c, core])

            pieces.later_steps(t, count)

    gate = nn(normed_ref[...], gate_ref[...])
    up = nn(normed_ref[...], up_ref[...])
    grad = nn(cot_ref[...], outer_ref[...])
    if summed:
        tick(j)
    chance = 1.0 / (1.0 + jnp.exp(-gate))
    swish = gate * chance
    active = (swish * up).astype(bf16)
    gate_grad = (grad * up * (chance * (1.0 + gate * (1.0 - chance)))).astype(bf16)
    up_grad = (grad * swish).astype(bf16)
    g_up = nn(normed_t_ref[...], up_grad).astype(bf16)
    if summed:
        slot = j % SLOTS
        full[slot] = g_up.reshape(full.shape[1:])
        over_core(slot).start()
    else:
        g_up_ref[...] = g_up
    g_early_ref[:, :step] = nn(cot_t_ref[...], active).astype(bf16)
    g_early_ref[:, step:] = nn(normed_t_ref[...], gate_grad).astype(bf16)
    out_part = nt(active, outer_ref[...])
    back_part = nt(gate_grad, gate_ref[...]) + nt(up_grad, up_ref[...])

    @pl.when(j == 0)
    def _():
        out_acc[...] = out_part
        back_acc[...] = back_part

    @pl.when(j > 0)
    def _():
        out_acc[...] += out_part
        back_acc[...] += back_part

    @pl.when(j == pl.num_programs(0) - 1)
    def _():
        out_ref[...] = out_acc[...].astype(bf16)
        back_ref[...] = back_acc[...].astype(bf16)
        if summed:
            for t in range(count, count + 4):
                tick(t)
            pieces.finish(count)


FFN_STEP = 256


def feed_forward(normed, normed_t, cotangent, weights, hidden, step=FFN_STEP):
    rows, width = normed.shape
    steps = hidden // step
    seq_count = lax.axis_size("seq")
    share = width // seq_count
    summed = steps if seq_count == 16 and share % 16 == 0 else 0
    whole = lambda shape: pl.BlockSpec(shape, lambda j: (0, 0))
    column = lambda first: pl.BlockSpec((width, step), lambda j: (0, first + j))
    scratch = [pltpu.VMEM((rows, width), f32)] * 2
    if summed:
        scratch += [pltpu.VMEM((SLOTS, 2, 2, 2, 2, share, step), bf16)]
        scratch += Pieces.scratch(share, step)
        up_spec = pl.BlockSpec(memory_space=pl.ANY)
        up_shape = jax.ShapeDtypeStruct((share, hidden), f32)
        params = pltpu.CompilerParams(
            dimension_semantics=("arbitrary",),
            collective_id=3,
            has_side_effects=True,
            vmem_limit_bytes=58 * 1024 * 1024,
        )
    else:
        up_spec = column(0)
        up_shape = jax.ShapeDtypeStruct((width, hidden), bf16)
        params = kernel_params(1, 56)
    outs = pl.pallas_call(
        functools.partial(ffn_kernel, summed=summed),
        grid=(steps,),
        in_specs=[
            whole((rows, width)),
            whole((width, rows)),
            whole((rows, width)),
            whole((width, rows)),
            column(0),
            column(steps),
            column(2 * steps),
        ],
        out_specs=[
            pl.BlockSpec((width, 2 * step), lambda j: (0, j)),
            up_spec,
            whole((rows, width)),
            whole((rows, width)),
        ],
        out_shape=[
            jax.ShapeDtypeStruct((width, 2 * hidden), bf16),
            up_shape,
            jax.ShapeDtypeStruct((rows, width), bf16),
            jax.ShapeDtypeStruct((rows, width), bf16),
        ],
        scratch_shapes=scratch,
        compiler_params=params,
        cost_estimate=pl.CostEstimate(
            flops=18 * rows * width * hidden,
            bytes_accessed=12 * width * hidden,
            transcendentals=rows * hidden,
        ),
        name="feed_forward",
    )(normed, normed_t, cotangent, cotangent.T, weights, weights, weights)
    if summed:
        return outs
    up_total = lax.psum_scatter(outs[1].astype(f32), "seq", scatter_dimension=0, tiled=True)
    return outs[0], up_total, outs[2], outs[3]


def qkv_back_kernel(
    own_ref, after_ref, before_ref, normed_t_ref, weight_ref, table_ref,
    grad_ref, back_ref, acc, *, kind_steps, micro, block_rows,
):
    j = pl.program_id(0)
    kind = j // kind_steps
    edges = (kind > 0).astype(f32)
    turned = kind < 2
    near_rows = block_rows + 2 * HALF

    def own_table(index):
        return jnp.concatenate(
            [
                table_ref[index, m * near_rows + HALF : (m + 1) * near_rows - HALF]
                for m in range(micro)
            ],
            axis=0,
        )

    own_factor = jnp.where(turned, own_table(0), 1.0)
    below_factor = jnp.where(turned, -own_table(1), 0.0)
    above_factor = jnp.where(turned, -own_table(2), 0.0)
    total = []
    for m in range(micro):
        first = m * block_rows
        total.append(own_ref[first : first + HALF] + edges * after_ref[m].astype(f32))
        if block_rows > 2 * HALF:
            total.append(own_ref[first + HALF : first + block_rows - HALF])
        total.append(
            own_ref[first + block_rows - HALF : first + block_rows]
            + edges * before_ref[m].astype(f32)
        )
    total = jnp.concatenate(total, axis=0)
    grad = jnp.concatenate(
        [
            turn(total[:, i : i + 128], own_factor, below_factor, above_factor)
            for i in range(0, total.shape[1], 128)
        ],
        axis=1,
    ).astype(bf16)
    grad_ref[...] = nn(normed_t_ref[...], grad).astype(bf16)
    part = nt(grad, weight_ref[...])

    @pl.when(j == 0)
    def _():
        acc[...] = part

    @pl.when(j > 0)
    def _():
        acc[...] += part

    @pl.when(j == pl.num_programs(0) - 1)
    def _():
        back_ref[...] = acc[...].astype(bf16)


def qkv_back(own, after, before, normed_t, weights, table, micro, block_rows, step=256):
    _, rows, local = own.shape
    width = normed_t.shape[0]
    kind_steps = local // step
    edge = pl.BlockSpec(
        (None, micro, HALF, step),
        lambda j: (jnp.maximum(j // kind_steps - 1, 0), 0, 0, j % kind_steps),
    )
    return pl.pallas_call(
        functools.partial(
            qkv_back_kernel, kind_steps=kind_steps, micro=micro, block_rows=block_rows
        ),
        grid=(3 * kind_steps,),
        in_specs=[
            pl.BlockSpec((None, rows, step), lambda j: (j // kind_steps, 0, j % kind_steps)),
            edge,
            edge,
            pl.BlockSpec((width, rows), lambda j: (0, 0)),
            pl.BlockSpec((width, step), lambda j: (0, j)),
            pl.BlockSpec(table.shape, lambda j: (0, 0, 0)),
        ],
        out_specs=[
            pl.BlockSpec((width, step), lambda j: (0, j)),
            pl.BlockSpec((rows, width), lambda j: (0, 0)),
        ],
        out_shape=[
            jax.ShapeDtypeStruct((width, 3 * local), bf16),
            jax.ShapeDtypeStruct((rows, width), bf16),
        ],
        scratch_shapes=[pltpu.VMEM((rows, width), f32)],
        compiler_params=kernel_params(1, 40),
        cost_estimate=pl.CostEstimate(
            flops=12 * rows * width * local,
            bytes_accessed=12 * width * local + 12 * rows * local,
            transcendentals=0,
        ),
        name="qkv_back",
    )(own, after, before, normed_t, weights, table)


def time_features(steps_row):
    half_width = TEMB // 2
    ladder = jnp.exp(-math.log(10000.0) * jnp.arange(half_width, dtype=f32) / half_width)
    angles = steps_row.astype(f32)[:, None] * ladder[None, :]
    return jnp.concatenate([jnp.cos(angles), jnp.sin(angles)], axis=-1)


def on_device(
    latents,
    context,
    lengths,
    text_len,
    timesteps,
    self_qkv,
    self_out,
    cross_query,
    cross_kv,
    cross_out,
    ffn_in,
    ffn_out,
    mod_weight,
    mod_bias,
    out_grad,
):
    micro, block_rows, model_width = latents.shape
    seq_count = lax.axis_size("seq")
    me = lax.axis_index("seq")
    frame_count = block_rows * seq_count
    item_count = lengths.shape[1]
    local = self_qkv.shape[2]
    hidden = ffn_in.shape[2]
    rows = micro * block_rows
    text_width = context.shape[2]

    attn_share = jnp.concatenate(
        [
            self_qkv[0],
            self_qkv[1],
            self_qkv[2],
            self_out.T,
            cross_query,
            cross_out.T,
            jnp.concatenate([cross_kv[0], cross_kv[1]], axis=0),
        ],
        axis=1,
    )
    ffn_share = jnp.concatenate([ffn_out.T, ffn_in[0], ffn_in[1]], axis=1)
    features = time_features(timesteps.reshape(-1))
    own_features = lax.dynamic_slice_in_dim(
        features, me * mod_weight.shape[0], mod_weight.shape[0], 1
    )
    bias_share = mod_bias.shape[1]
    bias_wide = lax.dynamic_update_slice_in_dim(
        jnp.zeros((6, model_width), f32), mod_bias.astype(f32), me * bias_share, 1
    )
    mod_part = jnp.dot(
        own_features, mod_weight.astype(f32).reshape(mod_weight.shape[0], -1), precision=highest
    ) + bias_wide.reshape(1, -1)
    (
        attn_all,
        normed_near,
        normed_one_t,
        two,
        later,
        near_table,
        self_bias,
        cross_bias,
    ) = gather_and_prepare(attn_share, mod_part, latents, lengths, text_len)
    ffn_share, attn_all = lax.optimization_barrier((ffn_share, attn_all))
    ffn_all = lax.all_gather(ffn_share, "seq", axis=0, tiled=True)
    pair_w = attn_all[:, 6 * local :].reshape(seq_count, 2, text_width // seq_count, local)
    key_w = pair_w[:, 0].reshape(text_width, local)
    value_w = pair_w[:, 1].reshape(text_width, local)

    first_frame = me * block_rows
    first_item = jnp.sum((jnp.cumsum(lengths, axis=1) <= first_frame).astype(jnp.int32), axis=1)
    base_item = jnp.minimum(first_item, item_count - 2)
    catalog = jnp.arange(item_count, dtype=jnp.int32)

    ahead = [(i, i + 1) for i in range(seq_count - 1)]
    behind = [(i + 1, i) for i in range(seq_count - 1)]
    latent = latents.reshape(rows, model_width)
    cotangent = out_grad.reshape(rows, model_width)
    near_context = jnp.concatenate(
        [
            lax.dynamic_slice_in_dim(context[m], base_item[m] * TXT, 2 * TXT, 0)
            for m in range(micro)
        ]
    )
    column = local // 128

    qkv = project(normed_near, attn_all, near_table, local)
    mixed_one, logs_one, part_one = self_attention(
        qkv, self_bias, attn_all, 3 * column, micro, block_rows
    )
    got_one = swap(part_one)
    text_keys = nn(near_context, key_w).astype(bf16)
    text_values = nn(near_context, value_w).astype(bf16)
    hidden_one, _, normed_two_t, query_two = norm_forward(
        latent, part_one, got_one, two, later, 2, micro, attn_all, 4, local
    )
    mixed_two, logs_two, part_two = cross_attention(
        query_two, text_keys, text_values, cross_bias, attn_all, 5 * column, micro, block_rows
    )
    got_two = swap(part_two)
    hidden_two, normed_three, normed_three_t = norm_forward(
        hidden_one, part_two, got_two, two, later, 4, micro
    )
    g_early, up_total, out_part, back_three = feed_forward(
        normed_three, normed_three_t, cotangent, ffn_all, hidden
    )

    got_three = swap(back_three)
    early = early_sum(g_early).reshape(-1, hidden // FFN_STEP, 2, FFN_STEP)
    outer_total = early[:, :, 0].reshape(-1, hidden)
    gate_total = early[:, :, 1].reshape(-1, hidden)
    hidden_two_grad, pieces_three, two_low_t, mixed_two_grad = norm_back(
        cotangent, back_three, got_three, hidden_two, two, later, 4, micro, attn_all, 5, local
    )
    out_part, hidden_two_grad = lax.optimization_barrier((out_part, hidden_two_grad))
    out_got = swap(out_part)
    query_two_low, text_key_low, text_value_low, back_two = cross_attention_back(
        query_two, text_keys, text_values, cross_bias, mixed_two_grad, logs_two,
        attn_all, 4 * column, micro, block_rows,
    )
    got_back_two = swap(back_two)
    share = text_width // seq_count
    pair_grad = jnp.concatenate(
        [
            tn(near_context, text_key_low).astype(bf16).reshape(seq_count, share, local),
            tn(near_context, text_value_low).astype(bf16).reshape(seq_count, share, local),
        ],
        axis=1,
    ).reshape(2 * text_width, local)
    g_cross_out = nn(two_low_t, mixed_two).astype(bf16)
    g_cross_query = nn(normed_two_t, query_two_low).astype(bf16)
    hidden_one_grad, pieces_two, one_low_t, mixed_one_grad = norm_back(
        hidden_two_grad, back_two, got_back_two, hidden_one, two, later, 2, micro,
        attn_all, 3, local,
    )
    own_grads, to_low, to_high = self_attention_back(
        qkv, self_bias, mixed_one_grad, logs_one, micro, block_rows
    )
    from_high = lax.ppermute(to_low, "seq", behind)
    from_low = lax.ppermute(to_high, "seq", ahead)
    g_self_out = nn(one_low_t, mixed_one).astype(bf16)
    g_qkv, back_one = qkv_back(
        own_grads, from_low, from_high, normed_one_t, attn_all, near_table, micro, block_rows
    )
    got_back_one = swap(back_one)
    grad_cross_out, grad_cross_query, grad_cross_kv, grad_self_out = scatter_sums(
        [g_cross_out, g_cross_query, pair_grad, g_self_out], 0
    )
    block_out = (hidden_two + (out_part.astype(f32) + out_got.astype(f32))).astype(bf16)
    got_back_one, grad_self_out = lax.optimization_barrier((got_back_one, grad_self_out))
    latent_grad, pieces_one = norm_back(
        hidden_one_grad, back_one, got_back_one, latent, two, later, 0, micro
    )

    pieces = jnp.concatenate([pieces_one, pieces_two, pieces_three], axis=2)
    spots = (base_item[:, None] + jnp.arange(2)[None, :])[:, :, None] == catalog[None, None, :]
    item_grad = jnp.concatenate(
        [
            jnp.sum(
                jnp.where(spots[m][:, :, None, None], pieces[m][:, None], 0.0), axis=0
            )
            for m in range(micro)
        ]
    ).reshape(micro * item_count, 6 * model_width)
    qkv_total, item_total = scatter_sums([g_qkv], 2, item_grad)
    mod_grad = jnp.dot(own_features.T, item_total, precision=highest).reshape(mod_weight.shape)
    bias_grad = lax.dynamic_slice_in_dim(
        jnp.sum(item_total, axis=0).reshape(6, model_width), me * bias_share, bias_share, 1
    )

    grad_qkv = jnp.stack([qkv_total[:, i * local : (i + 1) * local] for i in range(3)])
    return (
        block_out.reshape(latents.shape),
        latent_grad.reshape(latents.shape),
        grad_qkv,
        grad_self_out.T,
        grad_cross_query,
        grad_cross_kv.reshape(2, share, local),
        grad_cross_out.T,
        jnp.stack([gate_total, up_total]),
        outer_total.T,
        mod_grad,
        bias_grad,
    )


def solution(mesh):
    return jax.shard_map(
        on_device,
        mesh=mesh,
        in_specs=(
            P(None, "seq", None),
            P(),
            P(),
            P(),
            P(),
            P(None, "seq", "tensor"),
            P("tensor", "seq"),
            P("seq", "tensor"),
            P(None, "seq", "tensor"),
            P("tensor", "seq"),
            P(None, "seq", "tensor"),
            P("tensor", "seq"),
            P("seq", None, None),
            P(None, "seq"),
            P(None, "seq", None),
        ),
        out_specs=(
            P(None, "seq", None),
            P(None, "seq", None),
            P(None, "seq", "tensor"),
            P("tensor", "seq"),
            P("seq", "tensor"),
            P(None, "seq", "tensor"),
            P("tensor", "seq"),
            P(None, "seq", "tensor"),
            P("tensor", "seq"),
            P("seq", None, None),
            P(None, "seq"),
        ),
        check_vma=False,
    )
```

time: 946 us -> 779 us (0.82)
  Pallas kernels: 350 us -> 533 us
  local copies, waits for them, and re-layouts: 183 us -> 67.8 us
  other arithmetic: 102 us -> 9.07 us
  waiting for transfers between devices: 198 us -> 125 us
  starting transfers between devices: 46.2 us -> 10.7 us
  matrix products: 40.1 us -> 9.44 us
    pallas_call x1 -> x7, Pallas kernels: 61.9 us -> 250 us  [the longest x1 124 us: gather_and_prepare(): pl.pallas_call(functools.partial(gather_kernel, pieces=pieces, step=step,...]
    reduce_sum x15 -> x3, other arithmetic: 66.2 us -> 0.43 us  [the longest x2 0.31 us: on_device(): jnp.sum(jnp.where(spots[m][:, :, None, None], pieces[m][:, None], 0.0), a...]
    all_gather x1 -> x0, waiting for transfers between devices: 50.8 us -> none  [on_device(): attn_all = lax.all_gather(attn_share, 'seq', axis=0, tiled=True)]
    broadcast_in_dim x25 -> x2, local copies, waits for them, and re-layouts: 38.2 us -> 0.02 us  [on_device(): jnp.where(spots[m][:, :, None, None], pieces[m][:, None], 0.0)]
    reshape x10 -> x0, local copies, waits for them, and re-layouts: 34.5 us -> none  [the longest x3 16 us: norm_back(): cube = normed_grad.reshape(micro, block_rows, model_width)]
    dot_general x13 -> x7, matrix products: 38 us -> 8.35 us  [dot(): lax.dot_general(a, b, ((dims[0], dims[1]), ((), ())), preferred_element_t...]
    pallas_call x1 -> x2, Pallas kernels: 190 us -> 162 us  [scatter_sums(): pl.pallas_call(functools.partial(scatter_kernel, widths=widths, step=step...]
    ppermute x1, starting transfers between devices: 20.6 us -> 1.33 us  [on_device(): from_low = lax.ppermute(to_high, 'seq', ahead)]
  transfers between devices with their start and end apart: 21 -> 10, of which waited for: 13 -> 4; matrix products, arithmetic and copies ran while one was open for 29% -> 3% of each run, Pallas kernels for 31% -> 41%
where the time goes in v3:
time: 779 us; the launch traced here: 771 us
  Pallas kernels  533 us (68%)
  waiting for transfers between devices  125 us (16%)
  local copies, waits for them, and re-layouts  67.8 us (9%)
  between operations  16.5 us (2%)
  starting transfers between devices  10.7 us (1%)
  matrix products  9.44 us (1%)
  other arithmetic  9.07 us (1%)
    pallas_call x2, Pallas kernels, scatter_sums(): pl.pallas_call(functools.partial(scatter_kernel, widths=widths, step=step...  162 us
    ppermute x6, waiting for transfers between devices, swap(): lax.ppermute(part, 'tensor', [(i, (i + 1) % count) for i in range(count)])  124 us
    pallas_call x1, Pallas kernels, gather_and_prepare(): pl.pallas_call(functools.partial(gather_kernel, pieces=pieces, step=step,...  124 us
    pallas_call x1, Pallas kernels, feed_forward(): pl.pallas_call(functools.partial(ffn_kernel, summed=summed), grid=(steps,...  93.9 us
    unnamed x159, local copies, waits for them, and re-layouts  41.4 us
    pallas_call x1, Pallas kernels, self_attention(): pl.pallas_call(self_kernel, grid=(micro, pairs), in_specs=self_specs(bloc...  26.2 us
    pallas_call x1, Pallas kernels, cross_attention_back(): pl.pallas_call(cross_back_kernel, grid=(micro, pairs), in_specs=cross_spe...  24.2 us
    pallas_call x3, Pallas kernels, norm_back(): pl.pallas_call(functools.partial(norm_back_kernel, index=index, with_weig...  23.8 us
  transfers between devices with their start and end apart: 10, of which 4 were waited for; matrix products, arithmetic and copies ran while one was open for 3% of the time, Pallas kernels for 41%

profile of v3, /device:TPU:0, one launch (start us, length us, event | category | flops | bytes accessed | tf_op | source)
XLA Modules:
  0.0 771.4 jit_solution(217667874208259164)
XLA Ops:
  17.6 123.5 %gather_and_prepare.1 = (bf16[2,2,2,2,96,5376]{5,4,3,2,1,0:T(8,128)(2,1)}, bf16[1024,1536]{1,0:T(8,128)(2,1)}, bf16[1536,512]{1,0:T(8,128)(2,1)S(1)}, f32[2,2,92...) custom-call(bf16[96,5376]{1,0:T(8,128)(2,1)S(1)} %maximum_dynamic-up, ...), custom_call_target="tpu_custom_call" | custom-call | bytes 165150720 | tf_op jit(solution)/shard_map/gather_and_prepare/pallas_call | solution.py:419
  145.3 1.9 copy-done.32
  147.2 14.3 %qkv_projection.1.q_ref.k_ref.v_ref = bf16[1024,2304]{1,0:T(8,128)(2,1)S(1)} custom-call(bf16[1024,1536]{1,0:T(8,128)(2,1)S(1)} %copy-done.32, bf16[1536,5376]{1,0:T(8,128)(2,1)} %bitcast.83, f32[3,1024,128]{2,1,0:T(8,128)S(1)} %copy-done.36), custom_call_target="tpu_custom_call" | custom-call | flops 7247757312 | bytes 14942208 | tf_op jit(solution)/shard_map/qkv_projection/pallas_call | solution.py:719
  161.5 26.2 %self_attention.1 = (bf16[512,768]{1,0:T(8,128)(2,1)S(1)}, f32[512,128]{1,0:T(8,128)S(1)}, bf16[512,1536]{1,0:T(8,128)(2,1)S(1)}) custom-call(bf16[1024,2304]{1,0:T(8,128)(2,1)S(1)} %qkv_projection.1.q_ref.k_ref.v_ref, bf16[1024,2304]{1,0:T(8,128)(2,1)S(1)} %qkv_projection.1.q_ref.k_ref.v_ref, bf16[1024,2304]{1,0:T(8,128)(2,1)S(1)} %qkv_projection.1.q_ref.k_ref.v_ref, ...), custom_call_target="tpu_custom_call" | custom-call | flops 2415919104 | bytes 7864320 | tf_op jit(solution)/shard_map/self_attention/pallas_call | solution.py:991
  190.0 3.4 slice.92
  199.7 25.2 %collective-permute-done.refs_2_ = bf16[512,1536]{1,0:T(8,128)(2,1)} collective-permute-done((bf16[512,1536]{1,0:T(8,128)(2,1)S(1)}, bf16[512,1536]{1,0:T(8,128)(2,1)}, u32[]{:S(2)}, u32[]{:S(2)}) %collective-permute-start) | collective-permute-done | bytes 1572896 | tf_op jit(solution)/shard_map/ppermute | solution.py:56
  224.9 5.4 norm_forward.2
  230.3 1.7 copy-done.3
  233.2 6.3 copy-done
  239.5 18.8 %cross_attention.1 = (bf16[512,768]{1,0:T(8,128)(2,1)S(1)}, f32[512,128]{1,0:T(8,128)S(1)}, bf16[512,1536]{1,0:T(8,128)(2,1)}) custom-call(bf16[512,768]{1,0:T(8,128)(2,1)S(1)} %get-tuple-element.71.q_ref, bf16[512,768]{1,0:T(8,128)(2,1)S(1)} %convolution_convert_fusion.6.k_ref, bf16[512,768]{1,0:T(8,128)(2,1)S(1)} %convolution_convert_fusion.5.v_ref, ...), custom_call_target="tpu_custom_call" | custom-call | flops 2013265920 | bytes 6291456 | tf_op jit(solution)/shard_map/cross_attention/pallas_call | solution.py:1102
  263.0 32.7 %collective-permute-done.1.refs_2_ = bf16[512,1536]{1,0:T(8,128)(2,1)} collective-permute-done((bf16[512,1536]{1,0:T(8,128)(2,1)}, bf16[512,1536]{1,0:T(8,128)(2,1)}, u32[]{:S(2)}, u32[]{:S(2)}) %collective-permute-start.1) | collective-permute-done | bytes 1572896 | tf_op jit(solution)/shard_map/ppermute | solution.py:56
  295.7 1.9 copy-done.4
  297.6 3.4 norm_forward.3
  301.0 1.7 copy-done.5
  305.1 93.9 %feed_forward.1 = (bf16[1536,6144]{1,0:T(8,128)(2,1)}, f32[96,3072]{1,0:T(8,128)}, bf16[512,1536]{1,0:T(8,128)(2,1)}, bf16[512,1536]{1,0:T(8,128)(2,1)}) custom-call(bf16[512,1536]{1,0:T(8,128)(2,1)} %copy-done.42, bf16[1536,512]{1,0:T(8,128)(2,1)} %copy-done.43, bf16[512,1536]{1,0:T(8,128)(2,1)} %bitcast.99, bf16[1536,512]{1,0:T(8,128)(2,1)} %copy.35.refs_3_, ...), custom_call_target="tpu_custom_call" | custom-call | flops 43486543872 | bytes 56623104 | tf_op jit(solution)/shard_map/feed_forward/pallas_call | solution.py:1290
  400.5 31.5 %collective-permute-done.2.refs_2_ = bf16[512,1536]{1,0:T(8,128)(2,1)S(1)} collective-permute-done((bf16[512,1536]{1,0:T(8,128)(2,1)}, bf16[512,1536]{1,0:T(8,128)(2,1)S(1)}, u32[]{:S(2)}, u32[]{:S(2)}) %collective-permute-start.2) | collective-permute-done | bytes 1572896 | tf_op jit(solution)/shard_map/ppermute | solution.py:56
  434.6 9.0 %norm_back.3 = (f32[512,1536]{1,0:T(8,128)}, f32[2,2,2,1536]{3,2,1,0:T(2,128)S(1)}, bf16[1536,512]{1,0:T(8,128)(2,1)S(1)}, bf16[512,768]{1,0:T(8,128)(2,1)S(1)}) custom-call(bf16[512,1536]{1,0:T(8,128)(2,1)S(1)} %bitcast.101, bf16[512,1536]{1,0:T(8,128)(2,1)S(1)} %copy-done.22, bf16[512,1536]{1,0:T(8,128)(2,1)} %copy-done.52, f32[512,1536]{1,0:T(8,128)} %copy-done.5, ...), custom_call_target="tpu_custom_call" | custom-call | flops 1207959552 | bytes 15728640 | tf_op jit(solution)/shard_map/norm_back/pallas_call | solution.py:929
  444.8 24.2 %cross_attention_back.1 = (bf16[512,768]{1,0:T(8,128)(2,1)S(1)}, bf16[512,768]{1,0:T(8,128)(2,1)S(1)}, bf16[512,768]{1,0:T(8,128)(2,1)S(1)}, bf16[512,1536]{1,0:T(8,128)(2,1)S(1)}) custom-call(bf16[512,768]{1,0:T(8,128)(2,1)S(1)} %copy-done.14, bf16[512,768]{1,0:T(8,128)(2,1)S(1)} %copy-done.10, bf16[512,768]{1,0:T(8,128)(2,1)S(1)} %copy-done.12, ...), custom_call_target="tpu_custom_call" | custom-call | flops 3221225472 | bytes 11796480 | tf_op jit(solution)/shard_map/cross_attention_back/pallas_call | solution.py:1159
  471.4 35.1 %collective-permute-done.4.refs_2_ = bf16[512,1536]{1,0:T(8,128)(2,1)S(1)} collective-permute-done((bf16[512,1536]{1,0:T(8,128)(2,1)S(1)}, bf16[512,1536]{1,0:T(8,128)(2,1)S(1)}, u32[]{:S(2)}, u32[]{:S(2)}) %collective-permute-start.4) | collective-permute-done | bytes 1572896 | tf_op jit(solution)/shard_map/ppermute | solution.py:56
  506.5 8.8 %norm_back.4 = (f32[512,1536]{1,0:T(8,128)}, f32[2,2,2,1536]{3,2,1,0:T(2,128)S(1)}, bf16[1536,512]{1,0:T(8,128)(2,1)S(1)}, bf16[512,768]{1,0:T(8,128)(2,1)S(1)}) custom-call(f32[512,1536]{1,0:T(8,128)} %get-tuple-element.82.refs_0_, bf16[512,1536]{1,0:T(8,128)(2,1)S(1)} %get-tuple-element.85.refs_1_, bf16[512,1536]{1,0:T(8,128)(2,1)S(1)} %collective-permute-done.4.refs_2_, ...), custom_call_target="tpu_custom_call" | custom-call | flops 1207959552 | bytes 15728640 | tf_op jit(solution)/shard_map/norm_back/pallas_call | solution.py:929
  515.4 21.6 %self_attention_back.1 = (f32[3,512,768]{2,1,0:T(8,128)S(1)}, bf16[2,2,128,768]{3,2,1,0:T(8,128)(2,1)S(1)}, bf16[2,2,128,768]{3,2,1,0:T(8,128)(2,1)S(1)}) custom-call(bf16[1024,2304]{1,0:T(8,128)(2,1)S(1)} %bitcast.93, bf16[1024,2304]{1,0:T(8,128)(2,1)S(1)} %bitcast.93, bf16[1024,2304]{1,0:T(8,128)(2,1)S(1)} %bitcast.93, f32[512,384]{1,0:T(8,128)S(1)} %copy-done.16, ...), custom_call_target="tpu_custom_call" | custom-call | flops 3019898880 | bytes 15728640 | tf_op jit(solution)/shard_map/self_attention_back/pallas_call | solution.py:1051
  537.0 2.2 copy-done.31
  541.8 1.8 convolution_convert_fusion.3
  547.6 16.4 %qkv_back.1 = (bf16[1536,2304]{1,0:T(8,128)(2,1)}, bf16[512,1536]{1,0:T(8,128)(2,1)S(1)}) custom-call(f32[3,512,768]{2,1,0:T(8,128)S(1)} %bitcast.107, bf16[2,2,128,768]{3,2,1,0:T(8,128)(2,1)S(1)} %collective-permute-done.5.after_ref, bf16[2,2,128,768]{3,2,1,0:T(8,128)(2,1)S(1)} %collective-permute-done.6.before_ref, bf16[1536,512]{1,0:T(8,128)(2,1)S(1)} %copy-done.34, ...), custom_call_target="tpu_custom_call" | custom-call | flops 7247757312 | bytes 18874368 | tf_op jit(solution)/shard_map/qkv_back/pallas_call | solution.py:1393
  569.0 89.5 %scatter_sums.2 = f32[96,3072]{1,0:T(8,128)S(1)} custom-call(bf16[2,2,2,2,96,768]{5,4,3,2,1,0:T(8,128)(2,1)S(1)} %bitcast.102, bf16[2,2,2,2,96,768]{5,4,3,2,1,0:T(8,128)(2,1)S(1)} %bitcast.103, bf16[2,2,2,2,96,768]{5,4,3,2,1,0:T(8,128)(2,1)S(1)} %pad_maximum_fusion.refs_2_, bf16[2,2,2,2,96,768]{5,4,3,2,1,0:T(8,128)(2,1)S(1)} %bitcast.104), custom_call_target="tpu_custom_call" | custom-call | bytes 37748736 | tf_op jit(solution)/shard_map/scatter_sums/pallas_call | solution.py:662
  659.5 3.8 add_convert_fusion
  665.8 6.0 norm_back.5
  672.4 72.3 %scatter_sums.3 = (f32[96,2304]{1,0:T(8,128)S(1)}, f32[8,9216]{1,0:T(8,128)S(1)}) custom-call(bf16[2,2,2,2,96,2304]{5,4,3,2,1,0:T(8,128)(2,1)S(1)} %bitcast.98, f32[8,9216]{1,0:T(8,128)S(1)} %bitcast.105), custom_call_target="tpu_custom_call" | custom-call | bytes 28311552 | tf_op jit(solution)/shard_map/scatter_sums/pallas_call | solution.py:662
  748.1 3.6 reshape.148
  751.8 7.3 slice_reduce_fusion
  759.0 1.7 stack_reshape_squeeze.3
  760.9 1.8 copy.41
  (219 shorter events, 58.0 us)
Async XLA Ops:
  7.2 297.9 %all-gather.2.cloned.1.call-start = ((), (), s32[]{:S(2)}) async-start(), calls=%async_computation.1 | async-start | bytes 30081024 | tf_op jit(solution)/shard_map/all_gather | solution.py:1494
  143.4 18.1 %copy-start.17 = (f32[512,256]{1,0:T(8,128)}, f32[512,256]{1,0:T(8,128)S(1)}, u32[]{:S(2)}) copy-start(f32[512,256]{1,0:T(8,128)S(1)} %get-tuple-element.72.bias_ref) | copy-start | bytes 1572868
  143.4 18.1 %copy-start.15 = (f32[512,384]{1,0:T(8,128)}, f32[512,384]{1,0:T(8,128)S(1)}, u32[]{:S(2)}) copy-start(f32[512,384]{1,0:T(8,128)S(1)} %get-tuple-element.66.bias_ref) | copy-start | bytes 2359300
  143.5 604.6 %reduce-scatter.2.cloned.1.call-start = ((), (), s32[]{:S(2)}) async-start(), calls=%async_computation.2 | async-start | bytes 20054016 | tf_op jit(solution)/shard_map/reduce_scatter | solution.py:688
  161.5 26.2 %copy-start.1 = (bf16[1024,2304]{1,0:T(8,128)(2,1)}, bf16[1024,2304]{1,0:T(8,128)(2,1)S(1)}, u32[]{:S(2)}) copy-start(bf16[1024,2304]{1,0:T(8,128)(2,1)S(1)} %qkv_projection.1.q_ref.k_ref.v_ref) | copy-start | bytes 14155780
  188.5 36.4 %collective-permute-start = (bf16[512,1536]{1,0:T(8,128)(2,1)S(1)}, bf16[512,1536]{1,0:T(8,128)(2,1)}, u32[]{:S(2)}, u32[]{:S(2)}) collective-permute-start(bf16[512,1536]{1,0:T(8,128)(2,1)S(1)} %get-tuple-element.67.refs_1_), channel_id=1, source_target_pairs={{0,1},{1,0},{2,3},{3,2},{4,5},{5,4},{6,7},{7,6},{8,9},{9,8},{10,11... | collective-permute-start | bytes 4718600 | tf_op jit(solution)/shard_map/ppermute | solution.py:56
  198.8 34.4 %copy-start.9 = (bf16[512,768]{1,0:T(8,128)(2,1)}, bf16[512,768]{1,0:T(8,128)(2,1)S(1)}, u32[]{:S(2)}) copy-start(bf16[512,768]{1,0:T(8,128)(2,1)S(1)} %convolution_convert_fusion.6.k_ref) | copy-start | bytes 2359300
  198.9 26.0 %copy-start.2 = (bf16[2,256,1536]{2,1,0:T(8,128)(2,1)S(1)}, bf16[2,256,1536]{2,1,0:T(8,128)(2,1)}, u32[]{:S(2)}) copy-start(bf16[2,256,1536]{2,1,0:T(8,128)(2,1)} %latent_ref.1) | copy-start | bytes 4718596
  199.7 33.5 %copy-start.11 = (bf16[512,768]{1,0:T(8,128)(2,1)}, bf16[512,768]{1,0:T(8,128)(2,1)S(1)}, u32[]{:S(2)}) copy-start(bf16[512,768]{1,0:T(8,128)(2,1)S(1)} %convolution_convert_fusion.5.v_ref) | copy-start | bytes 2359300
  233.2 25.1 %copy-start.13 = (bf16[512,768]{1,0:T(8,128)(2,1)}, bf16[512,768]{1,0:T(8,128)(2,1)S(1)}, u32[]{:S(2)}) copy-start(bf16[512,768]{1,0:T(8,128)(2,1)S(1)} %get-tuple-element.71.q_ref) | copy-start | bytes 2359300
  239.5 22.0 %copy-start.7 = (bf16[2,256,1536]{2,1,0:T(8,128)(2,1)S(1)}, bf16[2,256,1536]{2,1,0:T(8,128)(2,1)}, u32[]{:S(2)}) copy-start(bf16[2,256,1536]{2,1,0:T(8,128)(2,1)} %param.30) | copy-start | bytes 4718596
  259.9 35.8 %collective-permute-start.1 = (bf16[512,1536]{1,0:T(8,128)(2,1)}, bf16[512,1536]{1,0:T(8,128)(2,1)}, u32[]{:S(2)}, u32[]{:S(2)}) collective-permute-start(bf16[512,1536]{1,0:T(8,128)(2,1)} %get-tuple-element.73.refs_1_), channel_id=1, source_target_pairs={{0,1},{1,0},{2,3},{3,2},{4,5},{5,4},{6,7},{7,6},{8,9},{9,8},{10,11... | collective-permute-start | bytes 4718600 | tf_op jit(solution)/shard_map/ppermute | solution.py:56
  399.0 34.2 %copy-start.8 = (bf16[2,256,1536]{2,1,0:T(8,128)(2,1)S(1)}, bf16[2,256,1536]{2,1,0:T(8,128)(2,1)}, u32[]{:S(2)}) copy-start(bf16[2,256,1536]{2,1,0:T(8,128)(2,1)} %param.30) | copy-start | bytes 4718596
  399.0 33.0 %collective-permute-start.2 = (bf16[512,1536]{1,0:T(8,128)(2,1)}, bf16[512,1536]{1,0:T(8,128)(2,1)S(1)}, u32[]{:S(2)}, u32[]{:S(2)}) collective-permute-start(bf16[512,1536]{1,0:T(8,128)(2,1)} %get-tuple-element.79.refs_1_), channel_id=1, source_target_pairs={{0,1},{1,0},{2,3},{3,2},{4,5},{5,4},{6,7},{7,6},{8,9},{9,8},{10,11... | collective-permute-start | bytes 4718600 | tf_op jit(solution)/shard_map/ppermute | solution.py:56
  444.8 25.5 %copy-start.68 = (s32[2]{0:T(128)S(1)}, s32[2]{0:T(128)}, u32[]{:S(2)}) copy-start(s32[2]{0:T(128)} %copy-done.67) | copy-start | bytes 28
  444.8 70.5 %slice-start = ((s8[4718592]{0:T(1024)(128)(4,1)}), s8[4194304]{0:T(1024)(128)(4,1)S(1)}, s32[]{:S(2)}) async-start(s8[4718592]{0:T(1024)(128)(4,1)} %bitcast.92), calls=%async_computation.3 | async-start | bytes 8388608
  469.1 46.2 %copy-start.48 = (bf16[512,768]{1,0:T(8,128)(2,1)}, bf16[512,768]{1,0:T(8,128)(2,1)S(1)}, u32[]{:S(2)}) copy-start(bf16[512,768]{1,0:T(8,128)(2,1)S(1)} %get-tuple-element.99) | copy-start | bytes 2359300
  469.1 37.4 %collective-permute-start.4 = (bf16[512,1536]{1,0:T(8,128)(2,1)S(1)}, bf16[512,1536]{1,0:T(8,128)(2,1)S(1)}, u32[]{:S(2)}, u32[]{:S(2)}) collective-permute-start(bf16[512,1536]{1,0:T(8,128)(2,1)S(1)} %get-tuple-element.85.refs_1_), channel_id=1, source_target_pairs={{0,1},{1,0},{2,3},{3,2},{4,5},{5,4},{6,7},{7,6},{8,9},{9,8},{10,11... | collective-permute-start | bytes 4718600 | tf_op jit(solution)/shard_map/ppermute | solution.py:56
  470.5 44.8 %slice-start.1 = ((s8[4718592]{0:T(1024)(128)(4,1)}), s8[524288]{0:T(1024)(128)(4,1)S(1)}, s32[]{:S(2)}) async-start(s8[4718592]{0:T(1024)(128)(4,1)} %bitcast.92), calls=%async_computation.4 | async-start | bytes 1048576
  470.5 44.9 %copy-start.16 = (f32[512,384]{1,0:T(8,128)S(1)}, f32[512,384]{1,0:T(8,128)}, u32[]{:S(2)}) copy-start(f32[512,384]{1,0:T(8,128)} %copy-done.15) | copy-start | bytes 2359300
  470.5 44.9 %copy-start.24 = (f32[512,128]{1,0:T(8,128)S(1)}, f32[512,128]{1,0:T(8,128)}, u32[]{:S(2)}) copy-start(f32[512,128]{1,0:T(8,128)} %copy-done.23) | copy-start | bytes 786436
  470.5 189.0 %collective-permute-start.3 = (bf16[512,1536]{1,0:T(8,128)(2,1)}, bf16[512,1536]{1,0:T(8,128)(2,1)}, u32[]{:S(2)}, u32[]{:S(2)}) collective-permute-start(bf16[512,1536]{1,0:T(8,128)(2,1)} %get-tuple-element.81), channel_id=1, source_target_pairs={{0,1},{1,0},{2,3},{3,2},{4,5},{5,4},{6,7},{7,6},{8,9},{9,8},{10,11... | collective-permute-start | bytes 4718600 | tf_op jit(solution)/shard_map/ppermute | solution.py:56
  515.3 26.4 %copy-start.49 = (bf16[512,768]{1,0:T(8,128)(2,1)S(1)}, bf16[512,768]{1,0:T(8,128)(2,1)}, u32[]{:S(2)}) copy-start(bf16[512,768]{1,0:T(8,128)(2,1)} %copy-done.48) | copy-start | bytes 2359300
  515.3 26.4 %copy-start.57 = (bf16[256,768]{1,0:T(8,128)(2,1)S(1)}, bf16[256,768]{1,0:T(8,128)(2,1)}, u32[]{:S(2)}) copy-start(bf16[256,768]{1,0:T(8,128)(2,1)} %copy-done.56) | copy-start | bytes 1179652
  515.4 26.4 %copy-start.59 = (bf16[256,768]{1,0:T(8,128)(2,1)S(1)}, bf16[256,768]{1,0:T(8,128)(2,1)}, u32[]{:S(2)}) copy-start(bf16[256,768]{1,0:T(8,128)(2,1)} %copy-done.58) | copy-start | bytes 1179652
  539.1 7.4 collective-permute-start.5
  540.5 6.0 collective-permute-start.6
  547.6 17.6 %copy-start.60 = (bf16[256,768]{1,0:T(8,128)(2,1)S(1)}, bf16[256,768]{1,0:T(8,128)(2,1)}, u32[]{:S(2)}) copy-start(bf16[256,768]{1,0:T(8,128)(2,1)} %copy-done.58) | copy-start | bytes 1179652
  564.0 99.3 %collective-permute-start.7 = (bf16[512,1536]{1,0:T(8,128)(2,1)S(1)}, bf16[512,1536]{1,0:T(8,128)(2,1)S(1)}, u32[]{:S(2)}, u32[]{:S(2)}) collective-permute-start(bf16[512,1536]{1,0:T(8,128)(2,1)S(1)} %get-tuple-element.93.refs_1_), channel_id=1, source_target_pairs={{0,1},{1,0},{2,3},{3,2},{4,5},{5,4},{6,7},{7,6},{8,9},{9,8},{10,11... | collective-permute-start | bytes 4718600 | tf_op jit(solution)/shard_map/ppermute | solution.py:56
  569.0 90.5 %copy-start.6 = (f32[512,1536]{1,0:T(8,128)S(1)}, f32[512,1536]{1,0:T(8,128)}, u32[]{:S(2)}) copy-start(f32[512,1536]{1,0:T(8,128)} %copy-done.5) | copy-start | bytes 9437188
  672.3 72.4 %copy-start.63 = (f32[8,128]{1,0:T(8,128)S(1)}, f32[8,128]{1,0:T(8,128)}, u32[]{:S(2)}) copy-start(f32[8,128]{1,0:T(8,128)} %copy-done.62) | copy-start | bytes 12292
  672.3 72.4 %copy-start.65 = (f32[8,128]{1,0:T(8,128)S(1)}, f32[8,128]{1,0:T(8,128)}, u32[]{:S(2)}) copy-start(f32[8,128]{1,0:T(8,128)} %copy-done.64) | copy-start | bytes 12292
  (54 other events, 171.9 us)
Sparse Core Ops, SparseCore 0:
  143.6 142.7 all-gather.1
  399.1 195.8 reduce-scatter.1

commit v4 on v3

--- a/solution.py
+++ b/solution.py
@@ -75,20 +75,21 @@
     return [(me // stride) % 2 for stride in STRIDES]
 
 
-def greet(me, digits, others=()):
+def greet(me, digits, others=(), mine=None):
     partners = [me + stride * (1 - 2 * digit) for stride, digit in zip(STRIDES, digits)]
     barrier = pltpu.get_barrier_semaphore()
 
-    def tell(target):
-        pl.semaphore_signal(
-            barrier, inc=1, device_id={"seq": target}, device_id_type=pl.DeviceIdType.MESH
-        )
+    def tell(**target):
+        pl.semaphore_signal(barrier, inc=1, device_id=target, device_id_type=pl.DeviceIdType.MESH)
 
     expected = len(partners)
     for partner in partners:
-        tell(partner)
+        tell(seq=partner)
+    if mine is not None:
+        tell(tensor=1 - mine)
+        expected += 1
     for there, target in others:
-        pl.when(there)(functools.partial(tell, target))
+        pl.when(there)(functools.partial(tell, seq=target))
         expected = expected + there.astype(jnp.int32)
     pl.semaphore_wait(barrier, expected)
     return partners
@@ -105,33 +106,60 @@
     )
 
 
-def small_sum(partners, part_ref, held, got, total_ref, send_sem, recv_sem):
+def greet_all(me, mine, digits, others=()):
+    return greet(me, digits, others, mine)
+
+
+def to_tensor(mine, source, target, send_sem, recv_sem):
+    return pltpu.make_async_remote_copy(
+        src_ref=source,
+        dst_ref=target,
+        send_sem=send_sem,
+        recv_sem=recv_sem,
+        device_id={"tensor": 1 - mine},
+        device_id_type=pl.DeviceIdType.MESH,
+    )
+
+
+SMALL_STEPS = 6
+
+
+def small_sum(partners, mine, core, fill, prep, held, got, total, finish, send_sem, recv_sem):
+    own = 2 * mine + core
+    half = pl.ds(2 * mine, 2)
+
     def exchange(k):
-        return send_to(partners[k], held.at[k], got.at[k], send_sem.at[k], recv_sem.at[k])
+        sems = send_sem.at[k], recv_sem.at[k]
+        if k == 0:
+            return send_to(partners[0], prep.at[2 * mine + 1 - core], got.at[0], *sems)
+        if k < 4:
+            return send_to(partners[k], held.at[k], got.at[k], *sems)
+        if k == 4:
+            return send_to(partners[0], total.at[own], total.at[own], *sems)
+        return to_tensor(mine, total.at[half], total.at[half], *sems)
 
     def step(k):
         if k == 0:
-            held[0] = part_ref[...]
+            fill(prep)
         else:
             exchange(k - 1).wait()
-            summed = held[k - 1] + got[k - 1]
-            if k == len(STRIDES):
-                total_ref[...] = summed
-            else:
-                held[k] = summed
-        if k < len(STRIDES):
+        if k == 1:
+            held[1] = prep[own] + got[0]
+        elif 1 < k < 4:
+            held[k] = held[k - 1] + got[k - 1]
+        elif k == 4:
+            total[own] = held[3] + got[3]
+        elif k == SMALL_STEPS:
+            finish(total)
+        if k < SMALL_STEPS:
             exchange(k).start()
 
     return step
 
 
 def small_scratch(shape):
-    return [
-        pltpu.VMEM((len(STRIDES),) + shape, f32),
-        pltpu.VMEM((len(STRIDES),) + shape, f32),
-        pltpu.SemaphoreType.DMA((len(STRIDES),)),
-        pltpu.SemaphoreType.DMA((len(STRIDES),)),
-    ]
+    quarter = (4, shape[0], shape[1] // 4)
+    return [pltpu.VMEM(quarter, f32)] * 4 + [pltpu.SemaphoreType.DMA((SMALL_STEPS,))] * 2
 
 
 def lane_ladder():
@@ -192,7 +220,7 @@
 def gather_kernel(
     share_ref, part_ref, latent_ref, lengths_ref, text_ref, ladder_ref,
     out_ref, near_normed_ref, normed_t_ref, two_ref, later_ref, table_ref, self_ref, cross_ref,
-    near_ref, total_ref, held, got, small_send, small_recv, copy_sem, send_sem, recv_sem,
+    near_ref, prep, held, got, total_ref, small_send, small_recv, copy_sem, send_sem, recv_sem,
     near_sem, halo_send, halo_recv, *, pieces, step, y_first, seq_count,
 ):
     micro, block_rows, width = latent_ref.shape
@@ -204,8 +232,18 @@
     first = me * block_rows
     has_low = me > 0
     has_high = me < seq_count - 1
-    partners = greet(me, digits, ((has_low, me - 1), (has_high, me + 1)))
-    small = small_sum(partners, part_ref, held, got, total_ref, small_send, small_recv)
+    mine = lax.axis_index("tensor")
+    partners = greet_all(me, mine, digits, ((has_low, me - 1), (has_high, me + 1)))
+
+    def fill(target):
+        span = target.shape[2]
+        for index in range(4):
+            target[index] = part_ref[:, index * span : (index + 1) * span]
+
+    small = small_sum(
+        partners, mine, core, fill, prep, held, got, total_ref, lambda total: None,
+        small_send, small_recv,
+    )
 
     def to_low():
         return send_to(
@@ -277,11 +315,17 @@
             table_ref[index, target : target + HALF, :] = values
 
     def modulation(m, base):
+        span = total_ref.shape[2]
         for which in range(2):
-            two_ref[m, which : which + 1] = sum(
-                jnp.where(base + which == k, total_ref[m * items + k : m * items + k + 1], 0.0)
-                for k in range(items)
-            )
+            for index in range(4):
+                two_ref[m, which : which + 1, index * span : (index + 1) * span] = sum(
+                    jnp.where(
+                        base + which == k,
+                        total_ref[index, m * items + k : m * items + k + 1],
+                        0.0,
+                    )
+                    for k in range(items)
+                )
 
     def norm(m, start):
         shift = [two_ref[m, which : which + 1, :width] for which in range(2)]
@@ -301,7 +345,7 @@
 
     beside = {}
     state = {}
-    gap = 4
+    gap = 3
 
     def add(t, work):
         beside.setdefault(t, []).append(work)
@@ -318,9 +362,9 @@
             tick += 1
             add(tick, functools.partial(tables, m, start))
         tick += 1
-    for k in range(1, len(STRIDES) + 1):
+    for k in range(1, SMALL_STEPS + 1):
         add(gap * k, functools.partial(small, k))
-    tick = gap * len(STRIDES)
+    tick = gap * SMALL_STEPS
     add(tick, finish_near)
     for m in range(micro):
         tick += 1
@@ -375,7 +419,7 @@
     near_rows = block_rows + 2 * HALF
     own_rows = micro * block_rows
     ladder = jnp.asarray(lane_ladder()).reshape(1, 128)
-    if count != 16 or rows % 16 or width % step:
+    if count != 16 or rows % 16 or width % step or lax.axis_size("tensor") != 2:
         ahead = [(i, i + 1) for i in range(count - 1)]
         behind = [(i + 1, i) for i in range(count - 1)]
         low_rows = lax.ppermute(latents[:, block_rows - HALF :], "seq", ahead)
@@ -438,7 +482,6 @@
         out_specs=[any_space] + [vmem] * 7,
         scratch_shapes=[
             pltpu.VMEM((micro, near_rows, model_width), bf16),
-            pltpu.VMEM(part.shape, f32),
         ]
         + small_scratch(part.shape)
         + [
@@ -460,7 +503,7 @@
     return [outs[0].reshape(count * rows, width)] + list(outs[1:])
 
 
-SLOTS = 5
+SLOTS = 6
 
 
 def when(condition):
@@ -470,7 +513,7 @@
 
 
 class Pieces:
-    def __init__(self, refs, out_ref, partners, digits, step):
+    def __init__(self, refs, out_ref, partners, digits, step, lag=2):
         (
             self.own, self.got0, self.got1, self.got2, self.got3, self.staged,
             self.out_sem, self.send_sem, self.recv_sem,
@@ -479,6 +522,7 @@
         self.partners = partners
         self.digits = digits
         self.step = step
+        self.lag = lag
 
     @staticmethod
     def scratch(rows, step):
@@ -506,17 +550,47 @@
     def over_core(self, source, slot):
         return self.exchange(0, source, self.got0.at[slot], slot)
 
-    def over_y(self, slot):
-        y = self.digits[1]
-        return self.exchange(1, self.own.at[slot, :, :, 1 - y], self.got1.at[slot], slot)
-
-    def over_z_lo(self, slot):
-        _, y, z_lo, _ = self.digits
-        return self.exchange(2, self.own.at[slot, :, 1 - z_lo, y], self.got2.at[slot], slot)
-
-    def over_z_hi(self, slot):
-        _, y, z_lo, z_hi = self.digits
-        return self.exchange(3, self.own.at[slot, 1 - z_hi, z_lo, y], self.got3.at[slot], slot)
+    PATHS = ((2, 1, 0),)
+
+    def spot(self, path, stage, other):
+        axes = (self.digits[3], self.digits[2], self.digits[1])
+        index = [slice(None)] * 3
+        for axis in path[: stage - 1]:
+            index[axis] = axes[axis]
+        axis = path[stage - 1]
+        index[axis] = 1 - axes[axis] if other else axes[axis]
+        return tuple(index)
+
+    def hop(self, path, stage, slot):
+        partner = (3, 2, 1)[path[stage - 1]]
+        target = (self.got1, self.got2, self.got3)[stage - 1].at[slot]
+        source = self.own.at[(slot,) + self.spot(path, stage, True)]
+        return send_to(
+            self.partners[partner],
+            source,
+            target,
+            self.send_sem.at[stage, slot],
+            self.recv_sem.at[stage, slot],
+        )
+
+    def by_path(self, item, work):
+        work(self.PATHS[0])
+
+    def add_hop(self, path, stage, slot):
+        got = (self.got1, self.got2, self.got3)[stage - 1]
+        index = self.spot(path, stage, False)
+        free = [k for k in range(3) if isinstance(index[k], slice)]
+        for count in range(2 ** len(free)):
+            bits = [(count >> k) & 1 for k in range(len(free))]
+            full = list(index)
+            for k, bit in zip(free, bits):
+                full[k] = bit
+            at = (slot,) + tuple(full)
+            total = self.own[at].astype(f32) + got[(slot,) + tuple(bits)].astype(f32)
+            if stage < 3:
+                self.own[at] = total.astype(bf16)
+            else:
+                self.staged[slot] = total
 
     def store(self, item, slot):
         columns = pl.ds(pl.multiple_of(item * self.step, self.step), self.step)
@@ -525,48 +599,98 @@
         )
 
     def wait_sent(self, slot):
-        self.over_y(slot).wait_send()
-        self.over_z_lo(slot).wait_send()
-        self.over_z_hi(slot).wait_send()
-
-    def add_core(self, slot, left):
+        for stage in (1, 2, 3):
+            self.hop(self.PATHS[0], stage, slot).wait_send()
+
+    def add_core(self, item, slot, left):
         for i in range(2):
             for j in range(2):
                 for k in range(2):
                     total = left(i, j, k).astype(f32) + self.got0[slot, i, j, k].astype(f32)
                     self.own[slot, i, j, k] = total.astype(bf16)
-        self.over_y(slot).start()
+        self.by_path(item, lambda path: self.hop(path, 1, slot).start())
 
     def later_steps(self, t, count):
-        own = self.own
-        _, y, z_lo, z_hi = self.digits
-
-        @when((t >= 2) & (t - 2 < count))
+        lag = self.lag
+
+        @when((t >= lag) & (t - lag < count))
         def _():
-            slot = (t - 2) % SLOTS
-            self.over_y(slot).wait_recv()
-            for i in range(2):
-                for j in range(2):
-                    total = own[slot, i, j, y].astype(f32) + self.got1[slot, i, j].astype(f32)
-                    own[slot, i, j, y] = total.astype(bf16)
-            self.over_z_lo(slot).start()
-
-        @when((t >= 3) & (t - 3 < count))
+            item = t - lag
+            slot = item % SLOTS
+            self.hop(self.PATHS[0], 1, slot).wait_recv()
+
+            def work(path):
+                self.add_hop(path, 1, slot)
+                self.hop(path, 2, slot).start()
+
+            self.by_path(item, work)
+
+        @when((t >= lag + 1) & (t - lag - 1 < count))
         def _():
-            slot = (t - 3) % SLOTS
-            self.over_z_lo(slot).wait_recv()
-            for i in range(2):
-                total = own[slot, i, z_lo, y].astype(f32) + self.got2[slot, i].astype(f32)
-                own[slot, i, z_lo, y] = total.astype(bf16)
-            self.over_z_hi(slot).start()
-
-        @when((t >= 4) & (t - 4 < count))
+            item = t - lag - 1
+            slot = item % SLOTS
+            self.hop(self.PATHS[0], 2, slot).wait_recv()
+
+            def work(path):
+                self.add_hop(path, 2, slot)
+                self.hop(path, 3, slot).start()
+
+            self.by_path(item, work)
+
+        @when((t >= lag + 2) & (t - lag - 2 < count))
         def _():
-            slot = (t - 4) % SLOTS
-            self.over_z_hi(slot).wait_recv()
-            when(t - 4 >= SLOTS)(lambda: self.store(0, slot).wait())
-            self.staged[slot] = own[slot, z_hi, z_lo, y].astype(f32) + self.got3[slot].astype(f32)
-            self.store(t - 4, slot).start()
+            item = t - lag - 2
+            slot = item % SLOTS
+            self.hop(self.PATHS[0], 3, slot).wait_recv()
+            when(item >= SLOTS)(lambda: self.store(0, slot).wait())
+            self.by_path(item, lambda path: self.add_hop(path, 3, slot))
+            self.store(item, slot).start()
+
+    def run(self, sources, spans, own_sem, beside=(), last=0):
+        core = self.digits[0]
+        step = self.step
+        count = sum(width for _, width in spans) // step
+
+        def over_core(source, column, slot):
+            return self.over_core(source.at[:, :, :, 1 - core, :, pl.ds(column, step)], slot)
+
+        def load(source, column, slot):
+            return pltpu.make_async_copy(
+                source.at[:, :, :, core, :, pl.ds(column, step)],
+                self.own.at[slot],
+                own_sem.at[slot],
+            )
+
+        def tick(t, carry):
+            @pl.when(t < count)
+            def _():
+                slot = t % SLOTS
+                pl.when(t >= SLOTS)(lambda: self.wait_sent(slot))
+                done = 0
+                for source, (column, width) in zip(sources, spans):
+
+                    @pl.when((t >= done) & (t < done + width // step))
+                    def _(source=source, done=done, column=column):
+                        spot = pl.multiple_of(column + (t - done) * step, step)
+                        over_core(source, spot, slot).start()
+                        load(source, spot, slot).start()
+
+                    done += width // step
+
+            @pl.when((t >= 1) & (t - 1 < count))
+            def _():
+                slot = (t - 1) % SLOTS
+                load(sources[0], 0, slot).wait()
+                over_core(sources[0], 0, slot).wait()
+                self.add_core(t - 1, slot, lambda i, j, k: self.own[slot, i, j, k])
+
+            self.later_steps(t, count)
+            for begin, end, work in beside:
+                pl.when((t >= begin) & (t < end))(functools.partial(work, t))
+            return carry
+
+        lax.fori_loop(0, max(count + self.lag + 2, last + 1), tick, 0)
+        self.finish(count)
 
     def finish(self, count):
         for back in range(min(SLOTS, count)):
@@ -578,110 +702,245 @@
 PIECE_REFS = 9
 
 
-def scatter_kernel(*refs, widths, step, with_small):
+def norm_back_tile(grad, upstream, hidden, shift_rows, factor):
+    xhat, scale = spread_rows(hidden)
+    inner = grad * (1.0 + factor)
+    mean_inner = jnp.mean(inner, axis=-1, keepdims=True)
+    mean_cross = jnp.mean(inner * xhat, axis=-1, keepdims=True)
+    total = upstream + scale * (inner - mean_inner - xhat * mean_cross)
+    scaled = grad * xhat
+    sums = [
+        [
+            jnp.sum(jnp.where(chosen, values, 0.0), axis=0, keepdims=True)
+            for values in (grad, scaled)
+        ]
+        for chosen in shift_rows
+    ]
+    return total, sums
+
+
+def finish_kernel(*refs, spans, step, micro):
     refs = list(refs)
-    sources = [refs.pop(0) for _ in widths]
-    if with_small:
-        part_ref = refs.pop(0)
-    out_ref = refs.pop(0)
-    if with_small:
-        total_ref = refs.pop(0)
-    own_sem = refs.pop(0)
+    sources = [refs.pop(0) for _ in spans]
+    (
+        own_ref, from_low_ref, from_high_ref, normed_t_ref, weight_ref, table_ref,
+        up_ref, latent_ref, two_ref, later_ref, sums_ref, lengths_ref, feature_ref, other_ref,
+        out_ref, grad_ref, mod_ref, bias_ref, got_other_ref,
+        own_sem, back_ref, got_back, qkv_w_ref, weight_sem, g_qkv_ref, first_sums,
+        back_send, back_recv, other_sem,
+    ) = refs[:29]
+    pieces_refs = refs[29 : 29 + PIECE_REFS]
+    prep, held, got, small_total, small_send, small_recv = refs[29 + PIECE_REFS :]
     me = lax.axis_index("seq")
+    mine = lax.axis_index("tensor")
     digits = seq_digits(me)
     core = digits[0]
-    partners = greet(me, digits)
-    pieces = Pieces(refs[:PIECE_REFS], out_ref, partners, digits, step)
-    if with_small:
-        small = small_sum(partners, part_ref, refs[-4], refs[-3], total_ref, refs[-2], refs[-1])
-        small(0)
-    count = sum(widths) // step
-
-    def over_core(source, column, slot):
-        return pieces.over_core(source.at[:, :, :, 1 - core, :, pl.ds(column, step)], slot)
-
-    def load(source, column, slot):
-        return pltpu.make_async_copy(
-            source.at[:, :, :, core, :, pl.ds(column, step)],
-            pieces.own.at[slot],
-            own_sem.at[slot],
-        )
-
-    def tick(t, carry):
-        @pl.when(t < count)
-        def _():
-            slot = t % SLOTS
-            pl.when(t >= SLOTS)(lambda: pieces.wait_sent(slot))
-            first = 0
-            for source, width in zip(sources, widths):
-
-                @pl.when((t >= first) & (t < first + width // step))
-                def _(source=source, first=first):
-                    column = pl.multiple_of((t - first) * step, step)
-                    over_core(source, column, slot).start()
-                    load(source, column, slot).start()
-
-                first += width // step
-
-        @pl.when((t >= 1) & (t - 1 < count))
-        def _():
-            slot = (t - 1) % SLOTS
-            load(sources[0], 0, slot).wait()
-            over_core(sources[0], 0, slot).wait()
-            pieces.add_core(slot, lambda i, j, k: pieces.own[slot, i, j, k])
-
-        pieces.later_steps(t, count)
-        if with_small:
-            for k in range(1, len(STRIDES) + 1):
-                pl.when(t == 3 * k)(functools.partial(small, k))
-        return carry
-
-    lax.fori_loop(0, count + 4, tick, 0)
-    pieces.finish(count)
-
-
-def scatter_sums(grads, which, part=None, step=256):
-    count = lax.axis_size("seq")
-    rows = grads[0].shape[0] // count
-    widths = tuple(grad.shape[1] for grad in grads)
-    if count != 16 or rows % 16 or any(width % step for width in widths):
-        sums = [
-            lax.psum_scatter(grad.astype(f32), "seq", scatter_dimension=0, tiled=True)
-            for grad in grads
-        ]
-        return sums if part is None else sums + [seq_sum(part)]
+    rows, width = latent_ref.shape
+    local = own_ref.shape[2]
+    block_rows = rows // micro
+    near_rows = block_rows + 2 * HALF
+    items = lengths_ref.shape[1]
+    load = pltpu.make_async_copy(weight_ref.at[:, : 3 * local], qkv_w_ref, weight_sem)
+    load.start()
+    partners = greet_all(me, mine, digits)
+    pieces = Pieces(pieces_refs, out_ref, partners, digits, step)
+
+    def over_tensor(m):
+        span = pl.ds(m * block_rows, block_rows)
+        return to_tensor(
+            mine, back_ref.at[span], got_back.at[span], back_send.at[m], back_recv.at[m]
+        )
+
+    def own_table(index):
+        return jnp.concatenate(
+            [
+                table_ref[index, m * near_rows + HALF : (m + 1) * near_rows - HALF]
+                for m in range(micro)
+            ],
+            axis=0,
+        )
+
+    def project_back(kind, column):
+        lanes = pl.ds(pl.multiple_of(column, step), step)
+        total = own_ref[kind, :, lanes]
+        if kind:
+            blocks = []
+            for m in range(micro):
+                first = m * block_rows
+                blocks.append(
+                    total[first : first + HALF] + from_low_ref[m, kind - 1, :, lanes].astype(f32)
+                )
+                if block_rows > 2 * HALF:
+                    blocks.append(total[first + HALF : first + block_rows - HALF])
+                blocks.append(
+                    total[first + block_rows - HALF : first + block_rows]
+                    + from_high_ref[m, kind - 1, :, lanes].astype(f32)
+                )
+            total = jnp.concatenate(blocks, axis=0)
+        if kind < 2:
+            tables = own_table(0), -own_table(1), -own_table(2)
+            total = jnp.concatenate(
+                [turn(total[:, i : i + 128], *tables) for i in range(0, step, 128)], axis=1
+            )
+        grad = total.astype(bf16)
+        lanes = pl.ds(pl.multiple_of(kind * local + column, step), step)
+        g_qkv_ref[:, :, :, :, :, lanes] = (
+            nn(normed_t_ref[...], grad).astype(bf16).reshape(g_qkv_ref.shape[:5] + (step,))
+        )
+        grad_ref[...] += nt(grad, qkv_w_ref[:, lanes])
+
+    def send_back():
+        back_ref[...] = grad_ref[...].astype(bf16)
+        for m in range(micro):
+            over_tensor(m).start()
+
+    def norm_one(m):
+        over_tensor(m).wait_recv()
+
+        def emit(span, start, total):
+            grad_ref[span, :] = total
+
+        norm_back_unit(
+            m, 0, block_rows,
+            lambda span: back_ref[span, :].astype(f32) + got_back[span, :].astype(f32),
+            up_ref, latent_ref, two_ref, later_ref, first_sums, emit,
+        )
+
+    def fill(target):
+        span = target.shape[2]
+        size = 128 * math.gcd(span // 128, width // 128)
+        for m in range(micro):
+            ends = [lengths_ref[m, 0]]
+            for k in range(1, items):
+                ends.append(ends[-1] + lengths_ref[m, k])
+            first_item = sum((end <= me * block_rows).astype(jnp.int32) for end in ends)
+            base = jnp.minimum(first_item, items - 2)
+            for k in range(items):
+                row = slice(m * items + k, m * items + k + 1)
+                for first in range(0, 6 * width, size):
+                    ref, at = (
+                        (first_sums, first) if first < 2 * width else (sums_ref, first - 2 * width)
+                    )
+                    target[first // span, row, first % span : first % span + size] = sum(
+                        jnp.where(
+                            base + item == k, ref[m, item : item + 1, at : at + size], 0.0
+                        )
+                        for item in range(2)
+                    )
+
+    def modulation_grads(total):
+        span = total.shape[2]
+        for index in range(4):
+            lanes = slice(index * span, (index + 1) * span)
+            bias_ref[:, lanes] = jnp.sum(total[index], axis=0, keepdims=True)
+            mod_ref[:, lanes] = sum(
+                feature_ref[:, i : i + 1] * total[index, i : i + 1] for i in range(micro * items)
+            )
+
+    small = small_sum(
+        partners, mine, core, fill, prep, held, got, small_total, modulation_grads,
+        small_send, small_recv,
+    )
+    work = []
+    spot = 0
+    columns = local // step
+    work.append((0, 1, lambda t: load.wait()))
+    for kind in range(3):
+        work.append(
+            (spot, spot + columns, lambda t, k=kind, s=spot: project_back(k, (t - s) * step))
+        )
+        spot += columns
+    work.append((spot - 1, spot, lambda t: send_back()))
+    spot += 3
+    for m in range(micro):
+        work.append((spot, spot + 1, lambda t, m=m: norm_one(m)))
+        spot += 4 if m < micro - 1 else 1
+    for k in range(SMALL_STEPS + 1):
+        work.append((spot, spot + 1, lambda t, k=k: small(k)))
+        spot += 2 if k < 3 else 1
+    grad_ref[...] = jnp.zeros_like(grad_ref)
+    over_other = to_tensor(
+        mine, other_ref.at[pl.ds(0, block_rows)], got_other_ref, other_sem.at[0], other_sem.at[1]
+    )
+    over_other.start()
+    pieces.run(sources + [g_qkv_ref], spans + ((0, 3 * local),), own_sem, work, spot)
+    for m in range(micro):
+        over_tensor(m).wait_send()
+    over_other.wait()
+
+
+def finish_stage(
+    own, from_low, from_high, normed_t, weights, table, upstream, latent, two, later, sums,
+    lengths, features, other, sources, spans, micro, which=0, step=256,
+):
+    seq_count = lax.axis_size("seq")
+    rows, width = latent.shape
+    items = lengths.shape[1]
+    local = own.shape[2]
+    share = width // seq_count
+    own_features = features.T
     any_space = pl.BlockSpec(memory_space=pl.ANY)
     vmem = pl.BlockSpec(memory_space=pltpu.VMEM)
-    scratch = [pltpu.SemaphoreType.DMA((SLOTS,))] + Pieces.scratch(rows, step)
-    out_shape = [jax.ShapeDtypeStruct((rows, sum(widths)), f32)]
-    extra = []
-    if part is not None:
-        scratch += small_scratch(part.shape)
-        out_shape.append(jax.ShapeDtypeStruct(part.shape, f32))
-        extra = [vmem]
-    outs = pl.pallas_call(
-        functools.partial(
-            scatter_kernel, widths=widths, step=step, with_small=part is not None
-        ),
-        out_shape=out_shape,
-        in_specs=[any_space] * len(grads) + extra,
-        out_specs=[any_space] + extra,
-        scratch_shapes=scratch,
+    smem = pl.BlockSpec(memory_space=pltpu.SMEM)
+    return pl.pallas_call(
+        functools.partial(finish_kernel, spans=spans, step=step, micro=micro),
+        out_shape=[
+            jax.ShapeDtypeStruct((share, sum(span for _, span in spans) + 3 * local), f32),
+            jax.ShapeDtypeStruct((rows, width), f32),
+            jax.ShapeDtypeStruct((own_features.shape[0], 6 * width), f32),
+            jax.ShapeDtypeStruct((1, 6 * width), f32),
+            jax.ShapeDtypeStruct((rows // micro, width), bf16),
+        ],
+        in_specs=[any_space] * len(sources)
+        + [vmem] * 4
+        + [any_space]
+        + [vmem] * 6
+        + [smem, vmem, any_space],
+        out_specs=[any_space, vmem, vmem, vmem, any_space],
+        scratch_shapes=[
+            pltpu.SemaphoreType.DMA((SLOTS,)),
+            pltpu.VMEM((rows, width), bf16),
+            pltpu.VMEM((rows, width), bf16),
+            pltpu.VMEM((width, 3 * local), bf16),
+            pltpu.SemaphoreType.DMA,
+            pltpu.VMEM((2, 2, 2, 2, share, 3 * local), bf16),
+            pltpu.VMEM((micro, 2, 2 * width), f32),
+            pltpu.SemaphoreType.DMA((micro,)),
+            pltpu.SemaphoreType.DMA((micro,)),
+            pltpu.SemaphoreType.DMA((2,)),
+        ]
+        + Pieces.scratch(share, step)
+        + small_scratch((micro * items, 6 * width)),
         compiler_params=pltpu.CompilerParams(
-            collective_id=which, has_side_effects=True, vmem_limit_bytes=40 * 1024 * 1024
+            collective_id=which, has_side_effects=True, vmem_limit_bytes=60 * 1024 * 1024
         ),
         cost_estimate=pl.CostEstimate(
-            flops=0, bytes_accessed=8 * count * rows * sum(widths), transcendentals=0
+            flops=12 * rows * width * local, bytes_accessed=40 * rows * width, transcendentals=0
         ),
-        name="scatter_sums",
+        name="finish_stage",
     )(
-        *[grad.reshape(2, 2, 2, 2, rows, grad.shape[1]) for grad in grads],
-        *([] if part is None else [part]),
-    )
-    firsts = [sum(widths[:i]) for i in range(len(widths))]
-    return [outs[0][:, first : first + width] for first, width in zip(firsts, widths)] + list(
-        outs[1:]
-    )
+        *[source.reshape(2, 2, 2, 2, share, source.shape[1]) for source in sources],
+        own, from_low, from_high, normed_t, weights, table,
+        upstream, latent, two, later, sums, lengths, own_features, other,
+    )
+
+
+def finish_apart(grads, back, upstream, latent, two, later, sums, lengths, features, other):
+    rows, width = latent.shape
+    micro, items = lengths.shape
+    totals = [early_sum(grad) for grad in grads]
+    latent_grad, first_sums = norm_back(upstream, back, swap(back), latent, two, later, 0, micro)
+    pieces = jnp.concatenate([first_sums.reshape(micro, 2, 2 * width), sums], axis=2)
+    first_item = jnp.sum(
+        (jnp.cumsum(lengths, axis=1) <= lax.axis_index("seq") * (rows // micro)).astype(jnp.int32),
+        axis=1,
+    )
+    base = jnp.minimum(first_item, items - 2)
+    spots = (base[:, None] + jnp.arange(2))[:, :, None] == jnp.arange(items)
+    item_grad = jnp.sum(jnp.where(spots[..., None], pieces[:, :, None], 0.0), axis=1)
+    total = seq_sum(item_grad.reshape(micro * items, 6 * width))
+    mod_grad = jnp.dot(features.T, total, precision=highest)
+    return totals, latent_grad, mod_grad, jnp.sum(total, axis=0, keepdims=True), swap(other)
 
 
 def early_sum(grad):
@@ -1191,18 +1450,18 @@
 def ffn_kernel(*refs, summed):
     (
         normed_ref, normed_t_ref, cot_ref, cot_t_ref, outer_ref, gate_ref, up_ref,
-        g_early_ref, g_up_ref, out_ref, back_ref, out_acc, back_acc,
-    ) = refs[:13]
+        g_outer_ref, g_gate_ref, g_up_ref, out_ref, back_ref, *refs,
+    ) = refs
     j = pl.program_id(0)
     step = gate_ref.shape[1]
     if summed:
-        full = refs[13]
+        sum_ref, out_acc, back_acc, full = refs[:4]
         me = lax.axis_index("seq")
         digits = seq_digits(me)
         core = digits[0]
         partners = [me + stride * (1 - 2 * digit) for stride, digit in zip(STRIDES, digits)]
         pl.when(j == 0)(lambda: [greet(me, digits), None][1])
-        pieces = Pieces(refs[14:], g_up_ref, partners, digits, step)
+        pieces = Pieces(refs[4:], sum_ref, partners, digits, step, lag=2)
         count = summed
 
         def over_core(slot):
@@ -1214,15 +1473,17 @@
                 slot = (t - 1) % SLOTS
                 when(t - 1 >= SLOTS)(lambda: pieces.wait_sent(slot))
                 over_core(slot).wait()
-                pieces.add_core(slot, lambda a, b, c: full[slot, a, b, c, core])
+                pieces.add_core(t - 1, slot, lambda a, b, c: full[slot, a, b, c, core])
 
             pieces.later_steps(t, count)
 
+    else:
+        out_acc, back_acc = refs
+    if summed:
+        tick(j)
     gate = nn(normed_ref[...], gate_ref[...])
     up = nn(normed_ref[...], up_ref[...])
     grad = nn(cot_ref[...], outer_ref[...])
-    if summed:
-        tick(j)
     chance = 1.0 / (1.0 + jnp.exp(-gate))
     swish = gate * chance
     active = (swish * up).astype(bf16)
@@ -1230,13 +1491,20 @@
     up_grad = (grad * swish).astype(bf16)
     g_up = nn(normed_t_ref[...], up_grad).astype(bf16)
     if summed:
-        slot = j % SLOTS
-        full[slot] = g_up.reshape(full.shape[1:])
-        over_core(slot).start()
+
+        @pl.when(j < count)
+        def _():
+            slot = j % SLOTS
+            full[slot] = g_up.reshape(full.shape[1:])
+            over_core(slot).start()
+
+        @pl.when(j >= count)
+        def _():
+            g_up_ref[...] = g_up
     else:
         g_up_ref[...] = g_up
-    g_early_ref[:, :step] = nn(cot_t_ref[...], active).astype(bf16)
-    g_early_ref[:, step:] = nn(normed_t_ref[...], gate_grad).astype(bf16)
+    g_gate_ref[...] = nn(normed_t_ref[...], gate_grad).astype(bf16)
+    g_outer_ref[...] = nn(cot_t_ref[...], active).astype(bf16)
     out_part = nt(active, outer_ref[...])
     back_part = nt(gate_grad, gate_ref[...]) + nt(up_grad, up_ref[...])
 
@@ -1255,12 +1523,13 @@
         out_ref[...] = out_acc[...].astype(bf16)
         back_ref[...] = back_acc[...].astype(bf16)
         if summed:
-            for t in range(count, count + 4):
+            for t in range(pl.num_programs(0), count + 4):
                 tick(t)
             pieces.finish(count)
 
 
 FFN_STEP = 256
+SUMMED_STEPS = 9
 
 
 def feed_forward(normed, normed_t, cotangent, weights, hidden, step=FFN_STEP):
@@ -1268,49 +1537,53 @@
     steps = hidden // step
     seq_count = lax.axis_size("seq")
     share = width // seq_count
-    summed = steps if seq_count == 16 and share % 16 == 0 else 0
+    summed = SUMMED_STEPS if seq_count == 16 and share % 16 == 0 else 0
+    assert not summed or summed < steps <= 2 * summed
     whole = lambda shape: pl.BlockSpec(shape, lambda j: (0, 0))
+    held = lambda shape: pl.BlockSpec(shape, lambda j: (0, 0), pipeline_mode=pl.Buffered(1))
     column = lambda first: pl.BlockSpec((width, step), lambda j: (0, first + j))
     scratch = [pltpu.VMEM((rows, width), f32)] * 2
+    out_specs = [
+        column(0),
+        column(0),
+        column(0),
+        whole((rows, width)),
+        whole((rows, width)),
+    ]
+    out_shape = [
+        jax.ShapeDtypeStruct((width, hidden), bf16),
+        jax.ShapeDtypeStruct((width, hidden), bf16),
+        jax.ShapeDtypeStruct((width, hidden - summed * step), bf16),
+        jax.ShapeDtypeStruct((rows, width), bf16),
+        jax.ShapeDtypeStruct((rows, width), bf16),
+    ]
+    params = kernel_params(1, 56)
     if summed:
         scratch += [pltpu.VMEM((SLOTS, 2, 2, 2, 2, share, step), bf16)]
         scratch += Pieces.scratch(share, step)
-        up_spec = pl.BlockSpec(memory_space=pl.ANY)
-        up_shape = jax.ShapeDtypeStruct((share, hidden), f32)
+        out_specs[2] = pl.BlockSpec((width, step), lambda j: (0, j // summed * (j - summed)))
+        out_specs.append(pl.BlockSpec(memory_space=pl.ANY))
+        out_shape.append(jax.ShapeDtypeStruct((share, summed * step), f32))
         params = pltpu.CompilerParams(
             dimension_semantics=("arbitrary",),
             collective_id=3,
             has_side_effects=True,
-            vmem_limit_bytes=58 * 1024 * 1024,
-        )
-    else:
-        up_spec = column(0)
-        up_shape = jax.ShapeDtypeStruct((width, hidden), bf16)
-        params = kernel_params(1, 56)
+            vmem_limit_bytes=60 * 1024 * 1024,
+        )
     outs = pl.pallas_call(
         functools.partial(ffn_kernel, summed=summed),
         grid=(steps,),
         in_specs=[
-            whole((rows, width)),
-            whole((width, rows)),
-            whole((rows, width)),
-            whole((width, rows)),
+            held((rows, width)),
+            held((width, rows)),
+            held((rows, width)),
+            held((width, rows)),
             column(0),
             column(steps),
             column(2 * steps),
         ],
-        out_specs=[
-            pl.BlockSpec((width, 2 * step), lambda j: (0, j)),
-            up_spec,
-            whole((rows, width)),
-            whole((rows, width)),
-        ],
-        out_shape=[
-            jax.ShapeDtypeStruct((width, 2 * hidden), bf16),
-            up_shape,
-            jax.ShapeDtypeStruct((rows, width), bf16),
-            jax.ShapeDtypeStruct((rows, width), bf16),
-        ],
+        out_specs=out_specs,
+        out_shape=out_shape,
         scratch_shapes=scratch,
         compiler_params=params,
         cost_estimate=pl.CostEstimate(
@@ -1320,10 +1593,7 @@
         ),
         name="feed_forward",
     )(normed, normed_t, cotangent, cotangent.T, weights, weights, weights)
-    if summed:
-        return outs
-    up_total = lax.psum_scatter(outs[1].astype(f32), "seq", scatter_dimension=0, tiled=True)
-    return outs[0], up_total, outs[2], outs[3]
+    return outs
 
 
 def qkv_back_kernel(
@@ -1429,6 +1699,407 @@
     return jnp.concatenate([jnp.cos(angles), jnp.sin(angles)], axis=-1)
 
 
+def norm_back_unit(m, index, block_rows, grad_of, up_ref, hidden_ref, two_ref, later_ref, sums_ref, emit):
+    width = hidden_ref.shape[1]
+    for start in range(0, block_rows, HALF):
+        span = slice(m * block_rows + start, m * block_rows + start + HALF)
+        later = later_ref[span, :] > 0.5
+        lanes = slice((index + 1) * width, (index + 2) * width)
+        factor = jnp.where(later, two_ref[m, 1:2, lanes], two_ref[m, 0:1, lanes])
+        total, sums = norm_back_tile(
+            grad_of(span),
+            up_ref[span, :].astype(f32),
+            hidden_ref[span, :].astype(f32),
+            (~later, later),
+            factor,
+        )
+        for item in range(2):
+            for kind in range(2):
+                at = slice(kind * width, (kind + 1) * width)
+                before = sums_ref[m, item : item + 1, at] if start else 0.0
+                sums_ref[m, item : item + 1, at] = sums[item][kind] + before
+        emit(span, start, total)
+
+
+def cross_stage_kernel(
+    back_ref, up_ref, hidden_ref, two_ref, later_ref, weight_ref, q_ref, k_ref, v_ref, bias_ref,
+    log_ref, *refs, spans, step, micro, ready,
+):
+    sources, refs = refs[: len(spans)], refs[len(spans) :]
+    (
+        grad_ref, sums_ref, low_t_ref, dq_ref, dk_ref, dv_ref, next_ref, got_next_ref, out_ref,
+        own_sem, got_ref, mixed_ref, acc_ref, out_w_ref, query_w_ref, weight_sem,
+        swap_send, swap_recv, next_send, next_recv,
+    ) = refs[:20]
+    refs = refs[20:]
+    me = lax.axis_index("seq")
+    mine = lax.axis_index("tensor")
+    digits = seq_digits(me)
+    partners = greet_all(me, mine, digits)
+    rows = back_ref.shape[0]
+    block_rows = rows // micro
+    pairs = q_ref.shape[1] // 128
+    text = k_ref.shape[0] // micro
+
+    def over_tensor(m):
+        span = pl.ds(m * block_rows, block_rows)
+        return to_tensor(
+            mine, back_ref.at[span], got_ref.at[span], swap_send.at[m], swap_recv.at[m]
+        )
+
+    def over_next(m):
+        span = pl.ds(m * block_rows, block_rows)
+        return to_tensor(
+            mine, next_ref.at[span], got_next_ref.at[span], next_send.at[m], next_recv.at[m]
+        )
+
+    def norm_unit(m):
+        over_tensor(m).wait_recv()
+        if m == 0:
+            for load in loads:
+                load.wait()
+
+        def emit(span, start, total):
+            grad_ref[span, :] = total
+            rounded = total.astype(bf16)
+            low_t_ref[:, span] = rounded.T
+            mixed_ref[start : start + HALF, :] = nn(rounded, out_w_ref[...]).astype(bf16)
+
+        norm_back_unit(
+            m, 4, block_rows,
+            lambda span: back_ref[span, :].astype(f32) + got_ref[span, :].astype(f32),
+            up_ref, hidden_ref, two_ref, later_ref, sums_ref, emit,
+        )
+
+    def pair_unit(m, pair):
+        lanes = pl.ds(pl.multiple_of(pair * 128, 128), 128)
+        keys = slice(m * text, (m + 1) * text)
+        key_total = value_total = None
+        for start in range(0, block_rows, HALF):
+            span = slice(m * block_rows + start, m * block_rows + start + HALF)
+            query_grad, key_grad, value_grad = attend_rows_back(
+                q_ref[span, lanes],
+                k_ref[keys, lanes],
+                v_ref[keys, lanes],
+                bias_ref[span, :],
+                get_logs(log_ref, span, pair),
+                mixed_ref[start : start + HALF, lanes],
+            )
+            dq_ref[span, lanes] = query_grad.astype(bf16)
+            key_total = key_grad if start == 0 else key_total + key_grad
+            value_total = value_grad if start == 0 else value_total + value_grad
+        dk_ref[keys, lanes] = key_total.astype(bf16)
+        dv_ref[keys, lanes] = value_total.astype(bf16)
+        own = slice(m * block_rows, (m + 1) * block_rows)
+        product = nt(dq_ref[own, lanes], query_w_ref[:, lanes])
+        acc_ref[...] = product + jnp.where(pair == 0, 0.0, acc_ref[...])
+
+    def close(m):
+        own = slice(m * block_rows, (m + 1) * block_rows)
+        next_ref[own, :] = acc_ref[...].astype(bf16)
+        if m < micro - 1:
+            over_next(m).start()
+
+    local = q_ref.shape[1]
+    loads = [
+        pltpu.make_async_copy(
+            weight_ref.at[:, k * local : (k + 1) * local], target, weight_sem.at[i]
+        )
+        for i, (k, target) in enumerate(((5, out_w_ref), (4, query_w_ref)))
+    ]
+    for load in loads:
+        load.start()
+    acc_ref[...] = jnp.zeros_like(acc_ref)
+    pieces = Pieces(refs, out_ref, partners, digits, step)
+    work = []
+    spot = 0
+    for m in range(micro):
+        spot = max(spot, ready * (m + 1))
+        work.append((spot, spot + 1, lambda t, m=m: norm_unit(m)))
+        spot += 1
+        begin = spot
+
+        def pair_units(t, m=m, begin=begin):
+            for k in range(2):
+                pair_unit(m, 2 * (t - begin) + k)
+
+        work.append((begin, begin + pairs // 2, pair_units))
+        spot += pairs // 2
+        work.append((spot - 1, spot, lambda t, m=m: close(m)))
+    for m in range(micro):
+        over_tensor(m).start()
+    pieces.run(sources, spans, own_sem, work, spot)
+    for m in range(micro):
+        over_tensor(m).wait_send()
+        if m < micro - 1:
+            over_next(m).wait()
+
+
+def cross_stage(
+    back, up, hidden, two, later, query, keys, values, bias, logs, weights, local, sources,
+    spans, micro, which=2, step=256,
+):
+    seq_count = lax.axis_size("seq")
+    rows, width = hidden.shape
+    share = width // seq_count
+    block_rows = rows // micro
+    any_space = pl.BlockSpec(memory_space=pl.ANY)
+    vmem = pl.BlockSpec(memory_space=pltpu.VMEM)
+    return pl.pallas_call(
+        functools.partial(
+            cross_stage_kernel, spans=spans, step=step, micro=micro, ready=4
+        ),
+        out_shape=[
+            jax.ShapeDtypeStruct((rows, width), f32),
+            jax.ShapeDtypeStruct((micro, 2, 2 * width), f32),
+            jax.ShapeDtypeStruct((width, rows), bf16),
+            jax.ShapeDtypeStruct((rows, local), bf16),
+            jax.ShapeDtypeStruct(keys.shape, bf16),
+            jax.ShapeDtypeStruct(keys.shape, bf16),
+            jax.ShapeDtypeStruct((rows, width), bf16),
+            jax.ShapeDtypeStruct((rows - block_rows, width), bf16),
+            jax.ShapeDtypeStruct((share, sum(span for _, span in spans)), f32),
+        ],
+        in_specs=[vmem] * 5 + [any_space] + [vmem] * 5 + [any_space] * len(spans),
+        out_specs=[vmem] * 7 + [any_space] * 2,
+        scratch_shapes=[
+            pltpu.SemaphoreType.DMA((SLOTS,)),
+            pltpu.VMEM((rows, width), bf16),
+            pltpu.VMEM((block_rows, local), bf16),
+            pltpu.VMEM((block_rows, width), f32),
+            pltpu.VMEM((width, local), bf16),
+            pltpu.VMEM((width, local), bf16),
+            pltpu.SemaphoreType.DMA((2,)),
+        ]
+        + [pltpu.SemaphoreType.DMA((micro,))] * 4
+        + Pieces.scratch(share, step),
+        compiler_params=pltpu.CompilerParams(
+            collective_id=which, has_side_effects=True, vmem_limit_bytes=56 * 1024 * 1024
+        ),
+        cost_estimate=pl.CostEstimate(
+            flops=8 * rows * width * local, bytes_accessed=40 * rows * width, transcendentals=0
+        ),
+        name="cross_stage",
+    )(
+        back, up, hidden, two, later, weights, query, keys, values, bias, logs,
+        *[source.reshape(2, 2, 2, 2, share, source.shape[1]) for source in sources],
+    )
+
+
+def self_stage_kernel(
+    back_ref, got_early_ref, up_ref, hidden_ref, two_ref, later_ref, weight_ref, qkv_ref, bias_ref,
+    log_ref, other_ref, *refs,
+    spans, step, micro, ready, seq_count,
+):
+    sources, refs = refs[: len(spans)], refs[len(spans) :]
+    (
+        grad_ref, sums_ref, low_t_ref, own_ref, from_low_ref, from_high_ref, got_other_ref, out_ref,
+        own_sem, got_ref, mixed_ref, to_low_ref, to_high_ref, out_w_ref, weight_sem, swap_sem,
+        halo_send, halo_recv,
+    ) = refs[:18]
+    refs = refs[18:]
+    me = lax.axis_index("seq")
+    mine = lax.axis_index("tensor")
+    digits = seq_digits(me)
+    has_low = me > 0
+    has_high = me < seq_count - 1
+    partners = greet_all(me, mine, digits, ((has_low, me - 1), (has_high, me + 1)))
+    rows = back_ref.shape[0]
+    block_rows = rows // micro
+    near_rows = block_rows + 2 * HALF
+    local = qkv_ref.shape[1] // 3
+    pairs = local // 128
+    last = micro - 1
+
+    def over_tensor():
+        return to_tensor(
+            mine,
+            back_ref.at[pl.ds(last * block_rows, block_rows)],
+            got_ref,
+            swap_sem.at[0],
+            swap_sem.at[1],
+        )
+
+    def over_other():
+        span = pl.ds(block_rows, rows - block_rows)
+        return to_tensor(
+            mine, other_ref.at[span], got_other_ref, swap_sem.at[2], swap_sem.at[3]
+        )
+
+    def to_low(m):
+        return send_to(
+            me - 1, to_low_ref.at[m], from_high_ref.at[m], halo_send.at[0, m], halo_recv.at[0, m]
+        )
+
+    def to_high(m):
+        return send_to(
+            me + 1, to_high_ref.at[m], from_low_ref.at[m], halo_send.at[1, m], halo_recv.at[1, m]
+        )
+
+    load = pltpu.make_async_copy(
+        weight_ref.at[:, 3 * local : 4 * local], out_w_ref, weight_sem
+    )
+    load.start()
+
+    def norm_unit(m):
+        if m == 0:
+            load.wait()
+        if m == last:
+            over_tensor().wait_recv()
+
+        def grad_of(span):
+            if m == last:
+                other = got_ref[span.start - last * block_rows : span.stop - last * block_rows, :]
+            else:
+                other = got_early_ref[span, :]
+            return back_ref[span, :].astype(f32) + other.astype(f32)
+
+        def emit(span, start, total):
+            grad_ref[span, :] = total
+            rounded = total.astype(bf16)
+            low_t_ref[:, span] = rounded.T
+            mixed_ref[start : start + HALF, :] = nn(rounded, out_w_ref[...]).astype(bf16)
+
+        norm_back_unit(
+            m, 2, block_rows, grad_of, up_ref, hidden_ref, two_ref, later_ref, sums_ref, emit
+        )
+
+    def pair_unit(m, pair):
+        def lanes(kind):
+            return pl.ds(pl.multiple_of(kind * local + pair * 128, 128), 128)
+
+        parts = block_rows // HALF
+        held = [[None] * (parts + 2), [None] * (parts + 2)]
+        at = lanes(0)
+        for part in range(parts):
+            span = slice(m * block_rows + part * HALF, m * block_rows + (part + 1) * HALF)
+            own_rows = slice(m * near_rows + (part + 1) * HALF, m * near_rows + (part + 2) * HALF)
+            near = slice(m * near_rows + part * HALF, m * near_rows + (part + 3) * HALF)
+            query_grad, key_grad, value_grad = attend_rows_back(
+                qkv_ref[own_rows, at],
+                qkv_ref[near, lanes(1)],
+                qkv_ref[near, lanes(2)],
+                bias_ref[span, :],
+                get_logs(log_ref, span, pair),
+                mixed_ref[part * HALF : (part + 1) * HALF, at],
+            )
+            own_ref[0, span, at] = query_grad
+            for kind, near_grad in enumerate((key_grad, value_grad)):
+                for third in range(3):
+                    piece = near_grad[third * HALF : (third + 1) * HALF]
+                    before = held[kind][part + third]
+                    held[kind][part + third] = piece if before is None else before + piece
+        for kind in range(2):
+            to_low_ref[m, kind, :, at] = held[kind][0].astype(bf16)
+            for part in range(parts):
+                span = slice(m * block_rows + part * HALF, m * block_rows + (part + 1) * HALF)
+                own_ref[1 + kind, span, at] = held[kind][part + 1]
+            to_high_ref[m, kind, :, at] = held[kind][parts + 1].astype(bf16)
+
+    def close(m):
+        pl.when(has_low)(lambda: to_low(m).start())
+        pl.when(has_high)(lambda: to_high(m).start())
+
+    pieces = Pieces(refs, out_ref, partners, digits, step)
+    work = []
+    spot = 1
+    for m in range(micro):
+        if m == last:
+            spot = max(spot, ready)
+        work.append((spot, spot + 1, lambda t, m=m: norm_unit(m)))
+        spot += 1
+        begin = spot
+
+        def pair_units(t, m=m, begin=begin):
+            for k in range(2):
+                pair_unit(m, 2 * (t - begin) + k)
+
+        work.append((begin, begin + pairs // 2, pair_units))
+        spot += pairs // 2
+        work.append((spot - 1, spot, lambda t, m=m: close(m)))
+    over_tensor().start()
+    over_other().start()
+
+    @pl.when(jnp.logical_not(has_low))
+    def _():
+        from_low_ref[...] = jnp.zeros_like(from_low_ref)
+
+    @pl.when(jnp.logical_not(has_high))
+    def _():
+        from_high_ref[...] = jnp.zeros_like(from_high_ref)
+
+    pieces.run(sources, spans, own_sem, work, spot)
+    over_tensor().wait_send()
+    over_other().wait()
+    for m in range(micro):
+
+        @pl.when(has_low)
+        def _(m=m):
+            to_low(m).wait_send()
+            to_high(m).wait_recv()
+
+        @pl.when(has_high)
+        def _(m=m):
+            to_high(m).wait_send()
+            to_low(m).wait_recv()
+
+
+def self_stage(
+    back, got_early, up, hidden, two, later, qkv, bias, logs, weights, local, other, sources,
+    spans, micro, which=4, step=256,
+):
+    seq_count = lax.axis_size("seq")
+    rows, width = hidden.shape
+    share = width // seq_count
+    block_rows = rows // micro
+    any_space = pl.BlockSpec(memory_space=pl.ANY)
+    vmem = pl.BlockSpec(memory_space=pltpu.VMEM)
+    edge = (micro, 2, HALF, local)
+    return pl.pallas_call(
+        functools.partial(
+            self_stage_kernel, spans=spans, step=step, micro=micro, ready=4, seq_count=seq_count
+        ),
+        out_shape=[
+            jax.ShapeDtypeStruct((rows, width), f32),
+            jax.ShapeDtypeStruct((micro, 2, 2 * width), f32),
+            jax.ShapeDtypeStruct((width, rows), bf16),
+            jax.ShapeDtypeStruct((3, rows, local), f32),
+            jax.ShapeDtypeStruct(edge, bf16),
+            jax.ShapeDtypeStruct(edge, bf16),
+            jax.ShapeDtypeStruct((rows - block_rows, width), bf16),
+            jax.ShapeDtypeStruct((share, sum(span for _, span in spans)), f32),
+        ],
+        in_specs=[vmem] * 6 + [any_space] + [vmem] * 3 + [any_space] * (1 + len(spans)),
+        out_specs=[vmem] * 6 + [any_space] * 2,
+        scratch_shapes=[
+            pltpu.SemaphoreType.DMA((SLOTS,)),
+            pltpu.VMEM((block_rows, width), bf16),
+            pltpu.VMEM((block_rows, local), bf16),
+            pltpu.VMEM(edge, bf16),
+            pltpu.VMEM(edge, bf16),
+            pltpu.VMEM((width, local), bf16),
+            pltpu.SemaphoreType.DMA,
+            pltpu.SemaphoreType.DMA((4,)),
+            pltpu.SemaphoreType.DMA((2, micro)),
+            pltpu.SemaphoreType.DMA((2, micro)),
+        ]
+        + Pieces.scratch(share, step),
+        compiler_params=pltpu.CompilerParams(
+            collective_id=which, has_side_effects=True, vmem_limit_bytes=58 * 1024 * 1024
+        ),
+        cost_estimate=pl.CostEstimate(
+            flops=8 * rows * width * local, bytes_accessed=40 * rows * width, transcendentals=0
+        ),
+        name="self_stage",
+    )(
+        back, got_early, up, hidden, two, later, weights, qkv, bias, logs, other,
+        *[source.reshape(2, 2, 2, 2, share, source.shape[1]) for source in sources],
+    )
+
+
+EARLY_COLUMNS = 1792
+
+
 def on_device(
     latents,
     context,
@@ -1530,71 +2201,100 @@
     hidden_two, normed_three, normed_three_t = norm_forward(
         hidden_one, part_two, got_two, two, later, 4, micro
     )
-    g_early, up_total, out_part, back_three = feed_forward(
+    g_outer, g_gate, g_up, out_part, back_three, *up_early = feed_forward(
         normed_three, normed_three_t, cotangent, ffn_all, hidden
     )
-
-    got_three = swap(back_three)
-    early = early_sum(g_early).reshape(-1, hidden // FFN_STEP, 2, FFN_STEP)
-    outer_total = early[:, :, 0].reshape(-1, hidden)
-    gate_total = early[:, :, 1].reshape(-1, hidden)
-    hidden_two_grad, pieces_three, two_low_t, mixed_two_grad = norm_back(
-        cotangent, back_three, got_three, hidden_two, two, later, 4, micro, attn_all, 5, local
-    )
-    out_part, hidden_two_grad = lax.optimization_barrier((out_part, hidden_two_grad))
-    out_got = swap(out_part)
-    query_two_low, text_key_low, text_value_low, back_two = cross_attention_back(
-        query_two, text_keys, text_values, cross_bias, mixed_two_grad, logs_two,
-        attn_all, 4 * column, micro, block_rows,
-    )
-    got_back_two = swap(back_two)
+    outer_total = early_sum(g_outer)
+
     share = text_width // seq_count
-    pair_grad = jnp.concatenate(
-        [
-            tn(near_context, text_key_low).astype(bf16).reshape(seq_count, share, local),
-            tn(near_context, text_value_low).astype(bf16).reshape(seq_count, share, local),
-        ],
-        axis=1,
-    ).reshape(2 * text_width, local)
-    g_cross_out = nn(two_low_t, mixed_two).astype(bf16)
-    g_cross_query = nn(normed_two_t, query_two_low).astype(bf16)
-    hidden_one_grad, pieces_two, one_low_t, mixed_one_grad = norm_back(
-        hidden_two_grad, back_two, got_back_two, hidden_one, two, later, 2, micro,
-        attn_all, 3, local,
-    )
-    own_grads, to_low, to_high = self_attention_back(
-        qkv, self_bias, mixed_one_grad, logs_one, micro, block_rows
-    )
-    from_high = lax.ppermute(to_low, "seq", behind)
-    from_low = lax.ppermute(to_high, "seq", ahead)
-    g_self_out = nn(one_low_t, mixed_one).astype(bf16)
-    g_qkv, back_one = qkv_back(
-        own_grads, from_low, from_high, normed_one_t, attn_all, near_table, micro, block_rows
-    )
-    got_back_one = swap(back_one)
-    grad_cross_out, grad_cross_query, grad_cross_kv, grad_self_out = scatter_sums(
-        [g_cross_out, g_cross_query, pair_grad, g_self_out], 0
-    )
+    fused = (
+        seq_count == 16 and lax.axis_size("tensor") == 2 and (model_width // seq_count) % 16 == 0
+    )
+
+    def cross_grads(two_low_t, query_two_low, text_key_low, text_value_low):
+        pair_grad = jnp.concatenate(
+            [
+                tn(near_context, text_key_low).astype(bf16).reshape(seq_count, share, local),
+                tn(near_context, text_value_low).astype(bf16).reshape(seq_count, share, local),
+            ],
+            axis=1,
+        ).reshape(2 * text_width, local)
+        return [
+            nn(two_low_t, mixed_two).astype(bf16),
+            nn(normed_two_t, query_two_low).astype(bf16),
+            pair_grad,
+        ]
+
+    if fused:
+        (
+            hidden_two_grad, sums_three, two_low_t, query_two_low, text_key_low, text_value_low,
+            back_two, got_early, totals_a,
+        ) = cross_stage(
+            back_three, cotangent, hidden_two, two, later, query_two, text_keys, text_values,
+            cross_bias, logs_two, attn_all, local, [g_gate], ((0, EARLY_COLUMNS),), micro,
+        )
+        (
+            hidden_one_grad, sums_two, one_low_t, own_grads, from_low, from_high, got_last,
+            totals_b,
+        ) = self_stage(
+            back_two, got_early, hidden_two_grad, hidden_one, two, later, qkv, self_bias, logs_one,
+            attn_all, local, out_part, [g_gate], ((EARLY_COLUMNS, hidden - EARLY_COLUMNS),), micro,
+        )
+        crossed = cross_grads(two_low_t, query_two_low, text_key_low, text_value_low)
+        g_self_out = nn(one_low_t, mixed_one).astype(bf16)
+        sums = jnp.concatenate([sums_two, sums_three], axis=2)
+        late = g_up.shape[1]
+        spans = ((0, late),) + ((0, local),) * 4
+        sources = [g_up] + crossed + [g_self_out]
+        totals_c, latent_grad, mod_grad, bias_sum, got_first = finish_stage(
+            own_grads, from_low, from_high, normed_one_t, attn_all, near_table, hidden_one_grad,
+            latent, two, later, sums, lengths, own_features, out_part,
+            sources, spans, micro,
+        )
+        totals = [totals_c[:, late + k * local : late + (k + 1) * local] for k in range(4)]
+        grad_cross_out, grad_cross_query, grad_cross_kv, grad_self_out = totals
+        qkv_total = totals_c[:, late + 4 * local :]
+        gate_total = jnp.concatenate([totals_a, totals_b], axis=1)
+        up_total = jnp.concatenate([up_early[0], totals_c[:, :late]], axis=1)
+        out_got = jnp.concatenate([got_first, got_last], axis=0)
+    else:
+        got_three = swap(back_three)
+        gate_total = early_sum(g_gate)
+        up_total = early_sum(g_up)
+        hidden_two_grad, sums_three, two_low_t, mixed_two_grad = norm_back(
+            cotangent, back_three, got_three, hidden_two, two, later, 4, micro, attn_all, 5, local
+        )
+        query_two_low, text_key_low, text_value_low, back_two = cross_attention_back(
+            query_two, text_keys, text_values, cross_bias, mixed_two_grad, logs_two,
+            attn_all, 4 * column, micro, block_rows,
+        )
+        got_back_two = swap(back_two)
+        hidden_one_grad, sums_two, one_low_t, mixed_one_grad = norm_back(
+            hidden_two_grad, back_two, got_back_two, hidden_one, two, later, 2, micro,
+            attn_all, 3, local,
+        )
+        own_grads, to_low, to_high = self_attention_back(
+            qkv, self_bias, mixed_one_grad, logs_one, micro, block_rows
+        )
+        from_high = lax.ppermute(to_low, "seq", behind)
+        from_low = lax.ppermute(to_high, "seq", ahead)
+        g_self_out = nn(one_low_t, mixed_one).astype(bf16)
+        g_qkv, back_one = qkv_back(
+            own_grads, from_low, from_high, normed_one_t, attn_all, near_table, micro, block_rows
+        )
+        crossed = cross_grads(two_low_t, query_two_low, text_key_low, text_value_low)
+        sums = jnp.concatenate(
+            [piece.reshape(micro, 2, 2 * model_width) for piece in (sums_two, sums_three)], axis=2
+        )
+        totals, latent_grad, mod_grad, bias_sum, out_got = finish_apart(
+            crossed + [g_self_out, g_qkv], back_one, hidden_one_grad, latent, two, later, sums,
+            lengths, own_features, out_part,
+        )
+        grad_cross_out, grad_cross_query, grad_cross_kv, grad_self_out, qkv_total = totals
     block_out = (hidden_two + (out_part.astype(f32) + out_got.astype(f32))).astype(bf16)
-    got_back_one, grad_self_out = lax.optimization_barrier((got_back_one, grad_self_out))
-    latent_grad, pieces_one = norm_back(
-        hidden_one_grad, back_one, got_back_one, latent, two, later, 0, micro
-    )
-
-    pieces = jnp.concatenate([pieces_one, pieces_two, pieces_three], axis=2)
-    spots = (base_item[:, None] + jnp.arange(2)[None, :])[:, :, None] == catalog[None, None, :]
-    item_grad = jnp.concatenate(
-        [
-            jnp.sum(
-                jnp.where(spots[m][:, :, None, None], pieces[m][:, None], 0.0), axis=0
-            )
-            for m in range(micro)
-        ]
-    ).reshape(micro * item_count, 6 * model_width)
-    qkv_total, item_total = scatter_sums([g_qkv], 2, item_grad)
-    mod_grad = jnp.dot(own_features.T, item_total, precision=highest).reshape(mod_weight.shape)
+    mod_grad = mod_grad.reshape(mod_weight.shape)
     bias_grad = lax.dynamic_slice_in_dim(
-        jnp.sum(item_total, axis=0).reshape(6, model_width), me * bias_share, bias_share, 1
+        bias_sum.reshape(6, model_width), me * bias_share, bias_share, 1
     )
 
     grad_qkv = jnp.stack([qkv_total[:, i * local : (i + 1) * local] for i in range(3)])

time: 779 us -> 717 us (0.920)
  waiting for transfers between devices: 125 us -> 51.9 us
  Pallas kernels: 533 us -> 556 us
  local copies, waits for them, and re-layouts: 67.8 us -> 53.2 us
    ppermute x6 -> x2, waiting for transfers between devices: 124 us -> 51.9 us  [swap(): lax.ppermute(part, 'tensor', [(i, (i + 1) % count) for i in range(count)])]
    pallas_call x8 -> x3, Pallas kernels: 248 us -> 285 us  [the longest x1 134 us: finish_stage(): pl.pallas_call(functools.partial(finish_kernel, spans=spans, step=step, m...]
    pallas_call x1, Pallas kernels: 124 us -> 113 us  [gather_and_prepare(): pl.pallas_call(functools.partial(gather_kernel, pieces=pieces, step=step,...]
    unnamed x159 -> x122, local copies, waits for them, and re-layouts: 41.4 us -> 35.2 us
  transfers between devices with their start and end apart: 10 -> 4, of which waited for: 4 -> 2; matrix products, arithmetic and copies ran while one was open for 3% -> 5% of each run, Pallas kernels for 41% -> 50%
where the time goes in v4:
time: 717 us; the launch traced here: 710 us
  Pallas kernels  556 us (78%)
  local copies, waits for them, and re-layouts  53.2 us (7%)
  waiting for transfers between devices  51.9 us (7%)
  between operations  16.2 us (2%)
  matrix products  15.2 us (2%)
  other arithmetic  13.2 us (2%)
    pallas_call x1, Pallas kernels, finish_stage(): pl.pallas_call(functools.partial(finish_kernel, spans=spans, step=step, m...  134 us
    pallas_call x1, Pallas kernels, gather_and_prepare(): pl.pallas_call(functools.partial(gather_kernel, pieces=pieces, step=step,...  113 us
    pallas_call x1, Pallas kernels, feed_forward(): pl.pallas_call(functools.partial(ffn_kernel, summed=summed), grid=(steps,...  88.7 us
    pallas_call x1, Pallas kernels, cross_stage(): pl.pallas_call(functools.partial(cross_stage_kernel, spans=spans, step=st...  87.7 us
    pallas_call x1, Pallas kernels, self_stage(): pl.pallas_call(functools.partial(self_stage_kernel, spans=spans, step=ste...  62.8 us
    ppermute x2, waiting for transfers between devices, swap(): lax.ppermute(part, 'tensor', [(i, (i + 1) % count) for i in range(count)])  51.9 us
    unnamed x122, local copies, waits for them, and re-layouts  35.2 us
    pallas_call x1, Pallas kernels, self_attention(): pl.pallas_call(self_kernel, grid=(micro, pairs), in_specs=self_specs(bloc...  27.2 us
  transfers between devices with their start and end apart: 4, of which 2 were waited for; matrix products, arithmetic and copies ran while one was open for 5% of the time, Pallas kernels for 50%

profile of v4, /device:TPU:0, one launch (start us, length us, event | category | flops | bytes accessed | tf_op | source)
XLA Modules:
  0.0 709.6 jit_solution(17464164615515229622)
XLA Ops:
  21.2 113.3 %gather_and_prepare.1 = (bf16[2,2,2,2,96,5376]{5,4,3,2,1,0:T(8,128)(2,1)}, bf16[1024,1536]{1,0:T(8,128)(2,1)}, bf16[1536,512]{1,0:T(8,128)(2,1)S(1)}, f32[2,2,92...) custom-call(bf16[96,5376]{1,0:T(8,128)(2,1)S(1)} %copy-done.19, ...), custom_call_target="tpu_custom_call" | custom-call | bytes 165150720 | tf_op jit(solution)/shard_map/gather_and_prepare/pallas_call | solution.py:463
  135.9 2.3 copy-done.17
  138.2 1.9 copy-done.26
  140.1 14.3 %qkv_projection.1.q_ref.k_ref.v_ref.qkv_ref = bf16[1024,2304]{1,0:T(8,128)(2,1)S(1)} custom-call(bf16[1024,1536]{1,0:T(8,128)(2,1)S(1)} %copy-done.26, bf16[1536,5376]{1,0:T(8,128)(2,1)} %bitcast.78, f32[3,1024,128]{2,1,0:T(8,128)S(1)} %copy-done.17), custom_call_target="tpu_custom_call" | custom-call | flops 7247757312 | bytes 14942208 | tf_op jit(solution)/shard_map/qkv_projection/pallas_call | solution.py:978
  154.5 27.2 %self_attention.1 = (bf16[512,768]{1,0:T(8,128)(2,1)S(1)}, f32[512,128]{1,0:T(8,128)S(1)}, bf16[512,1536]{1,0:T(8,128)(2,1)}) custom-call(bf16[1024,2304]{1,0:T(8,128)(2,1)S(1)} %qkv_projection.1.q_ref.k_ref.v_ref.qkv_ref, bf16[1024,2304]{1,0:T(8,128)(2,1)S(1)} %qkv_projection.1.q_ref.k_ref.v_ref.qkv_ref, ...), custom_call_target="tpu_custom_call" | custom-call | flops 2415919104 | bytes 7864320 | tf_op jit(solution)/shard_map/self_attention/pallas_call | solution.py:1250
  183.9 3.4 slice.81
  189.5 1.7 fusion.4
  193.5 23.0 %collective-permute-done.refs_2_ = bf16[512,1536]{1,0:T(8,128)(2,1)} collective-permute-done((bf16[512,1536]{1,0:T(8,128)(2,1)}, bf16[512,1536]{1,0:T(8,128)(2,1)}, u32[]{:S(2)}, u32[]{:S(2)}) %collective-permute-start) | collective-permute-done | bytes 1572896 | tf_op jit(solution)/shard_map/ppermute | solution.py:56
  216.6 5.8 norm_forward.2
  222.4 1.7 copy-done.3
  225.3 6.3 copy-done
  231.6 18.8 %cross_attention.1 = (bf16[512,768]{1,0:T(8,128)(2,1)S(1)}, f32[512,128]{1,0:T(8,128)S(1)}, bf16[512,1536]{1,0:T(8,128)(2,1)}) custom-call(bf16[512,768]{1,0:T(8,128)(2,1)S(1)} %get-tuple-element.70.q_ref, bf16[512,768]{1,0:T(8,128)(2,1)S(1)} %convolution_convert_fusion.6.k_ref, bf16[512,768]{1,0:T(8,128)(2,1)S(1)} %convolution_convert_fusion.5.v_ref, ...), custom_call_target="tpu_custom_call" | custom-call | flops 2013265920 | bytes 6291456 | tf_op jit(solution)/shard_map/cross_attention/pallas_call | solution.py:1361
  252.0 1.8 collective-permute-start.1
  253.8 2.7 copy.34.refs_3_
  256.5 28.8 %collective-permute-done.1.refs_2_ = bf16[512,1536]{1,0:T(8,128)(2,1)} collective-permute-done((bf16[512,1536]{1,0:T(8,128)(2,1)}, bf16[512,1536]{1,0:T(8,128)(2,1)}, u32[]{:S(2)}, u32[]{:S(2)}) %collective-permute-start.1) | collective-permute-done | bytes 1572896 | tf_op jit(solution)/shard_map/ppermute | solution.py:56
  285.3 3.4 norm_forward.3
  288.7 1.7 copy-done.5
  292.8 88.7 %feed_forward.1 = (bf16[1536,3072]{1,0:T(8,128)(2,1)}, bf16[1536,3072]{1,0:T(8,128)(2,1)}, bf16[1536,768]{1,0:T(8,128)(2,1)}, bf16[512,1536]{1,0:T(8,128)(2,1)},...) custom-call(bf16[512,1536]{1,0:T(8,128)(2,1)} %copy-done.29, bf16[1536,512]{1,0:T(8,128)(2,1)} %copy-done.30, ...), custom_call_target="tpu_custom_call" | custom-call | flops 43486543872 | bytes 56623104 | tf_op jit(solution)/shard_map/feed_forward/pallas_call | solution.py:1573
  382.9 87.7 %cross_stage.1 = (f32[512,1536]{1,0:T(8,128)}, f32[2,2,3072]{2,1,0:T(2,128)}, bf16[1536,512]{1,0:T(8,128)(2,1)}, bf16[512,768]{1,0:T(8,128)(2,1)}, bf16[512,768]...) custom-call(bf16[512,1536]{1,0:T(8,128)(2,1)} %get-tuple-element.79., ...), custom_call_target="tpu_custom_call" | custom-call | flops 4831838208 | bytes 31457280 | tf_op jit(solution)/shard_map/cross_stage/pallas_call | solution.py:1848
  470.7 2.0 convolution_convert_fusion.3
  473.5 1.7 pad_maximum_fusion.refs_3_
  476.0 2.8 convolution_convert_fusion.2
  478.8 2.8 convolution_convert_fusion.1
  481.6 62.8 %self_stage.1 = (f32[512,1536]{1,0:T(8,128)}, f32[2,2,3072]{2,1,0:T(2,128)}, bf16[1536,512]{1,0:T(8,128)(2,1)}, f32[3,512,768]{2,1,0:T(8,128)}, bf16[2,2,128,768...) custom-call(bf16[512,1536]{1,0:T(8,128)(2,1)} %get-tuple-element.88.back_re, ...), custom_call_target="tpu_custom_call" | custom-call | flops 4831838208 | bytes 31457280 | tf_op jit(solution)/shard_map/self_stage/pallas_call | solution.py:2058
  544.5 4.2 convolution_convert_fusion
  549.4 134.2 %finish_stage.1 = (f32[96,6144]{1,0:T(8,128)}, f32[512,1536]{1,0:T(8,128)}, f32[16,9216]{1,0:T(8,128)}, f32[1,9216]{1,0:T(1,128)}, bf16[256,1536]{1,0:T(8,128)(2,1)}) custom-call(bf16[2,2,2,2,96,768]{5,4,3,2,1,0:T(8,128)(2,1)} %bitcast.95, bf16[2,2,2,2,96,768]{5,4,3,2,1,0:T(8,128)(2,1)} %bitcast.96, bf16[2,2,2,2,96,768]{5,4,3,2,1,0:T(8,128)(2,1)} %bitcast.97, ...), custom_call_target="tpu_custom_call" | custom-call | flops 7247757312 | bytes 31457280 | tf_op jit(solution)/shard_map/finish_stage/pallas_call | solution.py:885
  683.6 1.9 copy.40
  688.2 2.7 fusion.2
  693.3 1.6 pad_maximum_fusion.1
  696.9 1.8 add_convert_fusion
  698.6 2.2 convert_bitcast_fusion
  700.8 1.7 copy.49
  (155 shorter events, 36.5 us)
Async XLA Ops:
  7.2 5.6 copy-start.53
  7.2 285.6 %all-gather.2.cloned.1.call-start = ((), (), s32[]{:S(2)}) async-start(), calls=%async_computation.1 | async-start | bytes 30081024 | tf_op jit(solution)/shard_map/all_gather | solution.py:2165
  11.0 3.5 copy-start.48
  13.1 4.5 copy-start.42
  135.6 18.8 %copy-start.13 = (f32[512,256]{1,0:T(8,128)}, f32[512,256]{1,0:T(8,128)S(1)}, u32[]{:S(2)}) copy-start(f32[512,256]{1,0:T(8,128)S(1)} %get-tuple-element.71.bias_ref) | copy-start | bytes 1572868
  135.6 18.8 %copy-start.15 = (bf16[1536,512]{1,0:T(8,128)(2,1)}, bf16[1536,512]{1,0:T(8,128)(2,1)S(1)}, u32[]{:S(2)}) copy-start(bf16[1536,512]{1,0:T(8,128)(2,1)S(1)} %get-tuple-element.97.refs_8_) | copy-start | bytes 4718596
  135.6 18.9 %copy-start.12 = (f32[512,384]{1,0:T(8,128)}, f32[512,384]{1,0:T(8,128)S(1)}, u32[]{:S(2)}) copy-start(f32[512,384]{1,0:T(8,128)S(1)} %get-tuple-element.65.bias_ref) | copy-start | bytes 2359300
  135.6 149.7 %copy-start.7 = (f32[512,1]{1,0:T(8,128)}, f32[512,1]{1,0:T(8,128)S(1)}, u32[]{:S(2)}) copy-start(f32[512,1]{1,0:T(8,128)S(1)} %get-tuple-element.68.refs_4_.later_ref.refs_14_) | copy-start | bytes 6148
  135.6 149.7 %copy-start.8 = (f32[2,2,9216]{2,1,0:T(2,128)}, f32[2,2,9216]{2,1,0:T(2,128)S(1)}, u32[]{:S(2)}) copy-start(f32[2,2,9216]{2,1,0:T(2,128)S(1)} %get-tuple-element.67.refs_3_.two_ref.refs_13_) | copy-start | bytes 442372
  135.6 563.0 %reduce-scatter.2.cloned.1.call-start = ((), (), s32[]{:S(2)}) async-start(), calls=%async_computation.2 | async-start | bytes 10027008 | tf_op jit(solution)/shard_map/reduce_scatter | solution.py:947
  154.4 27.2 %copy-start.1 = (bf16[1024,2304]{1,0:T(8,128)(2,1)}, bf16[1024,2304]{1,0:T(8,128)(2,1)S(1)}, u32[]{:S(2)}) copy-start(bf16[1024,2304]{1,0:T(8,128)(2,1)S(1)} %qkv_projection.1.q_ref.k_ref.v_ref.qkv_ref) | copy-start | bytes 14155780
  182.3 5.0 copy-start.31
  182.3 34.2 %collective-permute-start = (bf16[512,1536]{1,0:T(8,128)(2,1)}, bf16[512,1536]{1,0:T(8,128)(2,1)}, u32[]{:S(2)}, u32[]{:S(2)}) collective-permute-start(bf16[512,1536]{1,0:T(8,128)(2,1)} %get-tuple-element.66.refs_1_), channel_id=1, source_target_pairs={{0,1},{1,0},{2,3},{3,2},{4,5},{5,4},{6,7},{7,6},{8,9},{9,8},{10,11... | collective-permute-start | bytes 4718600 | tf_op jit(solution)/shard_map/ppermute | solution.py:56
  192.7 32.6 %copy-start.9 = (bf16[512,768]{1,0:T(8,128)(2,1)}, bf16[512,768]{1,0:T(8,128)(2,1)S(1)}, u32[]{:S(2)}) copy-start(bf16[512,768]{1,0:T(8,128)(2,1)S(1)} %convolution_convert_fusion.6.k_ref) | copy-start | bytes 2359300
  192.7 23.9 %copy-start.2 = (bf16[2,256,1536]{2,1,0:T(8,128)(2,1)S(1)}, bf16[2,256,1536]{2,1,0:T(8,128)(2,1)}, u32[]{:S(2)}) copy-start(bf16[2,256,1536]{2,1,0:T(8,128)(2,1)} %latent_ref.1) | copy-start | bytes 4718596
  193.5 31.8 %copy-start.10 = (bf16[512,768]{1,0:T(8,128)(2,1)}, bf16[512,768]{1,0:T(8,128)(2,1)S(1)}, u32[]{:S(2)}) copy-start(bf16[512,768]{1,0:T(8,128)(2,1)S(1)} %convolution_convert_fusion.5.v_ref) | copy-start | bytes 2359300
  216.6 8.7 %copy-start.14 = (f32[512,256]{1,0:T(8,128)S(1)}, f32[512,256]{1,0:T(8,128)}, u32[]{:S(2)}) copy-start(f32[512,256]{1,0:T(8,128)} %copy-done.13) | copy-start | bytes 1572868
  225.3 25.1 %copy-start.11 = (bf16[512,768]{1,0:T(8,128)(2,1)}, bf16[512,768]{1,0:T(8,128)(2,1)S(1)}, u32[]{:S(2)}) copy-start(bf16[512,768]{1,0:T(8,128)(2,1)S(1)} %get-tuple-element.70.q_ref) | copy-start | bytes 2359300
  225.3 6.3 copy-start
  252.0 33.4 %collective-permute-start.1 = (bf16[512,1536]{1,0:T(8,128)(2,1)}, bf16[512,1536]{1,0:T(8,128)(2,1)}, u32[]{:S(2)}, u32[]{:S(2)}) collective-permute-start(bf16[512,1536]{1,0:T(8,128)(2,1)} %get-tuple-element.72.refs_1_), channel_id=1, source_target_pairs={{0,1},{1,0},{2,3},{3,2},{4,5},{5,4},{6,7},{7,6},{8,9},{9,8},{10,11... | collective-permute-start | bytes 4718600 | tf_op jit(solution)/shard_map/ppermute | solution.py:56
  253.8 31.6 %copy-start.4 = (f32[512,1536]{1,0:T(8,128)S(1)}, f32[512,1536]{1,0:T(8,128)}, u32[]{:S(2)}) copy-start(f32[512,1536]{1,0:T(8,128)} %copy-done.3) | copy-start | bytes 9437188
  382.9 87.7 %copy-start.45 = (bf16[256,768]{1,0:T(8,128)(2,1)S(1)}, bf16[256,768]{1,0:T(8,128)(2,1)}, u32[]{:S(2)}) copy-start(bf16[256,768]{1,0:T(8,128)(2,1)} %copy-done.44) | copy-start | bytes 1179652
  382.9 87.8 %copy-start.47 = (bf16[256,768]{1,0:T(8,128)(2,1)S(1)}, bf16[256,768]{1,0:T(8,128)(2,1)}, u32[]{:S(2)}) copy-start(bf16[256,768]{1,0:T(8,128)(2,1)} %copy-done.46) | copy-start | bytes 1179652
  473.5 2.5 copy-start.54
  476.0 2.8 copy-start.28
  476.0 2.8 copy-start.55
  481.6 62.8 %copy-start.32 = (bf16[512,768]{1,0:T(8,128)(2,1)S(1)}, bf16[512,768]{1,0:T(8,128)(2,1)}, u32[]{:S(2)}) copy-start(bf16[512,768]{1,0:T(8,128)(2,1)} %copy-done.31) | copy-start | bytes 2359300
  544.4 4.2 copy-start.49
  544.5 4.2 copy-start.50
  693.2 3.1 copy-start.6
  693.2 3.6 copy-start.35
  696.9 4.0 copy-start.37
  (29 other events, 42.8 us)
Sparse Core Ops, SparseCore 0:
  135.8 144.5 all-gather.1
  381.7 122.3 reduce-scatter.1

commit v5 on v4

--- a/solution.py
+++ b/solution.py
@@ -513,7 +513,7 @@
 
 
 class Pieces:
-    def __init__(self, refs, out_ref, partners, digits, step, lag=2):
+    def __init__(self, refs, out_ref, partners, digits, step, lag=3):
         (
             self.own, self.got0, self.got1, self.got2, self.got3, self.staged,
             self.out_sem, self.send_sem, self.recv_sem,
@@ -719,7 +719,7 @@
     return total, sums
 
 
-def finish_kernel(*refs, spans, step, micro):
+def finish_kernel(*refs, spans, step, micro, loaded):
     refs = list(refs)
     sources = [refs.pop(0) for _ in spans]
     (
@@ -844,7 +844,9 @@
     work = []
     spot = 0
     columns = local // step
+    work.append((0, 1, lambda t: loaded()))
     work.append((0, 1, lambda t: load.wait()))
+    spot = 1
     for kind in range(3):
         work.append(
             (spot, spot + columns, lambda t, k=kind, s=spot: project_back(k, (t - s) * step))
@@ -882,8 +884,16 @@
     any_space = pl.BlockSpec(memory_space=pl.ANY)
     vmem = pl.BlockSpec(memory_space=pltpu.VMEM)
     smem = pl.BlockSpec(memory_space=pltpu.SMEM)
+    args = [
+        own, from_low, from_high, normed_t, weights, table,
+        upstream, latent, two, later, sums, lengths, own_features, other,
+    ]
+    places = (0, 1, 2, 3, 5, 6, 7, 8, 9, 10)
     return pl.pallas_call(
-        functools.partial(finish_kernel, spans=spans, step=step, micro=micro),
+        with_loads(
+            functools.partial(finish_kernel, spans=spans, step=step, micro=micro),
+            [len(sources) + place for place in places],
+        ),
         out_shape=[
             jax.ShapeDtypeStruct((share, sum(span for _, span in spans) + 3 * local), f32),
             jax.ShapeDtypeStruct((rows, width), f32),
@@ -891,11 +901,7 @@
             jax.ShapeDtypeStruct((1, 6 * width), f32),
             jax.ShapeDtypeStruct((rows // micro, width), bf16),
         ],
-        in_specs=[any_space] * len(sources)
-        + [vmem] * 4
-        + [any_space]
-        + [vmem] * 6
-        + [smem, vmem, any_space],
+        in_specs=[any_space] * (len(sources) + 11) + [smem, vmem, any_space],
         out_specs=[any_space, vmem, vmem, vmem, any_space],
         scratch_shapes=[
             pltpu.SemaphoreType.DMA((SLOTS,)),
@@ -910,7 +916,8 @@
             pltpu.SemaphoreType.DMA((2,)),
         ]
         + Pieces.scratch(share, step)
-        + small_scratch((micro * items, 6 * width)),
+        + small_scratch((micro * items, 6 * width))
+        + load_scratch([args[place] for place in places]),
         compiler_params=pltpu.CompilerParams(
             collective_id=which, has_side_effects=True, vmem_limit_bytes=60 * 1024 * 1024
         ),
@@ -920,8 +927,7 @@
         name="finish_stage",
     )(
         *[source.reshape(2, 2, 2, 2, share, source.shape[1]) for source in sources],
-        own, from_low, from_high, normed_t, weights, table,
-        upstream, latent, two, later, sums, lengths, own_features, other,
+        *args,
     )
 
 
@@ -1199,16 +1205,14 @@
     )(*args)
 
 
-def add_product(acc_ref, out_ref, product):
+def add_product(acc_ref, out_ref, left, right):
     pair = pl.program_id(1)
 
     @pl.when(pair == 0)
     def _():
-        acc_ref[...] = product
-
-    @pl.when(pair > 0)
-    def _():
-        acc_ref[...] += product
+        acc_ref[...] = jnp.zeros_like(acc_ref)
+
+    acc_ref[...] += nt(left, right)
 
     @pl.when(pair == pl.num_programs(1) - 1)
     def _():
@@ -1229,7 +1233,7 @@
         )
         out_ref[rows, :] = out.astype(bf16)
         put_logs(log_ref, rows, logs, pair)
-    add_product(acc_ref, sum_ref, nt(out_ref[...], weight_ref[...]))
+    add_product(acc_ref, sum_ref, out_ref[...], weight_ref[...])
 
 
 def self_specs(block_rows, pairs):
@@ -1342,7 +1346,7 @@
         out, logs = attend_rows(q_ref[rows, :], k_ref[...], v_ref[...], bias_ref[rows, :])
         out_ref[rows, :] = out.astype(bf16)
         put_logs(log_ref, rows, logs, pair)
-    add_product(acc_ref, sum_ref, nt(out_ref[...], weight_ref[...]))
+    add_product(acc_ref, sum_ref, out_ref[...], weight_ref[...])
 
 
 def cross_specs(block_rows, pairs):
@@ -1405,7 +1409,7 @@
         value_total = value_grad if part == 0 else value_total + value_grad
     dk_ref[...] = key_total.astype(bf16)
     dv_ref[...] = value_total.astype(bf16)
-    add_product(acc_ref, sum_ref, nt(dq_ref[...], weight_ref[...]))
+    add_product(acc_ref, sum_ref, dq_ref[...], weight_ref[...])
 
 
 def cross_attention_back(
@@ -1505,18 +1509,15 @@
         g_up_ref[...] = g_up
     g_gate_ref[...] = nn(normed_t_ref[...], gate_grad).astype(bf16)
     g_outer_ref[...] = nn(cot_t_ref[...], active).astype(bf16)
-    out_part = nt(active, outer_ref[...])
-    back_part = nt(gate_grad, gate_ref[...]) + nt(up_grad, up_ref[...])
 
     @pl.when(j == 0)
     def _():
-        out_acc[...] = out_part
-        back_acc[...] = back_part
-
-    @pl.when(j > 0)
-    def _():
-        out_acc[...] += out_part
-        back_acc[...] += back_part
+        out_acc[...] = jnp.zeros_like(out_acc)
+        back_acc[...] = jnp.zeros_like(back_acc)
+
+    out_acc[...] += nt(active, outer_ref[...])
+    back_acc[...] += nt(gate_grad, gate_ref[...])
+    back_acc[...] += nt(up_grad, up_ref[...])
 
     @pl.when(j == pl.num_programs(0) - 1)
     def _():
@@ -1699,6 +1700,36 @@
     return jnp.concatenate([jnp.cos(angles), jnp.sin(angles)], axis=-1)
 
 
+def with_loads(kernel, places):
+    def wrapped(*refs):
+        refs = list(refs)
+        sems = refs.pop()
+        targets = refs[-len(places) :]
+        refs = refs[: -len(places)]
+        copies = [
+            pltpu.make_async_copy(refs[place], target, sems.at[i])
+            for i, (place, target) in enumerate(zip(places, targets))
+        ]
+        for copy in copies:
+            copy.start()
+        for place, target in zip(places, targets):
+            refs[place] = target
+
+        def loaded():
+            for copy in copies:
+                copy.wait()
+
+        kernel(*refs, loaded=loaded)
+
+    return wrapped
+
+
+def load_scratch(arrays):
+    return [pltpu.VMEM(array.shape, array.dtype) for array in arrays] + [
+        pltpu.SemaphoreType.DMA((len(arrays),))
+    ]
+
+
 def norm_back_unit(m, index, block_rows, grad_of, up_ref, hidden_ref, two_ref, later_ref, sums_ref, emit):
     width = hidden_ref.shape[1]
     for start in range(0, block_rows, HALF):
@@ -1723,7 +1754,7 @@
 
 def cross_stage_kernel(
     back_ref, up_ref, hidden_ref, two_ref, later_ref, weight_ref, q_ref, k_ref, v_ref, bias_ref,
-    log_ref, *refs, spans, step, micro, ready,
+    log_ref, *refs, spans, step, micro, ready, loaded,
 ):
     sources, refs = refs[: len(spans)], refs[len(spans) :]
     (
@@ -1756,6 +1787,7 @@
     def norm_unit(m):
         over_tensor(m).wait_recv()
         if m == 0:
+            loaded()
             for load in loads:
                 load.wait()
 
@@ -1791,13 +1823,13 @@
         dk_ref[keys, lanes] = key_total.astype(bf16)
         dv_ref[keys, lanes] = value_total.astype(bf16)
         own = slice(m * block_rows, (m + 1) * block_rows)
-        product = nt(dq_ref[own, lanes], query_w_ref[:, lanes])
-        acc_ref[...] = product + jnp.where(pair == 0, 0.0, acc_ref[...])
+        acc_ref[...] += nt(dq_ref[own, lanes], query_w_ref[:, lanes])
 
     def close(m):
         own = slice(m * block_rows, (m + 1) * block_rows)
         next_ref[own, :] = acc_ref[...].astype(bf16)
         if m < micro - 1:
+            acc_ref[...] = jnp.zeros_like(acc_ref)
             over_next(m).start()
 
     local = q_ref.shape[1]
@@ -1845,9 +1877,12 @@
     block_rows = rows // micro
     any_space = pl.BlockSpec(memory_space=pl.ANY)
     vmem = pl.BlockSpec(memory_space=pltpu.VMEM)
+    args = [back, up, hidden, two, later, weights, query, keys, values, bias, logs]
+    places = (1, 2, 3, 4, 6, 7, 8, 9, 10)
     return pl.pallas_call(
-        functools.partial(
-            cross_stage_kernel, spans=spans, step=step, micro=micro, ready=4
+        with_loads(
+            functools.partial(cross_stage_kernel, spans=spans, step=step, micro=micro, ready=4),
+            places,
         ),
         out_shape=[
             jax.ShapeDtypeStruct((rows, width), f32),
@@ -1860,7 +1895,7 @@
             jax.ShapeDtypeStruct((rows - block_rows, width), bf16),
             jax.ShapeDtypeStruct((share, sum(span for _, span in spans)), f32),
         ],
-        in_specs=[vmem] * 5 + [any_space] + [vmem] * 5 + [any_space] * len(spans),
+        in_specs=[vmem] + [any_space] * (10 + len(spans)),
         out_specs=[vmem] * 7 + [any_space] * 2,
         scratch_shapes=[
             pltpu.SemaphoreType.DMA((SLOTS,)),
@@ -1872,7 +1907,8 @@
             pltpu.SemaphoreType.DMA((2,)),
         ]
         + [pltpu.SemaphoreType.DMA((micro,))] * 4
-        + Pieces.scratch(share, step),
+        + Pieces.scratch(share, step)
+        + load_scratch([args[place] for place in places]),
         compiler_params=pltpu.CompilerParams(
             collective_id=which, has_side_effects=True, vmem_limit_bytes=56 * 1024 * 1024
         ),
@@ -1881,7 +1917,7 @@
         ),
         name="cross_stage",
     )(
-        back, up, hidden, two, later, weights, query, keys, values, bias, logs,
+        *args,
         *[source.reshape(2, 2, 2, 2, share, source.shape[1]) for source in sources],
     )
 
@@ -1889,7 +1925,7 @@
 def self_stage_kernel(
     back_ref, got_early_ref, up_ref, hidden_ref, two_ref, later_ref, weight_ref, qkv_ref, bias_ref,
     log_ref, other_ref, *refs,
-    spans, step, micro, ready, seq_count,
+    spans, step, micro, ready, seq_count, loaded,
 ):
     sources, refs = refs[: len(spans)], refs[len(spans) :]
     (
@@ -1943,6 +1979,7 @@
 
     def norm_unit(m):
         if m == 0:
+            loaded()
             load.wait()
         if m == last:
             over_tensor().wait_recv()
@@ -2054,10 +2091,20 @@
     block_rows = rows // micro
     any_space = pl.BlockSpec(memory_space=pl.ANY)
     vmem = pl.BlockSpec(memory_space=pltpu.VMEM)
+    args = [back, got_early, up, hidden, two, later, weights, qkv, bias, logs, other]
+    places = (1, 2, 3, 4, 5, 7, 8, 9)
     edge = (micro, 2, HALF, local)
     return pl.pallas_call(
-        functools.partial(
-            self_stage_kernel, spans=spans, step=step, micro=micro, ready=4, seq_count=seq_count
+        with_loads(
+            functools.partial(
+                self_stage_kernel,
+                spans=spans,
+                step=step,
+                micro=micro,
+                ready=4,
+                seq_count=seq_count,
+            ),
+            places,
         ),
         out_shape=[
             jax.ShapeDtypeStruct((rows, width), f32),
@@ -2069,7 +2116,7 @@
             jax.ShapeDtypeStruct((rows - block_rows, width), bf16),
             jax.ShapeDtypeStruct((share, sum(span for _, span in spans)), f32),
         ],
-        in_specs=[vmem] * 6 + [any_space] + [vmem] * 3 + [any_space] * (1 + len(spans)),
+        in_specs=[vmem] + [any_space] * (10 + len(spans)),
         out_specs=[vmem] * 6 + [any_space] * 2,
         scratch_shapes=[
             pltpu.SemaphoreType.DMA((SLOTS,)),
@@ -2083,7 +2130,8 @@
             pltpu.SemaphoreType.DMA((2, micro)),
             pltpu.SemaphoreType.DMA((2, micro)),
         ]
-        + Pieces.scratch(share, step),
+        + Pieces.scratch(share, step)
+        + load_scratch([args[place] for place in places]),
         compiler_params=pltpu.CompilerParams(
             collective_id=which, has_side_effects=True, vmem_limit_bytes=58 * 1024 * 1024
         ),
@@ -2092,12 +2140,12 @@
         ),
         name="self_stage",
     )(
-        back, got_early, up, hidden, two, later, weights, qkv, bias, logs, other,
+        *args,
         *[source.reshape(2, 2, 2, 2, share, source.shape[1]) for source in sources],
     )
 
 
-EARLY_COLUMNS = 1792
+EARLY_COLUMNS = (1024, 1280)
 
 
 def on_device(
@@ -2226,26 +2274,31 @@
         ]
 
     if fused:
+        first, second = EARLY_COLUMNS
+        third = hidden - first - second
         (
             hidden_two_grad, sums_three, two_low_t, query_two_low, text_key_low, text_value_low,
             back_two, got_early, totals_a,
         ) = cross_stage(
             back_three, cotangent, hidden_two, two, later, query_two, text_keys, text_values,
-            cross_bias, logs_two, attn_all, local, [g_gate], ((0, EARLY_COLUMNS),), micro,
+            cross_bias, logs_two, attn_all, local, [g_gate], ((0, first),), micro,
         )
         (
             hidden_one_grad, sums_two, one_low_t, own_grads, from_low, from_high, got_last,
             totals_b,
         ) = self_stage(
             back_two, got_early, hidden_two_grad, hidden_one, two, later, qkv, self_bias, logs_one,
-            attn_all, local, out_part, [g_gate], ((EARLY_COLUMNS, hidden - EARLY_COLUMNS),), micro,
+            attn_all, local, out_part, [g_gate], ((first, second),), micro,
         )
         crossed = cross_grads(two_low_t, query_two_low, text_key_low, text_value_low)
         g_self_out = nn(one_low_t, mixed_one).astype(bf16)
         sums = jnp.concatenate([sums_two, sums_three], axis=2)
-        late = g_up.shape[1]
-        spans = ((0, late),) + ((0, local),) * 4
+        spans = ((0, g_up.shape[1]),) + ((0, local),) * 4
         sources = [g_up] + crossed + [g_self_out]
+        if third:
+            spans = ((first + second, third),) + spans
+            sources = [g_gate] + sources
+        late = third + g_up.shape[1]
         totals_c, latent_grad, mod_grad, bias_sum, got_first = finish_stage(
             own_grads, from_low, from_high, normed_one_t, attn_all, near_table, hidden_one_grad,
             latent, two, later, sums, lengths, own_features, out_part,
@@ -2254,8 +2307,8 @@
         totals = [totals_c[:, late + k * local : late + (k + 1) * local] for k in range(4)]
         grad_cross_out, grad_cross_query, grad_cross_kv, grad_self_out = totals
         qkv_total = totals_c[:, late + 4 * local :]
-        gate_total = jnp.concatenate([totals_a, totals_b], axis=1)
-        up_total = jnp.concatenate([up_early[0], totals_c[:, :late]], axis=1)
+        gate_total = jnp.concatenate([totals_a, totals_b, totals_c[:, :third]], axis=1)
+        up_total = jnp.concatenate([up_early[0], totals_c[:, third:late]], axis=1)
         out_got = jnp.concatenate([got_first, got_last], axis=0)
     else:
         got_three = swap(back_three)

time: 717 us -> 695 us (0.969)
  Pallas kernels: 556 us -> 534 us
    pallas_call x3, Pallas kernels: 285 us -> 267 us  [the longest x1 139 us: finish_stage(): pl.pallas_call(with_loads(functools.partial(finish_kernel, spans=spans, s...]
  transfers between devices with their start and end apart: 4 -> 4, of which waited for: 2 -> 2; matrix products, arithmetic and copies ran while one was open for 5% -> 6% of each run, Pallas kernels for 50% -> 49%
where the time goes in v5:
time: 695 us; the launch traced here: 688 us
  Pallas kernels  534 us (77%)
  local copies, waits for them, and re-layouts  53.1 us (8%)
  waiting for transfers between devices  52 us (7%)
  between operations  16.2 us (2%)
  matrix products  15.2 us (2%)
  other arithmetic  13.3 us (2%)
    pallas_call x1, Pallas kernels, finish_stage(): pl.pallas_call(with_loads(functools.partial(finish_kernel, spans=spans, s...  139 us
    pallas_call x1, Pallas kernels, gather_and_prepare(): pl.pallas_call(functools.partial(gather_kernel, pieces=pieces, step=step,...  113 us
    pallas_call x1, Pallas kernels, feed_forward(): pl.pallas_call(functools.partial(ffn_kernel, summed=summed), grid=(steps,...  84.8 us
    pallas_call x1, Pallas kernels, self_stage(): pl.pallas_call(with_loads(functools.partial(self_stage_kernel, spans=span...  68.5 us
    pallas_call x1, Pallas kernels, cross_stage(): pl.pallas_call(with_loads(functools.partial(cross_stage_kernel, spans=spa...  59.3 us
    ppermute x2, waiting for transfers between devices, swap(): lax.ppermute(part, 'tensor', [(i, (i + 1) % count) for i in range(count)])  52 us
    unnamed x122, local copies, waits for them, and re-layouts  35 us
    pallas_call x1, Pallas kernels, self_attention(): pl.pallas_call(self_kernel, grid=(micro, pairs), in_specs=self_specs(bloc...  27.5 us
  transfers between devices with their start and end apart: 4, of which 2 were waited for; matrix products, arithmetic and copies ran while one was open for 6% of the time, Pallas kernels for 49%

profile of v5, /device:TPU:0, one launch (start us, length us, event | category | flops | bytes accessed | tf_op | source)
XLA Modules:
  0.0 687.7 jit_solution(6602672654783688191)
XLA Ops:
  21.2 113.3 %gather_and_prepare.1 = (bf16[2,2,2,2,96,5376]{5,4,3,2,1,0:T(8,128)(2,1)}, bf16[1024,1536]{1,0:T(8,128)(2,1)}, bf16[1536,512]{1,0:T(8,128)(2,1)S(1)}, f32[2,2,92...) custom-call(bf16[96,5376]{1,0:T(8,128)(2,1)S(1)} %copy-done.19, ...), custom_call_target="tpu_custom_call" | custom-call | bytes 165150720 | tf_op jit(solution)/shard_map/gather_and_prepare/pallas_call | solution.py:463
  135.9 2.3 copy-done.17
  138.2 1.9 copy-done.26
  140.1 14.3 %qkv_projection.1.q_ref.k_ref.v_ref.refs_7_ = bf16[1024,2304]{1,0:T(8,128)(2,1)S(1)} custom-call(bf16[1024,1536]{1,0:T(8,128)(2,1)S(1)} %copy-done.26, bf16[1536,5376]{1,0:T(8,128)(2,1)} %bitcast.78, f32[3,1024,128]{2,1,0:T(8,128)S(1)} %copy-done.17), custom_call_target="tpu_custom_call" | custom-call | flops 7247757312 | bytes 14942208 | tf_op jit(solution)/shard_map/qkv_projection/pallas_call | solution.py:984
  154.5 27.5 %self_attention.1 = (bf16[512,768]{1,0:T(8,128)(2,1)S(1)}, f32[512,128]{1,0:T(8,128)S(1)}, bf16[512,1536]{1,0:T(8,128)(2,1)}) custom-call(bf16[1024,2304]{1,0:T(8,128)(2,1)S(1)} %qkv_projection.1.q_ref.k_ref.v_ref.refs_7_, bf16[1024,2304]{1,0:T(8,128)(2,1)S(1)} %qkv_projection.1.q_ref.k_ref.v_ref.refs_7_, ...), custom_call_target="tpu_custom_call" | custom-call | flops 2415919104 | bytes 7864320 | tf_op jit(solution)/shard_map/self_attention/pallas_call | solution.py:1254
  184.3 3.3 slice.84
  189.8 1.7 fusion.4
  193.8 23.1 %collective-permute-done.refs_2_ = bf16[512,1536]{1,0:T(8,128)(2,1)} collective-permute-done((bf16[512,1536]{1,0:T(8,128)(2,1)}, bf16[512,1536]{1,0:T(8,128)(2,1)}, u32[]{:S(2)}, u32[]{:S(2)}) %collective-permute-start) | collective-permute-done | bytes 1572896 | tf_op jit(solution)/shard_map/ppermute | solution.py:56
  217.0 5.9 norm_forward.2
  222.8 1.7 copy-done.3
  225.7 6.3 copy-done
  232.0 18.6 %cross_attention.1 = (bf16[512,768]{1,0:T(8,128)(2,1)S(1)}, f32[512,128]{1,0:T(8,128)S(1)}, bf16[512,1536]{1,0:T(8,128)(2,1)}) custom-call(bf16[512,768]{1,0:T(8,128)(2,1)S(1)} %get-tuple-element.70.q_ref.refs_6_, bf16[512,768]{1,0:T(8,128)(2,1)S(1)} %convolution_convert_fusion.6.k_ref.refs_7_, bf16[512,768]{1,0:T(8,128)(2,1)S(1)} %convolution_convert_fusion.5.v_ref.refs_8_, ...), custom_call_target="tpu_custom_call" | custom-call | flops 2013265920 | bytes 6291456 | tf_op jit(solution)/shard_map/cross_attention/pallas_call | solution.py:1365
  252.1 1.7 collective-permute-start.1
  253.9 2.7 copy.34.refs_3_
  256.6 28.8 %collective-permute-done.1.refs_2_ = bf16[512,1536]{1,0:T(8,128)(2,1)} collective-permute-done((bf16[512,1536]{1,0:T(8,128)(2,1)}, bf16[512,1536]{1,0:T(8,128)(2,1)}, u32[]{:S(2)}, u32[]{:S(2)}) %collective-permute-start.1) | collective-permute-done | bytes 1572896 | tf_op jit(solution)/shard_map/ppermute | solution.py:56
  285.5 3.4 norm_forward.3
  288.9 1.7 copy-done.5
  292.9 84.8 %feed_forward.1 = (bf16[1536,3072]{1,0:T(8,128)(2,1)}, bf16[1536,3072]{1,0:T(8,128)(2,1)}, bf16[1536,768]{1,0:T(8,128)(2,1)}, bf16[512,1536]{1,0:T(8,128)(2,1)},...) custom-call(bf16[512,1536]{1,0:T(8,128)(2,1)} %copy-done.29, bf16[1536,512]{1,0:T(8,128)(2,1)} %copy-done.30, ...), custom_call_target="tpu_custom_call" | custom-call | flops 43486543872 | bytes 56623104 | tf_op jit(solution)/shard_map/feed_forward/pallas_call | solution.py:1574
  379.1 59.3 %cross_stage.1 = (f32[512,1536]{1,0:T(8,128)}, f32[2,2,3072]{2,1,0:T(2,128)}, bf16[1536,512]{1,0:T(8,128)(2,1)}, bf16[512,768]{1,0:T(8,128)(2,1)}, bf16[512,768]...) custom-call(bf16[512,1536]{1,0:T(8,128)(2,1)} %get-tuple-element.80., ...), custom_call_target="tpu_custom_call" | custom-call | flops 4831838208 | bytes 31457280 | tf_op jit(solution)/shard_map/cross_stage/pallas_call | solution.py:1882
  438.4 2.0 convolution_convert_fusion.3
  441.3 1.7 pad_maximum_fusion.refs_4_
  443.8 2.8 convolution_convert_fusion.2
  446.6 2.8 convolution_convert_fusion.1
  449.4 68.5 %self_stage.1 = (f32[512,1536]{1,0:T(8,128)}, f32[2,2,3072]{2,1,0:T(2,128)}, bf16[1536,512]{1,0:T(8,128)(2,1)}, f32[3,512,768]{2,1,0:T(8,128)}, bf16[2,2,128,768...) custom-call(bf16[512,1536]{1,0:T(8,128)(2,1)} %get-tuple-element.88.refs_0_, ...), custom_call_target="tpu_custom_call" | custom-call | flops 4831838208 | bytes 31457280 | tf_op jit(solution)/shard_map/self_stage/pallas_call | solution.py:2097
  517.9 4.2 convolution_convert_fusion
  522.8 138.8 %finish_stage.1 = (f32[96,6912]{1,0:T(8,128)}, f32[512,1536]{1,0:T(8,128)}, f32[16,9216]{1,0:T(8,128)}, f32[1,9216]{1,0:T(1,128)}, bf16[256,1536]{1,0:T(8,128)(2,1)}) custom-call(bf16[2,2,2,2,96,3072]{5,4,3,2,1,0:T(8,128)(2,1)} %bitcast.90, bf16[2,2,2,2,96,768]{5,4,3,2,1,0:T(8,128)(2,1)} %bitcast.96, bf16[2,2,2,2,96,768]{5,4,3,2,1,0:T(8,128)(2,1)} %bitcast.97, ...), custom_call_target="tpu_custom_call" | custom-call | flops 7247757312 | bytes 31457280 | tf_op jit(solution)/shard_map/finish_stage/pallas_call | solution.py:892
  661.6 1.9 copy.40
  666.2 2.8 fusion.2
  671.4 1.6 pad_maximum_fusion.1
  675.0 1.8 add_convert_fusion
  676.8 2.2 convert_bitcast_fusion
  678.9 1.7 copy.49
  (155 shorter events, 36.3 us)
Async XLA Ops:
  7.2 5.6 copy-start.53
  7.2 285.7 %all-gather.2.cloned.1.call-start = ((), (), s32[]{:S(2)}) async-start(), calls=%async_computation.1 | async-start | bytes 30081024 | tf_op jit(solution)/shard_map/all_gather | solution.py:2213
  11.0 3.5 copy-start.48
  13.1 4.5 copy-start.41
  135.6 18.8 %copy-start.13 = (f32[512,256]{1,0:T(8,128)}, f32[512,256]{1,0:T(8,128)S(1)}, u32[]{:S(2)}) copy-start(f32[512,256]{1,0:T(8,128)S(1)} %get-tuple-element.71.bias_ref.refs_9_) | copy-start | bytes 1572868
  135.6 18.8 %copy-start.15 = (bf16[1536,512]{1,0:T(8,128)(2,1)}, bf16[1536,512]{1,0:T(8,128)(2,1)S(1)}, u32[]{:S(2)}) copy-start(bf16[1536,512]{1,0:T(8,128)(2,1)S(1)} %get-tuple-element.97.refs_9_) | copy-start | bytes 4718596
  135.6 18.9 %copy-start.12 = (f32[512,384]{1,0:T(8,128)}, f32[512,384]{1,0:T(8,128)S(1)}, u32[]{:S(2)}) copy-start(f32[512,384]{1,0:T(8,128)S(1)} %get-tuple-element.65.bias_ref.refs_8_) | copy-start | bytes 2359300
  135.6 149.8 %copy-start.7 = (f32[512,1]{1,0:T(8,128)}, f32[512,1]{1,0:T(8,128)S(1)}, u32[]{:S(2)}) copy-start(f32[512,1]{1,0:T(8,128)S(1)} %get-tuple-element.68.refs_4_.refs_5_.refs_15_) | copy-start | bytes 6148
  135.6 149.8 %copy-start.8 = (f32[2,2,9216]{2,1,0:T(2,128)}, f32[2,2,9216]{2,1,0:T(2,128)S(1)}, u32[]{:S(2)}) copy-start(f32[2,2,9216]{2,1,0:T(2,128)S(1)} %get-tuple-element.67.refs_3_.refs_4_.refs_14_) | copy-start | bytes 442372
  135.6 541.1 %reduce-scatter.2.cloned.1.call-start = ((), (), s32[]{:S(2)}) async-start(), calls=%async_computation.2 | async-start | bytes 10027008 | tf_op jit(solution)/shard_map/reduce_scatter | solution.py:953
  154.4 27.6 %copy-start.1 = (bf16[1024,2304]{1,0:T(8,128)(2,1)}, bf16[1024,2304]{1,0:T(8,128)(2,1)S(1)}, u32[]{:S(2)}) copy-start(bf16[1024,2304]{1,0:T(8,128)(2,1)S(1)} %qkv_projection.1.q_ref.k_ref.v_ref.refs_7_) | copy-start | bytes 14155780
  182.7 4.9 copy-start.31
  182.7 34.2 %collective-permute-start = (bf16[512,1536]{1,0:T(8,128)(2,1)}, bf16[512,1536]{1,0:T(8,128)(2,1)}, u32[]{:S(2)}, u32[]{:S(2)}) collective-permute-start(bf16[512,1536]{1,0:T(8,128)(2,1)} %get-tuple-element.66.refs_1_), channel_id=1, source_target_pairs={{0,1},{1,0},{2,3},{3,2},{4,5},{5,4},{6,7},{7,6},{8,9},{9,8},{10,11... | collective-permute-start | bytes 4718600 | tf_op jit(solution)/shard_map/ppermute | solution.py:56
  193.0 32.7 %copy-start.9 = (bf16[512,768]{1,0:T(8,128)(2,1)}, bf16[512,768]{1,0:T(8,128)(2,1)S(1)}, u32[]{:S(2)}) copy-start(bf16[512,768]{1,0:T(8,128)(2,1)S(1)} %convolution_convert_fusion.6.k_ref.refs_7_) | copy-start | bytes 2359300
  193.0 24.0 %copy-start.2 = (bf16[2,256,1536]{2,1,0:T(8,128)(2,1)S(1)}, bf16[2,256,1536]{2,1,0:T(8,128)(2,1)}, u32[]{:S(2)}) copy-start(bf16[2,256,1536]{2,1,0:T(8,128)(2,1)} %latent_ref.1) | copy-start | bytes 4718596
  193.8 31.9 %copy-start.10 = (bf16[512,768]{1,0:T(8,128)(2,1)}, bf16[512,768]{1,0:T(8,128)(2,1)S(1)}, u32[]{:S(2)}) copy-start(bf16[512,768]{1,0:T(8,128)(2,1)S(1)} %convolution_convert_fusion.5.v_ref.refs_8_) | copy-start | bytes 2359300
  217.0 8.7 %copy-start.14 = (f32[512,256]{1,0:T(8,128)S(1)}, f32[512,256]{1,0:T(8,128)}, u32[]{:S(2)}) copy-start(f32[512,256]{1,0:T(8,128)} %copy-done.13) | copy-start | bytes 1572868
  225.7 24.9 %copy-start.11 = (bf16[512,768]{1,0:T(8,128)(2,1)}, bf16[512,768]{1,0:T(8,128)(2,1)S(1)}, u32[]{:S(2)}) copy-start(bf16[512,768]{1,0:T(8,128)(2,1)S(1)} %get-tuple-element.70.q_ref.refs_6_) | copy-start | bytes 2359300
  225.7 6.3 copy-start
  252.1 33.3 %collective-permute-start.1 = (bf16[512,1536]{1,0:T(8,128)(2,1)}, bf16[512,1536]{1,0:T(8,128)(2,1)}, u32[]{:S(2)}, u32[]{:S(2)}) collective-permute-start(bf16[512,1536]{1,0:T(8,128)(2,1)} %get-tuple-element.72.refs_1_), channel_id=1, source_target_pairs={{0,1},{1,0},{2,3},{3,2},{4,5},{5,4},{6,7},{7,6},{8,9},{9,8},{10,11... | collective-permute-start | bytes 4718600 | tf_op jit(solution)/shard_map/ppermute | solution.py:56
  253.9 31.6 %copy-start.4 = (f32[512,1536]{1,0:T(8,128)S(1)}, f32[512,1536]{1,0:T(8,128)}, u32[]{:S(2)}) copy-start(f32[512,1536]{1,0:T(8,128)} %copy-done.3) | copy-start | bytes 9437188
  379.1 59.3 %copy-start.45 = (bf16[256,768]{1,0:T(8,128)(2,1)S(1)}, bf16[256,768]{1,0:T(8,128)(2,1)}, u32[]{:S(2)}) copy-start(bf16[256,768]{1,0:T(8,128)(2,1)} %copy-done.44) | copy-start | bytes 1179652
  379.1 59.3 %copy-start.47 = (bf16[256,768]{1,0:T(8,128)(2,1)S(1)}, bf16[256,768]{1,0:T(8,128)(2,1)}, u32[]{:S(2)}) copy-start(bf16[256,768]{1,0:T(8,128)(2,1)} %copy-done.46) | copy-start | bytes 1179652
  441.3 2.5 copy-start.54
  443.8 2.8 copy-start.28
  443.8 2.8 copy-start.55
  449.4 68.5 %copy-start.32 = (bf16[512,768]{1,0:T(8,128)(2,1)S(1)}, bf16[512,768]{1,0:T(8,128)(2,1)}, u32[]{:S(2)}) copy-start(bf16[512,768]{1,0:T(8,128)(2,1)} %copy-done.31) | copy-start | bytes 2359300
  517.9 4.2 copy-start.49
  517.9 4.2 copy-start.50
  671.4 3.1 copy-start.6
  671.4 3.6 copy-start.35
  675.0 4.0 copy-start.37
  (29 other events, 42.6 us)
Sparse Core Ops, SparseCore 0:
  135.8 144.5 all-gather.1
  377.9 128.3 reduce-scatter.1

commit v6 on v5

--- a/solution.py
+++ b/solution.py
@@ -493,7 +493,7 @@
             pltpu.SemaphoreType.DMA((2,)),
         ],
         compiler_params=pltpu.CompilerParams(
-            collective_id=1, has_side_effects=True, vmem_limit_bytes=48 * 1024 * 1024
+            collective_id=1, has_side_effects=True, vmem_limit_bytes=60 * 1024 * 1024
         ),
         cost_estimate=pl.CostEstimate(
             flops=0, bytes_accessed=20 * count * rows * width, transcendentals=0
@@ -991,7 +991,7 @@
         ],
         out_specs=pl.BlockSpec((rows, step), lambda j: (0, j)),
         out_shape=jax.ShapeDtypeStruct((rows, 3 * local), bf16),
-        compiler_params=kernel_params(1, 32),
+        compiler_params=kernel_params(1, 60),
         cost_estimate=pl.CostEstimate(
             flops=2 * rows * width * 3 * local,
             bytes_accessed=2 * (rows * width + 3 * local * (width + rows)),
@@ -1130,7 +1130,7 @@
         in_specs=in_specs,
         out_specs=out_specs,
         out_shape=out_shape,
-        compiler_params=kernel_params(1, 40),
+        compiler_params=kernel_params(1, 60),
         cost_estimate=pl.CostEstimate(
             flops=2 * rows * width * out_width, bytes_accessed=16 * rows * width, transcendentals=0
         ),
@@ -1197,7 +1197,7 @@
         in_specs=in_specs,
         out_specs=out_specs,
         out_shape=out_shape,
-        compiler_params=kernel_params(1, 48),
+        compiler_params=kernel_params(1, 60),
         cost_estimate=pl.CostEstimate(
             flops=2 * rows * width * out_width, bytes_accessed=20 * rows * width, transcendentals=0
         ),
@@ -1267,7 +1267,7 @@
             jax.ShapeDtypeStruct((rows, width), bf16),
         ],
         scratch_shapes=[pltpu.VMEM((block_rows, width), f32)],
-        compiler_params=kernel_params(2, 32),
+        compiler_params=kernel_params(2, 60),
         cost_estimate=pl.CostEstimate(
             flops=rows * 2 * local * (width + 12 * HALF),
             bytes_accessed=20 * rows * local,
@@ -1329,7 +1329,7 @@
             jax.ShapeDtypeStruct((2, micro, HALF, local), bf16),
             jax.ShapeDtypeStruct((2, micro, HALF, local), bf16),
         ],
-        compiler_params=kernel_params(2, 32),
+        compiler_params=kernel_params(2, 60),
         cost_estimate=pl.CostEstimate(
             flops=20 * rows * 3 * HALF * local,
             bytes_accessed=40 * rows * local,
@@ -1378,7 +1378,7 @@
             jax.ShapeDtypeStruct((rows, width), bf16),
         ],
         scratch_shapes=[pltpu.VMEM((block_rows, width), f32)],
-        compiler_params=kernel_params(2, 32),
+        compiler_params=kernel_params(2, 60),
         cost_estimate=pl.CostEstimate(
             flops=rows * 2 * local * (width + 8 * TXT),
             bytes_accessed=16 * rows * local,
@@ -1441,7 +1441,7 @@
             jax.ShapeDtypeStruct((rows, width), bf16),
         ],
         scratch_shapes=[pltpu.VMEM((block_rows, width), f32)],
-        compiler_params=kernel_params(2, 32),
+        compiler_params=kernel_params(2, 60),
         cost_estimate=pl.CostEstimate(
             flops=rows * 2 * local * (width + 20 * TXT),
             bytes_accessed=30 * rows * local,
@@ -1558,7 +1558,7 @@
         jax.ShapeDtypeStruct((rows, width), bf16),
         jax.ShapeDtypeStruct((rows, width), bf16),
     ]
-    params = kernel_params(1, 56)
+    params = kernel_params(1, 60)
     if summed:
         scratch += [pltpu.VMEM((SLOTS, 2, 2, 2, 2, share, step), bf16)]
         scratch += Pieces.scratch(share, step)
@@ -1683,7 +1683,7 @@
             jax.ShapeDtypeStruct((rows, width), bf16),
         ],
         scratch_shapes=[pltpu.VMEM((rows, width), f32)],
-        compiler_params=kernel_params(1, 40),
+        compiler_params=kernel_params(1, 60),
         cost_estimate=pl.CostEstimate(
             flops=12 * rows * width * local,
             bytes_accessed=12 * width * local + 12 * rows * local,
@@ -1910,7 +1910,7 @@
         + Pieces.scratch(share, step)
         + load_scratch([args[place] for place in places]),
         compiler_params=pltpu.CompilerParams(
-            collective_id=which, has_side_effects=True, vmem_limit_bytes=56 * 1024 * 1024
+            collective_id=which, has_side_effects=True, vmem_limit_bytes=60 * 1024 * 1024
         ),
         cost_estimate=pl.CostEstimate(
             flops=8 * rows * width * local, bytes_accessed=40 * rows * width, transcendentals=0
@@ -2133,7 +2133,7 @@
         + Pieces.scratch(share, step)
         + load_scratch([args[place] for place in places]),
         compiler_params=pltpu.CompilerParams(
-            collective_id=which, has_side_effects=True, vmem_limit_bytes=58 * 1024 * 1024
+            collective_id=which, has_side_effects=True, vmem_limit_bytes=60 * 1024 * 1024
         ),
         cost_estimate=pl.CostEstimate(
             flops=8 * rows * width * local, bytes_accessed=40 * rows * width, transcendentals=0

time: 695 us -> 677 us (0.974)
  local copies, waits for them, and re-layouts: 53.1 us -> 27.3 us
    unnamed x122 -> x58, local copies, waits for them, and re-layouts: 35 us -> 11.9 us
  transfers between devices with their start and end apart: 4 -> 4, of which waited for: 2 -> 2; matrix products, arithmetic and copies ran while one was open for 6% -> 6% of each run, Pallas kernels for 49% -> 51%
where the time goes in v6:
time: 677 us; the launch traced here: 670 us
  Pallas kernels  540 us (80%)
  waiting for transfers between devices  55 us (8%)
  local copies, waits for them, and re-layouts  27.3 us (4%)
  matrix products  17 us (3%)
  between operations  15.9 us (2%)
  other arithmetic  13.3 us (2%)
    pallas_call x1, Pallas kernels, finish_stage(): pl.pallas_call(with_loads(functools.partial(finish_kernel, spans=spans, s...  140 us
    pallas_call x1, Pallas kernels, gather_and_prepare(): pl.pallas_call(functools.partial(gather_kernel, pieces=pieces, step=step,...  116 us
    pallas_call x1, Pallas kernels, feed_forward(): pl.pallas_call(functools.partial(ffn_kernel, summed=summed), grid=(steps,...  84.8 us
    pallas_call x1, Pallas kernels, self_stage(): pl.pallas_call(with_loads(functools.partial(self_stage_kernel, spans=span...  66.1 us
    pallas_call x1, Pallas kernels, cross_stage(): pl.pallas_call(with_loads(functools.partial(cross_stage_kernel, spans=spa...  58.4 us
    ppermute x2, waiting for transfers between devices, swap(): lax.ppermute(part, 'tensor', [(i, (i + 1) % count) for i in range(count)])  55 us
    pallas_call x1, Pallas kernels, self_attention(): pl.pallas_call(self_kernel, grid=(micro, pairs), in_specs=self_specs(bloc...  27 us
    pallas_call x1, Pallas kernels, cross_attention(): pl.pallas_call(cross_kernel, grid=(micro, pairs), in_specs=cross_specs(bl...  19.6 us
  transfers between devices with their start and end apart: 4, of which 2 were waited for; matrix products, arithmetic and copies ran while one was open for 6% of the time, Pallas kernels for 51%

profile of v6, /device:TPU:0, one launch (start us, length us, event | category | flops | bytes accessed | tf_op | source)
XLA Modules:
  0.0 670.0 jit_solution(14427621747436016784)
XLA Ops:
  13.1 1.4 slice_bitcast_fusion.1
  17.6 1.3 pad_maximum_fusion.2
  18.9 115.6 %gather_and_prepare.1 = (bf16[2,2,2,2,96,5376]{5,4,3,2,1,0:T(8,128)(2,1)}, bf16[1024,1536]{1,0:T(8,128)(2,1)}, bf16[1536,512]{1,0:T(8,128)(2,1)}, f32[2,2,9216]{...) custom-call(bf16[96,5376]{1,0:T(8,128)(2,1)} %copy-done.5, ...), custom_call_target="tpu_custom_call" | custom-call | bytes 165150720 | tf_op jit(solution)/shard_map/gather_and_prepare/pallas_call | solution.py:463
  134.7 16.7 %qkv_projection.1.q_ref.k_ref.v_ref.refs_7_ = bf16[1024,2304]{1,0:T(8,128)(2,1)} custom-call(bf16[1024,1536]{1,0:T(8,128)(2,1)} %get-tuple-element.61.normed_ref, bf16[1536,5376]{1,0:T(8,128)(2,1)} %bitcast.78, f32[3,1024,128]{2,1,0:T(8,128)} %get-tuple-element.64.table_ref.refs_11_), custom_call_target="tpu_custom_call" | custom-call | flops 7247757312 | bytes 14942208 | tf_op jit(solution)/shard_map/qkv_projection/pallas_call | solution.py:984
  151.4 27.0 %self_attention.1 = (bf16[512,768]{1,0:T(8,128)(2,1)}, f32[512,128]{1,0:T(8,128)}, bf16[512,1536]{1,0:T(8,128)(2,1)}) custom-call(bf16[1024,2304]{1,0:T(8,128)(2,1)} %qkv_projection.1.q_ref.k_ref.v_ref.refs_7_, bf16[1024,2304]{1,0:T(8,128)(2,1)} %qkv_projection.1.q_ref.k_ref.v_ref.refs_7_, bf16[1024,2304]{1,0:T(8,128)(2,1)} %qkv_projection.1.q_ref.k_ref.v_ref.refs_7_, ...), custom_call_target="tpu_custom_call" | custom-call | flops 2415919104 | bytes 7864320 | tf_op jit(solution)/shard_map/self_attention/pallas_call | solution.py:1254
  179.0 1.9 slice.84
  183.0 1.5 fusion.4
  184.8 1.7 convolution_convert_fusion.6.k_ref.refs_7_
  186.5 1.7 convolution_convert_fusion.5.v_ref.refs_8_
  188.2 24.3 %collective-permute-done.refs_2_ = bf16[512,1536]{1,0:T(8,128)(2,1)} collective-permute-done((bf16[512,1536]{1,0:T(8,128)(2,1)}, bf16[512,1536]{1,0:T(8,128)(2,1)}, u32[]{:S(2)}, u32[]{:S(2)}) %collective-permute-start) | collective-permute-done | bytes 1572896 | tf_op jit(solution)/shard_map/ppermute | solution.py:56
  212.5 6.9 %norm_forward.2 = (f32[512,1536]{1,0:T(8,128)}, bf16[512,1536]{1,0:T(8,128)(2,1)}, bf16[1536,512]{1,0:T(8,128)(2,1)}, bf16[512,768]{1,0:T(8,128)(2,1)}) custom-call(bf16[512,1536]{1,0:T(8,128)(2,1)} %bitcast.89, bf16[512,1536]{1,0:T(8,128)(2,1)} %get-tuple-element.66.refs_1_, bf16[512,1536]{1,0:T(8,128)(2,1)} %collective-permute-done.refs_2_, ...), custom_call_target="tpu_custom_call" | custom-call | flops 1207959552 | bytes 12582912 | tf_op jit(solution)/shard_map/norm_forward/pallas_call | solution.py:1127
  219.5 19.6 %cross_attention.1 = (bf16[512,768]{1,0:T(8,128)(2,1)}, f32[512,128]{1,0:T(8,128)}, bf16[512,1536]{1,0:T(8,128)(2,1)}) custom-call(bf16[512,768]{1,0:T(8,128)(2,1)} %get-tuple-element.70.q_ref.refs_6_, bf16[512,768]{1,0:T(8,128)(2,1)} %convolution_convert_fusion.6.k_ref.refs_7_, bf16[512,768]{1,0:T(8,128)(2,1)} %convolution_convert_fusion.5.v_ref.refs_8_, ...), custom_call_target="tpu_custom_call" | custom-call | flops 2013265920 | bytes 6291456 | tf_op jit(solution)/shard_map/cross_attention/pallas_call | solution.py:1365
  240.1 1.6 copy.34.refs_3_
  241.7 30.6 %collective-permute-done.1.refs_2_ = bf16[512,1536]{1,0:T(8,128)(2,1)S(1)} collective-permute-done((bf16[512,1536]{1,0:T(8,128)(2,1)}, bf16[512,1536]{1,0:T(8,128)(2,1)S(1)}, u32[]{:S(2)}, u32[]{:S(2)}) %collective-permute-start.1) | collective-permute-done | bytes 1572896 | tf_op jit(solution)/shard_map/ppermute | solution.py:56
  272.3 1.2 copy-done.4
  273.4 5.0 norm_forward.3
  278.4 84.8 %feed_forward.1 = (bf16[1536,3072]{1,0:T(8,128)(2,1)}, bf16[1536,3072]{1,0:T(8,128)(2,1)}, bf16[1536,768]{1,0:T(8,128)(2,1)}, bf16[512,1536]{1,0:T(8,128)(2,1)},...) custom-call(bf16[512,1536]{1,0:T(8,128)(2,1)} %get-tuple-element.74.refs_0_, bf16[1536,512]{1,0:T(8,128)(2,1)} %get-tuple-element.75.refs_1_, ...), custom_call_target="tpu_custom_call" | custom-call | flops 43486543872 | bytes 56623104 | tf_op jit(solution)/shard_map/feed_forward/pallas_call | solution.py:1574
  363.9 58.4 %cross_stage.1 = (f32[512,1536]{1,0:T(8,128)}, f32[2,2,3072]{2,1,0:T(2,128)}, bf16[1536,512]{1,0:T(8,128)(2,1)}, bf16[512,768]{1,0:T(8,128)(2,1)}, bf16[512,768]...) custom-call(bf16[512,1536]{1,0:T(8,128)(2,1)} %get-tuple-element.80., ...), custom_call_target="tpu_custom_call" | custom-call | flops 4831838208 | bytes 31457280 | tf_op jit(solution)/shard_map/cross_stage/pallas_call | solution.py:1882
  422.3 2.0 convolution_convert_fusion.3
  425.2 1.8 pad_maximum_fusion.refs_4_
  427.6 2.8 convolution_convert_fusion.2
  430.4 2.8 convolution_convert_fusion.1
  433.2 66.1 %self_stage.1 = (f32[512,1536]{1,0:T(8,128)}, f32[2,2,3072]{2,1,0:T(2,128)}, bf16[1536,512]{1,0:T(8,128)(2,1)}, f32[3,512,768]{2,1,0:T(8,128)}, bf16[2,2,128,768...) custom-call(bf16[512,1536]{1,0:T(8,128)(2,1)} %get-tuple-element.88.refs_0_, ...), custom_call_target="tpu_custom_call" | custom-call | flops 4831838208 | bytes 31457280 | tf_op jit(solution)/shard_map/self_stage/pallas_call | solution.py:2097
  499.3 4.2 convolution_convert_fusion
  504.3 139.6 %finish_stage.1 = (f32[96,6912]{1,0:T(8,128)}, f32[512,1536]{1,0:T(8,128)}, f32[16,9216]{1,0:T(8,128)}, f32[1,9216]{1,0:T(1,128)}, bf16[256,1536]{1,0:T(8,128)(2,1)}) custom-call(bf16[2,2,2,2,96,3072]{5,4,3,2,1,0:T(8,128)(2,1)} %bitcast.88, bf16[2,2,2,2,96,768]{5,4,3,2,1,0:T(8,128)(2,1)} %bitcast.96, bf16[2,2,2,2,96,768]{5,4,3,2,1,0:T(8,128)(2,1)} %bitcast.97, ...), custom_call_target="tpu_custom_call" | custom-call | flops 7247757312 | bytes 31457280 | tf_op jit(solution)/shard_map/finish_stage/pallas_call | solution.py:892
  643.9 1.9 copy.40
  646.3 1.5 reduce.3
  648.5 2.8 fusion.2
  653.6 1.6 pad_maximum_fusion.1
  657.3 1.8 add_convert_fusion
  659.0 2.2 convert_bitcast_fusion
  661.2 1.7 copy.49
  (91 shorter events, 20.1 us)
Async XLA Ops:
  7.2 5.6 copy-start.18
  7.2 271.2 %all-gather.2.cloned.1.call-start = ((), (), s32[]{:S(2)}) async-start(), calls=%async_computation.1 | async-start | bytes 30081024 | tf_op jit(solution)/shard_map/all_gather | solution.py:2213
  11.0 3.5 copy-start.14
  13.1 4.5 copy-start.9
  16.5 2.4 copy-start.5
  134.5 524.5 %reduce-scatter.2.cloned.1.call-start = ((), (), s32[]{:S(2)}) async-start(), calls=%async_computation.2 | async-start | bytes 10027008 | tf_op jit(solution)/shard_map/reduce_scatter | solution.py:953
  178.4 2.4 copy-start.17
  178.4 34.1 %collective-permute-start = (bf16[512,1536]{1,0:T(8,128)(2,1)}, bf16[512,1536]{1,0:T(8,128)(2,1)}, u32[]{:S(2)}, u32[]{:S(2)}) collective-permute-start(bf16[512,1536]{1,0:T(8,128)(2,1)} %get-tuple-element.66.refs_1_), channel_id=1, source_target_pairs={{0,1},{1,0},{2,3},{3,2},{4,5},{5,4},{6,7},{7,6},{8,9},{9,8},{10,11... | collective-permute-start | bytes 4718600 | tf_op jit(solution)/shard_map/ppermute | solution.py:56
  184.6 1.9 copy-start.12
  219.5 20.6 %copy-start.2 = (bf16[2,256,1536]{2,1,0:T(8,128)(2,1)S(1)}, bf16[2,256,1536]{2,1,0:T(8,128)(2,1)}, u32[]{:S(2)}) copy-start(bf16[2,256,1536]{2,1,0:T(8,128)(2,1)} %param.30) | copy-start | bytes 4718596
  239.1 33.2 %collective-permute-start.1 = (bf16[512,1536]{1,0:T(8,128)(2,1)}, bf16[512,1536]{1,0:T(8,128)(2,1)S(1)}, u32[]{:S(2)}, u32[]{:S(2)}) collective-permute-start(bf16[512,1536]{1,0:T(8,128)(2,1)} %get-tuple-element.72.refs_1_), channel_id=1, source_target_pairs={{0,1},{1,0},{2,3},{3,2},{4,5},{5,4},{6,7},{7,6},{8,9},{9,8},{10,11... | collective-permute-start | bytes 4718600 | tf_op jit(solution)/shard_map/ppermute | solution.py:56
  272.3 1.2 copy-start.4
  363.9 58.4 %copy-start.13 = (bf16[256,768]{1,0:T(8,128)(2,1)S(1)}, bf16[256,768]{1,0:T(8,128)(2,1)}, u32[]{:S(2)}) copy-start(bf16[256,768]{1,0:T(8,128)(2,1)} %copy-done.12) | copy-start | bytes 1179652
  422.3 2.0 copy-start.24
  425.2 1.8 copy-start.20
  425.2 2.5 copy-start.22
  427.6 2.8 copy-start.19
  427.6 2.8 copy-start.23
  433.2 66.1 %copy-start.21 = (bf16[512,768]{1,0:T(8,128)(2,1)S(1)}, bf16[512,768]{1,0:T(8,128)(2,1)}, u32[]{:S(2)}) copy-start(bf16[512,768]{1,0:T(8,128)(2,1)} %get-tuple-element.93) | copy-start | bytes 2359300
  499.3 4.2 copy-start.15
  499.3 4.2 copy-start.16
  651.3 1.5 copy-start.6
  652.3 1.1 copy-start.10
  652.3 1.2 copy-start.11
  653.5 1.8 copy-start.7
  653.5 1.8 copy-start.8
  653.6 2.7 copy-start
  653.6 3.6 copy-start.1
  657.3 4.0 copy-start.3
Sparse Core Ops, SparseCore 0:
  134.6 143.4 all-gather.1
  363.3 127.5 reduce-scatter.1

commit v7 on v6

--- a/solution.py
+++ b/solution.py
@@ -1924,16 +1924,17 @@
 
 def self_stage_kernel(
     back_ref, got_early_ref, up_ref, hidden_ref, two_ref, later_ref, weight_ref, qkv_ref, bias_ref,
-    log_ref, other_ref, *refs,
+    log_ref, other_ref, mixed_one_ref, two_low_t_ref, mixed_two_ref, two_t_ref, dq_ref, *refs,
     spans, step, micro, ready, seq_count, loaded,
 ):
     sources, refs = refs[: len(spans)], refs[len(spans) :]
     (
-        grad_ref, sums_ref, low_t_ref, own_ref, from_low_ref, from_high_ref, got_other_ref, out_ref,
+        grad_ref, sums_ref, own_ref, from_low_ref, from_high_ref, got_other_ref, out_ref,
+        g_cross_out_ref, g_cross_query_ref, g_self_out_ref,
         own_sem, got_ref, mixed_ref, to_low_ref, to_high_ref, out_w_ref, weight_sem, swap_sem,
-        halo_send, halo_recv,
-    ) = refs[:18]
-    refs = refs[18:]
+        halo_send, halo_recv, low_t_ref, product_ref, product_sem,
+    ) = refs[:23]
+    refs = refs[23:]
     me = lax.axis_index("seq")
     mine = lax.axis_index("tensor")
     digits = seq_digits(me)
@@ -2033,6 +2034,20 @@
                 own_ref[1 + kind, span, at] = held[kind][part + 1]
             to_high_ref[m, kind, :, at] = held[kind][parts + 1].astype(bf16)
 
+    products = (
+        (two_low_t_ref, mixed_two_ref, g_cross_out_ref),
+        (two_t_ref, dq_ref, g_cross_query_ref),
+        (low_t_ref, mixed_one_ref, g_self_out_ref),
+    )
+
+    def put(k):
+        return pltpu.make_async_copy(product_ref.at[k], products[k][2], product_sem.at[k])
+
+    def product_unit(k):
+        left, right, _ = products[k]
+        product_ref[k] = nn(left[...], right[...]).astype(bf16)
+        put(k).start()
+
     def close(m):
         pl.when(has_low)(lambda: to_low(m).start())
         pl.when(has_high)(lambda: to_high(m).start())
@@ -2054,6 +2069,9 @@
         work.append((begin, begin + pairs // 2, pair_units))
         spot += pairs // 2
         work.append((spot - 1, spot, lambda t, m=m: close(m)))
+    for k in range(len(products)):
+        work.append((spot, spot + 1, lambda t, k=k: product_unit(k)))
+        spot += 1
     over_tensor().start()
     over_other().start()
 
@@ -2068,6 +2086,8 @@
     pieces.run(sources, spans, own_sem, work, spot)
     over_tensor().wait_send()
     over_other().wait()
+    for k in range(len(products)):
+        put(k).wait()
     for m in range(micro):
 
         @pl.when(has_low)
@@ -2082,7 +2102,7 @@
 
 
 def self_stage(
-    back, got_early, up, hidden, two, later, qkv, bias, logs, weights, local, other, sources,
+    back, got_early, up, hidden, two, later, qkv, bias, logs, weights, local, other, products, sources,
     spans, micro, which=4, step=256,
 ):
     seq_count = lax.axis_size("seq")
@@ -2091,8 +2111,8 @@
     block_rows = rows // micro
     any_space = pl.BlockSpec(memory_space=pl.ANY)
     vmem = pl.BlockSpec(memory_space=pltpu.VMEM)
-    args = [back, got_early, up, hidden, two, later, weights, qkv, bias, logs, other]
-    places = (1, 2, 3, 4, 5, 7, 8, 9)
+    args = [back, got_early, up, hidden, two, later, weights, qkv, bias, logs, other, *products]
+    places = (1, 2, 3, 4, 5, 7, 8, 9, 11, 12, 13, 14, 15)
     edge = (micro, 2, HALF, local)
     return pl.pallas_call(
         with_loads(
@@ -2109,15 +2129,15 @@
         out_shape=[
             jax.ShapeDtypeStruct((rows, width), f32),
             jax.ShapeDtypeStruct((micro, 2, 2 * width), f32),
-            jax.ShapeDtypeStruct((width, rows), bf16),
             jax.ShapeDtypeStruct((3, rows, local), f32),
             jax.ShapeDtypeStruct(edge, bf16),
             jax.ShapeDtypeStruct(edge, bf16),
             jax.ShapeDtypeStruct((rows - block_rows, width), bf16),
             jax.ShapeDtypeStruct((share, sum(span for _, span in spans)), f32),
-        ],
-        in_specs=[vmem] + [any_space] * (10 + len(spans)),
-        out_specs=[vmem] * 6 + [any_space] * 2,
+        ]
+        + [jax.ShapeDtypeStruct((width, local), bf16)] * 3,
+        in_specs=[vmem] + [any_space] * (15 + len(spans)),
+        out_specs=[vmem] * 5 + [any_space] * 5,
         scratch_shapes=[
             pltpu.SemaphoreType.DMA((SLOTS,)),
             pltpu.VMEM((block_rows, width), bf16),
@@ -2129,6 +2149,9 @@
             pltpu.SemaphoreType.DMA((4,)),
             pltpu.SemaphoreType.DMA((2, micro)),
             pltpu.SemaphoreType.DMA((2, micro)),
+            pltpu.VMEM((width, rows), bf16),
+            pltpu.VMEM((3, width, local), bf16),
+            pltpu.SemaphoreType.DMA((3,)),
         ]
         + Pieces.scratch(share, step)
         + load_scratch([args[place] for place in places]),
@@ -2259,19 +2282,14 @@
         seq_count == 16 and lax.axis_size("tensor") == 2 and (model_width // seq_count) % 16 == 0
     )
 
-    def cross_grads(two_low_t, query_two_low, text_key_low, text_value_low):
-        pair_grad = jnp.concatenate(
+    def pair_grads(text_key_low, text_value_low):
+        return jnp.concatenate(
             [
                 tn(near_context, text_key_low).astype(bf16).reshape(seq_count, share, local),
                 tn(near_context, text_value_low).astype(bf16).reshape(seq_count, share, local),
             ],
             axis=1,
         ).reshape(2 * text_width, local)
-        return [
-            nn(two_low_t, mixed_two).astype(bf16),
-            nn(normed_two_t, query_two_low).astype(bf16),
-            pair_grad,
-        ]
 
     if fused:
         first, second = EARLY_COLUMNS
@@ -2284,14 +2302,15 @@
             cross_bias, logs_two, attn_all, local, [g_gate], ((0, first),), micro,
         )
         (
-            hidden_one_grad, sums_two, one_low_t, own_grads, from_low, from_high, got_last,
-            totals_b,
+            hidden_one_grad, sums_two, own_grads, from_low, from_high, got_last, totals_b,
+            g_cross_out, g_cross_query, g_self_out,
         ) = self_stage(
             back_two, got_early, hidden_two_grad, hidden_one, two, later, qkv, self_bias, logs_one,
-            attn_all, local, out_part, [g_gate], ((first, second),), micro,
-        )
-        crossed = cross_grads(two_low_t, query_two_low, text_key_low, text_value_low)
-        g_self_out = nn(one_low_t, mixed_one).astype(bf16)
+            attn_all, local, out_part,
+            (mixed_one, two_low_t, mixed_two, normed_two_t, query_two_low),
+            [g_gate], ((first, second),), micro,
+        )
+        crossed = [g_cross_out, g_cross_query, pair_grads(text_key_low, text_value_low)]
         sums = jnp.concatenate([sums_two, sums_three], axis=2)
         spans = ((0, g_up.shape[1]),) + ((0, local),) * 4
         sources = [g_up] + crossed + [g_self_out]
@@ -2335,7 +2354,11 @@
         g_qkv, back_one = qkv_back(
             own_grads, from_low, from_high, normed_one_t, attn_all, near_table, micro, block_rows
         )
-        crossed = cross_grads(two_low_t, query_two_low, text_key_low, text_value_low)
+        crossed = [
+            nn(two_low_t, mixed_two).astype(bf16),
+            nn(normed_two_t, query_two_low).astype(bf16),
+            pair_grads(text_key_low, text_value_low),
+        ]
         sums = jnp.concatenate(
             [piece.reshape(micro, 2, 2 * model_width) for piece in (sums_two, sums_three)], axis=2
         )

time: 677 us -> 672 us (level)
  matrix products: 17 us -> 7.21 us
    dot_general x7 -> x4, matrix products: 16 us -> 6.22 us  [dot(): lax.dot_general(a, b, ((dims[0], dims[1]), ((), ())), preferred_element_t...]
    pallas_call x1, Pallas kernels: 66.1 us -> 75.1 us  [self_stage(): pl.pallas_call(with_loads(functools.partial(self_stage_kernel, spans=span...]
  transfers between devices with their start and end apart: 4 -> 4, of which waited for: 2 -> 2; matrix products, arithmetic and copies ran while one was open for 6% -> 4% of each run, Pallas kernels for 51% -> 52%
where the time goes in v7:
time: 672 us; the launch traced here: 665 us
  Pallas kernels  544 us (81%)
  waiting for transfers between devices  55 us (8%)
  local copies, waits for them, and re-layouts  26.6 us (4%)
  between operations  15.9 us (2%)
  other arithmetic  14 us (2%)
  matrix products  7.21 us (1%)
    pallas_call x1, Pallas kernels, finish_stage(): pl.pallas_call(with_loads(functools.partial(finish_kernel, spans=spans, s...  135 us
    pallas_call x1, Pallas kernels, gather_and_prepare(): pl.pallas_call(functools.partial(gather_kernel, pieces=pieces, step=step,...  116 us
    pallas_call x1, Pallas kernels, feed_forward(): pl.pallas_call(functools.partial(ffn_kernel, summed=summed), grid=(steps,...  84.8 us
    pallas_call x1, Pallas kernels, self_stage(): pl.pallas_call(with_loads(functools.partial(self_stage_kernel, spans=span...  75.1 us
    pallas_call x1, Pallas kernels, cross_stage(): pl.pallas_call(with_loads(functools.partial(cross_stage_kernel, spans=spa...  58.6 us
    ppermute x2, waiting for transfers between devices, swap(): lax.ppermute(part, 'tensor', [(i, (i + 1) % count) for i in range(count)])  55 us
    pallas_call x1, Pallas kernels, self_attention(): pl.pallas_call(self_kernel, grid=(micro, pairs), in_specs=self_specs(bloc...  27 us
    pallas_call x1, Pallas kernels, cross_attention(): pl.pallas_call(cross_kernel, grid=(micro, pairs), in_specs=cross_specs(bl...  19.6 us
  transfers between devices with their start and end apart: 4, of which 2 were waited for; matrix products, arithmetic and copies ran while one was open for 4% of the time, Pallas kernels for 52%

profile of v7, /device:TPU:0, one launch (start us, length us, event | category | flops | bytes accessed | tf_op | source)
XLA Modules:
  0.0 664.9 jit_solution(17962805212514745689)
XLA Ops:
  13.1 1.4 slice_bitcast_fusion.1
  16.6 1.0 convolution_add_fusion.part_ref
  17.6 1.3 pad_maximum_fusion.2
  18.9 115.5 %gather_and_prepare.1 = (bf16[2,2,2,2,96,5376]{5,4,3,2,1,0:T(8,128)(2,1)}, bf16[1024,1536]{1,0:T(8,128)(2,1)}, bf16[1536,512]{1,0:T(8,128)(2,1)}, f32[2,2,9216]{...) custom-call(bf16[96,5376]{1,0:T(8,128)(2,1)} %copy-done.5, ...), custom_call_target="tpu_custom_call" | custom-call | bytes 165150720 | tf_op jit(solution)/shard_map/gather_and_prepare/pallas_call | solution.py:463
  134.7 16.7 %qkv_projection.1.q_ref.k_ref.v_ref.refs_7_ = bf16[1024,2304]{1,0:T(8,128)(2,1)} custom-call(bf16[1024,1536]{1,0:T(8,128)(2,1)} %get-tuple-element.63.normed_ref, bf16[1536,5376]{1,0:T(8,128)(2,1)} %bitcast.72, f32[3,1024,128]{2,1,0:T(8,128)} %get-tuple-element.66.table_ref.refs_11_), custom_call_target="tpu_custom_call" | custom-call | flops 7247757312 | bytes 14942208 | tf_op jit(solution)/shard_map/qkv_projection/pallas_call | solution.py:984
  151.4 27.0 %self_attention.1 = (bf16[512,768]{1,0:T(8,128)(2,1)}, f32[512,128]{1,0:T(8,128)}, bf16[512,1536]{1,0:T(8,128)(2,1)}) custom-call(bf16[1024,2304]{1,0:T(8,128)(2,1)} %qkv_projection.1.q_ref.k_ref.v_ref.refs_7_, bf16[1024,2304]{1,0:T(8,128)(2,1)} %qkv_projection.1.q_ref.k_ref.v_ref.refs_7_, bf16[1024,2304]{1,0:T(8,128)(2,1)} %qkv_projection.1.q_ref.k_ref.v_ref.refs_7_, ...), custom_call_target="tpu_custom_call" | custom-call | flops 2415919104 | bytes 7864320 | tf_op jit(solution)/shard_map/self_attention/pallas_call | solution.py:1254
  179.0 1.9 slice.84
  183.0 1.5 fusion.4
  184.8 1.7 convolution_convert_fusion.3.k_ref.refs_7_
  186.5 1.7 convolution_convert_fusion.2.v_ref.refs_8_
  188.2 24.3 %collective-permute-done.refs_2_ = bf16[512,1536]{1,0:T(8,128)(2,1)} collective-permute-done((bf16[512,1536]{1,0:T(8,128)(2,1)}, bf16[512,1536]{1,0:T(8,128)(2,1)}, u32[]{:S(2)}, u32[]{:S(2)}) %collective-permute-start) | collective-permute-done | bytes 1572896 | tf_op jit(solution)/shard_map/ppermute | solution.py:56
  212.5 6.9 %norm_forward.2 = (f32[512,1536]{1,0:T(8,128)}, bf16[512,1536]{1,0:T(8,128)(2,1)}, bf16[1536,512]{1,0:T(8,128)(2,1)}, bf16[512,768]{1,0:T(8,128)(2,1)}) custom-call(bf16[512,1536]{1,0:T(8,128)(2,1)} %bitcast.83, bf16[512,1536]{1,0:T(8,128)(2,1)} %get-tuple-element.68.refs_1_, bf16[512,1536]{1,0:T(8,128)(2,1)} %collective-permute-done.refs_2_, ...), custom_call_target="tpu_custom_call" | custom-call | flops 1207959552 | bytes 12582912 | tf_op jit(solution)/shard_map/norm_forward/pallas_call | solution.py:1127
  219.5 19.6 %cross_attention.1 = (bf16[512,768]{1,0:T(8,128)(2,1)}, f32[512,128]{1,0:T(8,128)}, bf16[512,1536]{1,0:T(8,128)(2,1)}) custom-call(bf16[512,768]{1,0:T(8,128)(2,1)} %get-tuple-element.72.q_ref.refs_6_, bf16[512,768]{1,0:T(8,128)(2,1)} %convolution_convert_fusion.3.k_ref.refs_7_, bf16[512,768]{1,0:T(8,128)(2,1)} %convolution_convert_fusion.2.v_ref.refs_8_, ...), custom_call_target="tpu_custom_call" | custom-call | flops 2013265920 | bytes 6291456 | tf_op jit(solution)/shard_map/cross_attention/pallas_call | solution.py:1365
  240.0 1.6 copy.34.refs_3_
  241.6 30.7 %collective-permute-done.1.refs_2_ = bf16[512,1536]{1,0:T(8,128)(2,1)S(1)} collective-permute-done((bf16[512,1536]{1,0:T(8,128)(2,1)}, bf16[512,1536]{1,0:T(8,128)(2,1)S(1)}, u32[]{:S(2)}, u32[]{:S(2)}) %collective-permute-start.1) | collective-permute-done | bytes 1572896 | tf_op jit(solution)/shard_map/ppermute | solution.py:56
  272.3 1.2 copy-done.4
  273.4 5.0 norm_forward.3
  278.4 84.8 %feed_forward.1 = (bf16[1536,3072]{1,0:T(8,128)(2,1)}, bf16[1536,3072]{1,0:T(8,128)(2,1)}, bf16[1536,768]{1,0:T(8,128)(2,1)}, bf16[512,1536]{1,0:T(8,128)(2,1)},...) custom-call(bf16[512,1536]{1,0:T(8,128)(2,1)} %get-tuple-element.76.refs_0_, bf16[1536,512]{1,0:T(8,128)(2,1)} %get-tuple-element.77.refs_1_, ...), custom_call_target="tpu_custom_call" | custom-call | flops 43486543872 | bytes 56623104 | tf_op jit(solution)/shard_map/feed_forward/pallas_call | solution.py:1574
  363.9 58.6 %cross_stage.1 = (f32[512,1536]{1,0:T(8,128)}, f32[2,2,3072]{2,1,0:T(2,128)}, bf16[1536,512]{1,0:T(8,128)(2,1)}, bf16[512,768]{1,0:T(8,128)(2,1)}, bf16[512,768]...) custom-call(bf16[512,1536]{1,0:T(8,128)(2,1)} %get-tuple-element.82., ...), custom_call_target="tpu_custom_call" | custom-call | flops 4831838208 | bytes 31457280 | tf_op jit(solution)/shard_map/cross_stage/pallas_call | solution.py:1882
  422.5 2.0 convolution_convert_fusion
  425.3 1.7 pad_maximum_fusion.refs_4_
  427.0 75.1 %self_stage.1 = (f32[512,1536]{1,0:T(8,128)}, f32[2,2,3072]{2,1,0:T(2,128)}, f32[3,512,768]{2,1,0:T(8,128)}, bf16[2,2,128,768]{3,2,1,0:T(8,128)(2,1)}, bf16[2,2,...) custom-call(bf16[512,1536]{1,0:T(8,128)(2,1)} %get-tuple-element.84., ...), custom_call_target="tpu_custom_call" | custom-call | flops 4831838208 | bytes 31457280 | tf_op jit(solution)/shard_map/self_stage/pallas_call | solution.py:2117
  502.0 1.5 pad_maximum_fusion.5.refs_16_
  503.5 135.3 %finish_stage.1 = (f32[96,6912]{1,0:T(8,128)}, f32[512,1536]{1,0:T(8,128)}, f32[16,9216]{1,0:T(8,128)}, f32[1,9216]{1,0:T(1,128)}, bf16[256,1536]{1,0:T(8,128)(2,1)}) custom-call(bf16[2,2,2,2,96,3072]{5,4,3,2,1,0:T(8,128)(2,1)} %bitcast.82, bf16[2,2,2,2,96,768]{5,4,3,2,1,0:T(8,128)(2,1)} %bitcast.90, bf16[2,2,2,2,96,768]{5,4,3,2,1,0:T(8,128)(2,1)} %bitcast.91, ...), custom_call_target="tpu_custom_call" | custom-call | flops 7247757312 | bytes 31457280 | tf_op jit(solution)/shard_map/finish_stage/pallas_call | solution.py:892
  638.9 1.9 copy.40
  641.3 1.5 reduce.3
  643.5 2.8 fusion.2
  648.6 1.6 pad_maximum_fusion.1
  650.3 1.0 copy-done
  652.2 1.8 add_convert_fusion
  654.0 2.2 convert_bitcast_fusion
  656.2 1.7 copy.49
  (76 shorter events, 16.7 us)
Async XLA Ops:
  7.2 5.6 copy-start.17
  7.2 271.2 %all-gather.2.cloned.1.call-start = ((), (), s32[]{:S(2)}) async-start(), calls=%async_computation.1 | async-start | bytes 30081024 | tf_op jit(solution)/shard_map/all_gather | solution.py:2236
  11.0 3.5 copy-start.14
  13.1 4.5 copy-start.9
  16.5 2.4 copy-start.5
  134.5 519.6 %reduce-scatter.2.cloned.1.call-start = ((), (), s32[]{:S(2)}) async-start(), calls=%async_computation.2 | async-start | bytes 10027008 | tf_op jit(solution)/shard_map/reduce_scatter | solution.py:953
  178.4 2.4 copy-start.16
  178.4 34.1 %collective-permute-start = (bf16[512,1536]{1,0:T(8,128)(2,1)}, bf16[512,1536]{1,0:T(8,128)(2,1)}, u32[]{:S(2)}, u32[]{:S(2)}) collective-permute-start(bf16[512,1536]{1,0:T(8,128)(2,1)} %get-tuple-element.68.refs_1_), channel_id=1, source_target_pairs={{0,1},{1,0},{2,3},{3,2},{4,5},{5,4},{6,7},{7,6},{8,9},{9,8},{10,11... | collective-permute-start | bytes 4718600 | tf_op jit(solution)/shard_map/ppermute | solution.py:56
  184.6 1.9 copy-start.12
  219.4 20.6 %copy-start.2 = (bf16[2,256,1536]{2,1,0:T(8,128)(2,1)S(1)}, bf16[2,256,1536]{2,1,0:T(8,128)(2,1)}, u32[]{:S(2)}) copy-start(bf16[2,256,1536]{2,1,0:T(8,128)(2,1)} %param.30) | copy-start | bytes 4718596
  239.1 33.2 %collective-permute-start.1 = (bf16[512,1536]{1,0:T(8,128)(2,1)}, bf16[512,1536]{1,0:T(8,128)(2,1)S(1)}, u32[]{:S(2)}, u32[]{:S(2)}) collective-permute-start(bf16[512,1536]{1,0:T(8,128)(2,1)} %get-tuple-element.74.refs_1_), channel_id=1, source_target_pairs={{0,1},{1,0},{2,3},{3,2},{4,5},{5,4},{6,7},{7,6},{8,9},{9,8},{10,11... | collective-permute-start | bytes 4718600 | tf_op jit(solution)/shard_map/ppermute | solution.py:56
  272.3 1.2 copy-start.4
  363.9 58.6 %copy-start.13 = (bf16[256,768]{1,0:T(8,128)(2,1)S(1)}, bf16[256,768]{1,0:T(8,128)(2,1)}, u32[]{:S(2)}) copy-start(bf16[256,768]{1,0:T(8,128)(2,1)} %copy-done.12) | copy-start | bytes 1179652
  422.5 2.0 copy-start.18
  427.0 75.1 %copy-start.15 = (f32[2,2,3072]{2,1,0:T(2,128)S(1)}, f32[2,2,3072]{2,1,0:T(2,128)}, u32[]{:S(2)}) copy-start(f32[2,2,3072]{2,1,0:T(2,128)} %get-tuple-element.104) | copy-start | bytes 147460
  646.3 1.5 copy-start.6
  647.3 1.1 copy-start.10
  647.3 1.2 copy-start.11
  648.5 1.8 copy-start.7
  648.5 1.8 copy-start.8
  648.6 2.7 copy-start
  648.6 3.6 copy-start.1
  652.2 4.0 copy-start.3
Sparse Core Ops, SparseCore 0:
  134.6 143.4 all-gather.1
  363.3 129.3 reduce-scatter.1
